TPU v7x, 32 devices: a whole 2x2x4 slice. The times are simulated.
32 devices in a mesh: dp: 2 (over x), ctx: 4 (over z), exp: 4 (over y, core).
Axes of the slice: x: 2, y: 2, z: 4, core: 2. Of those that a mesh axis runs over, the one named last changes fastest.
Arguments:
- tokens: bfloat16 [2, 2048, 2048], P('dp', 'ctx'), may hold values from -6 to 6
- routes: int32 [2, 2048, 6], P('dp', 'ctx'), may hold values from 0 to 15, all different within a row; in each aligned block of 128 rows (0 to 127, 128 to 255, ..., all dimensions but the last counted through in order) at most 64 rows name the same one
- norm_attn: bfloat16 [2048], P(('dp', 'ctx')), may hold values from 0.25 to 1.75
- w_query: bfloat16 [2048, 2048], P(('dp', 'ctx'), 'exp'), may hold values from -0.125 to 0.125
- w_key: bfloat16 [2048, 2048], P(('dp', 'ctx'), 'exp'), may hold values from -0.125 to 0.125
- w_value: bfloat16 [2048, 2048], P(('dp', 'ctx'), 'exp'), may hold values from -0.125 to 0.125
- w_out: bfloat16 [2048, 2048], P('exp', ('dp', 'ctx')), may hold values from -2 to 2
- norm_mix: bfloat16 [2048], P(('dp', 'ctx')), may hold values from 0.25 to 1.75
- w_router: bfloat16 [2048, 16], P(('dp', 'ctx')), may hold values from -0.0625 to 0.0625
- shared_gate: bfloat16 [2048, 2816], P(('dp', 'ctx'), 'exp'), may hold values from -0.125 to 0.125
- shared_up: bfloat16 [2048, 2816], P(('dp', 'ctx'), 'exp'), may hold values from -0.125 to 0.125
- shared_down: bfloat16 [2816, 2048], P('exp', ('dp', 'ctx')), may hold values from -0.109375 to 0.109375
- expert_gate: bfloat16 [16, 2048, 1408], P(('ctx', 'exp'), None, 'dp'), may hold values from -0.125 to 0.125
- expert_up: bfloat16 [16, 2048, 1408], P(('ctx', 'exp'), None, 'dp'), may hold values from -0.125 to 0.125
- expert_down: bfloat16 [16, 1408, 2048], P(('ctx', 'exp'), 'dp'), may hold values from -6 to 6
- out_grad: bfloat16 [2, 2048, 2048], P('dp', 'ctx'), may hold values from -6 to 6
Outputs:
- mixed: bfloat16 [2, 2048, 2048], P('dp', 'ctx')
- tokens_grad: bfloat16 [2, 2048, 2048], P('dp', 'ctx')
- norm_attn_grad: float32 [2048], P(('dp', 'ctx'))
- w_query_grad: float32 [2048, 2048], P(('dp', 'ctx'), 'exp')
- w_key_grad: float32 [2048, 2048], P(('dp', 'ctx'), 'exp')
- w_value_grad: float32 [2048, 2048], P(('dp', 'ctx'), 'exp')
- w_out_grad: float32 [2048, 2048], P('exp', ('dp', 'ctx'))
- norm_mix_grad: float32 [2048], P(('dp', 'ctx'))
- w_router_grad: float32 [2048, 16], P(('dp', 'ctx'))
- shared_gate_grad: float32 [2048, 2816], P(('dp', 'ctx'), 'exp')
- shared_up_grad: float32 [2048, 2816], P(('dp', 'ctx'), 'exp')
- shared_down_grad: float32 [2816, 2048], P('exp', ('dp', 'ctx'))
- expert_gate_grad: float32 [16, 2048, 1408], P(('ctx', 'exp'), None, 'dp')
- expert_up_grad: float32 [16, 2048, 1408], P(('ctx', 'exp'), None, 'dp')
- expert_down_grad: float32 [16, 1408, 2048], P(('ctx', 'exp'), 'dp')
Inputs may be any that keep to these rules, and one draw needn't show every extreme that they name: `routes`: A token names 6 different experts. Within each aligned group of 128 tokens of a sequence no expert is named more than 64 times, and in every draw some expert is named exactly 64 times in some group.
All inputs are finite; a program needn't handle non-finite values.
Results may differ from a plain program's by a relative error of at most 0.025.
Values may be sent and summed in bfloat16 or wider, within the bound.
A program may use at most 320 MiB of HBM per device.

v0:
```python
import jax
import jax.numpy as jnp
from jax import lax
from jax.sharding import PartitionSpec as P

HDIM = 128
TOPK = 6


EPSILON = 1e-06
MASKED = -1e30
HIGHEST = lax.Precision.HIGHEST


def rms_scale(values, gain_row):
    return (
        values * lax.rsqrt(jnp.mean(values * values, axis=-1, keepdims=True) + EPSILON) * gain_row
    )


def rope_tables(positions, rope_width):
    inverse = 10000.0 ** (-jnp.arange(rope_width // 2).astype(jnp.float32) * 2.0 / rope_width)
    angles = positions.astype(jnp.float32)[:, None] * inverse[None, :]
    return (jnp.cos(angles), jnp.sin(angles))


def rotate(values, cosine, sine_table):
    half_size = values.shape[-1] // 2
    first_half = values[..., :half_size]
    second = values[..., half_size:]
    cosine = cosine[:, None, :]
    sine_table = sine_table[:, None, :]
    return jnp.concatenate(
        [first_half * cosine - second * sine_table, second * cosine + first_half * sine_table],
        axis=-1,
    )


def silu_mix(gate_rows, up_rows):
    return jax.nn.silu(gate_rows) * up_rows


def product(left_side, right_side):
    return jnp.dot(left_side, right_side, preferred_element_type=jnp.float32)


def transposed_left(left_side, right_side):
    return lax.dot_general(
        left_side, right_side, (((0,), (0,)), ((), ())), preferred_element_type=jnp.float32
    )


def transposed_right(left_side, right_side):
    return lax.dot_general(
        left_side, right_side, (((1,), (1,)), ((), ())), preferred_element_type=jnp.float32
    )


def place_rows(part, start_row, total_rows):
    blank = jnp.zeros((total_rows, part.shape[1]), jnp.float32)
    return lax.dynamic_update_slice_in_dim(blank, part, start_row, 0)


def to_owners(buffer):
    copies = lax.axis_size("dp")
    widened = jnp.broadcast_to(buffer[None], (copies,) + buffer.shape)
    widened = widened.reshape((copies * buffer.shape[0],) + buffer.shape[1:])
    return lax.all_to_all(widened, ("dp", "ctx", "exp"), split_axis=0, concat_axis=0, tiled=True)


def values_home(partial_value):
    returned = lax.all_to_all(
        partial_value, ("dp", "ctx", "exp"), split_axis=0, concat_axis=0, tiled=True
    )
    grouped = returned.reshape((lax.axis_size("dp"), -1) + returned.shape[1:])
    return jnp.sum(grouped.astype(jnp.float32), axis=0).astype(jnp.bfloat16)


def grads_home(partial_value):
    returned = lax.all_to_all(
        partial_value.astype(jnp.bfloat16),
        ("dp", "ctx", "exp"),
        split_axis=0,
        concat_axis=0,
        tiled=True,
    ).astype(partial_value.dtype)
    grouped = returned.reshape((lax.axis_size("dp"), -1) + returned.shape[1:])
    return jnp.sum(grouped, axis=0)


def body(
    tokens,
    routes,
    norm_attn,
    w_query,
    w_key,
    w_value,
    w_out,
    norm_mix,
    w_router,
    shared_gate,
    shared_up,
    shared_down,
    expert_gate,
    expert_up,
    expert_down,
    out_grad,
):
    gathered = (
        lax.all_gather(norm_attn, ("dp", "ctx"), axis=0, tiled=True),
        lax.all_gather(w_query, ("dp", "ctx"), axis=0, tiled=True),
        lax.all_gather(w_key, ("dp", "ctx"), axis=0, tiled=True),
        lax.all_gather(w_value, ("dp", "ctx"), axis=0, tiled=True),
        lax.all_gather(w_out, ("dp", "ctx"), axis=1, tiled=True),
        lax.all_gather(norm_mix, ("dp", "ctx"), axis=0, tiled=True),
        lax.all_gather(w_router, ("dp", "ctx"), axis=0, tiled=True),
        lax.all_gather(shared_gate, ("dp", "ctx"), axis=0, tiled=True),
        lax.all_gather(shared_up, ("dp", "ctx"), axis=0, tiled=True),
        lax.all_gather(shared_down, ("dp", "ctx"), axis=1, tiled=True),
    )
    (
        attention_gain,
        query_matrix,
        key_matrix,
        value_matrix,
        output_matrix,
        mixer_gain,
        router_matrix,
        shared_gate_matrix,
        shared_up_matrix,
        shared_down_matrix,
    ) = gathered
    rows_here = tokens.shape[1]
    model_width = tokens.shape[2]
    heads_here = query_matrix.shape[1] // HDIM
    quarter = rows_here // lax.axis_size("exp")
    start_row = lax.axis_index("exp") * quarter
    layer_input = tokens[0].astype(jnp.float32)
    grad_rows = out_grad[0]
    grad_float = grad_rows.astype(jnp.float32)
    seq_length = rows_here * lax.axis_size("ctx")
    positions = lax.axis_index("ctx") * rows_here + jnp.arange(rows_here, dtype=jnp.int32)
    cosine, sine_table = rope_tables(positions, HDIM)
    visible = positions[:, None] >= jnp.arange(seq_length, dtype=jnp.int32)[None, :]
    scale = HDIM ** (-0.5)
    head_shape = (rows_here, heads_here, HDIM)
    normed = rms_scale(layer_input, attention_gain).astype(jnp.bfloat16)
    query_rot = rotate(
        product(normed, query_matrix).reshape(head_shape), cosine, sine_table
    ).astype(jnp.bfloat16)
    key_rot = (
        rotate(product(normed, key_matrix).reshape(head_shape), cosine, sine_table)
        .astype(jnp.bfloat16)
        .reshape(rows_here, -1)
    )
    value_low = product(normed, value_matrix).astype(jnp.bfloat16)
    key_all, value_all = (
        lax.all_gather(key_rot, "ctx", axis=0, tiled=True),
        lax.all_gather(value_low, "ctx", axis=0, tiled=True),
    )
    key_heads = key_all.reshape(seq_length, heads_here, HDIM)
    value_heads = value_all.reshape(seq_length, heads_here, HDIM)

    def attention_scores():
        scores = (
            jnp.einsum("qhd,khd->hqk", query_rot, key_heads, preferred_element_type=jnp.float32)
            * scale
        )
        return jnp.where(visible[None], scores, MASKED)

    scores = attention_scores()
    largest = jnp.max(scores, axis=-1, keepdims=True)
    log_total = largest + jnp.log(jnp.sum(jnp.exp(scores - largest), axis=-1, keepdims=True))
    weights_low = jnp.exp(scores - log_total).astype(jnp.bfloat16)
    heads_out = (
        jnp.einsum("hqk,khd->qhd", weights_low, value_heads, preferred_element_type=jnp.float32)
        .reshape(rows_here, -1)
        .astype(jnp.bfloat16)
    )
    attn_total = lax.psum(product(heads_out, output_matrix), "exp")
    middle = layer_input + attn_total
    normed_mix = rms_scale(middle, mixer_gain).astype(jnp.bfloat16)
    normed_quarter = lax.dynamic_slice_in_dim(normed_mix, start_row, quarter, 0)
    route_quarter = lax.dynamic_slice_in_dim(routes[0], start_row, quarter, 0)
    grad_quarter = lax.dynamic_slice_in_dim(grad_rows, start_row, quarter, 0)
    logits = product(normed_quarter, router_matrix)
    probabilities = jax.nn.softmax(logits, axis=-1)
    owners = lax.axis_size(("ctx", "exp"))
    local_experts = expert_gate.shape[0]
    experts = local_experts * owners
    capacity = max(quarter * TOPK * 4 // (3 * experts), 2)
    expert_choice_index = jnp.arange(experts, dtype=jnp.int32)
    chosen = (route_quarter[:, :, None] == expert_choice_index[None, None, :]).astype(jnp.float32)
    gates = jnp.sum(chosen * probabilities[:, None, :], axis=-1)
    route_flat = route_quarter.reshape(-1)
    expert_hits = (route_flat[:, None] == expert_choice_index[None, :]).astype(jnp.int32)
    slot_index = jnp.sum(jnp.cumsum(expert_hits, axis=0) * expert_hits, axis=1) - 1
    slot_place = route_flat * capacity + slot_index
    matches = (
        jnp.arange(experts * capacity, dtype=jnp.int32)[:, None] == slot_place[None, :]
    ).astype(jnp.float32)
    dispatch = jnp.sum(matches.reshape(experts * capacity, quarter, TOPK), axis=2).astype(
        jnp.bfloat16
    )
    slot_gates = jnp.dot(matches, gates.reshape(-1), precision=HIGHEST)
    buffer_shape = (owners, local_experts, capacity, model_width)
    outgoing = product(dispatch, normed_quarter).astype(jnp.bfloat16).reshape(buffer_shape)
    arrived = to_owners(outgoing)
    gate_hidden = jnp.einsum(
        "sicd,idf->sicf", arrived, expert_gate, preferred_element_type=jnp.float32
    )
    up_hidden = jnp.einsum("sicd,idf->sicf", arrived, expert_up, preferred_element_type=jnp.float32)
    expert_act = silu_mix(gate_hidden, up_hidden).astype(jnp.bfloat16)
    partial_value = jnp.einsum(
        "sicf,ifd->sicd", expert_act, expert_down, preferred_element_type=jnp.float32
    ).astype(jnp.bfloat16)
    expert_values = values_home(partial_value).reshape(experts * capacity, model_width)
    route_values = expert_values[slot_place].astype(jnp.float32).reshape(quarter, TOPK, model_width)
    combined = jnp.sum(route_values * gates[:, :, None], axis=1)
    shared_gate_rows = product(normed_mix, shared_gate_matrix)
    shared_up_rows = product(normed_mix, shared_up_matrix)
    shared_act = silu_mix(shared_gate_rows, shared_up_rows).astype(jnp.bfloat16)
    branch_part = product(shared_act, shared_down_matrix) + place_rows(
        combined, start_row, rows_here
    )
    result = middle + lax.psum(branch_part.astype(jnp.bfloat16), "exp").astype(jnp.float32)
    grad_slots = (
        (product(dispatch, grad_quarter) * slot_gates[:, None])
        .astype(jnp.bfloat16)
        .reshape(buffer_shape)
    )
    grad_arrived = to_owners(grad_slots)
    act_grad = jnp.einsum(
        "sicd,ifd->sicf", grad_arrived, expert_down, preferred_element_type=jnp.float32
    )
    down_grad = jnp.einsum(
        "sicf,sicd->ifd", expert_act, grad_arrived, preferred_element_type=jnp.float32
    )
    _, mix_back = jax.vjp(silu_mix, gate_hidden, up_hidden)
    gate_back, up_back = mix_back(act_grad)
    gate_back = gate_back.astype(jnp.bfloat16)
    up_back = up_back.astype(jnp.bfloat16)
    gate_grad = jnp.einsum("sicd,sicf->idf", arrived, gate_back, preferred_element_type=jnp.float32)
    up_grad = jnp.einsum("sicd,sicf->idf", arrived, up_back, preferred_element_type=jnp.float32)
    input_back = jnp.einsum(
        "sicf,idf->sicd", gate_back, expert_gate, preferred_element_type=jnp.float32
    ) + jnp.einsum("sicf,idf->sicd", up_back, expert_up, preferred_element_type=jnp.float32)
    rows_back = grads_home(input_back).reshape(experts * capacity, model_width)
    moe_back = jnp.sum(rows_back[slot_place].reshape(quarter, TOPK, model_width), axis=1)
    gate_route_back = jnp.sum(route_values * grad_quarter.astype(jnp.float32)[:, None, :], axis=-1)
    prob_back = jnp.sum(chosen * gate_route_back[:, :, None], axis=1)
    _, soft_back = jax.vjp(lambda values: jax.nn.softmax(values, axis=-1), logits)
    logit_back = soft_back(prob_back)[0].astype(jnp.bfloat16)
    router_term = transposed_left(normed_quarter, logit_back)
    shared_back = transposed_right(grad_rows, shared_down_matrix)
    _, shared_mix_back = jax.vjp(silu_mix, shared_gate_rows, shared_up_rows)
    sgate_back, sup_back = shared_mix_back(shared_back)
    sgate_back = sgate_back.astype(jnp.bfloat16)
    sup_back = sup_back.astype(jnp.bfloat16)
    quarter_back = transposed_right(logit_back, router_matrix) + moe_back
    mix_part = (
        transposed_right(sgate_back, shared_gate_matrix)
        + transposed_right(sup_back, shared_up_matrix)
        + place_rows(quarter_back, start_row, rows_here)
    )
    mix_total, router_grad = (
        lax.psum(mix_part.astype(jnp.bfloat16), "exp").astype(jnp.float32),
        lax.psum(router_term.astype(jnp.bfloat16), "exp").astype(jnp.float32),
    )
    _, norm_mix_back = jax.vjp(rms_scale, middle, mixer_gain.astype(jnp.float32))
    middle_norm_back, gain_mix_grad = norm_mix_back(mix_total)
    middle_grad = grad_float + middle_norm_back
    sdown_grad = transposed_left(shared_act, grad_rows)
    sgate_grad = transposed_left(normed_mix, sgate_back)
    sup_grad = transposed_left(normed_mix, sup_back)
    attn_back = middle_grad.astype(jnp.bfloat16)
    heads_back = transposed_right(attn_back, output_matrix).astype(jnp.bfloat16).reshape(head_shape)
    weights_full = jnp.exp(attention_scores() - log_total)
    weights_again = weights_full.astype(jnp.bfloat16)
    weight_back = jnp.einsum(
        "qhd,khd->hqk", heads_back, value_heads, preferred_element_type=jnp.float32
    )
    value_term = jnp.einsum(
        "hqk,qhd->khd", weights_again, heads_back, preferred_element_type=jnp.float32
    ).reshape(seq_length, -1)
    score_back = (
        weights_full * (weight_back - jnp.sum(weights_full * weight_back, axis=-1, keepdims=True))
    ).astype(jnp.bfloat16)
    query_rot_back = (
        jnp.einsum("hqk,khd->qhd", score_back, key_heads, preferred_element_type=jnp.float32)
        * scale
    )
    key_term = (
        jnp.einsum("hqk,qhd->khd", score_back, query_rot, preferred_element_type=jnp.float32)
        * scale
    ).reshape(seq_length, -1)
    key_sum, value_sum = (
        lax.psum_scatter(
            key_term.astype(jnp.bfloat16), "ctx", scatter_dimension=0, tiled=True
        ).astype(jnp.float32),
        lax.psum_scatter(
            value_term.astype(jnp.bfloat16), "ctx", scatter_dimension=0, tiled=True
        ).astype(jnp.float32),
    )
    _, rotate_back = jax.vjp(
        lambda values: rotate(values, cosine, sine_table), jnp.zeros(head_shape, jnp.float32)
    )
    query_low = rotate_back(query_rot_back)[0].reshape(rows_here, -1).astype(jnp.bfloat16)
    key_low = (
        rotate_back(key_sum.reshape(head_shape))[0].reshape(rows_here, -1).astype(jnp.bfloat16)
    )
    value_back_low = value_sum.astype(jnp.bfloat16)
    normed_part = (
        transposed_right(query_low, query_matrix)
        + transposed_right(key_low, key_matrix)
        + transposed_right(value_back_low, value_matrix)
    )
    normed_back = lax.psum(normed_part.astype(jnp.bfloat16), "exp").astype(jnp.float32)
    _, norm_attn_back = jax.vjp(rms_scale, layer_input, attention_gain.astype(jnp.float32))
    input_norm_back, gain_attn_grad = norm_attn_back(normed_back)
    tokens_back = (middle_grad + input_norm_back).astype(jnp.bfloat16)
    out_weight_grad = transposed_left(heads_out, attn_back)
    query_grad = transposed_left(normed, query_low)
    key_grad = transposed_left(normed, key_low)
    value_grad = transposed_left(normed, value_back_low)
    all_sums = (
        lax.psum_scatter(
            gain_attn_grad.astype(jnp.bfloat16), ("dp", "ctx"), scatter_dimension=0, tiled=True
        ).astype(jnp.float32),
        lax.psum_scatter(
            query_grad.astype(jnp.bfloat16), ("dp", "ctx"), scatter_dimension=0, tiled=True
        ).astype(jnp.float32),
        lax.psum_scatter(
            key_grad.astype(jnp.bfloat16), ("dp", "ctx"), scatter_dimension=0, tiled=True
        ).astype(jnp.float32),
        lax.psum_scatter(
            value_grad.astype(jnp.bfloat16), ("dp", "ctx"), scatter_dimension=0, tiled=True
        ).astype(jnp.float32),
        lax.psum_scatter(
            out_weight_grad.astype(jnp.bfloat16), ("dp", "ctx"), scatter_dimension=1, tiled=True
        ).astype(jnp.float32),
        lax.psum_scatter(
            gain_mix_grad.astype(jnp.bfloat16), ("dp", "ctx"), scatter_dimension=0, tiled=True
        ).astype(jnp.float32),
        lax.psum_scatter(
            router_grad.astype(jnp.bfloat16), ("dp", "ctx"), scatter_dimension=0, tiled=True
        ).astype(jnp.float32),
        lax.psum_scatter(
            sgate_grad.astype(jnp.bfloat16), ("dp", "ctx"), scatter_dimension=0, tiled=True
        ).astype(jnp.float32),
        lax.psum_scatter(
            sup_grad.astype(jnp.bfloat16), ("dp", "ctx"), scatter_dimension=0, tiled=True
        ).astype(jnp.float32),
        lax.psum_scatter(
            sdown_grad.astype(jnp.bfloat16), ("dp", "ctx"), scatter_dimension=1, tiled=True
        ).astype(jnp.float32),
    )
    (
        gain_attn_sum,
        query_sum,
        key_sum_out,
        value_sum_out,
        out_sum,
        gain_mix_sum,
        router_sum,
        sgate_sum,
        sup_sum,
        sdown_sum,
    ) = all_sums
    return (
        result.astype(jnp.bfloat16)[None],
        tokens_back[None],
        gain_attn_sum,
        query_sum,
        key_sum_out,
        value_sum_out,
        out_sum,
        gain_mix_sum,
        router_sum,
        sgate_sum,
        sup_sum,
        sdown_sum,
        gate_grad,
        up_grad,
        down_grad,
    )


def solution(mesh):
    in_specs = (
        P("dp", "ctx", None),
        P("dp", "ctx", None),
        P(("dp", "ctx")),
        P(("dp", "ctx"), "exp"),
        P(("dp", "ctx"), "exp"),
        P(("dp", "ctx"), "exp"),
        P("exp", ("dp", "ctx")),
        P(("dp", "ctx")),
        P(("dp", "ctx"), None),
        P(("dp", "ctx"), "exp"),
        P(("dp", "ctx"), "exp"),
        P("exp", ("dp", "ctx")),
        P(("ctx", "exp"), None, "dp"),
        P(("ctx", "exp"), None, "dp"),
        P(("ctx", "exp"), "dp", None),
        P("dp", "ctx", None),
    )
    out_specs = (
        P("dp", "ctx", None),
        P("dp", "ctx", None),
        P(("dp", "ctx")),
        P(("dp", "ctx"), "exp"),
        P(("dp", "ctx"), "exp"),
        P(("dp", "ctx"), "exp"),
        P("exp", ("dp", "ctx")),
        P(("dp", "ctx")),
        P(("dp", "ctx"), None),
        P(("dp", "ctx"), "exp"),
        P(("dp", "ctx"), "exp"),
        P("exp", ("dp", "ctx")),
        P(("ctx", "exp"), None, "dp"),
        P(("ctx", "exp"), None, "dp"),
        P(("ctx", "exp"), "dp", None),
    )
    return jax.shard_map(body, mesh=mesh, in_specs=in_specs, out_specs=out_specs, check_vma=False)
```

profile of v0, /device:TPU:0, one launch (start us, length us, event | category | flops | bytes accessed | tf_op | source)
XLA Modules:
  0.0 2229.1 jit_solution(8501698013247039847)
XLA Ops:
  36.3 25.9 %all-gather.18.cloned.1.call-done = bf16[2048,512]{1,0:T(8,128)(2,1)} async-done(((bf16[256,512]{1,0:T(8,128)(2,1)}), bf16[2048,512]{1,0:T(8,128)(2,1)}) %all-gather.18.cloned.1.call-update) | async-done | bytes 2097168 | tf_op jit(solution)/shard_map/all_gather | solution.py:112
  66.1 46.0 %all-gather.16.cloned.1.call-done = bf16[2048,512]{1,0:T(8,128)(2,1)} async-done(((bf16[256,512]{1,0:T(8,128)(2,1)}), bf16[2048,512]{1,0:T(8,128)(2,1)}) %all-gather.16.cloned.1.call-update) | async-done | bytes 2097168 | tf_op jit(solution)/shard_map/all_gather | solution.py:111
  122.6 39.5 %all-gather.12.cloned.1.call-done = bf16[2048,512]{1,0:T(8,128)(2,1)} async-done(((bf16[256,512]{1,0:T(8,128)(2,1)}), bf16[2048,512]{1,0:T(8,128)(2,1)}) %all-gather.12.cloned.1.call-update) | async-done | bytes 2097168 | tf_op jit(solution)/shard_map/all_gather | solution.py:113
  168.9 39.6 %all-gather.20.cloned.1.call-done = bf16[2048,512]{0,1:T(8,128)(2,1)} async-done(((bf16[512,512]{0,1:T(8,128)(2,1)}), bf16[2048,512]{0,1:T(8,128)(2,1)}) %all-gather.20.cloned.1.call-update) | async-done | bytes 2097168 | tf_op jit(solution)/shard_map/all_gather | solution.py:158
  220.0 35.0 %all-gather.14.cloned.1.call-done = bf16[2048,512]{1,0:T(8,128)(2,1)} async-done(((bf16[512,512]{1,0:T(8,128)(2,1)}), bf16[2048,512]{1,0:T(8,128)(2,1)}) %all-gather.14.cloned.1.call-update) | async-done | bytes 2097168 | tf_op jit(solution)/shard_map/all_gather | solution.py:159
  264.0 42.8 %all-gather.22.cloned.1.call-done = bf16[512,2048]{1,0:T(8,128)(2,1)} async-done(((bf16[512,256]{1,0:T(8,128)(2,1)}), bf16[512,2048]{1,0:T(8,128)(2,1)}) %all-gather.22.cloned.1.call-update) | async-done | bytes 2097168 | tf_op jit(solution)/shard_map/all_gather | solution.py:114
  332.9 30.8 %all_gather.47 = bf16[2048,16]{0,1:T(8,128)(2,1)S(1)} all-gather(bf16[256,16]{0,1:T(8,128)(2,1)S(1)} %copy-done.66), channel_id=1, replica_groups=mesh['dp'=2,'ctx'=4,'exp'=4] {'dp','ctx'}, dimensions={0}, use_global_device_ids=true | all-gather | bytes 73728 | tf_op jit(solution)/shard_map/all_gather | solution.py:116
  364.1 31.4 %all-reduce.12.cloned.1.call-done = f32[512,2048]{1,0:T(8,128)} async-done(((f32[512,2048]{1,0:T(8,128)}), f32[512,2048]{1,0:T(8,128)}) %all-reduce.12.cloned.1.call-update) | async-done | bytes 4194320 | tf_op jit(solution)/shard_map/psum | solution.py:180
  425.8 180.5 %all-to-all-done.2 = bf16[32,1,64,2048]{3,2,1,0:T(8,128)(2,1)} async-done(((bf16[32,1,64,2048]{3,2,1,0:T(8,128)(2,1)}), bf16[32,1,64,2048]{3,2,1,0:T(8,128)(2,1)}, u32[]{:S(2)}, u32[]{:S(2)}) %all-to-all-start.2) | async-done | bytes 8388640 | tf_op jit(solution)/shard_map/all_to_all | solution.py:68
  629.0 173.0 %all-to-all-done = bf16[32,1,64,2048]{3,2,1,0:T(8,128)(2,1)} async-done(((bf16[32,1,64,2048]{3,2,1,0:T(8,128)(2,1)}), bf16[32,1,64,2048]{3,2,1,0:T(8,128)(2,1)}, u32[]{:S(2)}, u32[]{:S(2)}) %all-to-all-start) | async-done | bytes 8388640 | tf_op jit(solution)/shard_map/all_to_all | solution.py:68
  869.5 193.7 %all-to-all-done.1 = bf16[32,1,64,2048]{3,2,1,0:T(8,128)(2,1)} async-done(((bf16[32,1,64,2048]{3,2,1,0:T(8,128)(2,1)}), bf16[32,1,64,2048]{3,2,1,0:T(8,128)(2,1)}, u32[]{:S(2)}, u32[]{:S(2)}) %all-to-all-start.1) | async-done | bytes 8388640 | tf_op jit(solution)/shard_map/all_to_all | solution.py:72
  1075.3 120.8 %all-gather.24.cloned.1.call-done = bf16[2048,704]{0,1:T(8,128)(2,1)} async-done(((bf16[256,704]{0,1:T(8,128)(2,1)}), bf16[2048,704]{0,1:T(8,128)(2,1)}) %all-gather.24.cloned.1.call-update) | async-done | bytes 2883600 | tf_op jit(solution)/shard_map/all_gather | solution.py:117
  1200.7 98.8 %all-gather.28.cloned.1.call-done = bf16[704,2048]{1,0:T(8,128)(2,1)} async-done(((bf16[704,256]{1,0:T(8,128)(2,1)}), bf16[704,2048]{1,0:T(8,128)(2,1)}) %all-gather.28.cloned.1.call-update) | async-done | bytes 2883600 | tf_op jit(solution)/shard_map/all_gather | solution.py:119
  1385.9 50.5 %all-reduce.14.cloned.1.call-done = bf16[512,2048]{1,0:T(8,128)(2,1)} async-done(((bf16[512,2048]{1,0:T(8,128)(2,1)}), bf16[512,2048]{1,0:T(8,128)(2,1)}) %all-reduce.14.cloned.1.call-update) | async-done | bytes 2097168 | tf_op jit(solution)/shard_map/psum | solution.py:267
  1531.6 35.9 %reduce-scatter.13.cloned.1.call-done = bf16[512,512]{0,1:T(8,128)(2,1)} async-done(((bf16[2048,512]{0,1:T(8,128)(2,1)}), bf16[512,512]{0,1:T(8,128)(2,1)}) %reduce-scatter.13.cloned.1.call-update) | async-done | bytes 524304 | tf_op jit(solution)/shard_map/reduce_scatter | solution.py:301
  1584.0 58.6 %reduce-scatter.27.cloned.1.call-done = bf16[704,256]{1,0:T(8,128)(2,1)} async-done(((bf16[704,2048]{1,0:T(8,128)(2,1)}), bf16[704,256]{1,0:T(8,128)(2,1)}) %reduce-scatter.27.cloned.1.call-update) | async-done | bytes 360464 | tf_op jit(solution)/shard_map/reduce_scatter | solution.py:354
  1644.5 73.0 %reduce-scatter.25.cloned.1.call-done = bf16[256,704]{0,1:T(8,128)(2,1)} async-done(((bf16[2048,704]{0,1:T(8,128)(2,1)}), bf16[256,704]{0,1:T(8,128)(2,1)}) %reduce-scatter.25.cloned.1.call-update) | async-done | bytes 360464 | tf_op jit(solution)/shard_map/reduce_scatter | solution.py:351
  1719.4 73.1 %reduce-scatter.23.cloned.1.call-done = bf16[256,704]{0,1:T(8,128)(2,1)} async-done(((bf16[2048,704]{0,1:T(8,128)(2,1)}), bf16[256,704]{0,1:T(8,128)(2,1)}) %reduce-scatter.23.cloned.1.call-update) | async-done | bytes 360464 | tf_op jit(solution)/shard_map/reduce_scatter | solution.py:348
  1855.6 63.9 %reduce-scatter.21.cloned.1.call-done = bf16[512,256]{1,0:T(8,128)(2,1)} async-done(((bf16[512,2048]{1,0:T(8,128)(2,1)}), bf16[512,256]{1,0:T(8,128)(2,1)}) %reduce-scatter.21.cloned.1.call-update) | async-done | bytes 262160 | tf_op jit(solution)/shard_map/reduce_scatter | solution.py:339
  1921.3 85.9 %all-reduce.16.cloned.1.call-done = (bf16[512,2048]{1,0:T(8,128)(2,1)}, bf16[512,2048]{1,0:T(8,128)(2,1)}) async-done(((bf16[512,2048]{1,0:T(8,128)(2,1)}, bf16[512,2048]{1,0:T(8,128)(2,1)}), (bf16[512,2048]{1,0:T(8,128)(2,1)}, bf16[512,2048]{1,0:T(8,128)(2,1)})) %all-reduce.16.cloned.1.call-update) | async-done | bytes 4194320 | tf_op jit(solution)/shard_map/psum | solution.py:226
  2010.5 22.3 %all-reduce.6 = (bf16[2048]{0:T(1024)(128)(2,1)S(1)}, bf16[2048]{0:T(1024)(128)(2,1)S(1)}) all-reduce(bf16[2048]{0:T(1024)(128)(2,1)S(1)} %get-tuple-element.19, bf16[2048]{0:T(1024)(128)(2,1)S(1)} %get-tuple-element.17), channel_id=4, replica_groups=mesh['dp'=2,'ctx'=4,'exp'=4] {'dp','ctx'}, use_global_device_ids=true, to_apply=%region_28.29.clone | all-reduce | flops 4096 | bytes 16384
  2042.8 36.3 %reduce-scatter.19.cloned.1.call-done = bf16[256,512]{1,0:T(8,128)(2,1)} async-done(((bf16[2048,512]{1,0:T(8,128)(2,1)}), bf16[256,512]{1,0:T(8,128)(2,1)}) %reduce-scatter.19.cloned.1.call-update) | async-done | bytes 262160 | tf_op jit(solution)/shard_map/reduce_scatter | solution.py:336
  2081.0 68.7 %reduce-scatter.15.cloned.1.call-done = bf16[256,512]{1,0:T(8,128)(2,1)} async-done(((bf16[2048,512]{1,0:T(8,128)(2,1)}), bf16[256,512]{1,0:T(8,128)(2,1)}) %reduce-scatter.15.cloned.1.call-update) | async-done | bytes 262160 | tf_op jit(solution)/shard_map/reduce_scatter | solution.py:330
  2151.5 68.7 %reduce-scatter.17.cloned.1.call-done = bf16[256,512]{1,0:T(8,128)(2,1)} async-done(((bf16[2048,512]{1,0:T(8,128)(2,1)}), bf16[256,512]{1,0:T(8,128)(2,1)}) %reduce-scatter.17.cloned.1.call-update) | async-done | bytes 262160 | tf_op jit(solution)/shard_map/reduce_scatter | solution.py:333
  (336 shorter events, 518.0 us)
Async XLA Ops:
  7.9 104.2 %all-gather.16.cloned.1.call-start = ((), (), s32[]{:S(2)}) async-start(), calls=%async_computation.16 | async-start | bytes 2359296 | tf_op jit(solution)/shard_map/all_gather | solution.py:111
  8.7 153.4 %all-gather.12.cloned.1.call-start = ((), (), s32[]{:S(2)}) async-start(), calls=%async_computation.14 | async-start | bytes 2359296 | tf_op jit(solution)/shard_map/all_gather | solution.py:113
  9.4 199.1 %all-gather.20.cloned.1.call-start = ((), (), s32[]{:S(2)}) async-start(), calls=%async_computation.18 | async-start | bytes 2621440 | tf_op jit(solution)/shard_map/all_gather | solution.py:158
  122.6 132.5 %all-gather.14.cloned.1.call-start = ((), (), s32[]{:S(2)}) async-start(), calls=%async_computation.15 | async-start | bytes 2621440 | tf_op jit(solution)/shard_map/all_gather | solution.py:159
  166.4 140.3 %all-gather.22.cloned.1.call-start = ((), (), s32[]{:S(2)}) async-start(), calls=%async_computation.19 | async-start | bytes 2359296 | tf_op jit(solution)/shard_map/all_gather | solution.py:114
  167.0 228.5 %all-reduce.12.cloned.1.call-start = ((), (), s32[]{:S(2)}) async-start(), calls=%async_computation.20 | async-start | bytes 8388608 | tf_op jit(solution)/shard_map/psum | solution.py:180
  416.6 189.6 %all-to-all-start.2 = ((bf16[32,1,64,2048]{3,2,1,0:T(8,128)(2,1)}), bf16[32,1,64,2048]{3,2,1,0:T(8,128)(2,1)}, u32[]{:S(2)}, u32[]{:S(2)}) async-start(bf16[32,1,64,2048]{3,2,1,0:T(8,128)(2,1)} %bitcast.315), calls=%async_computation.2 | async-start | bytes 16777216 | tf_op jit(solution)/shard_map/all_to_all | solution.py:68
  613.1 188.9 %all-to-all-start = ((bf16[32,1,64,2048]{3,2,1,0:T(8,128)(2,1)}), bf16[32,1,64,2048]{3,2,1,0:T(8,128)(2,1)}, u32[]{:S(2)}, u32[]{:S(2)}) async-start(bf16[32,1,64,2048]{3,2,1,0:T(8,128)(2,1)} %bitcast.316), calls=%async_computation | async-start | bytes 16777216 | tf_op jit(solution)/shard_map/all_to_all | solution.py:68
  840.4 222.9 %all-to-all-start.1 = ((bf16[32,1,64,2048]{3,2,1,0:T(8,128)(2,1)}), bf16[32,1,64,2048]{3,2,1,0:T(8,128)(2,1)}, u32[]{:S(2)}, u32[]{:S(2)}) async-start(bf16[32,1,64,2048]{3,2,1,0:T(8,128)(2,1)} %convert_bitcast_fusion), calls=%async_computation.1 | async-start | bytes 16777216 | tf_op jit(solution)/shard_map/all_to_all | solution.py:72
  844.1 226.7 %all-gather.26.cloned.1.call-start = ((), (), s32[]{:S(2)}) async-start(), calls=%async_computation.22 | async-start | bytes 3244032 | tf_op jit(solution)/shard_map/all_gather | solution.py:118
  1063.2 282.1 %all-to-all-start.3 = ((bf16[32,1,64,2048]{3,2,1,0:T(8,128)(2,1)}), bf16[32,1,64,2048]{3,2,1,0:T(8,128)(2,1)}, u32[]{:S(2)}, u32[]{:S(2)}) async-start(bf16[32,1,64,2048]{3,2,1,0:T(8,128)(2,1)} %fusion.2), calls=%async_computation.3 | async-start | bytes 16777216 | tf_op jit(solution)/shard_map/all_to_all | solution.py:80
  1066.9 129.2 %all-gather.24.cloned.1.call-start = ((), (), s32[]{:S(2)}) async-start(), calls=%async_computation.21 | async-start | bytes 3244032 | tf_op jit(solution)/shard_map/all_gather | solution.py:117
  1067.6 231.8 %all-gather.28.cloned.1.call-start = ((), (), s32[]{:S(2)}) async-start(), calls=%async_computation.23 | async-start | bytes 3244032 | tf_op jit(solution)/shard_map/all_gather | solution.py:119
  1068.2 368.1 %all-reduce.14.cloned.1.call-start = ((), (), s32[]{:S(2)}) async-start(), calls=%async_computation.24 | async-start | bytes 4194304 | tf_op jit(solution)/shard_map/psum | solution.py:267
  1385.8 136.0 %reduce-scatter.11.cloned.1.call-start = ((), (), s32[]{:S(2)}) async-start(), calls=%async_computation.25 | async-start | bytes 2621440 | tf_op jit(solution)/shard_map/reduce_scatter | solution.py:298
  1487.9 154.7 %reduce-scatter.27.cloned.1.call-start = ((), (), s32[]{:S(2)}) async-start(), calls=%async_computation.33 | async-start | bytes 3244032 | tf_op jit(solution)/shard_map/reduce_scatter | solution.py:354
  1493.3 224.2 %reduce-scatter.25.cloned.1.call-start = ((), (), s32[]{:S(2)}) async-start(), calls=%async_computation.32 | async-start | bytes 3244032 | tf_op jit(solution)/shard_map/reduce_scatter | solution.py:351
  1496.6 295.9 %reduce-scatter.23.cloned.1.call-start = ((), (), s32[]{:S(2)}) async-start(), calls=%async_computation.31 | async-start | bytes 3244032 | tf_op jit(solution)/shard_map/reduce_scatter | solution.py:348
  1501.3 347.6 %reduce-scatter.29.cloned.1.call-start = ((), (), s32[]{:S(2)}) async-start(), calls=%async_computation.34 | async-start | bytes 73728 | tf_op jit(solution)/shard_map/reduce_scatter | solution.py:345
  1502.2 417.3 %reduce-scatter.21.cloned.1.call-start = ((), (), s32[]{:S(2)}) async-start(), calls=%async_computation.30 | async-start | bytes 2359296 | tf_op jit(solution)/shard_map/reduce_scatter | solution.py:339
  1507.2 500.0 %all-reduce.16.cloned.1.call-start = ((), (), s32[]{:S(2)}) async-start(), calls=%async_computation.35 | async-start | bytes 8388608 | tf_op jit(solution)/shard_map/psum | solution.py:226
  1574.3 504.9 %reduce-scatter.19.cloned.1.call-start = ((), (), s32[]{:S(2)}) async-start(), calls=%async_computation.29 | async-start | bytes 2359296 | tf_op jit(solution)/shard_map/reduce_scatter | solution.py:336
  1579.8 569.9 %reduce-scatter.15.cloned.1.call-start = ((), (), s32[]{:S(2)}) async-start(), calls=%async_computation.27 | async-start | bytes 2359296 | tf_op jit(solution)/shard_map/reduce_scatter | solution.py:330
  1582.7 637.5 %reduce-scatter.17.cloned.1.call-start = ((), (), s32[]{:S(2)}) async-start(), calls=%async_computation.28 | async-start | bytes 2359296 | tf_op jit(solution)/shard_map/reduce_scatter | solution.py:333
  (78 other events, 2791.5 us)
Sparse Core Ops, SparseCore 0:
  10.2 52.0 all-gather.17
  64.3 47.7 all-gather.15
  114.3 47.7 all-gather.11
  164.1 44.4 all-gather.19
  210.5 44.4 all-gather.13
  256.9 49.8 all-gather.21
  311.8 83.6 all-reduce.11
  847.1 126.2 all-gather.25
  1069.9 126.1 all-gather.23
  1198.1 101.2 all-gather.27
  1385.9 50.3 all-reduce.13
  1477.8 43.9 reduce-scatter.10
  1524.2 43.2 reduce-scatter.12
  1570.9 71.6 reduce-scatter.26
  1646.0 71.4 reduce-scatter.24
  1720.9 71.5 reduce-scatter.22
  1796.1 52.7 reduce-scatter.28
  1852.3 67.1 reduce-scatter.20
  1922.5 84.6 all-reduce.15
  2011.0 68.1 reduce-scatter.18
  2083.1 66.5 reduce-scatter.14
  2153.6 66.5 reduce-scatter.16
where the time goes:
time: 2240 us; the launch traced here: 2230 us
  waiting for transfers between devices  1670 us (75%)
  matrix products  245 us (11%)
  other arithmetic  105 us (5%)
  blocking collectives  99.1 us (4%)
  local copies, waits for them, and re-layouts  76.3 us (3%)
    all_to_all x2, waiting for transfers between devices, to_owners(): lax.all_to_all(widened, ('dp', 'ctx', 'exp'), split_axis=0, concat_axis=0...  353 us
    all_to_all x1, waiting for transfers between devices, values_home(): lax.all_to_all(partial_value, ('dp', 'ctx', 'exp'), split_axis=0, concat_...  194 us
    all_gather x1, waiting for transfers between devices, body(): lax.all_gather(shared_gate, ('dp', 'ctx'), axis=0, tiled=True)  121 us
    all_gather x1, waiting for transfers between devices, body(): lax.all_gather(shared_down, ('dp', 'ctx'), axis=1, tiled=True)  98.8 us
    psum x1, waiting for transfers between devices, body(): lax.psum(branch_part.astype(jnp.bfloat16), 'exp').astype(jnp.float32)  85.9 us
    reduce_scatter x1, waiting for transfers between devices, body(): lax.psum_scatter(sgate_grad.astype(jnp.bfloat16), ('dp', 'ctx'), scatter_...  73.1 us
    reduce_scatter x1, waiting for transfers between devices, body(): lax.psum_scatter(sup_grad.astype(jnp.bfloat16), ('dp', 'ctx'), scatter_di...  73 us
    reduce_scatter x1, waiting for transfers between devices, body(): lax.psum_scatter(key_grad.astype(jnp.bfloat16), ('dp', 'ctx'), scatter_di...  68.7 us
  transfers between devices with their start and end apart: 26, of which 24 were waited for; matrix products, arithmetic and copies ran while one was open for 12% of the time, Pallas kernels for 0%

commit v1 on v0

--- a/solution.py
+++ b/solution.py
@@ -1,6 +1,11 @@
+import functools
+
 import jax
 import jax.numpy as jnp
+import numpy as np
 from jax import lax
+from jax.experimental import pallas as pl
+from jax.experimental.pallas import tpu as pltpu
 from jax.sharding import PartitionSpec as P
 
 HDIM = 128
@@ -386,7 +391,717 @@
     )
 
 
+MESH = pl.DeviceIdType.MESH
+BF = jnp.bfloat16
+F32 = jnp.float32
+
+
+class Place:
+    def __init__(self, wide):
+        self.wide = wide
+        self.x = lax.axis_index("dp")
+        self.z = lax.axis_index("ctx")
+        self.e = lax.axis_index("exp")
+        self.y = lax.div(self.e, 2)
+        self.c = lax.rem(self.e, 2)
+        z = self.z
+        high = lax.div(z, 2)
+        self.zs = [z, z + 1 - 2 * lax.rem(z, 2), 2 - high, 3 - 3 * high]
+        self.inner = 3 - z
+        self.inside = lax.div(z * (3 - z), 2)
+        self.middle = self.inside == 1
+        self.dx = 1 - 2 * self.x
+        self.dy = 2 - 4 * self.y
+        self.dc = 1 - 2 * self.c
+
+    def far(self, f, g):
+        if not self.wide:
+            return 0, f * self.dy
+        a, b = (1 - self.c), self.c
+        return (f * a + g * b) * self.dx, (f * b + g * a) * self.dy
+
+    def far_twin(self, f, g):
+        if not self.wide:
+            return 0, f * self.dy
+        a, b = self.c, (1 - self.c)
+        return (f * a + g * b) * self.dx, (f * b + g * a) * self.dy
+
+    def device(self, ox=0, oe=0, zi=0):
+        return (self.x + ox, self.zs[zi], self.e + oe)
+
+    def inward(self):
+        return (self.x, self.inner, self.e)
+
+    def shard(self, ox, oe, zi):
+        rank = self.zs[zi] * 4 + self.e + oe
+        if self.wide:
+            rank = rank + (self.x + ox) * 16
+        return rank
+
+
+def greet(at):
+    barrier = pltpu.get_barrier_semaphore()
+    peers = [at.device(zi=1), at.device(*at.far(1, 0)), at.device(oe=at.dc)]
+    if at.wide:
+        peers.append(at.device(*at.far(0, 1)))
+    for peer in peers:
+        pl.semaphore_signal(barrier, inc=1, device_id=peer, device_id_type=MESH)
+
+    @pl.when(at.middle)
+    def _():
+        pl.semaphore_signal(barrier, inc=1, device_id=at.inward(), device_id_type=MESH)
+
+    pl.semaphore_wait(barrier, len(peers) + at.inside)
+
+
+def gather_kernel(wide, rows, parts, x_ref, out_ref, own_sem, send_sem, recv_sem):
+    at = Place(wide)
+    greet(at)
+    piece = rows // parts
+    kinds = 4 if wide else 2
+    slot_z, slot_f, slot_g, slot_s = 0, 3, 7, 15
+    started, inside = [], []
+
+    def where(f, g, zi, p):
+        ox, oe = at.far(f, g)
+        return pl.ds(pl.multiple_of(at.shard(ox, oe, zi) * rows + p * piece, piece), piece)
+
+    def push(src, dst, slot, p, device, sends=None, record=None):
+        k = slot * parts + p
+        j = k if sends is None else sends * parts + p
+        copy = pltpu.make_async_remote_copy(
+            src_ref=src,
+            dst_ref=out_ref.at[dst],
+            send_sem=send_sem.at[j],
+            recv_sem=recv_sem.at[k],
+            device_id=device,
+            device_id_type=MESH,
+        )
+        copy.start()
+        (started if record is None else record).append(j)
+
+    def gone(j):
+        pltpu.make_async_remote_copy(
+            src_ref=x_ref.at[pl.ds(0, piece)],
+            dst_ref=out_ref.at[pl.ds(0, piece)],
+            send_sem=send_sem.at[j],
+            recv_sem=recv_sem.at[0],
+            device_id=s_dev,
+            device_id_type=MESH,
+        ).wait_send()
+
+    def arrive(slot, p):
+        k = slot * parts + p
+        pltpu.make_async_remote_copy(
+            src_ref=x_ref.at[pl.ds(0, piece)],
+            dst_ref=out_ref.at[pl.ds(0, piece)],
+            send_sem=send_sem.at[k],
+            recv_sem=recv_sem.at[k],
+            device_id=at.device(oe=at.dc),
+            device_id_type=MESH,
+        ).wait_recv()
+
+    f_dev, s_dev, z_dev = at.device(*at.far(1, 0)), at.device(oe=at.dc), at.device(zi=1)
+    g_dev = at.device(*at.far(0, 1)) if wide else None
+    own = pltpu.make_async_copy(
+        x_ref, out_ref.at[pl.ds(pl.multiple_of(at.shard(0, 0, 0) * rows, rows), rows)], own_sem
+    )
+    own.start()
+
+    def source(f, g, zi, p):
+        if (f, g, zi) == (0, 0, 0):
+            return x_ref.at[pl.ds(p * piece, piece)]
+        return out_ref.at[where(f, g, zi, p)]
+
+    def along(zi, p):
+        src, dst = source(0, 0, zi, p), where(0, 0, zi, p)
+        if zi == 0:
+            push(src, dst, slot_z, p, z_dev)
+        if zi < 2:
+            pl.when(at.middle)(
+                lambda: push(src, dst, slot_z + 1 + zi, p, at.inward(), 31 + zi, inside)
+            )
+        else:
+            pl.when(at.middle)(lambda: push(src, dst, slot_z + zi - 1, p, z_dev, 31 + zi, inside))
+
+    def forward(f, g, zi, p):
+        src, dst = source(f, g, zi, p), where(f, g, zi, p)
+        if f == 0 and g == 0:
+            along(zi, p)
+            push(src, dst, slot_f + zi, p, f_dev)
+        if wide and g == 0:
+            push(src, dst, slot_g + f * 4 + zi, p, g_dev)
+        push(src, dst, slot_s + (g * 2 + f) * 4 + zi, p, s_dev)
+
+    for zi in range(4):
+        for p in range(parts):
+            if zi > 0:
+                arrive(slot_z + zi - 1, p)
+            forward(0, 0, zi, p)
+        for p in range(parts):
+            arrive(slot_f + zi, p)
+            forward(1, 0, zi, p)
+    if wide:
+        for f in range(2):
+            for zi in range(4):
+                for p in range(parts):
+                    arrive(slot_g + f * 4 + zi, p)
+                    forward(f, 1, zi, p)
+    for k in range(4 * kinds):
+        for p in range(parts):
+            arrive(slot_s + k, p)
+    own.wait()
+    for j in started:
+        gone(j)
+
+    @pl.when(at.middle)
+    def _():
+        for j in inside:
+            gone(j)
+
+
+def all_rows(x, wide, cid, parts=1):
+    rows, width = x.shape
+    n = 32 if wide else 16
+    return pl.pallas_call(
+        functools.partial(gather_kernel, wide, rows, parts),
+        out_shape=jax.ShapeDtypeStruct((n * rows, width), x.dtype),
+        in_specs=[pl.BlockSpec(memory_space=pl.ANY)],
+        out_specs=pl.BlockSpec(memory_space=pl.ANY),
+        scratch_shapes=[
+            pltpu.SemaphoreType.DMA,
+            pltpu.SemaphoreType.DMA((35 * parts,)),
+            pltpu.SemaphoreType.DMA((31 * parts,)),
+        ],
+        compiler_params=pltpu.CompilerParams(collective_id=cid, has_side_effects=True),
+    )(x)
+
+
+def scatter_kernel(wide, rows, in_ref, out_ref, acc, got_s, got_g, got_f, got_z, load_sem, send_sem, recv_sem):
+    at = Place(wide)
+    greet(at)
+    slot_z, slot_f, slot_g, slot_s = 0, 5, 9, 17
+    f_dev, s_dev, z_dev = at.device(*at.far(1, 0)), at.device(oe=at.dc), at.device(zi=1)
+    g_dev = at.device(*at.far(0, 1)) if wide else None
+    started, in_middle, at_end = [], [], []
+
+    def rows_of(rank):
+        return in_ref.at[pl.ds(pl.multiple_of(rank * rows, rows), rows)]
+
+    def push(src, dst, slot, device, sends=None, record=started):
+        copy = pltpu.make_async_remote_copy(
+            src_ref=src,
+            dst_ref=dst,
+            send_sem=send_sem.at[slot if sends is None else sends],
+            recv_sem=recv_sem.at[slot],
+            device_id=device,
+            device_id_type=MESH,
+        )
+        copy.start()
+        record.append(slot if sends is None else sends)
+
+    def gone(j):
+        pltpu.make_async_remote_copy(
+            src_ref=acc.at[0],
+            dst_ref=acc.at[0],
+            send_sem=send_sem.at[j],
+            recv_sem=recv_sem.at[0],
+            device_id=s_dev,
+            device_id_type=MESH,
+        ).wait_send()
+
+    def arrive(dst, slot):
+        pltpu.make_async_remote_copy(
+            src_ref=acc.at[0],
+            dst_ref=dst,
+            send_sem=send_sem.at[slot],
+            recv_sem=recv_sem.at[slot],
+            device_id=s_dev,
+            device_id_type=MESH,
+        ).wait_recv()
+
+    gs = (1, 0) if wide else (0,)
+    order = [(f, g, zi) for g in gs for f in (1, 0) for zi in (3, 2, 1, 0)]
+    loads = {}
+    for f, g, zi in order:
+        k = (g * 2 + f) * 4 + zi
+        ox, oe = at.far_twin(f, g)
+        push(rows_of(at.shard(ox, oe + at.dc, zi)), got_s.at[k], slot_s + k, s_dev)
+        ox, oe = at.far(f, g)
+        loads[k] = pltpu.make_async_copy(rows_of(at.shard(ox, oe, zi)), acc.at[k], load_sem.at[k])
+        loads[k].start()
+
+    def add(k, *others, into=None):
+        @pl.loop(0, rows // 16)
+        def _(i):
+            span = pl.ds(pl.multiple_of(i * 16, 16), 16)
+            total = acc[k, span, :].astype(F32)
+            for ref, j in others:
+                total = total + ref[j, span, :].astype(F32)
+            if into is None:
+                acc[k, span, :] = total.astype(BF)
+            else:
+                into[span, :] = total
+
+    for f, g, zi in order:
+        k = (g * 2 + f) * 4 + zi
+        arrive(got_s.at[k], slot_s + k)
+        loads[k].wait()
+        others = [(got_s, k)]
+        if g == 1:
+            add(k, *others)
+            push(acc.at[k], got_g.at[f * 4 + zi], slot_g + f * 4 + zi, g_dev)
+            continue
+        if wide:
+            arrive(got_g.at[f * 4 + zi], slot_g + f * 4 + zi)
+            others.append((got_g, f * 4 + zi))
+        if f == 1:
+            add(k, *others)
+            push(acc.at[k], got_f.at[zi], slot_f + zi, f_dev)
+            continue
+        arrive(got_f.at[zi], slot_f + zi)
+        others.append((got_f, zi))
+        if zi >= 2:
+
+            @pl.when(at.middle)
+            def _():
+                arrive(got_z.at[3 - zi], slot_z + 3 - zi)
+                add(k, *others, (got_z, 3 - zi))
+                push(acc.at[k], got_z.at[4 if zi == 2 else 3], slot_z + (4 if zi == 2 else 3), at.inward(), slot_z + zi, in_middle)
+
+            @pl.when(jnp.logical_not(at.middle))
+            def _():
+                add(k, *others)
+                push(acc.at[k], got_z.at[3 - zi], slot_z + 3 - zi, z_dev, slot_z + zi, at_end)
+        elif zi == 1:
+
+            @pl.when(at.middle)
+            def _():
+                arrive(got_z.at[3], slot_z + 3)
+                add(k, *others, (got_z, 3))
+                push(acc.at[k], got_z.at[4], slot_z + 4, z_dev, slot_z + 1, in_middle)
+
+            @pl.when(jnp.logical_not(at.middle))
+            def _():
+                add(k, *others)
+                push(acc.at[k], got_z.at[2], slot_z + 2, z_dev, slot_z + 1, at_end)
+        else:
+
+            @pl.when(at.middle)
+            def _():
+                arrive(got_z.at[2], slot_z + 2)
+                arrive(got_z.at[4], slot_z + 4)
+                add(k, *others, (got_z, 2), (got_z, 4), into=out_ref)
+
+            @pl.when(jnp.logical_not(at.middle))
+            def _():
+                arrive(got_z.at[4], slot_z + 4)
+                add(k, *others, (got_z, 4), into=out_ref)
+
+    for j in started:
+        gone(j)
+
+    @pl.when(at.middle)
+    def _():
+        for j in in_middle:
+            gone(j)
+
+    @pl.when(jnp.logical_not(at.middle))
+    def _():
+        for j in at_end:
+            gone(j)
+
+
+def own_rows(x, wide, cid):
+    n = 32 if wide else 16
+    rows, width = x.shape[0] // n, x.shape[1]
+    half = n // 2
+    return pl.pallas_call(
+        functools.partial(scatter_kernel, wide, rows),
+        out_shape=jax.ShapeDtypeStruct((rows, width), F32),
+        in_specs=[pl.BlockSpec(memory_space=pl.ANY)],
+        out_specs=pl.BlockSpec(memory_space=pltpu.VMEM),
+        scratch_shapes=[
+            pltpu.VMEM((half, rows, width), BF),
+            pltpu.VMEM((half, rows, width), BF),
+            pltpu.VMEM((8, rows, width) if wide else (1, 16, 128), BF),
+            pltpu.VMEM((4, rows, width), BF),
+            pltpu.VMEM((5, rows, width), BF),
+            pltpu.SemaphoreType.DMA((half,)),
+            pltpu.SemaphoreType.DMA((33,)),
+            pltpu.SemaphoreType.DMA((33,)),
+        ],
+        compiler_params=pltpu.CompilerParams(
+            collective_id=cid, has_side_effects=True, vmem_limit_bytes=56 * 1024 * 1024
+        ),
+    )(x)
+
+
+ALL = ("dp", "ctx", "exp")
+DENSE = ("dp", "ctx")
+
+
+def swap(blocks):
+    return lax.all_to_all(blocks, DENSE, split_axis=0, concat_axis=0, tiled=True)
+
+
+def for_heads(matrix):
+    rows = matrix.shape[0]
+    cut = matrix.reshape(rows, 4, HDIM).transpose(1, 0, 2)
+    return jnp.concatenate([cut, cut], axis=0)
+
+
+def attend_kernel(scale, block, q_ref, k_ref, v_ref, out_ref, lse_ref):
+    length = q_ref.shape[0]
+    for i in range(length // block):
+        seen = (i + 1) * block
+        rows = pl.ds(i * block, block)
+        scores = transposed_right(q_ref[rows, :], k_ref[0:seen, :]) * scale
+        row_at = lax.broadcasted_iota(jnp.int32, scores.shape, 0) + i * block
+        col_at = lax.broadcasted_iota(jnp.int32, scores.shape, 1)
+        scores = jnp.where(row_at >= col_at, scores, MASKED)
+        top = jnp.max(scores, axis=-1, keepdims=True)
+        lse = top + jnp.log(jnp.sum(jnp.exp(scores - top), axis=-1, keepdims=True))
+        probs = jnp.exp(scores - lse).astype(BF)
+        out_ref[rows, :] = product(probs, v_ref[0:seen, :]).astype(BF)
+        lse_ref[rows, :] = jnp.broadcast_to(lse, (block, HDIM))
+
+
+def attend(q, k, v):
+    length = q.shape[0]
+    return pl.pallas_call(
+        functools.partial(attend_kernel, HDIM ** (-0.5), 256),
+        out_shape=(
+            jax.ShapeDtypeStruct((length, HDIM), BF),
+            jax.ShapeDtypeStruct((length, HDIM), F32),
+        ),
+        in_specs=[pl.BlockSpec(memory_space=pltpu.VMEM)] * 3,
+        out_specs=(pl.BlockSpec(memory_space=pltpu.VMEM),) * 2,
+        compiler_params=pltpu.CompilerParams(vmem_limit_bytes=56 * 1024 * 1024),
+    )(q, k, v)
+
+
+def attend_back_kernel(scale, block, q_ref, k_ref, v_ref, do_ref, lse_ref, dq_ref, dk_ref, dv_ref):
+    length = q_ref.shape[0]
+    dk_ref[...] = jnp.zeros_like(dk_ref)
+    dv_ref[...] = jnp.zeros_like(dv_ref)
+    for i in range(length // block):
+        seen = (i + 1) * block
+        rows = pl.ds(i * block, block)
+        q = q_ref[rows, :]
+        do = do_ref[rows, :]
+        scores = transposed_right(q, k_ref[0:seen, :]) * scale
+        row_at = lax.broadcasted_iota(jnp.int32, scores.shape, 0) + i * block
+        col_at = lax.broadcasted_iota(jnp.int32, scores.shape, 1)
+        scores = jnp.where(row_at >= col_at, scores, MASKED)
+        probs = jnp.exp(scores - lse_ref[rows, 0:1])
+        weight_back = transposed_right(do, v_ref[0:seen, :])
+        inner = jnp.sum(probs * weight_back, axis=-1, keepdims=True)
+        score_back = (probs * (weight_back - inner)).astype(BF)
+        dv_ref[0:seen, :] += transposed_left(probs.astype(BF), do)
+        dk_ref[0:seen, :] += transposed_left(score_back, q) * scale
+        dq_ref[rows, :] = product(score_back, k_ref[0:seen, :]) * scale
+
+
+def attend_back(q, k, v, do, lse):
+    length = q.shape[0]
+    return pl.pallas_call(
+        functools.partial(attend_back_kernel, HDIM ** (-0.5), 256),
+        out_shape=(jax.ShapeDtypeStruct((length, HDIM), F32),) * 3,
+        in_specs=[pl.BlockSpec(memory_space=pltpu.VMEM)] * 5,
+        out_specs=(pl.BlockSpec(memory_space=pltpu.VMEM),) * 3,
+        compiler_params=pltpu.CompilerParams(vmem_limit_bytes=56 * 1024 * 1024),
+    )(q, k, v, do, lse)
+
+
+def turn_tables(length):
+    inverse = 10000.0 ** (-np.arange(HDIM // 2).astype(np.float64) * 2.0 / HDIM)
+    angles = np.arange(length).astype(np.float64)[:, None] * inverse[None, :]
+    return np.cos(angles).astype(np.float32), np.sin(angles).astype(np.float32)
+
+
+def turn(rows, cosine, sine):
+    a, b = rows[:, : HDIM // 2], rows[:, HDIM // 2 :]
+    return jnp.concatenate([a * cosine - b * sine, b * cosine + a * sine], axis=1)
+
+
+def turn_back(rows, cosine, sine):
+    a, b = rows[:, : HDIM // 2], rows[:, HDIM // 2 :]
+    return jnp.concatenate([a * cosine + b * sine, b * cosine - a * sine], axis=1)
+
+
+def silu_parts(gate, up):
+    s = jax.nn.sigmoid(gate)
+    act = gate * s
+    return act * up, s * (1.0 + gate * (1.0 - s)) * up, act
+
+
+def fast_body(
+    tokens,
+    routes,
+    norm_attn,
+    w_query,
+    w_key,
+    w_value,
+    w_out,
+    norm_mix,
+    w_router,
+    shared_gate,
+    shared_up,
+    shared_down,
+    expert_gate,
+    expert_up,
+    expert_down,
+    out_grad,
+):
+    dp, ctx, exp = lax.axis_index("dp"), lax.axis_index("ctx"), lax.axis_index("exp")
+    rows_here, width = tokens.shape[1], tokens.shape[2]
+    quarter = rows_here // 4
+    group = 8
+    length = rows_here * 4
+    total = length * 2
+    experts = w_router.shape[1]
+    capacity = quarter * TOPK * 4 // (3 * experts)
+    groups = total // quarter
+    dense = w_query.shape[0]
+    hidden = expert_gate.shape[2]
+    cut = shared_gate.shape[1] // group
+    wide = 128
+    start = exp * quarter
+    tokens_own = lax.dynamic_slice_in_dim(tokens[0], start, quarter, 0)
+    dy_own = lax.dynamic_slice_in_dim(out_grad[0], start, quarter, 0)
+
+    named = jnp.any(
+        routes[0][:, :, None] == (jnp.arange(4, dtype=jnp.int32) * 4 + exp)[None, None, :], axis=1
+    )
+    named = named.astype(BF).reshape(dense, 2, 4).transpose(2, 0, 1)
+    named = jnp.concatenate([named, named], axis=0)
+    little = jnp.concatenate([w_router, norm_attn[:, None], norm_mix[:, None]], axis=1)
+    little = jnp.broadcast_to(little[None], (group,) + little.shape)
+    little = jnp.concatenate([little, named], axis=2)
+    little = jnp.pad(little, ((0, 0), (0, 0), (0, wide - little.shape[2])))
+    early = swap(
+        jnp.concatenate([for_heads(w_query), for_heads(w_key), for_heads(w_value), little], axis=2)
+    ).reshape(width, 4 * HDIM)
+    w_qkv = early[:, : 3 * HDIM]
+    little = early[:, 3 * HDIM :]
+    router_matrix = little[:, :experts]
+    attention_gain = little[:, experts].astype(F32)
+    mixer_gain = little[:, experts + 1].astype(F32)
+    hits = little[:, experts + 2 : experts + 4].astype(F32)
+    hits = hits.reshape(group, dense, 2).reshape(groups, quarter)
+
+    def units(matrix):
+        return jnp.pad(
+            matrix.reshape(dense, group, cut).transpose(1, 0, 2), ((0, 0), (0, 0), (0, wide - cut))
+        )
+
+    out_cut = w_out.reshape(4, HDIM, dense)
+    down_cut = jnp.pad(shared_down.reshape(group, cut, dense), ((0, 0), (0, wide - cut), (0, 0)))
+    late = swap(
+        jnp.concatenate(
+            [
+                units(shared_gate),
+                units(shared_up),
+                jnp.concatenate([jnp.concatenate([out_cut, out_cut], axis=0), down_cut], axis=1),
+            ],
+            axis=2,
+        )
+    )
+    shared_in = late[:, :, : 2 * wide].reshape(width, 2 * wide)
+    w_out_head = late[:, :HDIM, 2 * wide :].transpose(1, 0, 2).reshape(HDIM, width)
+    shared_out = late[:, HDIM:, 2 * wide :].transpose(1, 0, 2).reshape(wide, width)
+
+    cosine, sine = turn_tables(length)
+    tokens_all = all_rows(tokens_own, False, 1)
+    normed = rms_scale(tokens_all.astype(F32), attention_gain).astype(BF)
+    qkv = product(normed, w_qkv)
+    query = turn(qkv[:, :HDIM], cosine, sine).astype(BF)
+    key = turn(qkv[:, HDIM : 2 * HDIM], cosine, sine).astype(BF)
+    value = qkv[:, 2 * HDIM :].astype(BF)
+    heads_out, lse = attend(query, key, value)
+    attn = own_rows(product(heads_out, w_out_head).astype(BF), False, 2)
+    middle = tokens_own.astype(F32) + attn
+    normed_own = rms_scale(middle, mixer_gain).astype(BF)
+
+    dy_all = all_rows(dy_own, True, 3)
+    mix_all = all_rows(normed_own, True, 3)
+    logits = product(mix_all, router_matrix)
+    router = jax.nn.softmax(logits, axis=-1)
+    mine = ctx * 4 + exp
+    router_mine = jnp.sum(
+        jnp.where(jnp.arange(experts, dtype=jnp.int32)[None, :] == mine, router, 0.0), axis=1
+    ).reshape(groups, quarter)
+    place = jnp.cumsum(hits, axis=1) - 1.0
+    matches = jnp.where(
+        (jnp.arange(capacity).astype(F32)[None, :, None] == place[:, None, :])
+        & (hits[:, None, :] > 0.5),
+        1.0,
+        0.0,
+    )
+    dispatch = matches.astype(BF)
+    slot_gate = jnp.sum(matches * router_mine[:, None, :], axis=2).reshape(-1, 1)
+
+    def pick(rows):
+        return jnp.einsum(
+            "gst,gtd->gsd",
+            dispatch,
+            rows.reshape(groups, quarter, width),
+            preferred_element_type=F32,
+        ).astype(BF).reshape(groups * capacity, width)
+
+    def spread(rows):
+        return jnp.einsum(
+            "gst,gsd->gtd",
+            dispatch,
+            rows.reshape(groups, capacity, width),
+            preferred_element_type=F32,
+        ).reshape(total, width)
+
+    picked = pick(mix_all)
+    picked_dy = pick(dy_all)
+    gate_hidden = product(picked, expert_gate[0])
+    up_hidden = product(picked, expert_up[0])
+    act, by_gate, by_up = silu_parts(gate_hidden, up_hidden)
+    dy_down = transposed_right(picked_dy, expert_down[0])
+    act_back = slot_gate * dy_down
+    g_back = (act_back * by_gate).astype(BF)
+    u_back = (act_back * by_up).astype(BF)
+    act_low = act.astype(BF)
+    gate_back = jnp.sum(act_low.astype(F32) * dy_down, axis=1)
+    input_back = transposed_right(g_back, expert_gate[0]) + transposed_right(u_back, expert_up[0])
+
+    shared_hidden = product(mix_all, shared_in)
+    shared_act, shared_by_gate, shared_by_up = silu_parts(
+        shared_hidden[:, :wide], shared_hidden[:, wide:]
+    )
+    shared_act = shared_act.astype(BF)
+    shared_back = transposed_right(dy_all, shared_out)
+    shared_gu_back = jnp.concatenate(
+        [(shared_back * shared_by_gate).astype(BF), (shared_back * shared_by_up).astype(BF)], axis=1
+    )
+    mix_part = (
+        transposed_right(shared_gu_back, shared_in) + spread(input_back.astype(BF))
+    ).astype(BF)
+    mix_back = own_rows(mix_part, True, 4)
+
+    gate_back_tokens = jnp.sum(
+        dispatch.astype(F32) * gate_back.reshape(groups, capacity, 1), axis=1
+    ).reshape(1, total)
+    gate_back_all = lax.all_gather(gate_back_tokens, ALL, axis=0, tiled=True)
+    gate_back_all = jnp.sum(gate_back_all.reshape(2, experts, total), axis=0).T
+    logit_back = (
+        router * (gate_back_all - jnp.sum(router * gate_back_all, axis=-1, keepdims=True))
+    ).astype(BF)
+    rank = (dp * 4 + ctx) * 4 + exp
+    logit_back_own = lax.dynamic_slice_in_dim(logit_back, rank * quarter, quarter, 0)
+    mix_columns = lax.dynamic_slice_in_dim(mix_all, (dp * 4 + ctx) * dense, dense, 1)
+    router_grad = transposed_left(mix_columns, logit_back)
+
+    half_out = product(act_low, expert_down[0])
+    mixed_part = (
+        product(shared_act, shared_out) + spread((half_out * slot_gate).astype(BF))
+    ).astype(BF)
+    mixed_own = (middle + own_rows(mixed_part, True, 4)).astype(BF)
+
+    gate_grad = transposed_left(picked, g_back)[None]
+    up_grad = transposed_left(picked, u_back)[None]
+    down_grad = transposed_left((act * slot_gate).astype(BF), picked_dy)[None]
+    shared_gu_grad = transposed_left(mix_all, shared_gu_back).astype(BF)
+    shared_down_part = transposed_left(shared_act, dy_all).astype(BF)
+
+    mix_back = mix_back + transposed_right(logit_back_own, router_matrix)
+    _, norm_mix_back = jax.vjp(rms_scale, middle, mixer_gain)
+    middle_norm_back, gain_mix_part = norm_mix_back(mix_back)
+    middle_back = dy_own.astype(F32) + middle_norm_back
+    attn_back = middle_back.astype(BF)
+    attn_back_all = all_rows(attn_back, False, 1)
+    heads_back = transposed_right(attn_back_all, w_out_head).astype(BF)
+    out_part = transposed_left(heads_out, attn_back_all).astype(BF)
+    dq, dk, dv = attend_back(query, key, value, heads_back, lse)
+    qkv_back = jnp.concatenate(
+        [
+            turn_back(dq, cosine, sine).astype(BF),
+            turn_back(dk, cosine, sine).astype(BF),
+            dv.astype(BF),
+        ],
+        axis=1,
+    )
+    normed_back = own_rows(transposed_right(qkv_back, w_qkv).astype(BF), False, 2)
+    qkv_part = transposed_left(normed, qkv_back).astype(BF)
+    _, norm_attn_back = jax.vjp(rms_scale, tokens_own.astype(F32), attention_gain)
+    input_norm_back, gain_attn_part = norm_attn_back(normed_back)
+    tokens_back_own = (middle_back + input_norm_back).astype(BF)
+
+    tokens_back = lax.all_gather(tokens_back_own, "exp", axis=0, tiled=True)
+    mixed = lax.all_gather(mixed_own, "exp", axis=0, tiled=True)
+    gains = jnp.stack([gain_attn_part, gain_mix_part], axis=0)
+    gains = gains.reshape(2, group, 1, dense).transpose(1, 2, 0, 3)
+    gains = jnp.broadcast_to(gains, (group, 4, 2, dense)).reshape(32, 2 * dense)
+    gains = lax.all_to_all(gains, ALL, split_axis=0, concat_axis=0, tiled=True)
+    gains = jnp.sum(gains, axis=0)
+    dense_parts = swap(
+        jnp.concatenate(
+            [
+                qkv_part.reshape(group, dense, 3 * HDIM),
+                shared_gu_grad.reshape(group, dense, 2 * wide),
+                jnp.concatenate(
+                    [
+                        out_part.reshape(HDIM, group, dense).transpose(1, 0, 2),
+                        shared_down_part.reshape(wide, group, dense).transpose(1, 0, 2),
+                    ],
+                    axis=1,
+                ),
+            ],
+            axis=2,
+        )
+    ).astype(F32)
+
+    def head_columns(parts):
+        summed = parts[:4] + parts[4:]
+        return summed.transpose(1, 0, 2).reshape(dense, 4 * HDIM)
+
+    def unit_columns(parts):
+        return parts[:, :, :cut].transpose(1, 0, 2).reshape(dense, group * cut)
+
+    query_grad = head_columns(dense_parts[:, :, :HDIM])
+    key_grad = head_columns(dense_parts[:, :, HDIM : 2 * HDIM])
+    value_grad = head_columns(dense_parts[:, :, 2 * HDIM : 3 * HDIM])
+    base = 3 * HDIM
+    sgate_grad = unit_columns(dense_parts[:, :, base : base + wide])
+    sup_grad = unit_columns(dense_parts[:, :, base + wide : base + 2 * wide])
+    base = base + 2 * wide
+    out_blocks = dense_parts[:, :HDIM, base:]
+    out_grad_weights = (out_blocks[:4] + out_blocks[4:]).reshape(4 * HDIM, dense)
+    sdown_grad = dense_parts[:, HDIM : HDIM + cut, base:].reshape(group * cut, dense)
+    return (
+        mixed[None],
+        tokens_back[None],
+        gains[:dense],
+        query_grad,
+        key_grad,
+        value_grad,
+        out_grad_weights,
+        gains[dense:],
+        router_grad,
+        sgate_grad,
+        sup_grad,
+        sdown_grad,
+        gate_grad,
+        up_grad,
+        down_grad,
+    )
+
+
 def solution(mesh):
+    sizes = dict(mesh.shape)
+
+    def chosen(*args):
+        heads = args[3].shape[1] * sizes["exp"] // HDIM
+        one_head_each = heads == sizes["ctx"] * sizes["exp"]
+        built_for = (sizes["dp"], sizes["ctx"], sizes["exp"]) == (2, 4, 4)
+        return fast_body(*args) if one_head_each and built_for else body(*args)
+
     in_specs = (
         P("dp", "ctx", None),
         P("dp", "ctx", None),
@@ -422,4 +1137,4 @@
         P(("ctx", "exp"), None, "dp"),
         P(("ctx", "exp"), "dp", None),
     )
-    return jax.shard_map(body, mesh=mesh, in_specs=in_specs, out_specs=out_specs, check_vma=False)
+    return jax.shard_map(chosen, mesh=mesh, in_specs=in_specs, out_specs=out_specs, check_vma=False)

time: 2240 us -> 1210 us (0.54)
  waiting for transfers between devices: 1670 us -> 89.9 us
  Pallas kernels: 0 us -> 638 us
  blocking collectives: 99.1 us -> 41.6 us
  other arithmetic: 105 us -> 55.9 us
  matrix products: 245 us -> 285 us
    pallas_call x0 -> x10, Pallas kernels: none -> 638 us  [the longest x4 311 us: all_rows(): pl.pallas_call(functools.partial(gather_kernel, wide, rows, parts), out_s...]
    reduce_scatter x10 -> x0, waiting for transfers between devices: 501 us -> none  [the longest x1 73.1 us: body(): lax.psum_scatter(sgate_grad.astype(jnp.bfloat16), ('dp', 'ctx'), scatter_...]
    all_to_all x4, waiting for transfers between devices: 547 us -> 89.4 us  [the longest x3 89.4 us: swap(): lax.all_to_all(blocks, DENSE, split_axis=0, concat_axis=0, tiled=True)]
    all_gather x9 -> x2, waiting for transfers between devices: 448 us -> 0.01 us  [the longest x1 0.01 us: fast_body(): tokens_back = lax.all_gather(tokens_back_own, 'exp', axis=0, tiled=True)]
    psum x3 -> x0, waiting for transfers between devices: 168 us -> none  [the longest x1 85.9 us: body(): lax.psum(branch_part.astype(jnp.bfloat16), 'exp').astype(jnp.float32)]
    dot_general x16 -> x4, matrix products: 152 us -> 55.5 us  [the longest x2 32.6 us: spread(): jnp.einsum('gst,gsd->gtd', dispatch, rows.reshape(groups, capacity, width...]
    dot_general x8, matrix products: 29.5 us -> 87.9 us  [transposed_right(): lax.dot_general(left_side, right_side, (((1,), (1,)), ((), ())), preferre...]
    dot_general x10 -> x8, matrix products: 35.5 us -> 83.9 us  [product(): return jnp.dot(left_side, right_side, preferred_element_type=jnp.float32)]
  transfers between devices with their start and end apart: 26 -> 6, of which waited for: 24 -> 2; matrix products, arithmetic and copies ran while one was open for 12% -> 10% of each run, Pallas kernels for 0% -> 22%
where the time goes in v1:
time: 1210 us; the launch traced here: 1200 us
  Pallas kernels  638 us (53%)
  matrix products  285 us (24%)
  waiting for transfers between devices  89.9 us (7%)
  other arithmetic  55.9 us (5%)
  local copies, waits for them, and re-layouts  54.1 us (4%)
  blocking collectives  41.6 us (3%)
  starting transfers between devices  19.8 us (2%)
  between operations  15.5 us (1%)
    pallas_call x4, Pallas kernels, all_rows(): pl.pallas_call(functools.partial(gather_kernel, wide, rows, parts), out_s...  311 us
    pallas_call x4, Pallas kernels, own_rows(): pl.pallas_call(functools.partial(scatter_kernel, wide, rows), out_shape=j...  306 us
    all_to_all x3, waiting for transfers between devices, swap(): lax.all_to_all(blocks, DENSE, split_axis=0, concat_axis=0, tiled=True)  89.4 us
    dot_general x8, matrix products, transposed_right(): lax.dot_general(left_side, right_side, (((1,), (1,)), ((), ())), preferre...  87.9 us
    dot_general x8, matrix products, product(): return jnp.dot(left_side, right_side, preferred_element_type=jnp.float32)  83.9 us
    dot_general x8, matrix products, transposed_left(): lax.dot_general(left_side, right_side, (((0,), (0,)), ((), ())), preferre...  57.7 us
    all_gather x1, blocking collectives, fast_body(): gate_back_all = lax.all_gather(gate_back_tokens, ALL, axis=0, tiled=True)  41.6 us
    dot_general x2, matrix products, spread(): jnp.einsum('gst,gsd->gtd', dispatch, rows.reshape(groups, capacity, width...  32.6 us
  transfers between devices with their start and end apart: 6, of which 2 were waited for; matrix products, arithmetic and copies ran while one was open for 10% of the time, Pallas kernels for 22%

profile of v1, /device:TPU:0, one launch (start us, length us, event | category | flops | bytes accessed | tf_op | source)
XLA Modules:
  0.0 1200.0 jit_solution(11843350011888844849)
XLA Ops:
  34.3 43.1 %all-to-all-done = bf16[8,256,512]{1,2,0:T(8,128)(2,1)} async-done(((bf16[8,256,512]{1,2,0:T(8,128)(2,1)}), bf16[8,256,512]{1,2,0:T(8,128)(2,1)}, u32[]{:S(2)}, u32[]{:S(2)}) %all-to-all-start) | async-done | bytes 2097184 | tf_op jit(solution)/shard_map/all_to_all | solution.py:745
  83.7 91.5 %shard_map.289 = bf16[2048,2048]{1,0:T(8,128)(2,1)} custom-call(bf16[128,2048]{1,0:T(8,128)(2,1)} %get-tuple-element.34.x_ref), custom_call_target="tpu_custom_call" | custom-call | tf_op jit(solution)/shard_map/pallas_call | solution.py:566
  177.1 80.8 %shard_map.294 = bf16[4096,2048]{1,0:T(8,128)(2,1)} custom-call(bf16[128,2048]{1,0:T(8,128)(2,1)} %dynamic-slice_bitcast_fusion.x_ref), custom_call_target="tpu_custom_call" | custom-call | tf_op jit(solution)/shard_map/pallas_call | solution.py:566
  305.4 59.6 %shard_map.291 = f32[128,2048]{1,0:T(8,128)} custom-call(bf16[2048,2048]{1,0:T(8,128)(2,1)} %convolution_convert_fusion.1.in_ref), custom_call_target="tpu_custom_call" | custom-call | tf_op jit(solution)/shard_map/pallas_call | solution.py:719
  368.5 76.8 %shard_map.292 = bf16[4096,2048]{1,0:T(8,128)(2,1)} custom-call(bf16[128,2048]{1,0:T(8,128)(2,1)} %multiply_convert_fusion.9.x_ref), custom_call_target="tpu_custom_call" | custom-call | tf_op jit(solution)/shard_map/pallas_call | solution.py:566
  457.8 12.6 %fusion.98 = f32[4096,256]{0,1:T(8,128)} fusion(bf16[4096,2048]{1,0:T(8,128)(2,1)} %shard_map.292, bf16[2048,256]{1,0:T(8,128)(2,1)} %bitcast.198), kind=kOutput, calls=%fused_computation.197 | convolution fusion | flops 4294967296 | bytes 22020096 | tf_op jit(solution)/shard_map/dot_general | solution.py:49
  470.4 11.5 convolution_convert_fusion.3
  499.7 11.5 convolution_convert_fusion.2
  511.2 13.2 %multiply_reduce_fusion = (f32[2048]{0:T(1024)S(1)}, bf16[2048,704]{0,1:T(8,128)(2,1)}, f32[2048,704]{0,1:T(8,128)}) fusion(f32[2048,704]{0,1:T(8,128)S(1)} %fusion.16, f32[2048,704]{0,1:T(8,128)} %fusion.20, bf16[2048,2048]{1,0:T(8,128)(2,1)} %bitcast.178, bf16[1,704,2048]{2,1,0:T(8,128)(2,1)S(1)} %copy-done), kind=kOutput, calls=%fused_computation.16 | convolution fusion | flops 5918554112 | bytes 31465472 | tf_op jit(solution)/shard_map/dot_general | solution.py:59
  524.8 41.6 %all-gather = f32[32,1,4096]{2,1,0:T(1,128)S(1)} all-gather(f32[1,1,4096]{2,1,0:T(1,128)S(1)} %bitcast.229), channel_id=1, replica_groups=mesh['dp'=2,'ctx'=4,'exp'=4] {'dp','ctx','exp'}, dimensions={0}, use_global_device_ids=true | all-gather | bytes 540672 | tf_op jit(solution)/shard_map/all_gather | solution.py:991
  588.2 11.3 add_convert_fusion
  599.5 13.4 %fusion.45 = f32[32,128,2048]{2,1,0:T(8,128)} fusion(bf16[32,64,2048]{2,1,0:T(8,128)(2,1)S(1)} %bitcast.187, f32[32,128]{1,0:T(8,128)S(1)} %broadcast_add_fusion, f32[64]{0:T(128)S(1)} %iota_convert_fusion, pred[32,128]{1,0:T(8,128)(4,1)S(1)} %broadcast_compare_fusion), kind=kOutput, calls=%fused_computation.110 | convolution fusion | flops 1074790400 | bytes 41963776 | tf_op jit(solution)/shard_map/gst,gsd->gtd/dot_general | solution.py:954
  612.9 15.1 %multiply_convert_fusion.7 = (bf16[4096,128]{0,1:T(8,128)(2,1)}, bf16[4096,128]{0,1:T(8,128)(2,1)}, bf16[4096,128]{0,1:T(8,128)(2,1)}) fusion(f32[4096,256]{0,1:T(8,128)} %fusion.98, bf16[4096,2048]{1,0:T(8,128)(2,1)} %shard_map.294, bf16[128,2048]{0,1:T(8,128)(2,1)} %bitcast.200), kind=kOutput, calls=%fused_computation.64 | convolution fusion | flops 2155347968 | bytes 24641536 | tf_op jit(solution)/shard_map/dot_general | solution.py:59
  628.0 19.0 %fusion.in_ref = bf16[4096,2048]{1,0:T(8,128)(2,1)} fusion(f32[32,128,2048]{2,1,0:T(8,128)} %fusion.45, bf16[2048,256]{1,0:T(8,128)(2,1)} %bitcast.199, bf16[4096,128]{0,1:T(8,128)(2,1)} %get-tuple-element.47, bf16[4096,128]{0,1:T(8,128)(2,1)} %get-tuple-element.46), kind=kOutput, calls=%fused_computation.1 | convolution fusion | flops 4315938816 | bytes 53477376 | tf_op jit(solution)/shard_map/dot_general | solution.py:59
  647.0 93.5 %shard_map.295 = f32[128,2048]{1,0:T(8,128)} custom-call(bf16[4096,2048]{1,0:T(8,128)(2,1)} %fusion.in_ref), custom_call_target="tpu_custom_call" | custom-call | tf_op jit(solution)/shard_map/pallas_call | solution.py:719
  745.7 62.5 %shard_map.296 = bf16[2048,2048]{1,0:T(8,128)(2,1)} custom-call(bf16[128,2048]{1,0:T(8,128)(2,1)} %fusion.94.x_ref), custom_call_target="tpu_custom_call" | custom-call | tf_op jit(solution)/shard_map/pallas_call | solution.py:566
  834.1 11.9 shard_map.297
  865.6 59.4 %shard_map.298 = f32[128,2048]{1,0:T(8,128)} custom-call(bf16[2048,2048]{1,0:T(8,128)(2,1)} %convolution_convert_fusion.in_ref), custom_call_target="tpu_custom_call" | custom-call | tf_op jit(solution)/shard_map/pallas_call | solution.py:719
  930.6 19.2 %fusion.46 = f32[32,128,2048]{2,1,0:T(8,128)} fusion(bf16[32,64,2048]{2,1,0:T(8,128)(2,1)} %bitcast.186, f32[32,128]{1,0:T(8,128)S(1)} %broadcast_add_fusion, f32[64]{0:T(128)S(1)} %iota_convert_fusion, pred[32,128]{1,0:T(8,128)(4,1)S(1)} %broadcast_compare_fusion), kind=kOutput, calls=%fused_computation.111 | convolution fusion | flops 1074790400 | bytes 41963776 | tf_op jit(solution)/shard_map/gst,gsd->gtd/dot_general | solution.py:954
  949.8 19.0 %fusion.1.in_ref = bf16[4096,2048]{1,0:T(8,128)(2,1)} fusion(f32[32,128,2048]{2,1,0:T(8,128)} %fusion.46, bf16[4096,128]{0,1:T(8,128)(2,1)S(1)} %copy-done.11, bf16[128,2048]{0,1:T(8,128)(2,1)S(1)} %bitcast.201), kind=kOutput, calls=%fused_computation.3 | convolution fusion | flops 2164260864 | bytes 51904512 | tf_op jit(solution)/shard_map/dot_general | solution.py:49
  968.8 93.7 %shard_map.293 = f32[128,2048]{1,0:T(8,128)} custom-call(bf16[4096,2048]{1,0:T(8,128)(2,1)} %fusion.1.in_ref), custom_call_target="tpu_custom_call" | custom-call | tf_op jit(solution)/shard_map/pallas_call | solution.py:719
  1091.0 11.1 convolution_bitcast_fusion
  1102.2 10.7 convolution_bitcast_fusion.1
  1124.3 46.2 %all-to-all-done.3 = bf16[8,256,896]{2,1,0:T(8,128)(2,1)} async-done(((bf16[8,256,896]{2,1,0:T(8,128)(2,1)}), bf16[8,256,896]{2,1,0:T(8,128)(2,1)}, u32[]{:S(2)}, u32[]{:S(2)}) %all-to-all-start.3) | async-done | bytes 3670048 | tf_op jit(solution)/shard_map/all_to_all | solution.py:745
  (225 shorter events, 256.5 us)
Async XLA Ops:
  7.2 504.0 %copy-start = (bf16[1,704,2048]{2,1,0:T(8,128)(2,1)S(1)}, bf16[1,704,2048]{2,1,0:T(8,128)(2,1)}, u32[]{:S(2)}) copy-start(bf16[1,704,2048]{2,1,0:T(8,128)(2,1)} %param.32) | copy-start | bytes 8650756
  20.9 56.5 %all-to-all-start = ((bf16[8,256,512]{1,2,0:T(8,128)(2,1)}), bf16[8,256,512]{1,2,0:T(8,128)(2,1)}, u32[]{:S(2)}, u32[]{:S(2)}) async-start(bf16[8,256,512]{1,2,0:T(8,128)(2,1)} %pad_maximum_fusion), calls=%async_computation | async-start | bytes 4194304 | tf_op jit(solution)/shard_map/all_to_all | solution.py:745
  77.4 196.3 %all-to-all-start.1 = ((bf16[8,256,512]{2,1,0:T(8,128)(2,1)}), bf16[8,256,512]{2,1,0:T(8,128)(2,1)}, u32[]{:S(2)}, u32[]{:S(2)}) async-start(bf16[8,256,512]{2,1,0:T(8,128)(2,1)} %fusion.28), calls=%async_computation.1 | async-start | bytes 4194304 | tf_op jit(solution)/shard_map/all_to_all | solution.py:745
  83.7 174.2 %copy-start.39 = (f32[128]{0:T(128)}, f32[128]{0:T(128)S(1)}, u32[]{:S(2)}) copy-start(f32[128]{0:T(128)S(1)} %get-tuple-element.33) | copy-start | bytes 1540
  273.7 92.9 %copy-start.30 = (f32[2048]{0:T(1024)}, f32[2048]{0:T(1024)S(1)}, u32[]{:S(2)}) copy-start(f32[2048]{0:T(1024)S(1)} %get-tuple-element.27) | copy-start | bytes 24580
  305.4 59.7 %copy-start.5 = (bf16[128,2048]{1,0:T(8,128)(2,1)S(1)}, bf16[128,2048]{1,0:T(8,128)(2,1)}, u32[]{:S(2)}) copy-start(bf16[128,2048]{1,0:T(8,128)(2,1)} %get-tuple-element.34.x_ref) | copy-start | bytes 1572868
  646.9 93.5 %copy-start.2 = (f32[128,2048]{1,0:T(8,128)S(1)}, f32[128,2048]{1,0:T(8,128)}, u32[]{:S(2)}) copy-start(f32[128,2048]{1,0:T(8,128)} %copy-done.1) | copy-start | bytes 3145732
  646.9 93.5 %copy-start.31 = (f32[2048]{0:T(1024)S(1)}, f32[2048]{0:T(1024)}, u32[]{:S(2)}) copy-start(f32[2048]{0:T(1024)} %copy-done.30) | copy-start | bytes 24580
  646.9 93.5 %copy-start.37 = (f32[128]{0:T(128)S(1)}, f32[128]{0:T(128)}, u32[]{:S(2)}) copy-start(f32[128]{0:T(128)} %copy-done.36) | copy-start | bytes 1540
  647.0 95.5 %copy-start.42 = (f32[128]{0:T(128)S(1)}, f32[128]{0:T(128)}, u32[]{:S(2)}) copy-start(f32[128]{0:T(128)} %copy-done.41) | copy-start | bytes 1540
  743.4 64.7 %copy-start.12 = (bf16[2048,128]{1,0:T(8,128)(2,1)S(1)}, bf16[2048,128]{1,0:T(8,128)(2,1)}, u32[]{:S(2)}) copy-start(bf16[2048,128]{1,0:T(8,128)(2,1)} %get-tuple-element.20) | copy-start | bytes 1572868
  865.6 59.4 %copy-start.6 = (bf16[128,2048]{1,0:T(8,128)(2,1)S(1)}, bf16[128,2048]{1,0:T(8,128)(2,1)}, u32[]{:S(2)}) copy-start(bf16[128,2048]{1,0:T(8,128)(2,1)} %get-tuple-element.34.x_ref) | copy-start | bytes 1572868
  865.6 59.5 %copy-start.33 = (f32[2048]{0:T(1024)S(1)}, f32[2048]{0:T(1024)}, u32[]{:S(2)}) copy-start(f32[2048]{0:T(1024)} %copy-done.32) | copy-start | bytes 24580
  865.6 59.5 %copy-start.38 = (f32[128]{0:T(128)S(1)}, f32[128]{0:T(128)}, u32[]{:S(2)}) copy-start(f32[128]{0:T(128)} %fusion.83) | copy-start | bytes 1540
  865.6 61.1 %copy-start.40 = (f32[128]{0:T(128)S(1)}, f32[128]{0:T(128)}, u32[]{:S(2)}) copy-start(f32[128]{0:T(128)} %copy-done.39) | copy-start | bytes 1540
  927.5 158.0 %all-to-all-start.2 = ((f32[32,1,512]{2,1,0:T(1,128)}), f32[32,1,512]{2,1,0:T(1,128)S(1)}, u32[]{:S(2)}, u32[]{:S(2)}) async-start(f32[32,1,512]{2,1,0:T(1,128)} %all_to_all.17), calls=%async_computation.2 | async-start | bytes 131072 | tf_op jit(solution)/shard_map/all_to_all | solution.py:1041
  930.5 193.8 %all-gather.6.cloned.1.call-start = ((), (), s32[]{:S(2)}) async-start(), calls=%async_computation.5 | async-start | bytes 2621440 | tf_op jit(solution)/shard_map/all_gather | solution.py:1036
  968.8 93.7 %copy-start.3 = (f32[128,2048]{1,0:T(8,128)S(1)}, f32[128,2048]{1,0:T(8,128)}, u32[]{:S(2)}) copy-start(f32[128,2048]{1,0:T(8,128)} %copy-done.1) | copy-start | bytes 3145732
  968.8 93.8 %copy-start.7 = (f32[128,2048]{1,0:T(8,128)S(1)}, f32[128,2048]{1,0:T(8,128)}, u32[]{:S(2)}) copy-start(f32[128,2048]{1,0:T(8,128)} %shard_map.298) | copy-start | bytes 3145732
  968.8 93.8 %copy-start.9 = (f32[128,2048]{1,0:T(8,128)S(1)}, f32[128,2048]{1,0:T(8,128)}, u32[]{:S(2)}) copy-start(f32[128,2048]{1,0:T(8,128)} %copy-done.8) | copy-start | bytes 3145732
  1085.5 85.1 %all-to-all-start.3 = ((bf16[8,256,896]{2,1,0:T(8,128)(2,1)}), bf16[8,256,896]{2,1,0:T(8,128)(2,1)}, u32[]{:S(2)}, u32[]{:S(2)}) async-start(bf16[8,256,896]{2,1,0:T(8,128)(2,1)} %maximum_maximum_fusion), calls=%async_computation.3 | async-start | bytes 7340032 | tf_op jit(solution)/shard_map/all_to_all | solution.py:745
  1090.3 34.1 %all-gather.4.cloned.1.call-start = ((), (), s32[]{:S(2)}) async-start(), calls=%async_computation.4 | async-start | bytes 2621440 | tf_op jit(solution)/shard_map/all_gather | solution.py:1037
  1091.0 24.4 %slice-start.4 = ((s8[8388608]{0:T(1024)(128)(4,1)}), s8[4194304]{0:T(1024)(128)(4,1)S(1)}, s32[]{:S(2)}) async-start(s8[8388608]{0:T(1024)(128)(4,1)} %bitcast.179), calls=%async_computation.10 | async-start | bytes 8388608
  1091.0 24.4 %slice-start.6 = ((s8[5767168]{0:T(1024)(128)(4,1)}), s8[4194304]{0:T(1024)(128)(4,1)S(1)}, s32[]{:S(2)}) async-start(s8[5767168]{0:T(1024)(128)(4,1)} %bitcast.194), calls=%async_computation.12 | async-start | bytes 8388608
  (38 other events, 387.3 us)
Sparse Core Ops, SparseCore 0:
  1065.6 24.4 all-gather.5
  1093.2 25.3 all-gather.3

commit v2 on v1

--- a/solution.py
+++ b/solution.py
@@ -397,13 +397,10 @@
 
 
 class Place:
-    def __init__(self, wide):
-        self.wide = wide
+    def __init__(self):
         self.x = lax.axis_index("dp")
         self.z = lax.axis_index("ctx")
         self.e = lax.axis_index("exp")
-        self.y = lax.div(self.e, 2)
-        self.c = lax.rem(self.e, 2)
         z = self.z
         high = lax.div(z, 2)
         self.zs = [z, z + 1 - 2 * lax.rem(z, 2), 2 - high, 3 - 3 * high]
@@ -411,20 +408,8 @@
         self.inside = lax.div(z * (3 - z), 2)
         self.middle = self.inside == 1
         self.dx = 1 - 2 * self.x
-        self.dy = 2 - 4 * self.y
-        self.dc = 1 - 2 * self.c
-
-    def far(self, f, g):
-        if not self.wide:
-            return 0, f * self.dy
-        a, b = (1 - self.c), self.c
-        return (f * a + g * b) * self.dx, (f * b + g * a) * self.dy
-
-    def far_twin(self, f, g):
-        if not self.wide:
-            return 0, f * self.dy
-        a, b = self.c, (1 - self.c)
-        return (f * a + g * b) * self.dx, (f * b + g * a) * self.dy
+        self.dy = 2 - 4 * lax.div(self.e, 2)
+        self.dc = 1 - 2 * lax.rem(self.e, 2)
 
     def device(self, ox=0, oe=0, zi=0):
         return (self.x + ox, self.zs[zi], self.e + oe)
@@ -432,20 +417,22 @@
     def inward(self):
         return (self.x, self.inner, self.e)
 
-    def shard(self, ox, oe, zi):
-        rank = self.zs[zi] * 4 + self.e + oe
-        if self.wide:
-            rank = rank + (self.x + ox) * 16
-        return rank
-
-
-def greet(at):
+    def shard(self, oe, zi):
+        return self.zs[zi] * 4 + self.e + oe
+
+
+def greet(at, everyone, pair=False):
     barrier = pltpu.get_barrier_semaphore()
-    peers = [at.device(zi=1), at.device(*at.far(1, 0)), at.device(oe=at.dc)]
-    if at.wide:
-        peers.append(at.device(*at.far(0, 1)))
+    peers = [at.device(zi=1), at.device(oe=at.dy), at.device(oe=at.dc)]
+    if everyone or pair:
+        peers.append(at.device(ox=at.dx))
+    if everyone:
+        peers += [at.device(zi=2), at.device(zi=3)]
     for peer in peers:
         pl.semaphore_signal(barrier, inc=1, device_id=peer, device_id_type=MESH)
+    if everyone:
+        pl.semaphore_wait(barrier, len(peers))
+        return
 
     @pl.when(at.middle)
     def _():
@@ -454,103 +441,172 @@
     pl.semaphore_wait(barrier, len(peers) + at.inside)
 
 
-def gather_kernel(wide, rows, parts, x_ref, out_ref, own_sem, send_sem, recv_sem):
-    at = Place(wide)
-    greet(at)
+def remote(src, dst, send, recv, device):
+    return pltpu.make_async_remote_copy(
+        src_ref=src, dst_ref=dst, send_sem=send, recv_sem=recv, device_id=device, device_id_type=MESH
+    )
+
+
+def cross(at, sent, got, send_sem, recv_sem):
+    return [
+        remote(a, b, send_sem.at[m], recv_sem.at[m], at.device(ox=at.dx))
+        for m, (a, b) in enumerate(zip(sent, got))
+    ]
+
+
+class Exchange:
+    def __init__(self, at, sent, got, local_sem, send_sem, recv_sem):
+        self.at, self.sent, self.got = at, sent, got
+        self.local_sem, self.send_sem, self.recv_sem = local_sem, send_sem, recv_sem
+        self.waits = []
+
+    def push(self, src, m, z_from, slot, device):
+        at = self.at
+        spot = self.got[m].at[at.x * 4 + z_from]
+        copy = remote(
+            src, spot, self.send_sem.at[m * 7 + slot], self.recv_sem.at[m * 8 + (0 if slot < 3 else 4) + z_from], device
+        )
+        copy.start()
+        self.waits.append(copy)
+
+    def start(self):
+        at = self.at
+        for m, sent in enumerate(self.sent):
+            for zi in (1, 2, 3):
+                self.push(sent.at[at.zs[zi]], m, at.z, zi - 1, at.device(zi=zi))
+            self.push(sent.at[at.z], m, at.z, 3, at.device(ox=at.dx))
+            pltpu.make_async_copy(
+                sent.at[at.z], self.got[m].at[at.x * 4 + at.z], self.local_sem.at[m]
+            ).start()
+
+    def arrive(self, m, slot):
+        src = self.sent[m].at[0]
+        remote(
+            src, self.got[m].at[0], self.send_sem.at[0], self.recv_sem.at[slot], self.at.device(ox=self.at.dx)
+        ).wait_recv()
+
+    def forward(self, zi):
+        at = self.at
+        for m in range(len(self.sent)):
+            self.arrive(m, m * 8 + at.zs[zi])
+            self.push(self.got[m].at[at.x * 4 + at.zs[zi]], m, at.zs[zi], 3 + zi, at.device(ox=at.dx))
+
+    def finish(self):
+        at = self.at
+        for m, sent in enumerate(self.sent):
+            for z in range(4):
+                self.arrive(m, m * 8 + 4 + z)
+            pltpu.make_async_copy(
+                sent.at[at.z], self.got[m].at[at.x * 4 + at.z], self.local_sem.at[m]
+            ).wait()
+        for copy in self.waits:
+            copy.wait_send()
+
+
+def gather_kernel(block, rows, parts, extras, swaps, *refs):
+    refs = list(refs)
+
+    def take(count):
+        taken = refs[:count]
+        del refs[:count]
+        return taken
+
+    (x_ref,), sent, given = take(1), take(extras), take(swaps)
+    (out_ref,), got, taken = take(1), take(extras), take(swaps)
+    own_sem, send_sem, recv_sem = take(3)
+    extra_sems = take(3 if extras else 0)
+    at = Place()
+    greet(at, extras > 0, swaps > 0)
+    crossing = cross(at, given, taken, *refs) if swaps else []
     piece = rows // parts
-    kinds = 4 if wide else 2
-    slot_z, slot_f, slot_g, slot_s = 0, 3, 7, 15
+    slot_z, slot_f, slot_s = 0, 3, 7
     started, inside = [], []
-
-    def where(f, g, zi, p):
-        ox, oe = at.far(f, g)
-        return pl.ds(pl.multiple_of(at.shard(ox, oe, zi) * rows + p * piece, piece), piece)
+    firsts = 1 if block else 0
+    shift = at.e * rows if block else 0
+
+    def where(f, zi, p):
+        return pl.ds(
+            pl.multiple_of(at.shard(f * at.dy, zi) * rows + p * piece, piece), piece
+        )
 
     def push(src, dst, slot, p, device, sends=None, record=None):
         k = slot * parts + p
         j = k if sends is None else sends * parts + p
-        copy = pltpu.make_async_remote_copy(
-            src_ref=src,
-            dst_ref=out_ref.at[dst],
-            send_sem=send_sem.at[j],
-            recv_sem=recv_sem.at[k],
-            device_id=device,
-            device_id_type=MESH,
-        )
-        copy.start()
+        remote(src, out_ref.at[dst], send_sem.at[j], recv_sem.at[k], device).start()
         (started if record is None else record).append(j)
 
+    f_dev, s_dev, z_dev = at.device(oe=at.dy), at.device(oe=at.dc), at.device(zi=1)
+
     def gone(j):
-        pltpu.make_async_remote_copy(
-            src_ref=x_ref.at[pl.ds(0, piece)],
-            dst_ref=out_ref.at[pl.ds(0, piece)],
-            send_sem=send_sem.at[j],
-            recv_sem=recv_sem.at[0],
-            device_id=s_dev,
-            device_id_type=MESH,
+        remote(
+            x_ref.at[pl.ds(0, piece)], out_ref.at[pl.ds(0, piece)], send_sem.at[j], recv_sem.at[0], s_dev
         ).wait_send()
 
     def arrive(slot, p):
         k = slot * parts + p
-        pltpu.make_async_remote_copy(
-            src_ref=x_ref.at[pl.ds(0, piece)],
-            dst_ref=out_ref.at[pl.ds(0, piece)],
-            send_sem=send_sem.at[k],
-            recv_sem=recv_sem.at[k],
-            device_id=at.device(oe=at.dc),
-            device_id_type=MESH,
+        remote(
+            x_ref.at[pl.ds(0, piece)], out_ref.at[pl.ds(0, piece)], send_sem.at[k], recv_sem.at[k], s_dev
         ).wait_recv()
 
-    f_dev, s_dev, z_dev = at.device(*at.far(1, 0)), at.device(oe=at.dc), at.device(zi=1)
-    g_dev = at.device(*at.far(0, 1)) if wide else None
-    own = pltpu.make_async_copy(
-        x_ref, out_ref.at[pl.ds(pl.multiple_of(at.shard(0, 0, 0) * rows, rows), rows)], own_sem
-    )
-    own.start()
-
-    def source(f, g, zi, p):
-        if (f, g, zi) == (0, 0, 0):
-            return x_ref.at[pl.ds(p * piece, piece)]
-        return out_ref.at[where(f, g, zi, p)]
+    if block:
+        spot = pl.ds(pl.multiple_of(at.z * 4 * rows, 4 * rows), 4 * rows)
+    else:
+        spot = pl.ds(pl.multiple_of(at.shard(0, 0) * rows, rows), rows)
+    own = pltpu.make_async_copy(x_ref, out_ref.at[spot], own_sem)
+
+    def source(f, zi, p):
+        if f == 0 and zi == 0:
+            return x_ref.at[pl.ds(pl.multiple_of(shift + p * piece, piece), piece)]
+        return out_ref.at[where(f, zi, p)]
 
     def along(zi, p):
-        src, dst = source(0, 0, zi, p), where(0, 0, zi, p)
+        src, dst = source(0, zi, p), where(0, zi, p)
         if zi == 0:
             push(src, dst, slot_z, p, z_dev)
         if zi < 2:
             pl.when(at.middle)(
-                lambda: push(src, dst, slot_z + 1 + zi, p, at.inward(), 31 + zi, inside)
+                lambda: push(src, dst, slot_z + 1 + zi, p, at.inward(), 15 + zi, inside)
             )
         else:
-            pl.when(at.middle)(lambda: push(src, dst, slot_z + zi - 1, p, z_dev, 31 + zi, inside))
-
-    def forward(f, g, zi, p):
-        src, dst = source(f, g, zi, p), where(f, g, zi, p)
-        if f == 0 and g == 0:
+            pl.when(at.middle)(lambda: push(src, dst, slot_z + zi - 1, p, z_dev, 15 + zi, inside))
+
+    def forward(f, zi, p):
+        src, dst = source(f, zi, p), where(f, zi, p)
+        if f == 0:
             along(zi, p)
-            push(src, dst, slot_f + zi, p, f_dev)
-        if wide and g == 0:
-            push(src, dst, slot_g + f * 4 + zi, p, g_dev)
-        push(src, dst, slot_s + (g * 2 + f) * 4 + zi, p, s_dev)
-
+        if zi >= firsts:
+            if f == 0:
+                push(src, dst, slot_f + zi, p, f_dev)
+            push(src, dst, slot_s + f * 4 + zi, p, s_dev)
+
+    for p in range(parts):
+        forward(0, 0, p)
+    own.start()
+    for copy in crossing:
+        copy.start()
+    if extras:
+        swap_in = Exchange(at, sent, got, *extra_sems)
+        swap_in.start()
     for zi in range(4):
-        for p in range(parts):
-            if zi > 0:
+        if zi > 0:
+            for p in range(parts):
                 arrive(slot_z + zi - 1, p)
-            forward(0, 0, zi, p)
-        for p in range(parts):
-            arrive(slot_f + zi, p)
-            forward(1, 0, zi, p)
-    if wide:
-        for f in range(2):
-            for zi in range(4):
-                for p in range(parts):
-                    arrive(slot_g + f * 4 + zi, p)
-                    forward(f, 1, zi, p)
-    for k in range(4 * kinds):
-        for p in range(parts):
-            arrive(slot_s + k, p)
+                forward(0, zi, p)
+        if zi >= firsts:
+            for p in range(parts):
+                arrive(slot_f + zi, p)
+                forward(1, zi, p)
+        if extras and zi > 0:
+            swap_in.forward(zi)
+    for f in range(2):
+        for zi in range(firsts, 4):
+            for p in range(parts):
+                arrive(slot_s + f * 4 + zi, p)
     own.wait()
+    if extras:
+        swap_in.finish()
+    for copy in crossing:
+        copy.wait()
     for j in started:
         gone(j)
 
@@ -560,75 +616,73 @@
             gone(j)
 
 
-def all_rows(x, wide, cid, parts=1):
+def all_rows(x, block, cid, sent=(), given=(), parts=2):
     rows, width = x.shape
-    n = 32 if wide else 16
-    return pl.pallas_call(
-        functools.partial(gather_kernel, wide, rows, parts),
-        out_shape=jax.ShapeDtypeStruct((n * rows, width), x.dtype),
-        in_specs=[pl.BlockSpec(memory_space=pl.ANY)],
-        out_specs=pl.BlockSpec(memory_space=pl.ANY),
-        scratch_shapes=[
-            pltpu.SemaphoreType.DMA,
-            pltpu.SemaphoreType.DMA((35 * parts,)),
-            pltpu.SemaphoreType.DMA((31 * parts,)),
-        ],
+    total = rows * (4 if block else 16)
+    rows = rows // 4 if block else rows
+    extras, swaps = len(sent), len(given)
+    hbm = pl.BlockSpec(memory_space=pl.ANY)
+    outs = [jax.ShapeDtypeStruct((total, width), x.dtype)]
+    outs += [jax.ShapeDtypeStruct((8,) + a.shape[1:], a.dtype) for a in sent]
+    outs += [jax.ShapeDtypeStruct(a.shape, a.dtype) for a in given]
+    scratch = [
+        pltpu.SemaphoreType.DMA,
+        pltpu.SemaphoreType.DMA((19 * parts,)),
+        pltpu.SemaphoreType.DMA((15 * parts,)),
+    ]
+    if extras:
+        scratch += [
+            pltpu.SemaphoreType.DMA((extras,)),
+            pltpu.SemaphoreType.DMA((7 * extras,)),
+            pltpu.SemaphoreType.DMA((8 * extras,)),
+        ]
+    if swaps:
+        scratch += [pltpu.SemaphoreType.DMA((swaps,)), pltpu.SemaphoreType.DMA((swaps,))]
+    got = pl.pallas_call(
+        functools.partial(gather_kernel, block, rows, parts, extras, swaps),
+        out_shape=outs,
+        in_specs=[hbm] * len(outs),
+        out_specs=[hbm] * len(outs),
+        scratch_shapes=scratch,
         compiler_params=pltpu.CompilerParams(collective_id=cid, has_side_effects=True),
-    )(x)
-
-
-def scatter_kernel(wide, rows, in_ref, out_ref, acc, got_s, got_g, got_f, got_z, load_sem, send_sem, recv_sem):
-    at = Place(wide)
-    greet(at)
-    slot_z, slot_f, slot_g, slot_s = 0, 5, 9, 17
-    f_dev, s_dev, z_dev = at.device(*at.far(1, 0)), at.device(oe=at.dc), at.device(zi=1)
-    g_dev = at.device(*at.far(0, 1)) if wide else None
+    )(x, *sent, *given)
+    return got if extras or swaps else got[0]
+
+
+def scatter_kernel(rows, swaps, in_ref, *refs):
+    given, out_ref, taken = refs[:swaps], refs[swaps], refs[swaps + 1 : 2 * swaps + 1]
+    acc, got_s, got_f, got_z, load_sem, send_sem, recv_sem = refs[2 * swaps + 1 : 2 * swaps + 8]
+    at = Place()
+    greet(at, False, swaps > 0)
+    crossing = cross(at, given, taken, *refs[2 * swaps + 8 :]) if swaps else []
+    for copy in crossing:
+        copy.start()
+    slot_z, slot_f, slot_s = 0, 5, 9
+    f_dev, s_dev, z_dev = at.device(oe=at.dy), at.device(oe=at.dc), at.device(zi=1)
     started, in_middle, at_end = [], [], []
 
     def rows_of(rank):
         return in_ref.at[pl.ds(pl.multiple_of(rank * rows, rows), rows)]
 
     def push(src, dst, slot, device, sends=None, record=started):
-        copy = pltpu.make_async_remote_copy(
-            src_ref=src,
-            dst_ref=dst,
-            send_sem=send_sem.at[slot if sends is None else sends],
-            recv_sem=recv_sem.at[slot],
-            device_id=device,
-            device_id_type=MESH,
+        j = slot if sends is None else sends
+        remote(src, dst, send_sem.at[j], recv_sem.at[slot], device).start()
+        record.append(j)
+
+    def gone(j):
+        remote(acc.at[0], acc.at[0], send_sem.at[j], recv_sem.at[0], s_dev).wait_send()
+
+    def arrive(dst, slot):
+        remote(acc.at[0], dst, send_sem.at[slot], recv_sem.at[slot], s_dev).wait_recv()
+
+    order = [(f, zi) for f in (1, 0) for zi in (3, 2, 1, 0)]
+    loads = {}
+    for f, zi in order:
+        k = f * 4 + zi
+        push(rows_of(at.shard(f * at.dy + at.dc, zi)), got_s.at[k], slot_s + k, s_dev)
+        loads[k] = pltpu.make_async_copy(
+            rows_of(at.shard(f * at.dy, zi)), acc.at[k], load_sem.at[k]
         )
-        copy.start()
-        record.append(slot if sends is None else sends)
-
-    def gone(j):
-        pltpu.make_async_remote_copy(
-            src_ref=acc.at[0],
-            dst_ref=acc.at[0],
-            send_sem=send_sem.at[j],
-            recv_sem=recv_sem.at[0],
-            device_id=s_dev,
-            device_id_type=MESH,
-        ).wait_send()
-
-    def arrive(dst, slot):
-        pltpu.make_async_remote_copy(
-            src_ref=acc.at[0],
-            dst_ref=dst,
-            send_sem=send_sem.at[slot],
-            recv_sem=recv_sem.at[slot],
-            device_id=s_dev,
-            device_id_type=MESH,
-        ).wait_recv()
-
-    gs = (1, 0) if wide else (0,)
-    order = [(f, g, zi) for g in gs for f in (1, 0) for zi in (3, 2, 1, 0)]
-    loads = {}
-    for f, g, zi in order:
-        k = (g * 2 + f) * 4 + zi
-        ox, oe = at.far_twin(f, g)
-        push(rows_of(at.shard(ox, oe + at.dc, zi)), got_s.at[k], slot_s + k, s_dev)
-        ox, oe = at.far(f, g)
-        loads[k] = pltpu.make_async_copy(rows_of(at.shard(ox, oe, zi)), acc.at[k], load_sem.at[k])
         loads[k].start()
 
     def add(k, *others, into=None):
@@ -643,18 +697,11 @@
             else:
                 into[span, :] = total
 
-    for f, g, zi in order:
-        k = (g * 2 + f) * 4 + zi
+    for f, zi in order:
+        k = f * 4 + zi
         arrive(got_s.at[k], slot_s + k)
         loads[k].wait()
         others = [(got_s, k)]
-        if g == 1:
-            add(k, *others)
-            push(acc.at[k], got_g.at[f * 4 + zi], slot_g + f * 4 + zi, g_dev)
-            continue
-        if wide:
-            arrive(got_g.at[f * 4 + zi], slot_g + f * 4 + zi)
-            others.append((got_g, f * 4 + zi))
         if f == 1:
             add(k, *others)
             push(acc.at[k], got_f.at[zi], slot_f + zi, f_dev)
@@ -667,7 +714,10 @@
             def _():
                 arrive(got_z.at[3 - zi], slot_z + 3 - zi)
                 add(k, *others, (got_z, 3 - zi))
-                push(acc.at[k], got_z.at[4 if zi == 2 else 3], slot_z + (4 if zi == 2 else 3), at.inward(), slot_z + zi, in_middle)
+                there = 4 if zi == 2 else 3
+                push(
+                    acc.at[k], got_z.at[there], slot_z + there, at.inward(), slot_z + zi, in_middle
+                )
 
             @pl.when(jnp.logical_not(at.middle))
             def _():
@@ -698,6 +748,8 @@
                 arrive(got_z.at[4], slot_z + 4)
                 add(k, *others, (got_z, 4), into=out_ref)
 
+    for copy in crossing:
+        copy.wait()
     for j in started:
         gone(j)
 
@@ -712,29 +764,87 @@
             gone(j)
 
 
-def own_rows(x, wide, cid):
-    n = 32 if wide else 16
-    rows, width = x.shape[0] // n, x.shape[1]
-    half = n // 2
-    return pl.pallas_call(
-        functools.partial(scatter_kernel, wide, rows),
-        out_shape=jax.ShapeDtypeStruct((rows, width), F32),
-        in_specs=[pl.BlockSpec(memory_space=pl.ANY)],
-        out_specs=pl.BlockSpec(memory_space=pltpu.VMEM),
+def own_rows(x, cid, given=()):
+    rows, width = x.shape[0] // 16, x.shape[1]
+    swaps = len(given)
+    hbm = pl.BlockSpec(memory_space=pl.ANY)
+    crossing = [pltpu.SemaphoreType.DMA((swaps,))] * 2 if swaps else []
+    got = pl.pallas_call(
+        functools.partial(scatter_kernel, rows, swaps),
+        out_shape=[jax.ShapeDtypeStruct((rows, width), F32)]
+        + [jax.ShapeDtypeStruct(a.shape, a.dtype) for a in given],
+        in_specs=[hbm] * (1 + swaps),
+        out_specs=[pl.BlockSpec(memory_space=pltpu.VMEM)] + [hbm] * swaps,
         scratch_shapes=[
-            pltpu.VMEM((half, rows, width), BF),
-            pltpu.VMEM((half, rows, width), BF),
-            pltpu.VMEM((8, rows, width) if wide else (1, 16, 128), BF),
+            pltpu.VMEM((8, rows, width), BF),
+            pltpu.VMEM((8, rows, width), BF),
             pltpu.VMEM((4, rows, width), BF),
             pltpu.VMEM((5, rows, width), BF),
-            pltpu.SemaphoreType.DMA((half,)),
-            pltpu.SemaphoreType.DMA((33,)),
-            pltpu.SemaphoreType.DMA((33,)),
+            pltpu.SemaphoreType.DMA((8,)),
+            pltpu.SemaphoreType.DMA((17,)),
+            pltpu.SemaphoreType.DMA((17,)),
+            *crossing,
         ],
         compiler_params=pltpu.CompilerParams(
-            collective_id=cid, has_side_effects=True, vmem_limit_bytes=56 * 1024 * 1024
+            collective_id=cid, has_side_effects=True, vmem_limit_bytes=40 * 1024 * 1024
         ),
-    )(x)
+    )(x, *given)
+    return got if swaps else got[0]
+
+
+def share_kernel(rows, count, *refs):
+    ins, outs = refs[:count], refs[count : 2 * count]
+    own_sem, send_sem, recv_sem = refs[2 * count :]
+    at = Place()
+    barrier = pltpu.get_barrier_semaphore()
+    f_dev, s_dev = at.device(oe=at.dy), at.device(oe=at.dc)
+    for peer in (f_dev, s_dev):
+        pl.semaphore_signal(barrier, inc=1, device_id=peer, device_id_type=MESH)
+    pl.semaphore_wait(barrier, 2)
+
+    def spot(oe):
+        return pl.ds(pl.multiple_of((at.e + oe) * rows, rows), rows)
+
+    copies = []
+    for m in range(count):
+        for j, device in enumerate((f_dev, s_dev)):
+            copy = remote(
+                ins[m], outs[m].at[spot(0)], send_sem.at[m * 3 + j], recv_sem.at[m * 3 + j], device
+            )
+            copy.start()
+            copies.append(copy)
+        local = pltpu.make_async_copy(ins[m], outs[m].at[spot(0)], own_sem.at[m])
+        local.start()
+        copies.append(local)
+    for m in range(count):
+        copies[m * 3].wait_recv()
+        src = outs[m].at[spot(at.dy)]
+        copy = remote(src, src, send_sem.at[m * 3 + 2], recv_sem.at[m * 3 + 2], s_dev)
+        copy.start()
+        copies.append(copy)
+    for m in range(count):
+        copies[m * 3].wait_send()
+        copies[m * 3 + 1].wait()
+        copies[m * 3 + 2].wait()
+        copies[count * 3 + m].wait()
+
+
+def share(arrays, cid):
+    count = len(arrays)
+    rows, width = arrays[0].shape
+    hbm = pl.BlockSpec(memory_space=pl.ANY)
+    return pl.pallas_call(
+        functools.partial(share_kernel, rows, count),
+        out_shape=[jax.ShapeDtypeStruct((4 * rows, width), a.dtype) for a in arrays],
+        in_specs=[hbm] * count,
+        out_specs=[hbm] * count,
+        scratch_shapes=[
+            pltpu.SemaphoreType.DMA((count,)),
+            pltpu.SemaphoreType.DMA((3 * count,)),
+            pltpu.SemaphoreType.DMA((3 * count,)),
+        ],
+        compiler_params=pltpu.CompilerParams(collective_id=cid, has_side_effects=True),
+    )(*arrays)
 
 
 ALL = ("dp", "ctx", "exp")
@@ -745,10 +855,13 @@
     return lax.all_to_all(blocks, DENSE, split_axis=0, concat_axis=0, tiled=True)
 
 
-def for_heads(matrix):
-    rows = matrix.shape[0]
-    cut = matrix.reshape(rows, 4, HDIM).transpose(1, 0, 2)
-    return jnp.concatenate([cut, cut], axis=0)
+def by_four(matrix):
+    rows, columns = matrix.shape
+    return matrix.reshape(rows, 4, columns // 4).transpose(1, 0, 2)
+
+
+def across(values):
+    return lax.ppermute(values, "dp", [(0, 1), (1, 0)])
 
 
 def attend_kernel(scale, block, q_ref, k_ref, v_ref, out_ref, lse_ref):
@@ -857,16 +970,13 @@
     dp, ctx, exp = lax.axis_index("dp"), lax.axis_index("ctx"), lax.axis_index("exp")
     rows_here, width = tokens.shape[1], tokens.shape[2]
     quarter = rows_here // 4
-    group = 8
     length = rows_here * 4
-    total = length * 2
     experts = w_router.shape[1]
     capacity = quarter * TOPK * 4 // (3 * experts)
-    groups = total // quarter
+    groups = length // quarter
     dense = w_query.shape[0]
-    hidden = expert_gate.shape[2]
-    cut = shared_gate.shape[1] // group
-    wide = 128
+    cut = shared_gate.shape[1] // 4
+    wide = 256
     start = exp * quarter
     tokens_own = lax.dynamic_slice_in_dim(tokens[0], start, quarter, 0)
     dy_own = lax.dynamic_slice_in_dim(out_grad[0], start, quarter, 0)
@@ -875,63 +985,60 @@
         routes[0][:, :, None] == (jnp.arange(4, dtype=jnp.int32) * 4 + exp)[None, None, :], axis=1
     )
     named = named.astype(BF).reshape(dense, 2, 4).transpose(2, 0, 1)
-    named = jnp.concatenate([named, named], axis=0)
     little = jnp.concatenate([w_router, norm_attn[:, None], norm_mix[:, None]], axis=1)
-    little = jnp.broadcast_to(little[None], (group,) + little.shape)
+    little = jnp.broadcast_to(little[None], (4,) + little.shape)
     little = jnp.concatenate([little, named], axis=2)
-    little = jnp.pad(little, ((0, 0), (0, 0), (0, wide - little.shape[2])))
-    early = swap(
-        jnp.concatenate([for_heads(w_query), for_heads(w_key), for_heads(w_value), little], axis=2)
-    ).reshape(width, 4 * HDIM)
+    little = jnp.pad(little, ((0, 0), (0, 0), (0, HDIM - little.shape[2])))
+    sent_head = jnp.concatenate([by_four(w_query), by_four(w_key), by_four(w_value), little], axis=2)
+    sent_out = w_out.reshape(4, HDIM, dense)
+    sent_units = jnp.concatenate([by_four(shared_gate), by_four(shared_up)], axis=2)
+    sent_units = jnp.pad(sent_units, ((0, 0), (0, 0), (0, 3 * HDIM - 2 * cut)))
+    sent_down = shared_down.reshape(4, cut, dense)
+    tokens_all, early, early_out, late, late_down = all_rows(
+        tokens[0], True, 1, (sent_head, sent_out, sent_units, sent_down)
+    )
+
+    tokens_all, sent_gate, sent_up, sent_down = lax.optimization_barrier(
+        (tokens_all, expert_gate[0], expert_up[0], expert_down[0])
+    )
+    other_gate, other_up, other_down = across(sent_gate), across(sent_up), across(sent_down)
+    early = early.reshape(width, 4 * HDIM)
     w_qkv = early[:, : 3 * HDIM]
     little = early[:, 3 * HDIM :]
     router_matrix = little[:, :experts]
     attention_gain = little[:, experts].astype(F32)
     mixer_gain = little[:, experts + 1].astype(F32)
-    hits = little[:, experts + 2 : experts + 4].astype(F32)
-    hits = hits.reshape(group, dense, 2).reshape(groups, quarter)
-
-    def units(matrix):
-        return jnp.pad(
-            matrix.reshape(dense, group, cut).transpose(1, 0, 2), ((0, 0), (0, 0), (0, wide - cut))
-        )
-
-    out_cut = w_out.reshape(4, HDIM, dense)
-    down_cut = jnp.pad(shared_down.reshape(group, cut, dense), ((0, 0), (0, wide - cut), (0, 0)))
-    late = swap(
-        jnp.concatenate(
-            [
-                units(shared_gate),
-                units(shared_up),
-                jnp.concatenate([jnp.concatenate([out_cut, out_cut], axis=0), down_cut], axis=1),
-            ],
-            axis=2,
-        )
-    )
-    shared_in = late[:, :, : 2 * wide].reshape(width, 2 * wide)
-    w_out_head = late[:, :HDIM, 2 * wide :].transpose(1, 0, 2).reshape(HDIM, width)
-    shared_out = late[:, HDIM:, 2 * wide :].transpose(1, 0, 2).reshape(wide, width)
+    hits = little[:, experts + 2 : experts + 4].reshape(2, length)
+    hits = lax.dynamic_index_in_dim(hits, dp, 0, False).astype(F32).reshape(groups, quarter)
+    w_out_head = early_out.transpose(1, 0, 2).reshape(HDIM, width)
+
+    dy_all = all_rows(out_grad[0], True, 2)
+    late = late.reshape(width, 3 * HDIM)
+    pads = ((0, 0), (0, wide - cut))
+    shared_in = jnp.concatenate(
+        [jnp.pad(late[:, :cut], pads), jnp.pad(late[:, cut : 2 * cut], pads)], axis=1
+    )
+    shared_out = jnp.pad(
+        late_down.transpose(1, 0, 2).reshape(cut, width), ((0, wide - cut), (0, 0))
+    )
 
     cosine, sine = turn_tables(length)
-    tokens_all = all_rows(tokens_own, False, 1)
     normed = rms_scale(tokens_all.astype(F32), attention_gain).astype(BF)
     qkv = product(normed, w_qkv)
     query = turn(qkv[:, :HDIM], cosine, sine).astype(BF)
     key = turn(qkv[:, HDIM : 2 * HDIM], cosine, sine).astype(BF)
     value = qkv[:, 2 * HDIM :].astype(BF)
     heads_out, lse = attend(query, key, value)
-    attn = own_rows(product(heads_out, w_out_head).astype(BF), False, 2)
+    attn = own_rows(product(heads_out, w_out_head).astype(BF), 3)
     middle = tokens_own.astype(F32) + attn
     normed_own = rms_scale(middle, mixer_gain).astype(BF)
 
-    dy_all = all_rows(dy_own, True, 3)
-    mix_all = all_rows(normed_own, True, 3)
+    mix_all = all_rows(normed_own, False, 4)
     logits = product(mix_all, router_matrix)
     router = jax.nn.softmax(logits, axis=-1)
     mine = ctx * 4 + exp
-    router_mine = jnp.sum(
-        jnp.where(jnp.arange(experts, dtype=jnp.int32)[None, :] == mine, router, 0.0), axis=1
-    ).reshape(groups, quarter)
+    columns = jnp.arange(experts, dtype=jnp.int32)[None, :] == mine
+    router_mine = jnp.sum(jnp.where(columns, router, 0.0), axis=1).reshape(groups, quarter)
     place = jnp.cumsum(hits, axis=1) - 1.0
     matches = jnp.where(
         (jnp.arange(capacity).astype(F32)[None, :, None] == place[:, None, :])
@@ -956,20 +1063,32 @@
             dispatch,
             rows.reshape(groups, capacity, width),
             preferred_element_type=F32,
-        ).reshape(total, width)
+        ).reshape(length, width)
 
     picked = pick(mix_all)
     picked_dy = pick(dy_all)
-    gate_hidden = product(picked, expert_gate[0])
-    up_hidden = product(picked, expert_up[0])
-    act, by_gate, by_up = silu_parts(gate_hidden, up_hidden)
-    dy_down = transposed_right(picked_dy, expert_down[0])
-    act_back = slot_gate * dy_down
-    g_back = (act_back * by_gate).astype(BF)
-    u_back = (act_back * by_up).astype(BF)
-    act_low = act.astype(BF)
-    gate_back = jnp.sum(act_low.astype(F32) * dy_down, axis=1)
-    input_back = transposed_right(g_back, expert_gate[0]) + transposed_right(u_back, expert_up[0])
+
+    def half(gate_matrix, up_matrix, down_matrix):
+        gate_hidden = product(picked, gate_matrix)
+        up_hidden = product(picked, up_matrix)
+        act, by_gate, by_up = silu_parts(gate_hidden, up_hidden)
+        dy_down = transposed_right(picked_dy, down_matrix)
+        act_back = slot_gate * dy_down
+        g_back = (act_back * by_gate).astype(BF)
+        u_back = (act_back * by_up).astype(BF)
+        act_low = act.astype(BF)
+        gate_back = jnp.sum(act_low.astype(F32) * dy_down, axis=1)
+        return act_low, (act * slot_gate).astype(BF), g_back, u_back, gate_back
+
+    act_a, scaled_a, g_a, u_a, gb_a = half(expert_gate[0], expert_up[0], expert_down[0])
+    act_b, scaled_b, g_b, u_b, gb_b = half(other_gate, other_up, other_down)
+    input_back = (
+        transposed_right(g_a, expert_gate[0])
+        + transposed_right(u_a, expert_up[0])
+        + transposed_right(g_b, other_gate)
+        + transposed_right(u_b, other_up)
+    )
+    gate_back = gb_a + gb_b
 
     shared_hidden = product(mix_all, shared_in)
     shared_act, shared_by_gate, shared_by_up = silu_parts(
@@ -983,39 +1102,37 @@
     mix_part = (
         transposed_right(shared_gu_back, shared_in) + spread(input_back.astype(BF))
     ).astype(BF)
-    mix_back = own_rows(mix_part, True, 4)
-
     gate_back_tokens = jnp.sum(
-        dispatch.astype(F32) * gate_back.reshape(groups, capacity, 1), axis=1
-    ).reshape(1, total)
-    gate_back_all = lax.all_gather(gate_back_tokens, ALL, axis=0, tiled=True)
-    gate_back_all = jnp.sum(gate_back_all.reshape(2, experts, total), axis=0).T
+        matches * gate_back.reshape(groups, capacity, 1), axis=1
+    ).reshape(length, 1)
+    gate_columns = jnp.where(
+        jnp.arange(HDIM, dtype=jnp.int32)[None, :] == mine, gate_back_tokens, 0.0
+    ).astype(BF)
+    mix_sum = jnp.concatenate([mix_part, gate_columns], axis=1)
+    gate_grad_b, up_grad_b, down_grad_b, mix_sum = lax.optimization_barrier(
+        (
+            transposed_left(picked, g_b).astype(BF),
+            transposed_left(picked, u_b).astype(BF),
+            transposed_left(scaled_b, picked_dy).astype(BF),
+            mix_sum,
+        )
+    )
+    mix_back, gate_grad_b = own_rows(mix_sum, 5, (gate_grad_b,))
+    gate_back_own = mix_back[:, width : width + experts]
+    mix_back = mix_back[:, :width]
+
+    router_own = jax.nn.softmax(product(normed_own, router_matrix), axis=-1)
     logit_back = (
-        router * (gate_back_all - jnp.sum(router * gate_back_all, axis=-1, keepdims=True))
+        router_own * (gate_back_own - jnp.sum(router_own * gate_back_own, axis=-1, keepdims=True))
     ).astype(BF)
-    rank = (dp * 4 + ctx) * 4 + exp
-    logit_back_own = lax.dynamic_slice_in_dim(logit_back, rank * quarter, quarter, 0)
-    mix_columns = lax.dynamic_slice_in_dim(mix_all, (dp * 4 + ctx) * dense, dense, 1)
-    router_grad = transposed_left(mix_columns, logit_back)
-
-    half_out = product(act_low, expert_down[0])
-    mixed_part = (
-        product(shared_act, shared_out) + spread((half_out * slot_gate).astype(BF))
-    ).astype(BF)
-    mixed_own = (middle + own_rows(mixed_part, True, 4)).astype(BF)
-
-    gate_grad = transposed_left(picked, g_back)[None]
-    up_grad = transposed_left(picked, u_back)[None]
-    down_grad = transposed_left((act * slot_gate).astype(BF), picked_dy)[None]
-    shared_gu_grad = transposed_left(mix_all, shared_gu_back).astype(BF)
-    shared_down_part = transposed_left(shared_act, dy_all).astype(BF)
-
-    mix_back = mix_back + transposed_right(logit_back_own, router_matrix)
+    router_part = transposed_left(normed_own, logit_back)
+
+    mix_back = mix_back + transposed_right(logit_back, router_matrix)
     _, norm_mix_back = jax.vjp(rms_scale, middle, mixer_gain)
     middle_norm_back, gain_mix_part = norm_mix_back(mix_back)
     middle_back = dy_own.astype(F32) + middle_norm_back
     attn_back = middle_back.astype(BF)
-    attn_back_all = all_rows(attn_back, False, 1)
+    attn_back_all, up_grad_b = all_rows(attn_back, False, 7, (), (up_grad_b,))
     heads_back = transposed_right(attn_back_all, w_out_head).astype(BF)
     out_part = transposed_left(heads_out, attn_back_all).astype(BF)
     dq, dk, dv = attend_back(query, key, value, heads_back, lse)
@@ -1027,69 +1144,66 @@
         ],
         axis=1,
     )
-    normed_back = own_rows(transposed_right(qkv_back, w_qkv).astype(BF), False, 2)
+    normed_back, down_grad_b = own_rows(transposed_right(qkv_back, w_qkv).astype(BF), 8, (down_grad_b,))
     qkv_part = transposed_left(normed, qkv_back).astype(BF)
     _, norm_attn_back = jax.vjp(rms_scale, tokens_own.astype(F32), attention_gain)
     input_norm_back, gain_attn_part = norm_attn_back(normed_back)
     tokens_back_own = (middle_back + input_norm_back).astype(BF)
 
-    tokens_back = lax.all_gather(tokens_back_own, "exp", axis=0, tiled=True)
-    mixed = lax.all_gather(mixed_own, "exp", axis=0, tiled=True)
-    gains = jnp.stack([gain_attn_part, gain_mix_part], axis=0)
-    gains = gains.reshape(2, group, 1, dense).transpose(1, 2, 0, 3)
-    gains = jnp.broadcast_to(gains, (group, 4, 2, dense)).reshape(32, 2 * dense)
-    gains = lax.all_to_all(gains, ALL, split_axis=0, concat_axis=0, tiled=True)
-    gains = jnp.sum(gains, axis=0)
-    dense_parts = swap(
-        jnp.concatenate(
-            [
-                qkv_part.reshape(group, dense, 3 * HDIM),
-                shared_gu_grad.reshape(group, dense, 2 * wide),
-                jnp.concatenate(
-                    [
-                        out_part.reshape(HDIM, group, dense).transpose(1, 0, 2),
-                        shared_down_part.reshape(wide, group, dense).transpose(1, 0, 2),
-                    ],
-                    axis=1,
-                ),
-            ],
-            axis=2,
-        )
+    half_a = product(act_a, expert_down[0]).astype(BF).astype(F32)
+    half_b = product(act_b, other_down).astype(BF).astype(F32)
+    mixed_part = (
+        product(shared_act, shared_out) + spread(((half_a + half_b) * slot_gate).astype(BF))
+    ).astype(BF)
+    mixed_own = (middle + own_rows(mixed_part, 3)).astype(BF)
+
+    mixed, tokens_back = share([mixed_own, tokens_back_own], 6)
+    small = jnp.concatenate(
+        [gain_attn_part[:, None], gain_mix_part[:, None], router_part], axis=1
+    ).reshape(8, 1, dense * (experts + 2))
+    small = jnp.broadcast_to(small, (8, 4, dense * (experts + 2))).reshape(32, -1)
+    small = lax.all_to_all(small, ALL, split_axis=0, concat_axis=0, tiled=True)
+    small = jnp.sum(small, axis=0).reshape(dense, experts + 2)
+    shared_gu_grad = transposed_left(mix_all, shared_gu_back).astype(BF)
+    shared_gu_grad = jnp.concatenate(
+        [shared_gu_grad[:, :cut], shared_gu_grad[:, wide : wide + cut]], axis=1
+    )
+    shared_gu_grad = jnp.pad(shared_gu_grad, ((0, 0), (0, 3 * HDIM - 2 * cut)))
+    shared_down_part = transposed_left(shared_act, dy_all).astype(BF)[:cut]
+    home_rows = swap(
+        jnp.concatenate([qkv_part, shared_gu_grad], axis=1).reshape(8, dense, 6 * HDIM)
     ).astype(F32)
-
-    def head_columns(parts):
-        summed = parts[:4] + parts[4:]
-        return summed.transpose(1, 0, 2).reshape(dense, 4 * HDIM)
-
-    def unit_columns(parts):
-        return parts[:, :, :cut].transpose(1, 0, 2).reshape(dense, group * cut)
-
-    query_grad = head_columns(dense_parts[:, :, :HDIM])
-    key_grad = head_columns(dense_parts[:, :, HDIM : 2 * HDIM])
-    value_grad = head_columns(dense_parts[:, :, 2 * HDIM : 3 * HDIM])
-    base = 3 * HDIM
-    sgate_grad = unit_columns(dense_parts[:, :, base : base + wide])
-    sup_grad = unit_columns(dense_parts[:, :, base + wide : base + 2 * wide])
-    base = base + 2 * wide
-    out_blocks = dense_parts[:, :HDIM, base:]
-    out_grad_weights = (out_blocks[:4] + out_blocks[4:]).reshape(4 * HDIM, dense)
-    sdown_grad = dense_parts[:, HDIM : HDIM + cut, base:].reshape(group * cut, dense)
+    home_columns = swap(
+        jnp.concatenate([out_part, shared_down_part], axis=0)
+        .reshape(HDIM + cut, 8, dense)
+        .transpose(1, 0, 2)
+    ).astype(F32)
+    home_rows = home_rows[:4] + home_rows[4:]
+    home_columns = home_columns[:4] + home_columns[4:]
+
+    def columns_of(parts):
+        return parts.transpose(1, 0, 2).reshape(dense, -1)
+
+    units = 3 * HDIM
+    gate_grad = transposed_left(picked, g_a) + gate_grad_b.astype(F32)
+    up_grad = transposed_left(picked, u_a) + up_grad_b.astype(F32)
+    down_grad = transposed_left(scaled_a, picked_dy) + down_grad_b.astype(F32)
     return (
         mixed[None],
         tokens_back[None],
-        gains[:dense],
-        query_grad,
-        key_grad,
-        value_grad,
-        out_grad_weights,
-        gains[dense:],
-        router_grad,
-        sgate_grad,
-        sup_grad,
-        sdown_grad,
-        gate_grad,
-        up_grad,
-        down_grad,
+        small[:, 0],
+        columns_of(home_rows[:, :, :HDIM]),
+        columns_of(home_rows[:, :, HDIM : 2 * HDIM]),
+        columns_of(home_rows[:, :, 2 * HDIM : 3 * HDIM]),
+        home_columns[:, :HDIM].reshape(4 * HDIM, dense),
+        small[:, 1],
+        small[:, 2:],
+        columns_of(home_rows[:, :, units : units + cut]),
+        columns_of(home_rows[:, :, units + cut : units + 2 * cut]),
+        home_columns[:, HDIM:].reshape(4 * cut, dense),
+        gate_grad[None],
+        up_grad[None],
+        down_grad[None],
     )
 
 

time: 1210 us -> 1010 us (0.83)
  waiting for transfers between devices: 89.9 us -> 13.7 us
  blocking collectives: 41.6 us -> 0 us
  matrix products: 285 us -> 257 us
  Pallas kernels: 638 us -> 613 us
  between operations: 15.5 us -> 2.24 us
    all_to_all x3 -> x2, waiting for transfers between devices: 89.4 us -> 4.79 us  [swap(): lax.all_to_all(blocks, DENSE, split_axis=0, concat_axis=0, tiled=True)]
    all_gather x1 -> x0, blocking collectives: 41.6 us -> none  [fast_body(): gate_back_all = lax.all_gather(gate_back_tokens, ALL, axis=0, tiled=True)]
    pallas_call x8 -> x9, Pallas kernels: 618 us -> 592 us  [the longest x4 306 us: all_rows(): pl.pallas_call(functools.partial(gather_kernel, block, rows, parts, extra...]
    dot_general x2, matrix products: 32.6 us -> 16.4 us  [spread(): jnp.einsum('gst,gsd->gtd', dispatch, rows.reshape(groups, capacity, width...]
    dot_general x2, matrix products: 23 us -> 8.22 us  [pick(): jnp.einsum('gst,gtd->gsd', dispatch, rows.reshape(groups, quarter, width)...]
    unnamed x121 -> x168, local copies, waits for them, and re-layouts: 15.6 us -> 29.7 us
    dot_general x8 -> x11, matrix products: 57.7 us -> 69.7 us  [transposed_left(): lax.dot_general(left_side, right_side, (((0,), (0,)), ((), ())), preferre...]
    dot_general x8 -> x12, matrix products: 83.9 us -> 74.1 us  [product(): return jnp.dot(left_side, right_side, preferred_element_type=jnp.float32)]
  transfers between devices with their start and end apart: 6 -> 6, of which waited for: 2 -> 2; matrix products, arithmetic and copies ran while one was open for 10% -> 20% of each run, Pallas kernels for 22% -> 28%
where the time goes in v2:
time: 1010 us; the launch traced here: 1000 us
  Pallas kernels  613 us (61%)
  matrix products  257 us (25%)
  local copies, waits for them, and re-layouts  55.1 us (5%)
  other arithmetic  48.9 us (5%)
  starting transfers between devices  15.1 us (1%)
  waiting for transfers between devices  13.7 us (1%)
    pallas_call x4, Pallas kernels, all_rows(): pl.pallas_call(functools.partial(gather_kernel, block, rows, parts, extra...  306 us
    pallas_call x4, Pallas kernels, own_rows(): pl.pallas_call(functools.partial(scatter_kernel, rows, swaps), out_shape=...  252 us
    dot_general x11, matrix products, transposed_right(): lax.dot_general(left_side, right_side, (((1,), (1,)), ((), ())), preferre...  88.1 us
    dot_general x12, matrix products, product(): return jnp.dot(left_side, right_side, preferred_element_type=jnp.float32)  74.1 us
    dot_general x11, matrix products, transposed_left(): lax.dot_general(left_side, right_side, (((0,), (0,)), ((), ())), preferre...  69.7 us
    pallas_call x1, Pallas kernels, share(): pl.pallas_call(functools.partial(share_kernel, rows, count), out_shape=[j...  33.4 us
    unnamed x168, local copies, waits for them, and re-layouts  29.7 us
  transfers between devices with their start and end apart: 6, of which 2 were waited for; matrix products, arithmetic and copies ran while one was open for 20% of the time, Pallas kernels for 28%

profile of v2, /device:TPU:0, one launch (start us, length us, event | category | flops | bytes accessed | tf_op | source)
XLA Modules:
  0.0 1004.1 jit_solution(17169127429733525593)
XLA Ops:
  11.7 111.1 %shard_map.289 = (bf16[2048,2048]{1,0:T(8,128)(2,1)}, bf16[8,256,512]{2,1,0:T(8,128)(2,1)}, bf16[8,128,256]{2,1,0:T(8,128)(2,1)}, bf16[8,256,384]{2,1,0:T(8,128)(2,1)}, bf16[8,176,256]{2,1,0:T(8,128)(2,1)}) custom-call(bf16[512,2048]{1,0:T(8,128)(2,1)} %bitcast.186, bf16[4,256,512]{2,1,0:T(8,128)(2,1)} %pad_maximum_fusion.6.refs_1_, ...), custom_call_target="tpu_custom_call" | custom-call | tf_op jit(solution)/shard_map/pallas_call | solution.py:641
  145.8 8.6 shard_map.290
  157.7 56.4 %shard_map.291 = f32[128,2048]{1,0:T(8,128)S(1)} custom-call(bf16[2048,2048]{1,0:T(8,128)(2,1)S(1)} %convolution_convert_fusion.1.in_ref), custom_call_target="tpu_custom_call" | custom-call | tf_op jit(solution)/shard_map/pallas_call | solution.py:772
  217.4 58.8 %shard_map.292 = bf16[2048,2048]{1,0:T(8,128)(2,1)} custom-call(bf16[128,2048]{1,0:T(8,128)(2,1)} %copy-done.11), custom_call_target="tpu_custom_call" | custom-call | tf_op jit(solution)/shard_map/pallas_call | solution.py:641
  299.1 65.7 %shard_map.294 = bf16[2048,2048]{1,0:T(8,128)(2,1)} custom-call(bf16[512,2048]{1,0:T(8,128)(2,1)} %bitcast.189), custom_call_target="tpu_custom_call" | custom-call | tf_op jit(solution)/shard_map/pallas_call | solution.py:641
  375.9 9.7 fusion.34
  436.5 8.9 convolution_convert_fusion.6.refs_0_
  480.2 11.4 %add_convert_fusion = bf16[1024,2048]{1,0:T(8,128)(2,1)S(1)} fusion(f32[1024,2048]{1,0:T(8,128)} %fusion.114, f32[1024,2048]{1,0:T(8,128)} %fusion.87, f32[1024,2048]{1,0:T(8,128)} %fusion.83, bf16[1024,704]{0,1:T(8,128)(2,1)S(1)} %get-tuple-element.201, bf16[2048,704]{0,1:T(8,128)(2,1)} %collective-permute-done.1), kind=kOutput, calls=%fused_computation.10 | convolution fusion | flops 2961178624 | bytes 33685504 | tf_op jit(solution)/shard_map/dot_general | solution.py:59
  491.6 8.2 fusion.46
  499.8 14.9 %fusion.3 = bf16[2048,2048]{1,0:T(8,128)(2,1)} fusion(f32[16,128,2048]{2,1,0:T(8,128)} %fusion.46, bf16[2048,256]{0,1:T(8,128)(2,1)} %copy-done.72, bf16[2048,256]{0,1:T(8,128)(2,1)} %copy-done.71, bf16[2048,176]{1,0:T(8,128)(2,1)} %slice.170, bf16[2048,256]{1,0:T(8,128)(2,1)} %slice_select_fusion), kind=kOutput, calls=%fused_computation.6 | convolution fusion | flops 4313841664 | bytes 29032448 | tf_op jit(solution)/shard_map/dot_general | solution.py:59
  515.8 8.1 pad_maximum_fusion.in_ref
  524.0 71.7 %shard_map.295 = (f32[128,2176]{1,0:T(8,128)S(1)}, bf16[2048,704]{1,0:T(8,128)(2,1)S(1)}) custom-call(bf16[2048,2176]{1,0:T(8,128)(2,1)} %pad_maximum_fusion.in_ref, bf16[2048,704]{1,0:T(8,128)(2,1)S(1)} %convolution_convert_fusion.5.refs_0_), custom_call_target="tpu_custom_call" | custom-call | tf_op jit(solution)/shard_map/pallas_call | solution.py:772
  601.6 70.6 %shard_map.296 = (bf16[2048,2048]{1,0:T(8,128)(2,1)}, bf16[2048,704]{1,0:T(8,128)(2,1)}) custom-call(bf16[128,2048]{1,0:T(8,128)(2,1)} %fusion.104.refs_0_, bf16[2048,704]{1,0:T(8,128)(2,1)} %convolution_convert_fusion.4.refs_1_), custom_call_target="tpu_custom_call" | custom-call | tf_op jit(solution)/shard_map/pallas_call | solution.py:641
  678.7 12.0 %shard_map.297 = (f32[2048,128]{1,0:T(8,128)}, f32[2048,128]{1,0:T(8,128)}, f32[2048,128]{1,0:T(8,128)}) custom-call(bf16[2048,128]{1,0:T(8,128)(2,1)} %get-tuple-element.209.q_ref, bf16[2048,128]{1,0:T(8,128)(2,1)} %get-tuple-element.210.k_ref, bf16[2048,128]{1,0:T(8,128)(2,1)} %slice.243.v_ref, bf16[2048,128]{1,0:T(8,128)(2,1)} %convolution_convert_fusion.10.do_ref, ...), custom_call_target="tpu_custom_call" | custom-call | tf_op jit(solution)/shard_map/pallas_call | solution.py:921
  700.4 8.4 convolution_convert_fusion.in_ref
  708.7 65.6 %shard_map.298 = (f32[128,2048]{1,0:T(8,128)S(1)}, bf16[704,2048]{1,0:T(8,128)(2,1)S(1)}) custom-call(bf16[2048,2048]{1,0:T(8,128)(2,1)} %convolution_convert_fusion.in_ref, bf16[704,2048]{1,0:T(8,128)(2,1)S(1)} %copy-done), custom_call_target="tpu_custom_call" | custom-call | tf_op jit(solution)/shard_map/pallas_call | solution.py:772
  792.1 8.9 all-to-all-done
  805.4 9.8 add_bitcast_fusion.1
  841.2 9.4 add_bitcast_fusion
  863.5 8.2 fusion.47
  871.8 8.2 fusion.4.in_ref
  880.0 58.8 %shard_map.293 = f32[128,2048]{1,0:T(8,128)S(1)} custom-call(bf16[2048,2048]{1,0:T(8,128)(2,1)S(1)} %fusion.4.in_ref), custom_call_target="tpu_custom_call" | custom-call | tf_op jit(solution)/shard_map/pallas_call | solution.py:772
  941.6 33.4 %shard_map.299 = (bf16[512,2048]{1,0:T(8,128)(2,1)}, bf16[512,2048]{1,0:T(8,128)(2,1)}) custom-call(bf16[128,2048]{1,0:T(8,128)(2,1)} %get-tuple-element.199.refs_0_, bf16[128,2048]{1,0:T(8,128)(2,1)} %get-tuple-element.198.refs_1_), custom_call_target="tpu_custom_call" | custom-call | tf_op jit(solution)/shard_map/pallas_call | solution.py:836
  974.9 10.6 %add_bitcast_fusion.2 = f32[1,704,2048]{2,1,0:T(8,128)} fusion(bf16[704,2048]{1,0:T(8,128)(2,1)} %copy-done.2, bf16[1024,2048]{1,0:T(8,128)(2,1)} %bitcast.172, f32[1024]{0:T(1024)S(1)} %mul.344, f32[1024,704]{0,1:T(8,128)} %fusion.85, f32[1024,704]{0,1:T(8,128)} %fusion.89), kind=kOutput, calls=%fused_computation.16 | convolution fusion | flops 2960719872 | bytes 18616320 | tf_op jit(solution)/shard_map/dot_general | solution.py:53
  (293 shorter events, 264.6 us)
Async XLA Ops:
  122.8 298.8 %collective-permute-start = (bf16[2048,704]{0,1:T(8,128)(2,1)}, bf16[2048,704]{0,1:T(8,128)(2,1)}, u32[]{:S(2)}, u32[]{:S(2)}) collective-permute-start(bf16[2048,704]{0,1:T(8,128)(2,1)} %bitcast.16), channel_id=1, source_target_pairs={{0,16},{16,0},{1,17},{17,1},{2,18},{18,2},{3,19},{19,3},{4,20},{20... | collective-permute-start | bytes 8650760 | tf_op jit(solution)/shard_map/ppermute | solution.py:864
  122.9 293.6 %collective-permute-start.1 = (bf16[2048,704]{0,1:T(8,128)(2,1)}, bf16[2048,704]{0,1:T(8,128)(2,1)}, u32[]{:S(2)}, u32[]{:S(2)}) collective-permute-start(bf16[2048,704]{0,1:T(8,128)(2,1)} %bitcast.17), channel_id=1, source_target_pairs={{0,16},{16,0},{1,17},{17,1},{2,18},{18,2},{3,19},{19,3},{4,20},{20... | collective-permute-start | bytes 8650760 | tf_op jit(solution)/shard_map/ppermute | solution.py:864
  124.9 302.9 %collective-permute-start.2 = (bf16[704,2048]{1,0:T(8,128)(2,1)}, bf16[704,2048]{1,0:T(8,128)(2,1)}, u32[]{:S(2)}, u32[]{:S(2)}) collective-permute-start(bf16[704,2048]{1,0:T(8,128)(2,1)} %bitcast.18), channel_id=1, source_target_pairs={{0,16},{16,0},{1,17},{17,1},{2,18},{18,2},{3,19},{19,3},{4,20},{20... | collective-permute-start | bytes 8650760 | tf_op jit(solution)/shard_map/ppermute | solution.py:864
  127.5 88.0 %copy-start.53 = (f32[2048]{0:T(1024)}, f32[2048]{0:T(1024)S(1)}, u32[]{:S(2)}) copy-start(f32[2048]{0:T(1024)S(1)} %get-tuple-element.161) | copy-start | bytes 24580
  215.5 60.8 %copy-start.69 = (f32[128]{0:T(128)}, f32[128]{0:T(128)S(1)}, u32[]{:S(2)}) copy-start(f32[128]{0:T(128)S(1)} %get-tuple-element.171) | copy-start | bytes 1540
  215.5 158.8 %copy-start.67 = (f32[128]{0:T(128)}, f32[128]{0:T(128)S(1)}, u32[]{:S(2)}) copy-start(f32[128]{0:T(128)S(1)} %get-tuple-element.195) | copy-start | bytes 1540
  215.5 60.8 %copy-start.61 = (f32[128]{0:T(128)}, f32[128]{0:T(128)S(1)}, u32[]{:S(2)}) copy-start(f32[128]{0:T(128)S(1)} %fusion.72) | copy-start | bytes 1540
  217.4 157.6 %copy-start.59 = (f32[128]{0:T(128)}, f32[128]{0:T(128)S(1)}, u32[]{:S(2)}) copy-start(f32[128]{0:T(128)S(1)} %get-tuple-element.206) | copy-start | bytes 1540
  299.1 65.7 %copy-start.48 = (bf16[8,176,256]{2,1,0:T(8,128)(2,1)S(1)}, bf16[8,176,256]{2,1,0:T(8,128)(2,1)}, u32[]{:S(2)}) copy-start(bf16[8,176,256]{2,1,0:T(8,128)(2,1)} %get-tuple-element.47) | copy-start | bytes 2162692
  299.1 65.8 %copy-start.34 = (bf16[8,256,384]{2,1,0:T(8,128)(2,1)S(1)}, bf16[8,256,384]{2,1,0:T(8,128)(2,1)}, u32[]{:S(2)}) copy-start(bf16[8,256,384]{2,1,0:T(8,128)(2,1)} %get-tuple-element.46) | copy-start | bytes 4718596
  524.0 71.8 %copy-start.47 = (f32[128,16]{1,0:T(8,128)S(1)}, f32[128,16]{1,0:T(8,128)}, u32[]{:S(2)}) copy-start(f32[128,16]{1,0:T(8,128)} %copy-done.46) | copy-start | bytes 24580
  524.0 71.8 %copy-start.60 = (f32[128]{0:T(128)S(1)}, f32[128]{0:T(128)}, u32[]{:S(2)}) copy-start(f32[128]{0:T(128)} %copy-done.59) | copy-start | bytes 1540
  524.0 71.8 %copy-start.63 = (f32[128]{0:T(128)S(1)}, f32[128]{0:T(128)}, u32[]{:S(2)}) copy-start(f32[128]{0:T(128)} %fusion.71) | copy-start | bytes 1540
  524.0 72.0 %copy-start.12 = (bf16[128,2048]{1,0:T(8,128)(2,1)S(1)}, bf16[128,2048]{1,0:T(8,128)(2,1)}, u32[]{:S(2)}) copy-start(bf16[128,2048]{1,0:T(8,128)(2,1)} %copy-done.11) | copy-start | bytes 1572868
  524.0 72.3 %copy-start.5 = (f32[128,2048]{1,0:T(8,128)S(1)}, f32[128,2048]{1,0:T(8,128)}, u32[]{:S(2)}) copy-start(f32[128,2048]{1,0:T(8,128)} %copy-done.4) | copy-start | bytes 3145732
  524.0 72.3 %copy-start.54 = (f32[2048]{0:T(1024)S(1)}, f32[2048]{0:T(1024)}, u32[]{:S(2)}) copy-start(f32[2048]{0:T(1024)} %copy-done.53) | copy-start | bytes 24580
  524.0 72.3 %copy-start.62 = (f32[128]{0:T(128)S(1)}, f32[128]{0:T(128)}, u32[]{:S(2)}) copy-start(f32[128]{0:T(128)} %copy-done.61) | copy-start | bytes 1540
  599.3 72.8 %copy-start.38 = (bf16[128,8,256]{0,2,1:T(8,128)(2,1)S(1)}, bf16[128,8,256]{0,2,1:T(8,128)(2,1)}, u32[]{:S(2)}) copy-start(bf16[128,8,256]{0,2,1:T(8,128)(2,1)} %copy-done.37) | copy-start | bytes 1572868
  708.7 67.2 %copy-start.56 = (f32[2048]{0:T(1024)S(1)}, f32[2048]{0:T(1024)}, u32[]{:S(2)}) copy-start(f32[2048]{0:T(1024)} %copy-done.55) | copy-start | bytes 24580
  708.7 67.2 %copy-start.64 = (f32[128]{0:T(128)S(1)}, f32[128]{0:T(128)}, u32[]{:S(2)}) copy-start(f32[128]{0:T(128)} %fusion.73) | copy-start | bytes 1540
  780.0 21.0 %all-to-all-start = ((f32[32,1,4608]{2,1,0:T(1,128)}), f32[32,1,4608]{2,1,0:T(1,128)}, u32[]{:S(2)}, u32[]{:S(2)}) async-start(f32[32,1,4608]{2,1,0:T(1,128)} %all_to_all.12), calls=%async_computation | async-start | bytes 1179648 | tf_op jit(solution)/shard_map/all_to_all | solution.py:1165
  801.0 35.4 %all-to-all-start.2 = ((bf16[8,304,256]{2,1,0:T(8,128)(2,1)}), bf16[8,304,256]{2,1,0:T(8,128)(2,1)}, u32[]{:S(2)}, u32[]{:S(2)}) async-start(bf16[8,304,256]{2,1,0:T(8,128)(2,1)} %bitcast.187), calls=%async_computation.2 | async-start | bytes 2490368 | tf_op jit(solution)/shard_map/all_to_all | solution.py:855
  836.4 155.7 %all-to-all-start.1 = ((bf16[8,256,768]{1,2,0:T(8,128)(2,1)}), bf16[8,256,768]{1,2,0:T(8,128)(2,1)}, u32[]{:S(2)}, u32[]{:S(2)}) async-start(bf16[8,256,768]{1,2,0:T(8,128)(2,1)} %bitcast.184), calls=%async_computation.1 | async-start | bytes 6291456 | tf_op jit(solution)/shard_map/all_to_all | solution.py:855
  880.0 58.9 %copy-start.6 = (f32[128,2048]{1,0:T(8,128)S(1)}, f32[128,2048]{1,0:T(8,128)}, u32[]{:S(2)}) copy-start(f32[128,2048]{1,0:T(8,128)} %copy-done.4) | copy-start | bytes 3145732
  (61 other events, 642.4 us)

commit v3 on v2

--- a/solution.py
+++ b/solution.py
@@ -847,6 +847,495 @@
     )(*arrays)
 
 
+def expert_gather_kernel(experts, *refs):
+    refs = list(refs)
+
+    def take(count):
+        taken = refs[:count]
+        del refs[:count]
+        return taken
+
+    x_ref, dy_ref, disp, w_router, shared_in, shared_out = take(6)
+    weights = take(6)
+    out_ref, picked, picked_dy, scaled_out, g_out, u_out, gb_out, sa_out, sg_out = take(9)
+    wg, wu, wd, xb, dyb, pk, pdy, sc, gg, uu, gb, sa, sg = take(13)
+    own_sem, send_sem, recv_sem, load_sem, block_sem, store_sem = take(6)
+    at = Place()
+    greet(at, False)
+    rows = x_ref.shape[0]
+    block = 4 * rows
+    slots = pk.shape[1]
+    groups = 4
+    slot_z, slot_f, slot_s = 0, 3, 7
+    started, inside = [], []
+    mine = at.z * 4 + at.e
+
+    def where(f, zi):
+        return pl.ds(pl.multiple_of(at.shard(f * at.dy, zi) * rows, rows), rows)
+
+    def push(src, dst, slot, device, sends=None, record=None):
+        j = slot if sends is None else sends
+        remote(src, out_ref.at[dst], send_sem.at[j], recv_sem.at[slot], device).start()
+        (started if record is None else record).append(j)
+
+    f_dev, s_dev, z_dev = at.device(oe=at.dy), at.device(oe=at.dc), at.device(zi=1)
+
+    def gone(j):
+        remote(x_ref, out_ref.at[pl.ds(0, rows)], send_sem.at[j], recv_sem.at[0], s_dev).wait_send()
+
+    def arrive(slot):
+        remote(
+            x_ref, out_ref.at[pl.ds(0, rows)], send_sem.at[slot], recv_sem.at[slot], s_dev
+        ).wait_recv()
+
+    own = pltpu.make_async_copy(x_ref, out_ref.at[where(0, 0)], own_sem)
+
+    def source(f, zi):
+        return x_ref if f == 0 and zi == 0 else out_ref.at[where(f, zi)]
+
+    def along(zi):
+        src, dst = source(0, zi), where(0, zi)
+        if zi == 0:
+            push(src, dst, slot_z, z_dev)
+        if zi < 2:
+            pl.when(at.middle)(lambda: push(src, dst, slot_z + 1 + zi, at.inward(), 15 + zi, inside))
+        else:
+            pl.when(at.middle)(lambda: push(src, dst, slot_z + zi - 1, z_dev, 15 + zi, inside))
+
+    def forward(f, zi):
+        src, dst = source(f, zi), where(f, zi)
+        if f == 0:
+            along(zi)
+            push(src, dst, slot_f + zi, f_dev)
+        push(src, dst, slot_s + f * 4 + zi, s_dev)
+
+    def span(zi, size):
+        return pl.ds(pl.multiple_of(at.zs[zi] * size, size), size)
+
+    def dy_load(zi):
+        return pltpu.make_async_copy(
+            dy_ref.at[span(zi, block)], dyb.at[zi % 2], block_sem.at[2 + zi % 2]
+        )
+
+    def x_load(zi):
+        return pltpu.make_async_copy(
+            out_ref.at[span(zi, block)], xb.at[zi % 2], block_sem.at[zi % 2]
+        )
+
+    def stores(zi):
+        b = zi % 2
+        pairs = [
+            (pk.at[b], picked.at[span(zi, slots)]),
+            (pdy.at[b], picked_dy.at[span(zi, slots)]),
+            (gb.at[b], gb_out.at[span(zi, slots)]),
+            (sa.at[b], sa_out.at[span(zi, block)]),
+            (sg.at[b], sg_out.at[span(zi, block)]),
+        ]
+        for h in range(2):
+            pairs += [
+                (sc.at[b, h], scaled_out.at[h, span(zi, slots)]),
+                (gg.at[b, h], g_out.at[h, span(zi, slots)]),
+                (uu.at[b, h], u_out.at[h, span(zi, slots)]),
+            ]
+        return [
+            pltpu.make_async_copy(src, dst, store_sem.at[b, j]) for j, (src, dst) in enumerate(pairs)
+        ]
+
+    def parts_of(gate, up):
+        s = 1.0 / (1.0 + jnp.exp(-gate))
+        act = gate * s
+        return act * up, s * (1.0 + gate * (1.0 - s)) * up, act
+
+    def work(zi):
+        b = zi % 2
+        dy_load(zi).wait()
+        x_load(zi).wait()
+        if zi >= 2:
+            for copy in stores(zi - 2):
+                copy.wait()
+
+        @pl.loop(0, groups)
+        def _(i):
+            hot = disp[at.zs[zi] * groups + i]
+            source_rows = pl.ds(pl.multiple_of(i * rows, rows), rows)
+            into = pl.ds(pl.multiple_of(i * (slots // groups), slots // groups), slots // groups)
+            pk[b, into, :] = product(hot, xb[b, source_rows, :]).astype(BF)
+            pdy[b, into, :] = product(hot, dyb[b, source_rows, :]).astype(BF)
+
+        logits = transposed_right(pk[b], w_router[...])
+        lane = lax.broadcasted_iota(jnp.int32, logits.shape, 1)
+        logits = jnp.where(lane < experts, logits, MASKED)
+        powers = jnp.exp(logits - jnp.max(logits, axis=1, keepdims=True))
+        own_power = jnp.sum(jnp.where(lane == mine, powers, 0.0), axis=1, keepdims=True)
+        gate_of = own_power / jnp.sum(powers, axis=1, keepdims=True)
+        gb[b] = jnp.zeros(gb.shape[1:], F32)
+
+        @pl.loop(0, 2)
+        def _(h):
+            hidden, by_gate, by_up = parts_of(
+                transposed_right(pk[b], wg[h]), transposed_right(pk[b], wu[h])
+            )
+            dy_down = transposed_right(pdy[b], wd[h])
+            act_back = gate_of * dy_down
+            gg[b, h] = (act_back * by_gate).astype(BF)
+            uu[b, h] = (act_back * by_up).astype(BF)
+            sc[b, h] = (hidden * gate_of).astype(BF)
+            gb[b] += jnp.broadcast_to(
+                jnp.sum(hidden * dy_down, axis=1, keepdims=True), gb.shape[1:]
+            )
+
+        @pl.loop(0, groups)
+        def _(i):
+            token_rows = pl.ds(pl.multiple_of(i * rows, rows), rows)
+            both = transposed_right(xb[b, token_rows, :], shared_in[...])
+            wide = both.shape[1] // 2
+            hidden, by_gate, by_up = parts_of(both[:, :wide], both[:, wide:])
+            back = transposed_right(dyb[b, token_rows, :], shared_out[...])
+            sa[b, token_rows, :] = hidden.astype(BF)
+            sg[b, token_rows, :wide] = (back * by_gate).astype(BF)
+            sg[b, token_rows, wide:] = (back * by_up).astype(BF)
+
+        for copy in stores(zi):
+            copy.start()
+
+    forward(0, 0)
+    own.start()
+    loads = []
+    for m, (ref, half) in enumerate([(wg, 0), (wu, 0), (wd, 0), (wg, 1), (wu, 1), (wd, 1)]):
+        loads.append(pltpu.make_async_copy(weights[m], ref.at[half], load_sem.at[m]))
+        loads[-1].start()
+    dy_load(0).start()
+    for zi in range(4):
+        arrive(slot_f + zi)
+        forward(1, zi)
+        if zi < 3:
+            arrive(slot_z + zi)
+            forward(0, zi + 1)
+            dy_load(zi + 1).start()
+        for f in range(2):
+            arrive(slot_s + f * 4 + zi)
+        if zi == 0:
+            own.wait()
+            for copy in loads:
+                copy.wait()
+        x_load(zi).start()
+        work(zi)
+    for zi in (2, 3):
+        for copy in stores(zi):
+            copy.wait()
+    for j in started:
+        gone(j)
+
+    @pl.when(at.middle)
+    def _():
+        for j in inside:
+            gone(j)
+
+
+def expert_rows(x, dy_all, dispatch, w_router, experts, shared_in, shared_out, weights, cid):
+    rows, width = x.shape
+    total, block = 16 * rows, 4 * rows
+    slots = 4 * dispatch.shape[1]
+    hidden = weights[0].shape[0]
+    wide = shared_out.shape[0]
+    hbm, vmem = pl.BlockSpec(memory_space=pl.ANY), pl.BlockSpec(memory_space=pltpu.VMEM)
+    shape = jax.ShapeDtypeStruct
+    return pl.pallas_call(
+        functools.partial(expert_gather_kernel, experts),
+        out_shape=[
+            shape((total, width), BF),
+            shape((4 * slots, width), BF),
+            shape((4 * slots, width), BF),
+            shape((2, 4 * slots, hidden), BF),
+            shape((2, 4 * slots, hidden), BF),
+            shape((2, 4 * slots, hidden), BF),
+            shape((4 * slots, 128), F32),
+            shape((total, wide), BF),
+            shape((total, 2 * wide), BF),
+        ],
+        in_specs=[hbm, hbm, vmem, vmem, vmem, vmem] + [hbm] * 6,
+        out_specs=[hbm] * 9,
+        scratch_shapes=[
+            pltpu.VMEM((2, hidden, width), BF),
+            pltpu.VMEM((2, hidden, width), BF),
+            pltpu.VMEM((2, hidden, width), BF),
+            pltpu.VMEM((2, block, width), BF),
+            pltpu.VMEM((2, block, width), BF),
+            pltpu.VMEM((2, slots, width), BF),
+            pltpu.VMEM((2, slots, width), BF),
+            pltpu.VMEM((2, 2, slots, hidden), BF),
+            pltpu.VMEM((2, 2, slots, hidden), BF),
+            pltpu.VMEM((2, 2, slots, hidden), BF),
+            pltpu.VMEM((2, slots, 128), F32),
+            pltpu.VMEM((2, block, wide), BF),
+            pltpu.VMEM((2, block, 2 * wide), BF),
+            pltpu.SemaphoreType.DMA,
+            pltpu.SemaphoreType.DMA((19,)),
+            pltpu.SemaphoreType.DMA((15,)),
+            pltpu.SemaphoreType.DMA((6,)),
+            pltpu.SemaphoreType.DMA((4,)),
+            pltpu.SemaphoreType.DMA((2, 11)),
+        ],
+        compiler_params=pltpu.CompilerParams(
+            collective_id=cid, has_side_effects=True, vmem_limit_bytes=60 * 1024 * 1024
+        ),
+    )(x, dy_all, dispatch, w_router, shared_in, shared_out, *weights)
+
+
+def expert_scatter_kernel(*refs):
+    refs = list(refs)
+
+    def take(count):
+        taken = refs[:count]
+        del refs[:count]
+        return taken
+
+    disp, gate_back, shared_in, g_ref, u_ref, sg_ref, picked_ref, dy_ref, scaled_ref = take(9)
+    weights = take(4)
+    out_ref, grad_gate, grad_up, grad_down = take(4)
+    wg, wu, gs, us, sg, picked, picked_dy, scaled, ib, grad, turned = take(11)
+    acc, got_s, got_f, got_z, out_s = take(5)
+    load_sem, store_sem, send_sem, recv_sem = take(4)
+    at = Place()
+    greet(at, False)
+    rows, full = acc.shape[1:]
+    width = shared_in.shape[1]
+    slots = ib.shape[0]
+    capacity = slots // 4
+    mine = at.z * 4 + at.e
+    slot_z, slot_f, slot_s = 0, 5, 9
+    f_dev, s_dev, z_dev = at.device(oe=at.dy), at.device(oe=at.dc), at.device(zi=1)
+    started, in_middle, at_end = [], [], []
+
+    def push(src, dst, slot, device, sends=None, record=started):
+        j = slot if sends is None else sends
+        remote(src, dst, send_sem.at[j], recv_sem.at[slot], device).start()
+        record.append(j)
+
+    def gone(j):
+        remote(acc.at[0], acc.at[0], send_sem.at[j], recv_sem.at[0], s_dev).wait_send()
+
+    def arrive(dst, slot):
+        remote(acc.at[0], dst, send_sem.at[slot], recv_sem.at[slot], s_dev).wait_recv()
+
+    pairs = [
+        (weights[0], wg.at[0]),
+        (weights[1], wu.at[0]),
+        (weights[2], wg.at[1]),
+        (weights[3], wu.at[1]),
+        (g_ref, gs),
+        (u_ref, us),
+        (sg_ref, sg),
+        (picked_ref, picked),
+        (dy_ref, picked_dy),
+        (scaled_ref.at[1], scaled),
+    ]
+    loads = [pltpu.make_async_copy(a, b, load_sem.at[j]) for j, (a, b) in enumerate(pairs)]
+    for copy in loads:
+        copy.start()
+
+    def work(zi):
+        place = at.zs[zi]
+        some = pl.ds(pl.multiple_of(place * slots, slots), slots)
+
+        @pl.loop(0, 4)
+        def _(n):
+            columns = pl.ds(pl.multiple_of(n * (width // 4), width // 4), width // 4)
+            total = product(gs[0, some, :], wg[0, :, columns])
+            total += product(us[0, some, :], wu[0, :, columns])
+            total += product(gs[1, some, :], wg[1, :, columns])
+            total += product(us[1, some, :], wu[1, :, columns])
+            ib[:, columns] = total.astype(BF)
+
+        for twin in range(2):
+            for f in range(2):
+                e = at.e + f * at.dy + twin * at.dc
+                hot = disp[place * 4 + e]
+                mine_slots = pl.ds(pl.multiple_of(e * capacity, capacity), capacity)
+                tokens = pl.ds(pl.multiple_of((place * 4 + e) * rows, rows), rows)
+                into, k = (out_s, f * 2 + zi % 2) if twin else (acc, f * 4 + zi)
+
+                @pl.loop(0, 2)
+                def _(n):
+                    columns = pl.ds(pl.multiple_of(n * (width // 2), width // 2), width // 2)
+                    total = transposed_left(hot, ib[mine_slots, columns])
+                    total += product(sg[tokens, :], shared_in[:, columns])
+                    into[k, :, columns] = total.astype(BF)
+
+                from_gates = gate_back[
+                    pl.ds(pl.multiple_of(place * slots + e * capacity, capacity), capacity), :
+                ]
+                lane = lax.broadcasted_iota(jnp.int32, from_gates.shape, 1)
+                from_gates = jnp.where(lane == mine, from_gates, 0.0).astype(BF)
+                into[k, :, width:] = transposed_left(hot, from_gates).astype(BF)
+
+    def to_twin(zi):
+        for f in range(2):
+            push(
+                out_s.at[f * 2 + zi % 2],
+                got_s.at[f * 4 + zi],
+                slot_s + f * 4 + zi,
+                s_dev,
+                None,
+                twins[zi],
+            )
+
+    twins = [[], [], [], []]
+
+    def add(k, *others, into=None):
+        @pl.loop(0, rows // 16)
+        def _(i):
+            span = pl.ds(pl.multiple_of(i * 16, 16), 16)
+            total = acc[k, span, :].astype(F32)
+            for ref, j in others:
+                total = total + ref[j, span, :].astype(F32)
+            if into is None:
+                acc[k, span, :] = total.astype(BF)
+            else:
+                into[span, :] = total
+
+    def first(zi):
+        arrive(got_s.at[4 + zi], slot_s + 4 + zi)
+        add(4 + zi, (got_s, 4 + zi))
+        push(acc.at[4 + zi], got_f.at[zi], slot_f + zi, f_dev)
+
+    def second(zi):
+        arrive(got_s.at[zi], slot_s + zi)
+        arrive(got_f.at[zi], slot_f + zi)
+        others = [(got_s, zi), (got_f, zi)]
+        if zi >= 2:
+
+            @pl.when(at.middle)
+            def _():
+                arrive(got_z.at[3 - zi], slot_z + 3 - zi)
+                add(zi, *others, (got_z, 3 - zi))
+                there = 4 if zi == 2 else 3
+                push(
+                    acc.at[zi], got_z.at[there], slot_z + there, at.inward(), slot_z + zi, in_middle
+                )
+
+            @pl.when(jnp.logical_not(at.middle))
+            def _():
+                add(zi, *others)
+                push(acc.at[zi], got_z.at[3 - zi], slot_z + 3 - zi, z_dev, slot_z + zi, at_end)
+        elif zi == 1:
+
+            @pl.when(at.middle)
+            def _():
+                arrive(got_z.at[3], slot_z + 3)
+                add(zi, *others, (got_z, 3))
+                push(acc.at[zi], got_z.at[4], slot_z + 4, z_dev, slot_z + 1, in_middle)
+
+            @pl.when(jnp.logical_not(at.middle))
+            def _():
+                add(zi, *others)
+                push(acc.at[zi], got_z.at[2], slot_z + 2, z_dev, slot_z + 1, at_end)
+        else:
+
+            @pl.when(at.middle)
+            def _():
+                arrive(got_z.at[2], slot_z + 2)
+                arrive(got_z.at[4], slot_z + 4)
+                add(zi, *others, (got_z, 2), (got_z, 4), into=out_ref)
+
+            @pl.when(jnp.logical_not(at.middle))
+            def _():
+                arrive(got_z.at[4], slot_z + 4)
+                add(zi, *others, (got_z, 4), into=out_ref)
+
+    def gradient(m):
+        step = 256
+        right = picked_dy if m == 2 else picked
+        turned[...] = (scaled[...] if m == 2 else gs[1] if m == 0 else us[1]).T
+
+        @pl.loop(0, width // step)
+        def _(n):
+            columns = pl.ds(pl.multiple_of(n * step, step), step)
+            grad[m, :, columns] = product(turned[...], right[:, columns]).astype(BF)
+
+    stores = [
+        pltpu.make_async_copy(grad.at[m], ref, store_sem.at[m])
+        for m, ref in enumerate((grad_gate, grad_up, grad_down))
+    ]
+    for copy in loads[:7]:
+        copy.wait()
+    for zi in (3, 2, 1, 0):
+        if zi < 2:
+            for j in twins[zi + 2]:
+                gone(j)
+        work(zi)
+        to_twin(zi)
+        first(zi)
+        if zi == 1:
+            second(3)
+    for copy in loads[7:]:
+        copy.wait()
+    for m, zi in ((0, 2), (1, 1), (2, 0)):
+        gradient(m)
+        stores[m].start()
+        second(zi)
+    for copy in stores:
+        copy.wait()
+    for j in started + twins[1] + twins[0]:
+        gone(j)
+
+    @pl.when(at.middle)
+    def _():
+        for j in in_middle:
+            gone(j)
+
+    @pl.when(jnp.logical_not(at.middle))
+    def _():
+        for j in at_end:
+            gone(j)
+
+
+def expert_back(dispatch, gate_back, shared_in, g, u, sg, picked, picked_dy, scaled, weights, cid):
+    total, wide = sg.shape
+    width = shared_in.shape[1]
+    rows, full = total // 16, width + 128
+    slots = picked.shape[0]
+    hidden = g.shape[2]
+    hbm, vmem = pl.BlockSpec(memory_space=pl.ANY), pl.BlockSpec(memory_space=pltpu.VMEM)
+    shape = jax.ShapeDtypeStruct
+    return pl.pallas_call(
+        expert_scatter_kernel,
+        out_shape=[
+            shape((rows, full), F32),
+            shape((hidden, width), BF),
+            shape((hidden, width), BF),
+            shape((hidden, width), BF),
+        ],
+        in_specs=[vmem] * 3 + [hbm] * 10,
+        out_specs=[vmem] + [hbm] * 3,
+        scratch_shapes=[
+            pltpu.VMEM((2, hidden, width), BF),
+            pltpu.VMEM((2, hidden, width), BF),
+            pltpu.VMEM((2, slots, hidden), BF),
+            pltpu.VMEM((2, slots, hidden), BF),
+            pltpu.VMEM((total, wide), BF),
+            pltpu.VMEM((slots, width), BF),
+            pltpu.VMEM((slots, width), BF),
+            pltpu.VMEM((slots, hidden), BF),
+            pltpu.VMEM((slots // 4, width), BF),
+            pltpu.VMEM((3, hidden, width), BF),
+            pltpu.VMEM((hidden, slots), BF),
+            pltpu.VMEM((8, rows, full), BF),
+            pltpu.VMEM((8, rows, full), BF),
+            pltpu.VMEM((4, rows, full), BF),
+            pltpu.VMEM((5, rows, full), BF),
+            pltpu.VMEM((4, rows, full), BF),
+            pltpu.SemaphoreType.DMA((10,)),
+            pltpu.SemaphoreType.DMA((3,)),
+            pltpu.SemaphoreType.DMA((17,)),
+            pltpu.SemaphoreType.DMA((17,)),
+        ],
+        compiler_params=pltpu.CompilerParams(
+            collective_id=cid, has_side_effects=True, vmem_limit_bytes=63 * 1024 * 1024
+        ),
+    )(dispatch, gate_back, shared_in, g, u, sg, picked, picked_dy, scaled, *weights)
+
+
 ALL = ("dp", "ctx", "exp")
 DENSE = ("dp", "ctx")
 
@@ -981,46 +1470,40 @@
     tokens_own = lax.dynamic_slice_in_dim(tokens[0], start, quarter, 0)
     dy_own = lax.dynamic_slice_in_dim(out_grad[0], start, quarter, 0)
 
-    named = jnp.any(
-        routes[0][:, :, None] == (jnp.arange(4, dtype=jnp.int32) * 4 + exp)[None, None, :], axis=1
-    )
-    named = named.astype(BF).reshape(dense, 2, 4).transpose(2, 0, 1)
-    little = jnp.concatenate([w_router, norm_attn[:, None], norm_mix[:, None]], axis=1)
-    little = jnp.broadcast_to(little[None], (4,) + little.shape)
-    little = jnp.concatenate([little, named], axis=2)
-    little = jnp.pad(little, ((0, 0), (0, 0), (0, HDIM - little.shape[2])))
-    sent_head = jnp.concatenate([by_four(w_query), by_four(w_key), by_four(w_value), little], axis=2)
+    route_rows = routes[0].T
+    theirs = jnp.arange(4, dtype=jnp.int32)[:, None, None] * 4 + exp
+    named = jnp.any(route_rows[None] == theirs, axis=1).astype(BF).reshape(4, 2, dense)
+    little = jnp.concatenate([w_router.T, norm_attn[None], norm_mix[None]], axis=0)
+    little = jnp.concatenate([jnp.broadcast_to(little[None], (4,) + little.shape), named], axis=1)
+    few = -(-little.shape[1] // 16) * 16
+    little = jnp.pad(little, ((0, 0), (0, few - little.shape[1]), (0, 0)))
+    sent_head = jnp.concatenate([by_four(w_query), by_four(w_key), by_four(w_value)], axis=2)
     sent_out = w_out.reshape(4, HDIM, dense)
-    sent_units = jnp.concatenate([by_four(shared_gate), by_four(shared_up)], axis=2)
-    sent_units = jnp.pad(sent_units, ((0, 0), (0, 0), (0, 3 * HDIM - 2 * cut)))
-    sent_down = shared_down.reshape(4, cut, dense)
-    tokens_all, early, early_out, late, late_down = all_rows(
-        tokens[0], True, 1, (sent_head, sent_out, sent_units, sent_down)
-    )
-
+    sent_units = jnp.stack([shared_gate.T, shared_up.T, shared_down], axis=0)
+    sent_units = sent_units.reshape(3, 4, cut, dense).transpose(1, 0, 2, 3).reshape(4, 3 * cut, dense)
+    tokens_all, early, early_out, late, early_little = all_rows(
+        tokens[0], True, 1, (sent_head, sent_out, sent_units, little)
+    )
+
+    own_gate, own_up, own_down = expert_gate[0].T, expert_up[0].T, expert_down[0]
     tokens_all, sent_gate, sent_up, sent_down = lax.optimization_barrier(
-        (tokens_all, expert_gate[0], expert_up[0], expert_down[0])
+        (tokens_all, own_gate, own_up, own_down)
     )
     other_gate, other_up, other_down = across(sent_gate), across(sent_up), across(sent_down)
-    early = early.reshape(width, 4 * HDIM)
-    w_qkv = early[:, : 3 * HDIM]
-    little = early[:, 3 * HDIM :]
-    router_matrix = little[:, :experts]
-    attention_gain = little[:, experts].astype(F32)
-    mixer_gain = little[:, experts + 1].astype(F32)
-    hits = little[:, experts + 2 : experts + 4].reshape(2, length)
+    w_qkv = early.reshape(width, 3 * HDIM)
+    early_little = early_little.transpose(1, 0, 2)
+    router_rows = early_little[:experts].reshape(experts, width)
+    attention_gain = early_little[experts].reshape(width).astype(F32)
+    mixer_gain = early_little[experts + 1].reshape(width).astype(F32)
+    hits = early_little[experts + 2 : experts + 4].transpose(1, 0, 2).reshape(2, length)
     hits = lax.dynamic_index_in_dim(hits, dp, 0, False).astype(F32).reshape(groups, quarter)
     w_out_head = early_out.transpose(1, 0, 2).reshape(HDIM, width)
 
     dy_all = all_rows(out_grad[0], True, 2)
-    late = late.reshape(width, 3 * HDIM)
-    pads = ((0, 0), (0, wide - cut))
-    shared_in = jnp.concatenate(
-        [jnp.pad(late[:, :cut], pads), jnp.pad(late[:, cut : 2 * cut], pads)], axis=1
-    )
-    shared_out = jnp.pad(
-        late_down.transpose(1, 0, 2).reshape(cut, width), ((0, wide - cut), (0, 0))
-    )
+    late = late.transpose(1, 0, 2).reshape(3, cut, width)
+    late = jnp.pad(late, ((0, 0), (0, wide - cut), (0, 0)))
+    shared_in = late[:2].reshape(2 * wide, width)
+    shared_out = late[2]
 
     cosine, sine = turn_tables(length)
     normed = rms_scale(tokens_all.astype(F32), attention_gain).astype(BF)
@@ -1033,29 +1516,28 @@
     middle = tokens_own.astype(F32) + attn
     normed_own = rms_scale(middle, mixer_gain).astype(BF)
 
-    mix_all = all_rows(normed_own, False, 4)
-    logits = product(mix_all, router_matrix)
-    router = jax.nn.softmax(logits, axis=-1)
     mine = ctx * 4 + exp
-    columns = jnp.arange(experts, dtype=jnp.int32)[None, :] == mine
-    router_mine = jnp.sum(jnp.where(columns, router, 0.0), axis=1).reshape(groups, quarter)
     place = jnp.cumsum(hits, axis=1) - 1.0
-    matches = jnp.where(
+    dispatch = jnp.where(
         (jnp.arange(capacity).astype(F32)[None, :, None] == place[:, None, :])
         & (hits[:, None, :] > 0.5),
         1.0,
         0.0,
-    )
-    dispatch = matches.astype(BF)
-    slot_gate = jnp.sum(matches * router_mine[:, None, :], axis=2).reshape(-1, 1)
-
-    def pick(rows):
-        return jnp.einsum(
-            "gst,gtd->gsd",
+    ).astype(BF)
+    router_wide = jnp.pad(router_rows, ((0, HDIM - experts), (0, 0)))
+    mix_all, picked, picked_dy, scaled, g_back, u_back, gate_back, shared_act, shared_gu_back = (
+        expert_rows(
+            normed_own,
+            dy_all,
             dispatch,
-            rows.reshape(groups, quarter, width),
-            preferred_element_type=F32,
-        ).astype(BF).reshape(groups * capacity, width)
+            router_wide,
+            experts,
+            shared_in,
+            shared_out,
+            (own_gate, own_up, own_down, other_gate, other_up, other_down),
+            4,
+        )
+    )
 
     def spread(rows):
         return jnp.einsum(
@@ -1065,74 +1547,34 @@
             preferred_element_type=F32,
         ).reshape(length, width)
 
-    picked = pick(mix_all)
-    picked_dy = pick(dy_all)
-
-    def half(gate_matrix, up_matrix, down_matrix):
-        gate_hidden = product(picked, gate_matrix)
-        up_hidden = product(picked, up_matrix)
-        act, by_gate, by_up = silu_parts(gate_hidden, up_hidden)
-        dy_down = transposed_right(picked_dy, down_matrix)
-        act_back = slot_gate * dy_down
-        g_back = (act_back * by_gate).astype(BF)
-        u_back = (act_back * by_up).astype(BF)
-        act_low = act.astype(BF)
-        gate_back = jnp.sum(act_low.astype(F32) * dy_down, axis=1)
-        return act_low, (act * slot_gate).astype(BF), g_back, u_back, gate_back
-
-    act_a, scaled_a, g_a, u_a, gb_a = half(expert_gate[0], expert_up[0], expert_down[0])
-    act_b, scaled_b, g_b, u_b, gb_b = half(other_gate, other_up, other_down)
-    input_back = (
-        transposed_right(g_a, expert_gate[0])
-        + transposed_right(u_a, expert_up[0])
-        + transposed_right(g_b, other_gate)
-        + transposed_right(u_b, other_up)
-    )
-    gate_back = gb_a + gb_b
-
-    shared_hidden = product(mix_all, shared_in)
-    shared_act, shared_by_gate, shared_by_up = silu_parts(
-        shared_hidden[:, :wide], shared_hidden[:, wide:]
-    )
-    shared_act = shared_act.astype(BF)
-    shared_back = transposed_right(dy_all, shared_out)
-    shared_gu_back = jnp.concatenate(
-        [(shared_back * shared_by_gate).astype(BF), (shared_back * shared_by_up).astype(BF)], axis=1
-    )
-    mix_part = (
-        transposed_right(shared_gu_back, shared_in) + spread(input_back.astype(BF))
-    ).astype(BF)
-    gate_back_tokens = jnp.sum(
-        matches * gate_back.reshape(groups, capacity, 1), axis=1
-    ).reshape(length, 1)
-    gate_columns = jnp.where(
-        jnp.arange(HDIM, dtype=jnp.int32)[None, :] == mine, gate_back_tokens, 0.0
-    ).astype(BF)
-    mix_sum = jnp.concatenate([mix_part, gate_columns], axis=1)
-    gate_grad_b, up_grad_b, down_grad_b, mix_sum = lax.optimization_barrier(
-        (
-            transposed_left(picked, g_b).astype(BF),
-            transposed_left(picked, u_b).astype(BF),
-            transposed_left(scaled_b, picked_dy).astype(BF),
-            mix_sum,
-        )
-    )
-    mix_back, gate_grad_b = own_rows(mix_sum, 5, (gate_grad_b,))
+    mix_back, gate_grad_b, up_grad_b, down_grad_b = expert_back(
+        dispatch,
+        gate_back,
+        shared_in,
+        g_back,
+        u_back,
+        shared_gu_back,
+        picked,
+        picked_dy,
+        scaled,
+        (own_gate, own_up, other_gate, other_up),
+        5,
+    )
     gate_back_own = mix_back[:, width : width + experts]
     mix_back = mix_back[:, :width]
 
-    router_own = jax.nn.softmax(product(normed_own, router_matrix), axis=-1)
+    router_own = jax.nn.softmax(transposed_right(normed_own, router_rows), axis=-1)
     logit_back = (
         router_own * (gate_back_own - jnp.sum(router_own * gate_back_own, axis=-1, keepdims=True))
     ).astype(BF)
-    router_part = transposed_left(normed_own, logit_back)
-
-    mix_back = mix_back + transposed_right(logit_back, router_matrix)
+    router_part = transposed_left(logit_back, normed_own)
+
+    mix_back = mix_back + product(logit_back, router_rows)
     _, norm_mix_back = jax.vjp(rms_scale, middle, mixer_gain)
     middle_norm_back, gain_mix_part = norm_mix_back(mix_back)
     middle_back = dy_own.astype(F32) + middle_norm_back
     attn_back = middle_back.astype(BF)
-    attn_back_all, up_grad_b = all_rows(attn_back, False, 7, (), (up_grad_b,))
+    attn_back_all, gate_grad_b = all_rows(attn_back, False, 7, (), (gate_grad_b,))
     heads_back = transposed_right(attn_back_all, w_out_head).astype(BF)
     out_part = transposed_left(heads_out, attn_back_all).astype(BF)
     dq, dk, dv = attend_back(query, key, value, heads_back, lse)
@@ -1150,32 +1592,26 @@
     input_norm_back, gain_attn_part = norm_attn_back(normed_back)
     tokens_back_own = (middle_back + input_norm_back).astype(BF)
 
-    half_a = product(act_a, expert_down[0]).astype(BF).astype(F32)
-    half_b = product(act_b, other_down).astype(BF).astype(F32)
-    mixed_part = (
-        product(shared_act, shared_out) + spread(((half_a + half_b) * slot_gate).astype(BF))
-    ).astype(BF)
-    mixed_own = (middle + own_rows(mixed_part, 3)).astype(BF)
+    expert_out = product(scaled[0], expert_down[0]) + product(scaled[1], other_down)
+    mixed_part = (product(shared_act, shared_out) + spread(expert_out.astype(BF))).astype(BF)
+    mixed_sum, up_grad_b = own_rows(mixed_part, 9, (up_grad_b,))
+    mixed_own = (middle + mixed_sum).astype(BF)
 
     mixed, tokens_back = share([mixed_own, tokens_back_own], 6)
-    small = jnp.concatenate(
-        [gain_attn_part[:, None], gain_mix_part[:, None], router_part], axis=1
-    ).reshape(8, 1, dense * (experts + 2))
-    small = jnp.broadcast_to(small, (8, 4, dense * (experts + 2))).reshape(32, -1)
+    small = jnp.concatenate([gain_attn_part[None], gain_mix_part[None], router_part], axis=0)
+    small = small.reshape(experts + 2, 8, 1, dense).transpose(1, 2, 0, 3)
+    small = jnp.broadcast_to(small, (8, 4, experts + 2, dense)).reshape(32, experts + 2, dense)
     small = lax.all_to_all(small, ALL, split_axis=0, concat_axis=0, tiled=True)
-    small = jnp.sum(small, axis=0).reshape(dense, experts + 2)
-    shared_gu_grad = transposed_left(mix_all, shared_gu_back).astype(BF)
-    shared_gu_grad = jnp.concatenate(
-        [shared_gu_grad[:, :cut], shared_gu_grad[:, wide : wide + cut]], axis=1
-    )
-    shared_gu_grad = jnp.pad(shared_gu_grad, ((0, 0), (0, 3 * HDIM - 2 * cut)))
-    shared_down_part = transposed_left(shared_act, dy_all).astype(BF)[:cut]
-    home_rows = swap(
-        jnp.concatenate([qkv_part, shared_gu_grad], axis=1).reshape(8, dense, 6 * HDIM)
-    ).astype(F32)
+    small = jnp.sum(small, axis=0)
+    shared_gu_grad = transposed_left(shared_gu_back, mix_all).astype(BF).reshape(2, wide, width)
+    shared_down_part = transposed_left(shared_act, dy_all).astype(BF)
+    home_rows = swap(qkv_part.reshape(8, dense, 3 * HDIM)).astype(F32)
     home_columns = swap(
-        jnp.concatenate([out_part, shared_down_part], axis=0)
-        .reshape(HDIM + cut, 8, dense)
+        jnp.concatenate(
+            [out_part, shared_gu_grad[0, :cut], shared_gu_grad[1, :cut], shared_down_part[:cut]],
+            axis=0,
+        )
+        .reshape(HDIM + 3 * cut, 8, dense)
         .transpose(1, 0, 2)
     ).astype(F32)
     home_rows = home_rows[:4] + home_rows[4:]
@@ -1184,25 +1620,27 @@
     def columns_of(parts):
         return parts.transpose(1, 0, 2).reshape(dense, -1)
 
-    units = 3 * HDIM
-    gate_grad = transposed_left(picked, g_a) + gate_grad_b.astype(F32)
-    up_grad = transposed_left(picked, u_a) + up_grad_b.astype(F32)
-    down_grad = transposed_left(scaled_a, picked_dy) + down_grad_b.astype(F32)
+    def rows_of(parts):
+        return parts.reshape(-1, dense)
+
+    gate_grad = transposed_left(g_back[0], picked) + gate_grad_b.astype(F32)
+    up_grad = transposed_left(u_back[0], picked) + up_grad_b.astype(F32)
+    down_grad = transposed_left(scaled[0], picked_dy) + down_grad_b.astype(F32)
     return (
         mixed[None],
         tokens_back[None],
-        small[:, 0],
+        small[0],
         columns_of(home_rows[:, :, :HDIM]),
         columns_of(home_rows[:, :, HDIM : 2 * HDIM]),
         columns_of(home_rows[:, :, 2 * HDIM : 3 * HDIM]),
-        home_columns[:, :HDIM].reshape(4 * HDIM, dense),
-        small[:, 1],
-        small[:, 2:],
-        columns_of(home_rows[:, :, units : units + cut]),
-        columns_of(home_rows[:, :, units + cut : units + 2 * cut]),
-        home_columns[:, HDIM:].reshape(4 * cut, dense),
-        gate_grad[None],
-        up_grad[None],
+        rows_of(home_columns[:, :HDIM]),
+        small[1],
+        small[2:].T,
+        rows_of(home_columns[:, HDIM : HDIM + cut]).T,
+        rows_of(home_columns[:, HDIM + cut : HDIM + 2 * cut]).T,
+        rows_of(home_columns[:, HDIM + 2 * cut :]),
+        gate_grad.T[None],
+        up_grad.T[None],
         down_grad[None],
     )
 

time: 1010 us -> 923 us (0.914)
  matrix products: 257 us -> 104 us
  Pallas kernels: 613 us -> 681 us
  waiting for transfers between devices: 13.7 us -> 38.7 us
  other arithmetic: 48.9 us -> 34.7 us
  local copies, waits for them, and re-layouts: 55.1 us -> 42.4 us
    pallas_call x0 -> x2, Pallas kernels: none -> 188 us  [the longest x1 96.6 us: expert_rows(): pl.pallas_call(functools.partial(expert_gather_kernel, experts), out_shap...]
    dot_general x11 -> x3, matrix products: 88.1 us -> 12.4 us  [transposed_right(): lax.dot_general(left_side, right_side, (((1,), (1,)), ((), ())), preferre...]
    pallas_call x4 -> x3, Pallas kernels: 306 us -> 236 us  [all_rows(): pl.pallas_call(functools.partial(gather_kernel, block, rows, parts, extra...]
    pallas_call x4 -> x3, Pallas kernels: 252 us -> 203 us  [own_rows(): pl.pallas_call(functools.partial(scatter_kernel, rows, swaps), out_shape=...]
    dot_general x12 -> x6, matrix products: 74.1 us -> 35.6 us  [product(): return jnp.dot(left_side, right_side, preferred_element_type=jnp.float32)]
    dot_general x11 -> x8, matrix products: 69.7 us -> 47.7 us  [transposed_left(): lax.dot_general(left_side, right_side, (((0,), (0,)), ((), ())), preferre...]
    ppermute x3, waiting for transfers between devices: 0.01 us -> 16.1 us  [across(): return lax.ppermute(values, 'dp', [(0, 1), (1, 0)])]
    unnamed x168 -> x107, local copies, waits for them, and re-layouts: 29.7 us -> 15.7 us
  transfers between devices with their start and end apart: 6 -> 6, of which waited for: 2 -> 3; matrix products, arithmetic and copies ran while one was open for 20% -> 12% of each run, Pallas kernels for 28% -> 27%
where the time goes in v3:
time: 923 us; the launch traced here: 918 us
  Pallas kernels  681 us (74%)
  matrix products  104 us (11%)
  local copies, waits for them, and re-layouts  42.4 us (5%)
  waiting for transfers between devices  38.7 us (4%)
  other arithmetic  34.7 us (4%)
  starting transfers between devices  15.9 us (2%)
    pallas_call x3, Pallas kernels, all_rows(): pl.pallas_call(functools.partial(gather_kernel, block, rows, parts, extra...  236 us
    pallas_call x3, Pallas kernels, own_rows(): pl.pallas_call(functools.partial(scatter_kernel, rows, swaps), out_shape=...  203 us
    pallas_call x1, Pallas kernels, expert_rows(): pl.pallas_call(functools.partial(expert_gather_kernel, experts), out_shap...  96.6 us
    pallas_call x1, Pallas kernels, expert_back(): pl.pallas_call(expert_scatter_kernel, out_shape=[shape((rows, full), F32)...  91.2 us
    dot_general x8, matrix products, transposed_left(): lax.dot_general(left_side, right_side, (((0,), (0,)), ((), ())), preferre...  47.7 us
    dot_general x6, matrix products, product(): return jnp.dot(left_side, right_side, preferred_element_type=jnp.float32)  35.6 us
    pallas_call x1, Pallas kernels, share(): pl.pallas_call(functools.partial(share_kernel, rows, count), out_shape=[j...  33.4 us
  transfers between devices with their start and end apart: 6, of which 3 were waited for; matrix products, arithmetic and copies ran while one was open for 12% of the time, Pallas kernels for 27%

profile of v3, /device:TPU:0, one launch (start us, length us, event | category | flops | bytes accessed | tf_op | source)
XLA Modules:
  0.0 918.2 jit_solution(15917414212899387669)
XLA Ops:
  9.5 104.9 %shard_map.289 = (bf16[2048,2048]{1,0:T(8,128)(2,1)}, bf16[8,256,384]{2,1,0:T(8,128)(2,1)}, bf16[8,128,256]{2,1,0:T(8,128)(2,1)}, bf16[8,528,256]{2,1,0:T(8,128)(2,1)}, bf16[8,32,256]{2,1,0:T(8,128)(2,1)}) custom-call(bf16[512,2048]{1,0:T(8,128)(2,1)} %bitcast.183, bf16[4,256,384]{2,1,0:T(8,128)(2,1)} %pad_maximum_fusion.1.refs_1_, ...), custom_call_target="tpu_custom_call" | custom-call | tf_op jit(solution)/shard_map/pallas_call | solution.py:641
  124.7 7.4 fusion.5
  135.3 8.6 shard_map.290
  147.3 57.1 %shard_map.291 = f32[128,2048]{1,0:T(8,128)S(1)} custom-call(bf16[2048,2048]{1,0:T(8,128)(2,1)S(1)} %convolution_convert_fusion.1.in_ref), custom_call_target="tpu_custom_call" | custom-call | tf_op jit(solution)/shard_map/pallas_call | solution.py:772
  206.6 65.8 %shard_map.292.refs_1_ = bf16[2048,2048]{1,0:T(8,128)(2,1)} custom-call(bf16[512,2048]{1,0:T(8,128)(2,1)} %bitcast.184), custom_call_target="tpu_custom_call" | custom-call | tf_op jit(solution)/shard_map/pallas_call | solution.py:641
  284.4 16.1 %collective-permute-done.2.refs_11_ = bf16[704,2048]{1,0:T(8,128)(2,1)} collective-permute-done((bf16[704,2048]{1,0:T(8,128)(2,1)}, bf16[704,2048]{1,0:T(8,128)(2,1)}, u32[]{:S(2)}, u32[]{:S(2)}) %collective-permute-start.2) | collective-permute-done | bytes 2883616 | tf_op jit(solution)/shard_map/ppermute | solution.py:1353
  300.5 96.6 %shard_map.293 = (bf16[2048,2048]{1,0:T(8,128)(2,1)}, bf16[1024,2048]{1,0:T(8,128)(2,1)}, bf16[1024,2048]{1,0:T(8,128)(2,1)}, bf16[2,1024,704]{2,1,0:T(8,128)(2,...) custom-call(bf16[128,2048]{1,0:T(8,128)(2,1)} %copy-done.14, ...), custom_call_target="tpu_custom_call" | custom-call | tf_op jit(solution)/shard_map/pallas_call | solution.py:1043
  397.1 91.2 %shard_map.294 = (f32[128,2176]{1,0:T(8,128)}, bf16[704,2048]{1,0:T(8,128)(2,1)}, bf16[704,2048]{1,0:T(8,128)(2,1)}, bf16[704,2048]{1,0:T(8,128)(2,1)}) custom-call(bf16[16,64,128]{2,1,0:T(8,128)(2,1)} %select_convert_fusion.refs_2_.refs_0_, f32[1024,128]{1,0:T(8,128)} %get-tuple-element.62.refs_1_, bf16[512,2048]{1,0:T(8,128)(2,1)} %bitcast.181, ...), custom_call_target="tpu_custom_call" | custom-call | tf_op jit(solution)/shard_map/pallas_call | solution.py:1301
  495.5 65.4 %shard_map.296 = (bf16[2048,2048]{1,0:T(8,128)(2,1)}, bf16[704,2048]{1,0:T(8,128)(2,1)}) custom-call(bf16[128,2048]{1,0:T(8,128)(2,1)} %fusion.40.refs_0_, bf16[704,2048]{1,0:T(8,128)(2,1)} %get-tuple-element.71.refs_1_), custom_call_target="tpu_custom_call" | custom-call | tf_op jit(solution)/shard_map/pallas_call | solution.py:641
  561.0 5.6 convolution_convert_fusion.4
  570.1 5.9 fusion.45
  576.1 6.1 convolution_convert_fusion.2
  582.2 12.0 %shard_map.297 = (f32[2048,128]{1,0:T(8,128)}, f32[2048,128]{1,0:T(8,128)}, f32[2048,128]{1,0:T(8,128)}) custom-call(bf16[2048,128]{1,0:T(8,128)(2,1)} %get-tuple-element.119.q_ref, bf16[2048,128]{1,0:T(8,128)(2,1)} %get-tuple-element.120.k_ref, bf16[2048,128]{1,0:T(8,128)(2,1)} %slice.249.v_ref, bf16[2048,128]{1,0:T(8,128)(2,1)} %convolution_convert_fusion.5.do_ref, ...), custom_call_target="tpu_custom_call" | custom-call | tf_op jit(solution)/shard_map/pallas_call | solution.py:1410
  603.1 9.0 convolution_convert_fusion.in_ref
  612.1 64.3 %shard_map.298 = (f32[128,2048]{1,0:T(8,128)S(1)}, bf16[704,2048]{1,0:T(8,128)(2,1)S(1)}) custom-call(bf16[2048,2048]{1,0:T(8,128)(2,1)} %convolution_convert_fusion.in_ref, bf16[704,2048]{1,0:T(8,128)(2,1)S(1)} %copy-done.5), custom_call_target="tpu_custom_call" | custom-call | tf_op jit(solution)/shard_map/pallas_call | solution.py:772
  688.3 9.5 %convolution_convert_fusion.3 = bf16[2048,384]{1,0:T(8,128)(2,1)} fusion(bf16[2048,384]{1,0:T(8,128)(2,1)S(1)} %copy-done.38, bf16[2048,2048]{1,0:T(8,128)(2,1)} %get-tuple-element.51, f32[2048]{0:T(1024)S(1)} %bitcast.230, f32[2048]{0:T(1024)S(1)} %add_rsqrt_fusion), kind=kOutput, calls=%fused_computation.16 | convolution fusion | flops 3238789120 | bytes 11550720 | tf_op jit(solution)/shard_map/dot_general | solution.py:53
  697.9 8.1 all-to-all-done
  720.2 5.6 add_convert_fusion
  725.8 8.2 fusion.31
  734.0 14.5 %all-to-all-done.1 = bf16[8,256,384]{2,1,0:T(8,128)(2,1)} async-done(((bf16[8,256,384]{2,1,0:T(8,128)(2,1)}), bf16[8,256,384]{2,1,0:T(8,128)(2,1)}, u32[]{:S(2)}, u32[]{:S(2)}) %all-to-all-start.1) | async-done | bytes 1572896 | tf_op jit(solution)/shard_map/all_to_all | solution.py:1344
  752.9 11.9 %fusion.3.in_ref = bf16[2048,2048]{1,0:T(8,128)(2,1)} fusion(f32[16,128,2048]{2,1,0:T(8,128)} %fusion.31, bf16[2048,256]{1,0:T(8,128)(2,1)} %get-tuple-element.60, bf16[3,176,2048]{2,1,0:T(8,128)(2,1)S(1)} %copy-done.8), kind=kOutput, calls=%fused_computation.6 | convolution fusion | flops 2155872256 | bytes 28377088 | tf_op jit(solution)/shard_map/dot_general | solution.py:49
  764.8 81.4 %shard_map.295 = (f32[128,2048]{1,0:T(8,128)S(1)}, bf16[704,2048]{1,0:T(8,128)(2,1)S(1)}) custom-call(bf16[2048,2048]{1,0:T(8,128)(2,1)} %fusion.3.in_ref, bf16[704,2048]{1,0:T(8,128)(2,1)S(1)} %copy-done.4), custom_call_target="tpu_custom_call" | custom-call | tf_op jit(solution)/shard_map/pallas_call | solution.py:772
  849.8 33.4 %shard_map.299 = (bf16[512,2048]{1,0:T(8,128)(2,1)}, bf16[512,2048]{1,0:T(8,128)(2,1)}) custom-call(bf16[128,2048]{1,0:T(8,128)(2,1)} %get-tuple-element.111.refs_0_, bf16[128,2048]{1,0:T(8,128)(2,1)} %get-tuple-element.110.refs_1_), custom_call_target="tpu_custom_call" | custom-call | tf_op jit(solution)/shard_map/pallas_call | solution.py:836
  883.2 9.4 %add_bitcast_fusion.2 = f32[1,2048,704]{1,2,0:T(8,128)} fusion(bf16[704,2048]{1,0:T(8,128)(2,1)} %get-tuple-element.82, bf16[1024,2048]{1,0:T(8,128)(2,1)} %get-tuple-element.66.refs_6_, bf16[2,1024,704]{2,1,0:T(8,128)(2,1)} %get-tuple-element.63.refs_3_), kind=kOutput, calls=%fused_computation.12 | convolution fusion | flops 2955673600 | bytes 14417920 | tf_op jit(solution)/shard_map/dot_general | solution.py:53
  (196 shorter events, 118.3 us)
Async XLA Ops:
  114.4 170.0 %collective-permute-start = (bf16[704,2048]{1,0:T(8,128)(2,1)}, bf16[704,2048]{1,0:T(8,128)(2,1)}, u32[]{:S(2)}, u32[]{:S(2)}) collective-permute-start(bf16[704,2048]{1,0:T(8,128)(2,1)} %bitcast.22.refs_6_.refs_9_), channel_id=1, source_target_pairs={{0,16},{16,0},{1,17},{17,1},{2,18},{18,2},{3,19},{19,3},{4,20},{20... | collective-permute-start | bytes 8650760 | tf_op jit(solution)/shard_map/ppermute | solution.py:1353
  115.4 169.0 %collective-permute-start.1 = (bf16[704,2048]{1,0:T(8,128)(2,1)}, bf16[704,2048]{1,0:T(8,128)(2,1)}, u32[]{:S(2)}, u32[]{:S(2)}) collective-permute-start(bf16[704,2048]{1,0:T(8,128)(2,1)} %bitcast.24.refs_7_.refs_10_), channel_id=1, source_target_pairs={{0,16},{16,0},{1,17},{17,1},{2,18},{18,2},{3,19},{19,3},{4,20},{20... | collective-permute-start | bytes 8650760 | tf_op jit(solution)/shard_map/ppermute | solution.py:1353
  116.5 184.0 %collective-permute-start.2 = (bf16[704,2048]{1,0:T(8,128)(2,1)}, bf16[704,2048]{1,0:T(8,128)(2,1)}, u32[]{:S(2)}, u32[]{:S(2)}) collective-permute-start(bf16[704,2048]{1,0:T(8,128)(2,1)} %bitcast.25.refs_8_), channel_id=1, source_target_pairs={{0,16},{16,0},{1,17},{17,1},{2,18},{18,2},{3,19},{19,3},{4,20},{20... | collective-permute-start | bytes 8650760 | tf_op jit(solution)/shard_map/ppermute | solution.py:1353
  124.7 19.2 %copy-start.35 = (bf16[128,8,256]{0,2,1:T(8,128)(2,1)}, bf16[128,8,256]{0,2,1:T(8,128)(2,1)S(1)}, u32[]{:S(2)}) copy-start(bf16[128,8,256]{0,2,1:T(8,128)(2,1)S(1)} %copy.189) | copy-start | bytes 1572868
  124.7 8.3 copy-start.24
  205.8 73.2 %copy-start.10 = (f32[128,2048]{1,0:T(8,128)}, f32[128,2048]{1,0:T(8,128)S(1)}, u32[]{:S(2)}) copy-start(f32[128,2048]{1,0:T(8,128)S(1)} %get-tuple-element.90) | copy-start | bytes 3145732
  206.6 65.9 %copy-start.30 = (bf16[8,528,256]{2,1,0:T(8,128)(2,1)S(1)}, bf16[8,528,256]{2,1,0:T(8,128)(2,1)}, u32[]{:S(2)}) copy-start(bf16[8,528,256]{2,1,0:T(8,128)(2,1)} %get-tuple-element.56) | copy-start | bytes 6488068
  397.1 92.4 %copy-start.15 = (bf16[128,2048]{1,0:T(8,128)(2,1)S(1)}, bf16[128,2048]{1,0:T(8,128)(2,1)}, u32[]{:S(2)}) copy-start(bf16[128,2048]{1,0:T(8,128)(2,1)} %copy-done.14) | copy-start | bytes 1572868
  492.9 68.1 %copy-start.20 = (bf16[2048,128]{1,0:T(8,128)(2,1)S(1)}, bf16[2048,128]{1,0:T(8,128)(2,1)}, u32[]{:S(2)}) copy-start(bf16[2048,128]{1,0:T(8,128)(2,1)} %get-tuple-element.54) | copy-start | bytes 1572868
  566.9 9.1 slice-start
  582.2 14.2 %copy-start.25 = (f32[2048,64]{1,0:T(8,128)S(1)}, f32[2048,64]{1,0:T(8,128)}, u32[]{:S(2)}) copy-start(f32[2048,64]{1,0:T(8,128)} %constant.75) | copy-start | bytes 1572868
  582.2 14.3 %copy-start.27 = (f32[2048,64]{1,0:T(8,128)S(1)}, f32[2048,64]{1,0:T(8,128)}, u32[]{:S(2)}) copy-start(f32[2048,64]{1,0:T(8,128)} %constant.62.clone) | copy-start | bytes 1572868
  603.1 9.0 copy-start.37
  603.1 9.0 copy-start.5
  680.5 25.5 %all-to-all-start = ((f32[32,18,256]{2,1,0:T(8,128)}), f32[32,18,256]{2,1,0:T(8,128)S(1)}, u32[]{:S(2)}, u32[]{:S(2)}) async-start(f32[32,18,256]{2,1,0:T(8,128)} %bitcast.50), calls=%async_computation | async-start | bytes 1572864 | tf_op jit(solution)/shard_map/all_to_all | solution.py:1604
  706.0 42.5 %all-to-all-start.1 = ((bf16[8,256,384]{2,1,0:T(8,128)(2,1)}), bf16[8,256,384]{2,1,0:T(8,128)(2,1)}, u32[]{:S(2)}, u32[]{:S(2)}) async-start(bf16[8,256,384]{2,1,0:T(8,128)(2,1)} %bitcast.199), calls=%async_computation.1 | async-start | bytes 3145728 | tf_op jit(solution)/shard_map/all_to_all | solution.py:1344
  734.0 18.9 %copy-start.8 = (bf16[3,176,2048]{2,1,0:T(8,128)(2,1)S(1)}, bf16[3,176,2048]{2,1,0:T(8,128)(2,1)}, u32[]{:S(2)}) copy-start(bf16[3,176,2048]{2,1,0:T(8,128)(2,1)} %copy-done.7) | copy-start | bytes 6488068
  748.5 161.0 %all-to-all-start.2 = ((bf16[8,656,256]{2,1,0:T(8,128)(2,1)}), bf16[8,656,256]{2,1,0:T(8,128)(2,1)}, u32[]{:S(2)}, u32[]{:S(2)}) async-start(bf16[8,656,256]{2,1,0:T(8,128)(2,1)} %copy.202), calls=%async_computation.2 | async-start | bytes 5373952 | tf_op jit(solution)/shard_map/all_to_all | solution.py:1344
  752.9 11.9 %copy-start.4 = (bf16[704,2048]{1,0:T(8,128)(2,1)S(1)}, bf16[704,2048]{1,0:T(8,128)(2,1)}, u32[]{:S(2)}) copy-start(bf16[704,2048]{1,0:T(8,128)(2,1)} %get-tuple-element.68.refs_0_) | copy-start | bytes 8650756
  764.8 81.5 %copy-start.12 = (f32[128,2048]{1,0:T(8,128)S(1)}, f32[128,2048]{1,0:T(8,128)}, u32[]{:S(2)}) copy-start(f32[128,2048]{1,0:T(8,128)} %copy-done.10) | copy-start | bytes 3145732
  764.8 81.5 %copy-start.22 = (f32[128,2048]{1,0:T(8,128)S(1)}, f32[128,2048]{1,0:T(8,128)}, u32[]{:S(2)}) copy-start(f32[128,2048]{1,0:T(8,128)} %copy-done.21) | copy-start | bytes 3145732
  883.2 9.4 %copy-start.1 = (bf16[704,2048]{1,0:T(8,128)(2,1)S(1)}, bf16[704,2048]{1,0:T(8,128)(2,1)}, u32[]{:S(2)}) copy-start(bf16[704,2048]{1,0:T(8,128)(2,1)} %copy-done) | copy-start | bytes 8650756
  883.2 9.4 %copy-start.13 = (bf16[1024,2048]{1,0:T(8,128)(2,1)S(1)}, bf16[1024,2048]{1,0:T(8,128)(2,1)}, u32[]{:S(2)}) copy-start(bf16[1024,2048]{1,0:T(8,128)(2,1)} %get-tuple-element.67.refs_7_) | copy-start | bytes 12582916
  883.2 9.4 %copy-start.19 = (bf16[2,1024,704]{2,1,0:T(8,128)(2,1)S(1)}, bf16[2,1024,704]{2,1,0:T(8,128)(2,1)}, u32[]{:S(2)}) copy-start(bf16[2,1024,704]{2,1,0:T(8,128)(2,1)} %get-tuple-element.61.refs_8_) | copy-start | bytes 8650756
  (29 other events, 133.7 us)

commit v4 on v3

--- a/solution.py
+++ b/solution.py
@@ -649,44 +649,46 @@
     return got if extras or swaps else got[0]
 
 
-def scatter_kernel(rows, swaps, in_ref, *refs):
-    given, out_ref, taken = refs[:swaps], refs[swaps], refs[swaps + 1 : 2 * swaps + 1]
-    acc, got_s, got_f, got_z, load_sem, send_sem, recv_sem = refs[2 * swaps + 1 : 2 * swaps + 8]
-    at = Place()
-    greet(at, False, swaps > 0)
-    crossing = cross(at, given, taken, *refs[2 * swaps + 8 :]) if swaps else []
-    for copy in crossing:
-        copy.start()
-    slot_z, slot_f, slot_s = 0, 5, 9
-    f_dev, s_dev, z_dev = at.device(oe=at.dy), at.device(oe=at.dc), at.device(zi=1)
-    started, in_middle, at_end = [], [], []
-
-    def rows_of(rank):
-        return in_ref.at[pl.ds(pl.multiple_of(rank * rows, rows), rows)]
-
-    def push(src, dst, slot, device, sends=None, record=started):
+class Scatter:
+    def __init__(self, at, acc, got_s, got_f, got_z, send_sem, recv_sem, out_ref):
+        self.at, self.acc, self.got_s, self.got_f, self.got_z = at, acc, got_s, got_f, got_z
+        self.send_sem, self.recv_sem, self.out_ref = send_sem, recv_sem, out_ref
+        self.rows = acc.shape[1]
+        self.f_dev, self.s_dev, self.z_dev = (
+            at.device(oe=at.dy),
+            at.device(oe=at.dc),
+            at.device(zi=1),
+        )
+        self.twins = [[], [], [], []]
+        self.started, self.in_middle, self.at_end = [], [], []
+
+    def push(self, src, dst, slot, device, sends=None, record=None):
         j = slot if sends is None else sends
-        remote(src, dst, send_sem.at[j], recv_sem.at[slot], device).start()
-        record.append(j)
-
-    def gone(j):
-        remote(acc.at[0], acc.at[0], send_sem.at[j], recv_sem.at[0], s_dev).wait_send()
-
-    def arrive(dst, slot):
-        remote(acc.at[0], dst, send_sem.at[slot], recv_sem.at[slot], s_dev).wait_recv()
-
-    order = [(f, zi) for f in (1, 0) for zi in (3, 2, 1, 0)]
-    loads = {}
-    for f, zi in order:
+        remote(src, dst, self.send_sem.at[j], self.recv_sem.at[slot], device).start()
+        (self.started if record is None else record).append(j)
+
+    def gone(self, j):
+        spot = self.acc.at[0]
+        remote(spot, spot, self.send_sem.at[j], self.recv_sem.at[0], self.s_dev).wait_send()
+
+    def arrive(self, dst, slot):
+        remote(
+            self.acc.at[0], dst, self.send_sem.at[slot], self.recv_sem.at[slot], self.s_dev
+        ).wait_recv()
+
+    def to_twin(self, src, f, zi):
         k = f * 4 + zi
-        push(rows_of(at.shard(f * at.dy + at.dc, zi)), got_s.at[k], slot_s + k, s_dev)
-        loads[k] = pltpu.make_async_copy(
-            rows_of(at.shard(f * at.dy, zi)), acc.at[k], load_sem.at[k]
-        )
-        loads[k].start()
-
-    def add(k, *others, into=None):
-        @pl.loop(0, rows // 16)
+        self.push(src, self.got_s.at[k], 9 + k, self.s_dev, None, self.twins[zi])
+
+    def twin_gone(self, zi):
+        for j in self.twins[zi]:
+            self.gone(j)
+        self.twins[zi] = []
+
+    def add(self, k, *others, into=None):
+        acc = self.acc
+
+        @pl.loop(0, self.rows // 16)
         def _(i):
             span = pl.ds(pl.multiple_of(i * 16, 16), 16)
             total = acc[k, span, :].astype(F32)
@@ -697,71 +699,112 @@
             else:
                 into[span, :] = total
 
+    def first(self, zi):
+        k = 4 + zi
+        self.arrive(self.got_s.at[k], 9 + k)
+        self.add(k, (self.got_s, k))
+        self.push(self.acc.at[k], self.got_f.at[zi], 5 + zi, self.f_dev)
+
+    def second(self, zi):
+        at, acc, got_z = self.at, self.acc, self.got_z
+        self.arrive(self.got_s.at[zi], 9 + zi)
+        self.arrive(self.got_f.at[zi], 5 + zi)
+        others = [(self.got_s, zi), (self.got_f, zi)]
+        if zi >= 2:
+
+            @pl.when(at.middle)
+            def _():
+                self.arrive(got_z.at[3 - zi], 3 - zi)
+                self.add(zi, *others, (got_z, 3 - zi))
+                there = 4 if zi == 2 else 3
+                self.push(acc.at[zi], got_z.at[there], there, at.inward(), zi, self.in_middle)
+
+            @pl.when(jnp.logical_not(at.middle))
+            def _():
+                self.add(zi, *others)
+                self.push(acc.at[zi], got_z.at[3 - zi], 3 - zi, self.z_dev, zi, self.at_end)
+        elif zi == 1:
+
+            @pl.when(at.middle)
+            def _():
+                self.arrive(got_z.at[3], 3)
+                self.add(zi, *others, (got_z, 3))
+                self.push(acc.at[zi], got_z.at[4], 4, self.z_dev, 1, self.in_middle)
+
+            @pl.when(jnp.logical_not(at.middle))
+            def _():
+                self.add(zi, *others)
+                self.push(acc.at[zi], got_z.at[2], 2, self.z_dev, 1, self.at_end)
+        else:
+
+            @pl.when(at.middle)
+            def _():
+                self.arrive(got_z.at[2], 2)
+                self.arrive(got_z.at[4], 4)
+                self.add(zi, *others, (got_z, 2), (got_z, 4), into=self.out_ref)
+
+            @pl.when(jnp.logical_not(at.middle))
+            def _():
+                self.arrive(got_z.at[4], 4)
+                self.add(zi, *others, (got_z, 4), into=self.out_ref)
+
+    def finish(self):
+        for zi in range(4):
+            self.twin_gone(zi)
+        for j in self.started:
+            self.gone(j)
+
+        @pl.when(self.at.middle)
+        def _():
+            for j in self.in_middle:
+                self.gone(j)
+
+        @pl.when(jnp.logical_not(self.at.middle))
+        def _():
+            for j in self.at_end:
+                self.gone(j)
+
+
+def scatter_buffers(rows, width):
+    return [
+        pltpu.VMEM((8, rows, width), BF),
+        pltpu.VMEM((8, rows, width), BF),
+        pltpu.VMEM((4, rows, width), BF),
+        pltpu.VMEM((5, rows, width), BF),
+        pltpu.SemaphoreType.DMA((17,)),
+        pltpu.SemaphoreType.DMA((17,)),
+    ]
+
+
+def scatter_kernel(rows, swaps, in_ref, *refs):
+    given, out_ref, taken = refs[:swaps], refs[swaps], refs[swaps + 1 : 2 * swaps + 1]
+    buffers, load_sem = refs[2 * swaps + 1 : 2 * swaps + 7], refs[2 * swaps + 7]
+    acc = buffers[0]
+    at = Place()
+    greet(at, False, swaps > 0)
+    crossing = cross(at, given, taken, *refs[2 * swaps + 8 :]) if swaps else []
+    total = Scatter(at, *buffers, out_ref)
+
+    def rows_of(rank):
+        return in_ref.at[pl.ds(pl.multiple_of(rank * rows, rows), rows)]
+
+    order = [(f, zi) for f in (1, 0) for zi in (3, 2, 1, 0)]
+    loads = {}
     for f, zi in order:
         k = f * 4 + zi
-        arrive(got_s.at[k], slot_s + k)
-        loads[k].wait()
-        others = [(got_s, k)]
-        if f == 1:
-            add(k, *others)
-            push(acc.at[k], got_f.at[zi], slot_f + zi, f_dev)
-            continue
-        arrive(got_f.at[zi], slot_f + zi)
-        others.append((got_f, zi))
-        if zi >= 2:
-
-            @pl.when(at.middle)
-            def _():
-                arrive(got_z.at[3 - zi], slot_z + 3 - zi)
-                add(k, *others, (got_z, 3 - zi))
-                there = 4 if zi == 2 else 3
-                push(
-                    acc.at[k], got_z.at[there], slot_z + there, at.inward(), slot_z + zi, in_middle
-                )
-
-            @pl.when(jnp.logical_not(at.middle))
-            def _():
-                add(k, *others)
-                push(acc.at[k], got_z.at[3 - zi], slot_z + 3 - zi, z_dev, slot_z + zi, at_end)
-        elif zi == 1:
-
-            @pl.when(at.middle)
-            def _():
-                arrive(got_z.at[3], slot_z + 3)
-                add(k, *others, (got_z, 3))
-                push(acc.at[k], got_z.at[4], slot_z + 4, z_dev, slot_z + 1, in_middle)
-
-            @pl.when(jnp.logical_not(at.middle))
-            def _():
-                add(k, *others)
-                push(acc.at[k], got_z.at[2], slot_z + 2, z_dev, slot_z + 1, at_end)
-        else:
-
-            @pl.when(at.middle)
-            def _():
-                arrive(got_z.at[2], slot_z + 2)
-                arrive(got_z.at[4], slot_z + 4)
-                add(k, *others, (got_z, 2), (got_z, 4), into=out_ref)
-
-            @pl.when(jnp.logical_not(at.middle))
-            def _():
-                arrive(got_z.at[4], slot_z + 4)
-                add(k, *others, (got_z, 4), into=out_ref)
-
+        total.to_twin(rows_of(at.shard(f * at.dy + at.dc, zi)), f, zi)
+        loads[k] = pltpu.make_async_copy(
+            rows_of(at.shard(f * at.dy, zi)), acc.at[k], load_sem.at[k]
+        )
+        loads[k].start()
+    for copy in crossing:
+        copy.start()
+    for f, zi in order:
+        loads[f * 4 + zi].wait()
+        (total.first if f else total.second)(zi)
     for copy in crossing:
         copy.wait()
-    for j in started:
-        gone(j)
-
-    @pl.when(at.middle)
-    def _():
-        for j in in_middle:
-            gone(j)
-
-    @pl.when(jnp.logical_not(at.middle))
-    def _():
-        for j in at_end:
-            gone(j)
+    total.finish()
 
 
 def own_rows(x, cid, given=()):
@@ -776,13 +819,8 @@
         in_specs=[hbm] * (1 + swaps),
         out_specs=[pl.BlockSpec(memory_space=pltpu.VMEM)] + [hbm] * swaps,
         scratch_shapes=[
-            pltpu.VMEM((8, rows, width), BF),
-            pltpu.VMEM((8, rows, width), BF),
-            pltpu.VMEM((4, rows, width), BF),
-            pltpu.VMEM((5, rows, width), BF),
+            *scatter_buffers(rows, width),
             pltpu.SemaphoreType.DMA((8,)),
-            pltpu.SemaphoreType.DMA((17,)),
-            pltpu.SemaphoreType.DMA((17,)),
             *crossing,
         ],
         compiler_params=pltpu.CompilerParams(
@@ -790,61 +828,6 @@
         ),
     )(x, *given)
     return got if swaps else got[0]
-
-
-def share_kernel(rows, count, *refs):
-    ins, outs = refs[:count], refs[count : 2 * count]
-    own_sem, send_sem, recv_sem = refs[2 * count :]
-    at = Place()
-    barrier = pltpu.get_barrier_semaphore()
-    f_dev, s_dev = at.device(oe=at.dy), at.device(oe=at.dc)
-    for peer in (f_dev, s_dev):
-        pl.semaphore_signal(barrier, inc=1, device_id=peer, device_id_type=MESH)
-    pl.semaphore_wait(barrier, 2)
-
-    def spot(oe):
-        return pl.ds(pl.multiple_of((at.e + oe) * rows, rows), rows)
-
-    copies = []
-    for m in range(count):
-        for j, device in enumerate((f_dev, s_dev)):
-            copy = remote(
-                ins[m], outs[m].at[spot(0)], send_sem.at[m * 3 + j], recv_sem.at[m * 3 + j], device
-            )
-            copy.start()
-            copies.append(copy)
-        local = pltpu.make_async_copy(ins[m], outs[m].at[spot(0)], own_sem.at[m])
-        local.start()
-        copies.append(local)
-    for m in range(count):
-        copies[m * 3].wait_recv()
-        src = outs[m].at[spot(at.dy)]
-        copy = remote(src, src, send_sem.at[m * 3 + 2], recv_sem.at[m * 3 + 2], s_dev)
-        copy.start()
-        copies.append(copy)
-    for m in range(count):
-        copies[m * 3].wait_send()
-        copies[m * 3 + 1].wait()
-        copies[m * 3 + 2].wait()
-        copies[count * 3 + m].wait()
-
-
-def share(arrays, cid):
-    count = len(arrays)
-    rows, width = arrays[0].shape
-    hbm = pl.BlockSpec(memory_space=pl.ANY)
-    return pl.pallas_call(
-        functools.partial(share_kernel, rows, count),
-        out_shape=[jax.ShapeDtypeStruct((4 * rows, width), a.dtype) for a in arrays],
-        in_specs=[hbm] * count,
-        out_specs=[hbm] * count,
-        scratch_shapes=[
-            pltpu.SemaphoreType.DMA((count,)),
-            pltpu.SemaphoreType.DMA((3 * count,)),
-            pltpu.SemaphoreType.DMA((3 * count,)),
-        ],
-        compiler_params=pltpu.CompilerParams(collective_id=cid, has_side_effects=True),
-    )(*arrays)
 
 
 def expert_gather_kernel(experts, *refs):
@@ -1092,31 +1075,18 @@
 
     disp, gate_back, shared_in, g_ref, u_ref, sg_ref, picked_ref, dy_ref, scaled_ref = take(9)
     weights = take(4)
-    out_ref, grad_gate, grad_up, grad_down = take(4)
+    out_ref, taken, *grads = take(7)
     wg, wu, gs, us, sg, picked, picked_dy, scaled, ib, grad, turned = take(11)
-    acc, got_s, got_f, got_z, out_s = take(5)
-    load_sem, store_sem, send_sem, recv_sem = take(4)
+    acc, got_s, got_f, got_z, send_sem, recv_sem = take(6)
+    out_s, load_sem, store_sem, cross_send, cross_recv = take(5)
     at = Place()
-    greet(at, False)
+    greet(at, False, True)
     rows, full = acc.shape[1:]
     width = shared_in.shape[1]
     slots = ib.shape[0]
     capacity = slots // 4
     mine = at.z * 4 + at.e
-    slot_z, slot_f, slot_s = 0, 5, 9
-    f_dev, s_dev, z_dev = at.device(oe=at.dy), at.device(oe=at.dc), at.device(zi=1)
-    started, in_middle, at_end = [], [], []
-
-    def push(src, dst, slot, device, sends=None, record=started):
-        j = slot if sends is None else sends
-        remote(src, dst, send_sem.at[j], recv_sem.at[slot], device).start()
-        record.append(j)
-
-    def gone(j):
-        remote(acc.at[0], acc.at[0], send_sem.at[j], recv_sem.at[0], s_dev).wait_send()
-
-    def arrive(dst, slot):
-        remote(acc.at[0], dst, send_sem.at[slot], recv_sem.at[slot], s_dev).wait_recv()
+    total = Scatter(at, acc, got_s, got_f, got_z, send_sem, recv_sem, out_ref)
 
     pairs = [
         (weights[0], wg.at[0]),
@@ -1141,11 +1111,11 @@
         @pl.loop(0, 4)
         def _(n):
             columns = pl.ds(pl.multiple_of(n * (width // 4), width // 4), width // 4)
-            total = product(gs[0, some, :], wg[0, :, columns])
-            total += product(us[0, some, :], wu[0, :, columns])
-            total += product(gs[1, some, :], wg[1, :, columns])
-            total += product(us[1, some, :], wu[1, :, columns])
-            ib[:, columns] = total.astype(BF)
+            terms = product(gs[0, some, :], wg[0, :, columns])
+            terms += product(us[0, some, :], wu[0, :, columns])
+            terms += product(gs[1, some, :], wg[1, :, columns])
+            terms += product(us[1, some, :], wu[1, :, columns])
+            ib[:, columns] = terms.astype(BF)
 
         for twin in range(2):
             for f in range(2):
@@ -1158,9 +1128,9 @@
                 @pl.loop(0, 2)
                 def _(n):
                     columns = pl.ds(pl.multiple_of(n * (width // 2), width // 2), width // 2)
-                    total = transposed_left(hot, ib[mine_slots, columns])
-                    total += product(sg[tokens, :], shared_in[:, columns])
-                    into[k, :, columns] = total.astype(BF)
+                    terms = transposed_left(hot, ib[mine_slots, columns])
+                    terms += product(sg[tokens, :], shared_in[:, columns])
+                    into[k, :, columns] = terms.astype(BF)
 
                 from_gates = gate_back[
                     pl.ds(pl.multiple_of(place * slots + e * capacity, capacity), capacity), :
@@ -1169,80 +1139,6 @@
                 from_gates = jnp.where(lane == mine, from_gates, 0.0).astype(BF)
                 into[k, :, width:] = transposed_left(hot, from_gates).astype(BF)
 
-    def to_twin(zi):
-        for f in range(2):
-            push(
-                out_s.at[f * 2 + zi % 2],
-                got_s.at[f * 4 + zi],
-                slot_s + f * 4 + zi,
-                s_dev,
-                None,
-                twins[zi],
-            )
-
-    twins = [[], [], [], []]
-
-    def add(k, *others, into=None):
-        @pl.loop(0, rows // 16)
-        def _(i):
-            span = pl.ds(pl.multiple_of(i * 16, 16), 16)
-            total = acc[k, span, :].astype(F32)
-            for ref, j in others:
-                total = total + ref[j, span, :].astype(F32)
-            if into is None:
-                acc[k, span, :] = total.astype(BF)
-            else:
-                into[span, :] = total
-
-    def first(zi):
-        arrive(got_s.at[4 + zi], slot_s + 4 + zi)
-        add(4 + zi, (got_s, 4 + zi))
-        push(acc.at[4 + zi], got_f.at[zi], slot_f + zi, f_dev)
-
-    def second(zi):
-        arrive(got_s.at[zi], slot_s + zi)
-        arrive(got_f.at[zi], slot_f + zi)
-        others = [(got_s, zi), (got_f, zi)]
-        if zi >= 2:
-
-            @pl.when(at.middle)
-            def _():
-                arrive(got_z.at[3 - zi], slot_z + 3 - zi)
-                add(zi, *others, (got_z, 3 - zi))
-                there = 4 if zi == 2 else 3
-                push(
-                    acc.at[zi], got_z.at[there], slot_z + there, at.inward(), slot_z + zi, in_middle
-                )
-
-            @pl.when(jnp.logical_not(at.middle))
-            def _():
-                add(zi, *others)
-                push(acc.at[zi], got_z.at[3 - zi], slot_z + 3 - zi, z_dev, slot_z + zi, at_end)
-        elif zi == 1:
-
-            @pl.when(at.middle)
-            def _():
-                arrive(got_z.at[3], slot_z + 3)
-                add(zi, *others, (got_z, 3))
-                push(acc.at[zi], got_z.at[4], slot_z + 4, z_dev, slot_z + 1, in_middle)
-
-            @pl.when(jnp.logical_not(at.middle))
-            def _():
-                add(zi, *others)
-                push(acc.at[zi], got_z.at[2], slot_z + 2, z_dev, slot_z + 1, at_end)
-        else:
-
-            @pl.when(at.middle)
-            def _():
-                arrive(got_z.at[2], slot_z + 2)
-                arrive(got_z.at[4], slot_z + 4)
-                add(zi, *others, (got_z, 2), (got_z, 4), into=out_ref)
-
-            @pl.when(jnp.logical_not(at.middle))
-            def _():
-                arrive(got_z.at[4], slot_z + 4)
-                add(zi, *others, (got_z, 4), into=out_ref)
-
     def gradient(m):
         step = 256
         right = picked_dy if m == 2 else picked
@@ -1253,41 +1149,37 @@
             columns = pl.ds(pl.multiple_of(n * step, step), step)
             grad[m, :, columns] = product(turned[...], right[:, columns]).astype(BF)
 
+    part = grad.shape[1] // 2
+    crossing = cross(at, [grad.at[0, pl.ds(0, part)]], [taken], cross_send, cross_recv)[0]
     stores = [
-        pltpu.make_async_copy(grad.at[m], ref, store_sem.at[m])
-        for m, ref in enumerate((grad_gate, grad_up, grad_down))
+        pltpu.make_async_copy(grad.at[j // 2, pl.ds(j % 2 * part, part)], grads[j - 1], store_sem.at[j])
+        for j in range(1, 6)
     ]
     for copy in loads[:7]:
         copy.wait()
     for zi in (3, 2, 1, 0):
         if zi < 2:
-            for j in twins[zi + 2]:
-                gone(j)
+            total.twin_gone(zi + 2)
         work(zi)
-        to_twin(zi)
-        first(zi)
+        for f in range(2):
+            total.to_twin(out_s.at[f * 2 + zi % 2], f, zi)
+        total.first(zi)
         if zi == 1:
-            second(3)
+            total.second(3)
     for copy in loads[7:]:
         copy.wait()
     for m, zi in ((0, 2), (1, 1), (2, 0)):
         gradient(m)
-        stores[m].start()
-        second(zi)
+        if m == 0:
+            crossing.start()
+        for j in (2 * m, 2 * m + 1):
+            if j > 0:
+                stores[j - 1].start()
+        total.second(zi)
     for copy in stores:
         copy.wait()
-    for j in started + twins[1] + twins[0]:
-        gone(j)
-
-    @pl.when(at.middle)
-    def _():
-        for j in in_middle:
-            gone(j)
-
-    @pl.when(jnp.logical_not(at.middle))
-    def _():
-        for j in at_end:
-            gone(j)
+    crossing.wait()
+    total.finish()
 
 
 def expert_back(dispatch, gate_back, shared_in, g, u, sg, picked, picked_dy, scaled, weights, cid):
@@ -1302,12 +1194,10 @@
         expert_scatter_kernel,
         out_shape=[
             shape((rows, full), F32),
-            shape((hidden, width), BF),
-            shape((hidden, width), BF),
-            shape((hidden, width), BF),
+            *[shape((hidden // 2, width), BF)] * 6,
         ],
         in_specs=[vmem] * 3 + [hbm] * 10,
-        out_specs=[vmem] + [hbm] * 3,
+        out_specs=[vmem] + [hbm] * 6,
         scratch_shapes=[
             pltpu.VMEM((2, hidden, width), BF),
             pltpu.VMEM((2, hidden, width), BF),
@@ -1320,20 +1210,768 @@
             pltpu.VMEM((slots // 4, width), BF),
             pltpu.VMEM((3, hidden, width), BF),
             pltpu.VMEM((hidden, slots), BF),
-            pltpu.VMEM((8, rows, full), BF),
-            pltpu.VMEM((8, rows, full), BF),
-            pltpu.VMEM((4, rows, full), BF),
-            pltpu.VMEM((5, rows, full), BF),
+            *scatter_buffers(rows, full),
             pltpu.VMEM((4, rows, full), BF),
             pltpu.SemaphoreType.DMA((10,)),
-            pltpu.SemaphoreType.DMA((3,)),
-            pltpu.SemaphoreType.DMA((17,)),
-            pltpu.SemaphoreType.DMA((17,)),
+            pltpu.SemaphoreType.DMA((6,)),
+            pltpu.SemaphoreType.DMA((1,)),
+            pltpu.SemaphoreType.DMA((1,)),
         ],
         compiler_params=pltpu.CompilerParams(
             collective_id=cid, has_side_effects=True, vmem_limit_bytes=63 * 1024 * 1024
         ),
     )(dispatch, gate_back, shared_in, g, u, sg, picked, picked_dy, scaled, *weights)
+
+
+def mixed_kernel(*refs):
+    refs = list(refs)
+
+    def take(count):
+        taken = refs[:count]
+        del refs[:count]
+        return taken
+
+    w_out, w_qkv, tables, q_ref, k_ref, v_ref, lse_ref, heads_out = take(8)
+    in_ref, back_ref, normed_ref, *given = take(5)
+    out_ref, normed_back, qkv_grad, out_grad, *taken = take(6)
+    rows_in, do, dk, dv, qkv, out_sum, qkv_sum, staged = take(8)
+    buffers = take(6)
+    first_sem, in_sem, store_sem, cross_send, cross_recv = take(5)
+    at = Place()
+    greet(at, False, True)
+    total = Scatter(at, *buffers, out_ref)
+    acc = buffers[0]
+    rows, width = acc.shape[1:]
+    length = q_ref.shape[0]
+    block = length // 4
+    crossing = cross(at, given, taken, cross_send, cross_recv)
+
+    def rows_of(rank):
+        return in_ref.at[pl.ds(pl.multiple_of(rank * rows, rows), rows)]
+
+    order = [(f, zi) for f in (1, 0) for zi in (3, 2, 1, 0)]
+    firsts = {}
+    for f, zi in order:
+        m = f * 4 + zi
+        total.to_twin(rows_of(at.shard(f * at.dy + at.dc, zi)), f, zi)
+        firsts[m] = pltpu.make_async_copy(
+            rows_of(at.shard(f * at.dy, zi)), acc.at[m], first_sem.at[m]
+        )
+        firsts[m].start()
+    for copy in crossing:
+        copy.start()
+
+    def rows_load(j):
+        ref = back_ref if j < 4 else normed_ref
+        return pltpu.make_async_copy(
+            ref.at[pl.ds(j % 4 * block, block)], rows_in.at[j % 2], in_sem.at[j % 2]
+        )
+
+    rows_load(0).start()
+    rows_load(1).start()
+
+    def heads_back(j):
+        rows_load(j).wait()
+        here = pl.ds(j * block, block)
+        do[here, :] = transposed_right(rows_in[j % 2], w_out[...]).astype(BF)
+        turned = heads_out[here, :].T
+
+        @pl.loop(0, 4)
+        def _(n):
+            columns = pl.ds(pl.multiple_of(n * (width // 4), width // 4), width // 4)
+            terms = product(turned, rows_in[j % 2, :, columns])
+            out_sum[:, columns] = terms if j == 0 else out_sum[:, columns] + terms
+
+        rows_load(j + 2).start()
+
+    scale = HDIM ** (-0.5)
+    step = 256
+
+    def attend_rows(i):
+        seen = (i + 1) * step
+        here = pl.ds(i * step, step)
+        q, go = q_ref[here, :], do[here, :]
+        scores = transposed_right(q, k_ref[0:seen, :]) * scale
+        row_at = lax.broadcasted_iota(jnp.int32, scores.shape, 0) + i * step
+        col_at = lax.broadcasted_iota(jnp.int32, scores.shape, 1)
+        scores = jnp.where(row_at >= col_at, scores, MASKED)
+        probs = jnp.exp(scores - lse_ref[here, 0:1])
+        weight_back = transposed_right(go, v_ref[0:seen, :])
+        inner = jnp.sum(probs * weight_back, axis=-1, keepdims=True)
+        score_back = (probs * (weight_back - inner)).astype(BF)
+        dv[0:seen, :] += transposed_left(probs.astype(BF), go)
+        dk[0:seen, :] += transposed_left(score_back, q) * scale
+        qkv[here, 0:HDIM] = turn_rows(product(score_back, k_ref[0:seen, :]) * scale, here)
+
+    def turn_rows(values, here):
+        other = pltpu.roll(values, HDIM // 2, 1)
+        return (values * tables[0, here, :] + other * tables[1, here, :]).astype(BF)
+
+    def finish_heads():
+        for j in range(8):
+            here = pl.ds(j * step, step)
+            qkv[here, HDIM : 2 * HDIM] = turn_rows(dk[here, :], here)
+            qkv[here, 2 * HDIM :] = dv[here, :].astype(BF)
+
+    def normed_store(j):
+        return pltpu.make_async_copy(
+            staged.at[j % 2], normed_back.at[pl.ds(j * step, step)], store_sem.at[j % 2]
+        )
+
+    def normed_rows(j):
+        if j >= 2:
+            normed_store(j - 2).wait()
+
+        @pl.loop(0, 4)
+        def _(n):
+            columns = pl.ds(pl.multiple_of(n * (width // 4), width // 4), width // 4)
+            staged[j % 2, :, columns] = product(
+                qkv[pl.ds(j * step, step), :], w_qkv[:, columns]
+            ).astype(BF)
+
+        normed_store(j).start()
+
+    def qkv_rows(j):
+        rows_load(4 + j).wait()
+        turned = qkv[pl.ds(j * block, block), :].T
+
+        @pl.loop(0, 4)
+        def _(n):
+            columns = pl.ds(pl.multiple_of(n * (width // 4), width // 4), width // 4)
+            terms = product(turned, rows_in[j % 2, :, columns])
+            qkv_sum[:, columns] = terms if j == 0 else qkv_sum[:, columns] + terms
+
+        if j < 2:
+            rows_load(6 + j).start()
+
+    for zi in (3, 2, 1, 0):
+        firsts[4 + zi].wait()
+        total.first(zi)
+    for j in range(4):
+        heads_back(j)
+    firsts[3].wait()
+    total.second(3)
+    dk[...] = jnp.zeros_like(dk)
+    dv[...] = jnp.zeros_like(dv)
+    for i in range(3):
+        attend_rows(i)
+    firsts[2].wait()
+    total.second(2)
+    for i in range(3, 6):
+        attend_rows(i)
+    firsts[1].wait()
+    total.second(1)
+    for i in range(6, 8):
+        attend_rows(i)
+    finish_heads()
+    for j in range(8):
+        normed_rows(j)
+    for j in range(4):
+        qkv_rows(j)
+    qkv_grad[...] = qkv_sum[...].astype(BF)
+    out_grad[...] = out_sum[...].astype(BF)
+    firsts[0].wait()
+    total.second(0)
+    for j in (6, 7):
+        normed_store(j).wait()
+    for copy in crossing:
+        copy.wait()
+    total.finish()
+
+
+def mixed_rows(
+    w_out, w_qkv, tables, q, k, v, lse, heads_out, mixed_part, attn_back, normed, given, cid
+):
+    length, width = attn_back.shape
+    rows = length // 16
+    hbm, vmem = pl.BlockSpec(memory_space=pl.ANY), pl.BlockSpec(memory_space=pltpu.VMEM)
+    shape = jax.ShapeDtypeStruct
+    return pl.pallas_call(
+        mixed_kernel,
+        out_shape=[
+            shape((rows, width), F32),
+            shape((length, width), BF),
+            shape((3 * HDIM, width), BF),
+            shape((HDIM, width), BF),
+            *[shape(a.shape, BF) for a in given],
+        ],
+        in_specs=[vmem] * 8 + [hbm] * 5,
+        out_specs=[vmem, hbm, vmem, vmem, hbm, hbm],
+        scratch_shapes=[
+            pltpu.VMEM((2, length // 4, width), BF),
+            pltpu.VMEM((length, HDIM), BF),
+            pltpu.VMEM((length, HDIM), F32),
+            pltpu.VMEM((length, HDIM), F32),
+            pltpu.VMEM((length, 3 * HDIM), BF),
+            pltpu.VMEM((HDIM, width), F32),
+            pltpu.VMEM((3 * HDIM, width), F32),
+            pltpu.VMEM((2, 256, width), BF),
+            *scatter_buffers(rows, width),
+            pltpu.SemaphoreType.DMA((8,)),
+            pltpu.SemaphoreType.DMA((2,)),
+            pltpu.SemaphoreType.DMA((2,)),
+            pltpu.SemaphoreType.DMA((2,)),
+            pltpu.SemaphoreType.DMA((2,)),
+        ],
+        compiler_params=pltpu.CompilerParams(
+            collective_id=cid, has_side_effects=True, vmem_limit_bytes=63 * 1024 * 1024
+        ),
+    )(w_out, w_qkv, tables, q, k, v, lse, heads_out, mixed_part, attn_back, normed, *given)
+
+
+class Gather:
+    def __init__(self, at, x_ref, out_ref, own_sem, send_sem, recv_sem):
+        self.at, self.x_ref, self.out_ref = at, x_ref, out_ref
+        self.send_sem, self.recv_sem = send_sem, recv_sem
+        self.rows = x_ref.shape[0]
+        self.f_dev, self.s_dev, self.z_dev = (
+            at.device(oe=at.dy),
+            at.device(oe=at.dc),
+            at.device(zi=1),
+        )
+        self.started, self.inside = [], []
+        self.own = pltpu.make_async_copy(x_ref, out_ref.at[self.where(0, 0)], own_sem)
+
+    def where(self, f, zi):
+        rows = self.rows
+        return pl.ds(pl.multiple_of(self.at.shard(f * self.at.dy, zi) * rows, rows), rows)
+
+    def push(self, f, zi, slot, device, sends=None, record=None):
+        src = self.x_ref if f == 0 and zi == 0 else self.out_ref.at[self.where(f, zi)]
+        dst = self.out_ref.at[self.where(f, zi)]
+        j = slot if sends is None else sends
+        remote(src, dst, self.send_sem.at[j], self.recv_sem.at[slot], device).start()
+        (self.started if record is None else record).append(j)
+
+    def spot(self):
+        return self.x_ref, self.out_ref.at[pl.ds(0, self.rows)]
+
+    def arrive(self, slot):
+        remote(*self.spot(), self.send_sem.at[slot], self.recv_sem.at[slot], self.s_dev).wait_recv()
+
+    def forward(self, f, zi):
+        if f == 0:
+            if zi == 0:
+                self.push(0, 0, 0, self.z_dev)
+            if zi < 2:
+                pl.when(self.at.middle)(
+                    lambda: self.push(0, zi, 1 + zi, self.at.inward(), 15 + zi, self.inside)
+                )
+            else:
+                pl.when(self.at.middle)(
+                    lambda: self.push(0, zi, zi - 1, self.z_dev, 15 + zi, self.inside)
+                )
+            self.push(0, zi, 3 + zi, self.f_dev)
+        self.push(f, zi, 7 + f * 4 + zi, self.s_dev)
+
+    def begin(self):
+        self.forward(0, 0)
+        self.own.start()
+
+    def line(self, zi):
+        self.arrive(zi - 1)
+        self.forward(0, zi)
+
+    def other(self, zi):
+        self.arrive(3 + zi)
+        self.forward(1, zi)
+
+    def finish(self):
+        for k in range(8):
+            self.arrive(7 + k)
+        self.own.wait()
+        for j in self.started:
+            remote(*self.spot(), self.send_sem.at[j], self.recv_sem.at[0], self.s_dev).wait_send()
+
+        @pl.when(self.at.middle)
+        def _():
+            for j in self.inside:
+                remote(
+                    *self.spot(), self.send_sem.at[j], self.recv_sem.at[0], self.s_dev
+                ).wait_send()
+
+
+def columns_loop(width, parts):
+    size = width // parts
+
+    def over(run):
+        @pl.loop(0, parts)
+        def _(n):
+            run(pl.ds(pl.multiple_of(n * size, size), size))
+
+    return over
+
+
+def gather_back_kernel(*refs):
+    refs = list(refs)
+
+    def take(count):
+        taken = refs[:count]
+        del refs[:count]
+        return taken
+
+    x_ref, disp, shared_out = take(3)
+    scaled_ref, act_ref, sg_ref, wd_a, wd_b, mix_ref, dy_ref, *given = take(9)
+    out_ref, mixed_part, units_grad, *taken = take(5)
+    scaled, acts, sg, wd, eb, rows_in, staged, unit_sum = take(8)
+    own_sem, send_sem, recv_sem, cross_send, cross_recv, load_sem, in_sem, store_sem = take(8)
+    at = Place()
+    greet(at, False, True)
+    gather = Gather(at, x_ref, out_ref, own_sem, send_sem, recv_sem)
+    crossing = cross(at, given, taken, cross_send, cross_recv)
+    rows, width = x_ref.shape
+    slots = eb.shape[0]
+    capacity = slots // 4
+    block = 4 * rows
+    units = acts.shape[1]
+    over = columns_loop(width, 4)
+
+    gather.begin()
+    for copy in crossing:
+        copy.start()
+    pairs = [
+        (scaled_ref, scaled),
+        (act_ref, acts),
+        (wd_a, wd.at[0]),
+        (wd_b, wd.at[1]),
+        (sg_ref, sg),
+    ]
+    loads = [pltpu.make_async_copy(a, b, load_sem.at[j]) for j, (a, b) in enumerate(pairs)]
+    for copy in loads:
+        copy.start()
+
+    def rows_load(j):
+        ref = mix_ref if j < 4 else dy_ref
+        return pltpu.make_async_copy(
+            ref.at[pl.ds(j % 4 * block, block)], rows_in.at[j % 2], in_sem.at[j % 2]
+        )
+
+    def mixed_store(j):
+        return pltpu.make_async_copy(
+            staged.at[j % 2], mixed_part.at[pl.ds(j * block, block)], store_sem.at[j % 2]
+        )
+
+    def mixed_rows_of(j):
+        some = pl.ds(j * slots, slots)
+
+        @over
+        def _(columns):
+            terms = product(scaled[0, some, :], wd[0, :, columns])
+            terms += product(scaled[1, some, :], wd[1, :, columns])
+            eb[:, columns] = terms.astype(BF)
+
+        if j >= 2:
+            mixed_store(j - 2).wait()
+        for i in range(4):
+            hot = disp[j * 4 + i]
+
+            @over
+            def _(columns):
+                terms = transposed_left(hot, eb[pl.ds(i * capacity, capacity), columns])
+                terms += product(acts[pl.ds((j * 4 + i) * rows, rows), :], shared_out[:, columns])
+                staged[j % 2, pl.ds(i * rows, rows), columns] = terms.astype(BF)
+
+        mixed_store(j).start()
+
+    def units_of(j):
+        rows_load(j).wait()
+        here = pl.ds(j % 4 * block, block)
+        turned = (sg[here, :] if j < 4 else acts[here, :]).T
+        into = pl.ds(0, 2 * units) if j < 4 else pl.ds(2 * units, units)
+
+        @over
+        def _(columns):
+            terms = product(turned, rows_in[j % 2, :, columns])
+            unit_sum[into, columns] = terms if j % 4 == 0 else unit_sum[into, columns] + terms
+
+        if j < 6:
+            rows_load(j + 2).start()
+
+    rows_load(0).start()
+    rows_load(1).start()
+    for copy in loads:
+        copy.wait()
+    for zi in range(4):
+        if zi > 0:
+            gather.line(zi)
+        mixed_rows_of(zi)
+        gather.other(zi)
+        units_of(2 * zi)
+        units_of(2 * zi + 1)
+    units_grad[...] = unit_sum[...].astype(BF)
+    for j in (2, 3):
+        mixed_store(j).wait()
+    for copy in crossing:
+        copy.wait()
+    gather.finish()
+
+
+def gather_back(x, given, dispatch, shared_out, scaled, acts, sg, wd_a, wd_b, mix_all, dy_all, cid):
+    rows, width = x.shape
+    length, units = acts.shape
+    slots, hidden = scaled.shape[1:]
+    hbm, vmem = pl.BlockSpec(memory_space=pl.ANY), pl.BlockSpec(memory_space=pltpu.VMEM)
+    shape = jax.ShapeDtypeStruct
+    return pl.pallas_call(
+        gather_back_kernel,
+        out_shape=[
+            shape((length, width), BF),
+            shape((length, width), BF),
+            shape((3 * units, width), BF),
+            *[shape(a.shape, BF) for a in given],
+        ],
+        in_specs=[hbm, vmem, vmem] + [hbm] * 9,
+        out_specs=[hbm, hbm, vmem, hbm, hbm],
+        scratch_shapes=[
+            pltpu.VMEM((2, slots, hidden), BF),
+            pltpu.VMEM(acts.shape, BF),
+            pltpu.VMEM(sg.shape, BF),
+            pltpu.VMEM((2, hidden, width), BF),
+            pltpu.VMEM((slots // 4, width), BF),
+            pltpu.VMEM((2, 4 * rows, width), BF),
+            pltpu.VMEM((2, 4 * rows, width), BF),
+            pltpu.VMEM((3 * units, width), F32),
+            pltpu.SemaphoreType.DMA,
+            pltpu.SemaphoreType.DMA((19,)),
+            pltpu.SemaphoreType.DMA((15,)),
+            pltpu.SemaphoreType.DMA((2,)),
+            pltpu.SemaphoreType.DMA((2,)),
+            pltpu.SemaphoreType.DMA((5,)),
+            pltpu.SemaphoreType.DMA((2,)),
+            pltpu.SemaphoreType.DMA((2,)),
+        ],
+        compiler_params=pltpu.CompilerParams(
+            collective_id=cid, has_side_effects=True, vmem_limit_bytes=60 * 1024 * 1024
+        ),
+    )(x, dispatch, shared_out, scaled, acts, sg, wd_a, wd_b, mix_all, dy_all, *given)
+
+
+class Home:
+    def __init__(self, at, home, home_out, mine, got, load_sem, x_send, x_recv, z_send, z_recv):
+        self.at, self.home, self.home_out, self.mine, self.got = at, home, home_out, mine, got
+        self.z_send, self.z_recv = z_send, z_recv
+        there = (1 - at.x) * 4
+        self.loads, self.crossing = [], []
+        for k in range(4):
+            spot = at.zs[k]
+            self.loads.append(
+                pltpu.make_async_copy(home.at[at.x * 4 + spot], mine.at[spot], load_sem.at[k])
+            )
+            self.crossing.append(
+                remote(
+                    home.at[there + spot], got.at[spot], x_send.at[k], x_recv.at[k], at.device(ox=at.dx)
+                )
+            )
+        self.keep = pltpu.make_async_copy(mine.at[at.z], home_out.at[at.z], load_sem.at[4])
+
+    def start(self):
+        for k in (3, 2, 1, 0):
+            self.loads[k].start()
+            self.crossing[k].start()
+
+    def line(self, k):
+        at = self.at
+        spot = at.zs[k]
+        self.loads[k].wait()
+        self.crossing[k].wait_recv()
+        mine, got = self.mine, self.got
+
+        @pl.loop(0, mine.shape[1] // 16)
+        def _(i):
+            span = pl.ds(pl.multiple_of(i * 16, 16), 16)
+            both = mine[spot, span, :].astype(F32) + got[spot, span, :].astype(F32)
+            mine[spot, span, :] = both.astype(BF)
+
+        if k == 0:
+            self.keep.start()
+        else:
+            self.copy(k).start()
+
+    def copy(self, k):
+        at = self.at
+        return remote(
+            self.mine.at[at.zs[k]],
+            self.home_out.at[at.z],
+            self.z_send.at[k - 1],
+            self.z_recv.at[at.z],
+            at.device(zi=k),
+        )
+
+    def finish(self):
+        at = self.at
+        for k in (1, 2, 3):
+            remote(
+                self.mine.at[at.z],
+                self.home_out.at[at.zs[k]],
+                self.z_send.at[k - 1],
+                self.z_recv.at[at.zs[k]],
+                at.device(zi=k),
+            ).wait_recv()
+            self.copy(k).wait_send()
+        self.keep.wait()
+        for copy in self.crossing:
+            copy.wait_send()
+
+
+class Share:
+    def __init__(self, at, ref, out, own_sem, send_sem, recv_sem):
+        self.at, rows = at, ref.shape[0]
+        spot = lambda oe: out.at[pl.ds(pl.multiple_of((at.e + oe) * rows, rows), rows)]
+        f_dev, s_dev = at.device(oe=at.dy), at.device(oe=at.dc)
+        self.local = pltpu.make_async_copy(ref, spot(0), own_sem)
+        self.far = remote(ref, spot(0), send_sem.at[0], recv_sem.at[0], f_dev)
+        self.near = remote(ref, spot(0), send_sem.at[1], recv_sem.at[1], s_dev)
+        self.over = remote(spot(at.dy), spot(at.dy), send_sem.at[2], recv_sem.at[2], s_dev)
+
+    def start(self):
+        for copy in (self.far, self.near, self.local):
+            copy.start()
+
+    def forward(self):
+        self.far.wait_recv()
+        self.over.start()
+
+    def finish(self):
+        self.far.wait_send()
+        self.near.wait()
+        self.over.wait()
+        self.local.wait()
+
+
+def last_scatter_kernel(*refs):
+    refs = list(refs)
+
+    def take(count):
+        taken = refs[:count]
+        del refs[:count]
+        return taken
+
+    in_ref, g_ref, u_ref, scaled_ref, picked_ref, dy_ref, home_ref, mixed_ref, given = take(9)
+    halves = take(5)
+    out_ref, taken, grad_gate, grad_up, grad_down, home_out, mixed_out = take(7)
+    right, left, other, grad, turned, mine, got = take(7)
+    buffers = take(6)
+    first_sem, cross_send, cross_recv, load_sem, store_sem = take(5)
+    home_sems, share_sems = take(5), take(3)
+    at = Place()
+    greet(at, True)
+    total = Scatter(at, *buffers, out_ref)
+    acc = buffers[0]
+    rows, width = acc.shape[1:]
+    part = given.shape[0]
+    crossing = cross(at, [given], [taken], cross_send, cross_recv)[0]
+    home = Home(at, home_ref, home_out, mine, got, *home_sems)
+    sharing = Share(at, mixed_ref, mixed_out, *share_sems)
+
+    def rows_of(rank):
+        return in_ref.at[pl.ds(pl.multiple_of(rank * rows, rows), rows)]
+
+    order = [(f, zi) for f in (1, 0) for zi in (3, 2, 1, 0)]
+    firsts = {}
+    for f, zi in order:
+        k = f * 4 + zi
+        total.to_twin(rows_of(at.shard(f * at.dy + at.dc, zi)), f, zi)
+        firsts[k] = pltpu.make_async_copy(
+            rows_of(at.shard(f * at.dy, zi)), acc.at[k], first_sem.at[k]
+        )
+        firsts[k].start()
+    home.start()
+    crossing.start()
+    pairs = [
+        (picked_ref, right.at[0]),
+        (dy_ref, right.at[1]),
+        (g_ref.at[0], left.at[0]),
+        (u_ref.at[0], left.at[1]),
+        (scaled_ref.at[0], left.at[2]),
+    ]
+    pairs += [
+        (ref, other.at[j // 2 % 2, pl.ds(j % 2 * part, part)])
+        for j, ref in enumerate(halves + [taken])
+    ]
+    loads = [pltpu.make_async_copy(a, b, load_sem.at[j]) for j, (a, b) in enumerate(pairs)]
+    for copy in loads[:9]:
+        copy.start()
+
+    def store(m):
+        ref = (grad_gate, grad_up, grad_down)[m]
+        return pltpu.make_async_copy(grad.at[m % 2], ref, store_sem.at[m])
+
+    def gradient(m):
+        turned[...] = left[m].T
+
+        @columns_loop(width, 8)
+        def _(columns):
+            terms = product(turned[...], right[m // 2, :, columns])
+            grad[m % 2, :, columns] = terms + other[m % 2, :, columns].astype(F32)
+
+        store(m).start()
+
+    for zi in (3, 2, 1, 0):
+        firsts[4 + zi].wait()
+        total.first(zi)
+    sharing.start()
+    for copy in loads[:9]:
+        copy.wait()
+    gradient(0)
+    loads[9].start()
+    home.line(3)
+    firsts[3].wait()
+    total.second(3)
+    gradient(1)
+    home.line(2)
+    firsts[2].wait()
+    total.second(2)
+    home.line(1)
+    firsts[1].wait()
+    total.second(1)
+    home.line(0)
+    sharing.forward()
+    crossing.wait_recv()
+    loads[10].start()
+    loads[9].wait()
+    loads[10].wait()
+    store(0).wait()
+    gradient(2)
+    firsts[0].wait()
+    total.second(0)
+    home.finish()
+    sharing.finish()
+    store(1).wait()
+    store(2).wait()
+    crossing.wait_send()
+    total.finish()
+
+
+def last_rows(x, g, u, scaled, picked, picked_dy, home, mixed_own, given, halves, cid):
+    rows, width = x.shape[0] // 16, x.shape[1]
+    slots, hidden = g.shape[1:]
+    hbm, vmem = pl.BlockSpec(memory_space=pl.ANY), pl.BlockSpec(memory_space=pltpu.VMEM)
+    shape, sems = jax.ShapeDtypeStruct, lambda n: pltpu.SemaphoreType.DMA((n,))
+    return pl.pallas_call(
+        last_scatter_kernel,
+        out_shape=[
+            shape((rows, width), F32),
+            shape(given.shape, BF),
+            *[shape((hidden, width), F32)] * 3,
+            shape((4,) + home.shape[1:], BF),
+            shape((4 * rows, width), BF),
+        ],
+        in_specs=[hbm] * 14,
+        out_specs=[vmem] + [hbm] * 6,
+        scratch_shapes=[
+            pltpu.VMEM((2, slots, width), BF),
+            pltpu.VMEM((3, slots, hidden), BF),
+            pltpu.VMEM((2, hidden, width), BF),
+            pltpu.VMEM((2, hidden, width), F32),
+            pltpu.VMEM((hidden, slots), BF),
+            pltpu.VMEM((4,) + home.shape[1:], BF),
+            pltpu.VMEM((4,) + home.shape[1:], BF),
+            *scatter_buffers(rows, width),
+            sems(8),
+            sems(1),
+            sems(1),
+            sems(11),
+            sems(3),
+            sems(5),
+            sems(4),
+            sems(4),
+            sems(3),
+            sems(4),
+            pltpu.SemaphoreType.DMA,
+            sems(3),
+            sems(3),
+        ],
+        compiler_params=pltpu.CompilerParams(
+            collective_id=cid, has_side_effects=True, vmem_limit_bytes=62 * 1024 * 1024
+        ),
+    )(x, g, u, scaled, picked, picked_dy, home, mixed_own, given, *halves)
+
+
+def end_kernel(tokens_ref, gain_ref, small_ref, out_ref, gain_out, small_out, *scratch):
+    gain_got, gain_sum, gain_all, small_all = scratch[:4]
+    share_sems = scratch[4:7]
+    gain_send, gain_recv, sum_send, sum_recv, small_send, small_recv = scratch[7:]
+    at = Place()
+    barrier = pltpu.get_barrier_semaphore()
+    blocks = [(at.device(ox=ox, zi=k), m * 4 + k) for m, ox in enumerate((0, at.dx)) for k in range(4)]
+    group = [at.device(oe=oe) for oe in (at.dy, at.dc, at.dy + at.dc)]
+    for peer in [device for device, j in blocks[1:]] + group:
+        pl.semaphore_signal(barrier, inc=1, device_id=peer, device_id_type=MESH)
+    pl.semaphore_wait(barrier, 10)
+    sharing = Share(at, tokens_ref, out_ref, *share_sems)
+    own = at.x * 4 + at.z
+    copies = []
+    for device, j in blocks[1:]:
+        copy = remote(
+            gain_ref.at[device[0] * 4 + device[1]],
+            gain_got.at[own],
+            gain_send.at[j],
+            gain_recv.at[own],
+            device,
+        )
+        copy.start()
+        copies.append(copy)
+    for j, device in enumerate(group):
+        copy = remote(small_ref, small_all.at[j], small_send.at[j], small_recv.at[j], device)
+        copy.start()
+        copies.append(copy)
+    sharing.start()
+    gain = gain_ref[own]
+    for device, j in blocks[1:]:
+        there = device[0] * 4 + device[1]
+        remote(
+            gain_ref.at[0], gain_got.at[there], gain_send.at[j], gain_recv.at[there], device
+        ).wait_recv()
+        gain = gain + gain_got[there]
+    gain_sum[...] = gain
+    for j, device in enumerate(group):
+        copy = remote(gain_sum, gain_all.at[j], sum_send.at[j], sum_recv.at[j], device)
+        copy.start()
+        copies.append(copy)
+    small = small_ref[...]
+    for j in range(3):
+        copies[7 + j].wait_recv()
+        copies[10 + j].wait_recv()
+        small = small + small_all[j]
+        gain = gain + gain_all[j]
+    gain_out[...] = gain
+    small_out[...] = small
+    sharing.forward()
+    sharing.finish()
+    for copy in copies:
+        copy.wait_send()
+
+
+def end(tokens_own, gain_part, small, cid):
+    rows, width = tokens_own.shape
+    vmem, hbm = pl.BlockSpec(memory_space=pltpu.VMEM), pl.BlockSpec(memory_space=pl.ANY)
+    shape, sems = jax.ShapeDtypeStruct, lambda n: pltpu.SemaphoreType.DMA((n,))
+    return pl.pallas_call(
+        end_kernel,
+        out_shape=[
+            shape((4 * rows, width), tokens_own.dtype),
+            shape(gain_part.shape[1:], F32),
+            shape(small.shape, F32),
+        ],
+        in_specs=[hbm, vmem, vmem],
+        out_specs=[hbm, vmem, vmem],
+        scratch_shapes=[
+            pltpu.VMEM(gain_part.shape, F32),
+            pltpu.VMEM(gain_part.shape[1:], F32),
+            pltpu.VMEM((3,) + gain_part.shape[1:], F32),
+            pltpu.VMEM((3,) + small.shape, F32),
+            pltpu.SemaphoreType.DMA,
+            sems(3),
+            sems(3),
+            sems(8),
+            sems(8),
+            sems(3),
+            sems(3),
+            sems(3),
+            sems(3),
+        ],
+        compiler_params=pltpu.CompilerParams(collective_id=cid, has_side_effects=True),
+    )(tokens_own, gain_part, small)
 
 
 ALL = ("dp", "ctx", "exp")
@@ -1383,39 +2021,6 @@
     )(q, k, v)
 
 
-def attend_back_kernel(scale, block, q_ref, k_ref, v_ref, do_ref, lse_ref, dq_ref, dk_ref, dv_ref):
-    length = q_ref.shape[0]
-    dk_ref[...] = jnp.zeros_like(dk_ref)
-    dv_ref[...] = jnp.zeros_like(dv_ref)
-    for i in range(length // block):
-        seen = (i + 1) * block
-        rows = pl.ds(i * block, block)
-        q = q_ref[rows, :]
-        do = do_ref[rows, :]
-        scores = transposed_right(q, k_ref[0:seen, :]) * scale
-        row_at = lax.broadcasted_iota(jnp.int32, scores.shape, 0) + i * block
-        col_at = lax.broadcasted_iota(jnp.int32, scores.shape, 1)
-        scores = jnp.where(row_at >= col_at, scores, MASKED)
-        probs = jnp.exp(scores - lse_ref[rows, 0:1])
-        weight_back = transposed_right(do, v_ref[0:seen, :])
-        inner = jnp.sum(probs * weight_back, axis=-1, keepdims=True)
-        score_back = (probs * (weight_back - inner)).astype(BF)
-        dv_ref[0:seen, :] += transposed_left(probs.astype(BF), do)
-        dk_ref[0:seen, :] += transposed_left(score_back, q) * scale
-        dq_ref[rows, :] = product(score_back, k_ref[0:seen, :]) * scale
-
-
-def attend_back(q, k, v, do, lse):
-    length = q.shape[0]
-    return pl.pallas_call(
-        functools.partial(attend_back_kernel, HDIM ** (-0.5), 256),
-        out_shape=(jax.ShapeDtypeStruct((length, HDIM), F32),) * 3,
-        in_specs=[pl.BlockSpec(memory_space=pltpu.VMEM)] * 5,
-        out_specs=(pl.BlockSpec(memory_space=pltpu.VMEM),) * 3,
-        compiler_params=pltpu.CompilerParams(vmem_limit_bytes=56 * 1024 * 1024),
-    )(q, k, v, do, lse)
-
-
 def turn_tables(length):
     inverse = 10000.0 ** (-np.arange(HDIM // 2).astype(np.float64) * 2.0 / HDIM)
     angles = np.arange(length).astype(np.float64)[:, None] * inverse[None, :]
@@ -1425,17 +2030,6 @@
 def turn(rows, cosine, sine):
     a, b = rows[:, : HDIM // 2], rows[:, HDIM // 2 :]
     return jnp.concatenate([a * cosine - b * sine, b * cosine + a * sine], axis=1)
-
-
-def turn_back(rows, cosine, sine):
-    a, b = rows[:, : HDIM // 2], rows[:, HDIM // 2 :]
-    return jnp.concatenate([a * cosine + b * sine, b * cosine - a * sine], axis=1)
-
-
-def silu_parts(gate, up):
-    s = jax.nn.sigmoid(gate)
-    act = gate * s
-    return act * up, s * (1.0 + gate * (1.0 - s)) * up, act
 
 
 def fast_body(
@@ -1539,15 +2133,7 @@
         )
     )
 
-    def spread(rows):
-        return jnp.einsum(
-            "gst,gsd->gtd",
-            dispatch,
-            rows.reshape(groups, capacity, width),
-            preferred_element_type=F32,
-        ).reshape(length, width)
-
-    mix_back, gate_grad_b, up_grad_b, down_grad_b = expert_back(
+    mix_back, gate_0, gate_1, up_0, up_1, down_0, down_1 = expert_back(
         dispatch,
         gate_back,
         shared_in,
@@ -1574,71 +2160,87 @@
     middle_norm_back, gain_mix_part = norm_mix_back(mix_back)
     middle_back = dy_own.astype(F32) + middle_norm_back
     attn_back = middle_back.astype(BF)
-    attn_back_all, gate_grad_b = all_rows(attn_back, False, 7, (), (gate_grad_b,))
-    heads_back = transposed_right(attn_back_all, w_out_head).astype(BF)
-    out_part = transposed_left(heads_out, attn_back_all).astype(BF)
-    dq, dk, dv = attend_back(query, key, value, heads_back, lse)
-    qkv_back = jnp.concatenate(
-        [
-            turn_back(dq, cosine, sine).astype(BF),
-            turn_back(dk, cosine, sine).astype(BF),
-            dv.astype(BF),
-        ],
-        axis=1,
-    )
-    normed_back, down_grad_b = own_rows(transposed_right(qkv_back, w_qkv).astype(BF), 8, (down_grad_b,))
-    qkv_part = transposed_left(normed, qkv_back).astype(BF)
+    attn_back_all, mixed_part, units_part, gate_1, up_0 = gather_back(
+        attn_back,
+        (gate_1, up_0),
+        dispatch,
+        shared_out,
+        scaled,
+        shared_act,
+        shared_gu_back,
+        own_down,
+        other_down,
+        mix_all,
+        dy_all,
+        7,
+    )
+    tables = jnp.stack(
+        [jnp.concatenate([cosine, cosine], axis=1), jnp.concatenate([sine, -sine], axis=1)]
+    )
+    mixed_sum, normed_part, qkv_part, out_part, up_1, down_0 = mixed_rows(
+        w_out_head,
+        w_qkv.T,
+        tables,
+        query,
+        key,
+        value,
+        lse,
+        heads_out,
+        mixed_part,
+        attn_back_all,
+        normed,
+        (up_1, down_0),
+        9,
+    )
+    mixed_own = (middle + mixed_sum).astype(BF)
+    units_part = units_part.reshape(3, wide, width)[:, :cut].reshape(3 * cut, width)
+    small_part = jnp.concatenate([gain_mix_part[None], router_part], axis=0).astype(BF)
+    small_rows = -(-(experts + 1) // 16) * 16
+    small_part = jnp.pad(small_part, ((0, small_rows - experts - 1), (0, 0)))
+    home = jnp.concatenate([qkv_part, out_part, units_part, small_part], axis=0)
+    home = home.reshape(-1, 8, dense).transpose(1, 0, 2)
+    normed_back, _, gate_grad, up_grad, down_grad, home, mixed = last_rows(
+        normed_part,
+        g_back,
+        u_back,
+        scaled,
+        picked,
+        picked_dy,
+        home,
+        mixed_own,
+        down_1,
+        (gate_0, gate_1, up_0, up_1, down_0),
+        8,
+    )
+    home = home.astype(F32)
+    small_part = jnp.sum(home[:, -small_rows:], axis=0)
     _, norm_attn_back = jax.vjp(rms_scale, tokens_own.astype(F32), attention_gain)
     input_norm_back, gain_attn_part = norm_attn_back(normed_back)
     tokens_back_own = (middle_back + input_norm_back).astype(BF)
 
-    expert_out = product(scaled[0], expert_down[0]) + product(scaled[1], other_down)
-    mixed_part = (product(shared_act, shared_out) + spread(expert_out.astype(BF))).astype(BF)
-    mixed_sum, up_grad_b = own_rows(mixed_part, 9, (up_grad_b,))
-    mixed_own = (middle + mixed_sum).astype(BF)
-
-    mixed, tokens_back = share([mixed_own, tokens_back_own], 6)
-    small = jnp.concatenate([gain_attn_part[None], gain_mix_part[None], router_part], axis=0)
-    small = small.reshape(experts + 2, 8, 1, dense).transpose(1, 2, 0, 3)
-    small = jnp.broadcast_to(small, (8, 4, experts + 2, dense)).reshape(32, experts + 2, dense)
-    small = lax.all_to_all(small, ALL, split_axis=0, concat_axis=0, tiled=True)
-    small = jnp.sum(small, axis=0)
-    shared_gu_grad = transposed_left(shared_gu_back, mix_all).astype(BF).reshape(2, wide, width)
-    shared_down_part = transposed_left(shared_act, dy_all).astype(BF)
-    home_rows = swap(qkv_part.reshape(8, dense, 3 * HDIM)).astype(F32)
-    home_columns = swap(
-        jnp.concatenate(
-            [out_part, shared_gu_grad[0, :cut], shared_gu_grad[1, :cut], shared_down_part[:cut]],
-            axis=0,
-        )
-        .reshape(HDIM + 3 * cut, 8, dense)
-        .transpose(1, 0, 2)
-    ).astype(F32)
-    home_rows = home_rows[:4] + home_rows[4:]
-    home_columns = home_columns[:4] + home_columns[4:]
+    gain_part = jnp.pad(gain_attn_part.reshape(8, 1, dense), ((0, 0), (0, 7), (0, 0)))
+    tokens_back, gain_attn, small = end(tokens_back_own, gain_part, small_part, 6)
 
     def columns_of(parts):
-        return parts.transpose(1, 0, 2).reshape(dense, -1)
+        return parts.transpose(2, 0, 1).reshape(dense, -1)
 
     def rows_of(parts):
         return parts.reshape(-1, dense)
 
-    gate_grad = transposed_left(g_back[0], picked) + gate_grad_b.astype(F32)
-    up_grad = transposed_left(u_back[0], picked) + up_grad_b.astype(F32)
-    down_grad = transposed_left(scaled[0], picked_dy) + down_grad_b.astype(F32)
+    units = 4 * HDIM
     return (
         mixed[None],
         tokens_back[None],
+        gain_attn[0],
+        columns_of(home[:, :HDIM]),
+        columns_of(home[:, HDIM : 2 * HDIM]),
+        columns_of(home[:, 2 * HDIM : 3 * HDIM]),
+        rows_of(home[:, 3 * HDIM : units]),
         small[0],
-        columns_of(home_rows[:, :, :HDIM]),
-        columns_of(home_rows[:, :, HDIM : 2 * HDIM]),
-        columns_of(home_rows[:, :, 2 * HDIM : 3 * HDIM]),
-        rows_of(home_columns[:, :HDIM]),
-        small[1],
-        small[2:].T,
-        rows_of(home_columns[:, HDIM : HDIM + cut]).T,
-        rows_of(home_columns[:, HDIM + cut : HDIM + 2 * cut]).T,
-        rows_of(home_columns[:, HDIM + 2 * cut :]),
+        small[1 : experts + 1].T,
+        rows_of(home[:, units : units + cut]).T,
+        rows_of(home[:, units + cut : units + 2 * cut]).T,
+        rows_of(home[:, units + 2 * cut : units + 3 * cut]),
         gate_grad.T[None],
         up_grad.T[None],
         down_grad[None],

time: 923 us -> 827 us (0.90)
  matrix products: 104 us -> 14.1 us
  waiting for transfers between devices: 38.7 us -> 4.46 us
  Pallas kernels: 681 us -> 701 us
  local copies, waits for them, and re-layouts: 42.4 us -> 62.1 us
  starting transfers between devices: 15.9 us -> 3.04 us
    pallas_call x2 -> x4, Pallas kernels: 45.4 us -> 276 us  [the longest x1 94 us: last_rows(): pl.pallas_call(last_scatter_kernel, out_shape=[shape((rows, width), F32),...]
    pallas_call x3 -> x1, Pallas kernels: 203 us -> 57.1 us  [own_rows(): pl.pallas_call(functools.partial(scatter_kernel, rows, swaps), out_shape=...]
    pallas_call x3 -> x2, Pallas kernels: 236 us -> 171 us  [all_rows(): pl.pallas_call(functools.partial(gather_kernel, block, rows, parts, extra...]
    dot_general x8 -> x1, matrix products: 47.7 us -> 1.15 us  [transposed_left(): lax.dot_general(left_side, right_side, (((0,), (0,)), ((), ())), preferre...]
    dot_general x6 -> x3, matrix products: 35.6 us -> 12.7 us  [product(): return jnp.dot(left_side, right_side, preferred_element_type=jnp.float32)]
    all_to_all x3 -> x0, waiting for transfers between devices: 22.6 us -> none  [the longest x2 14.5 us: swap(): lax.all_to_all(blocks, DENSE, split_axis=0, concat_axis=0, tiled=True)]
    all_to_all x3 -> x0, starting transfers between devices: 12.8 us -> none  [the longest x2 8.89 us: swap(): lax.all_to_all(blocks, DENSE, split_axis=0, concat_axis=0, tiled=True)]
    unnamed x107 -> x68, local copies, waits for them, and re-layouts: 15.7 us -> 28.2 us
  transfers between devices with their start and end apart: 6 -> 3, of which waited for: 3 -> 1; matrix products, arithmetic and copies ran while one was open for 12% -> 6% of each run, Pallas kernels for 27% -> 16%
where the time goes in v4:
time: 827 us; the launch traced here: 821 us
  Pallas kernels  701 us (85%)
  local copies, waits for them, and re-layouts  62.1 us (8%)
  other arithmetic  34.7 us (4%)
  matrix products  14.1 us (2%)
    pallas_call x2, Pallas kernels, all_rows(): pl.pallas_call(functools.partial(gather_kernel, block, rows, parts, extra...  171 us
    pallas_call x1, Pallas kernels, expert_rows(): pl.pallas_call(functools.partial(expert_gather_kernel, experts), out_shap...  96.6 us
    pallas_call x1, Pallas kernels, last_rows(): pl.pallas_call(last_scatter_kernel, out_shape=[shape((rows, width), F32),...  94 us
    pallas_call x1, Pallas kernels, expert_back(): pl.pallas_call(expert_scatter_kernel, out_shape=[shape((rows, full), F32)...  92.2 us
    pallas_call x1, Pallas kernels, gather_back(): pl.pallas_call(gather_back_kernel, out_shape=[shape((length, width), BF),...  91.4 us
    pallas_call x1, Pallas kernels, mixed_rows(): pl.pallas_call(mixed_kernel, out_shape=[shape((rows, width), F32), shape(...  69.4 us
    pallas_call x1, Pallas kernels, own_rows(): pl.pallas_call(functools.partial(scatter_kernel, rows, swaps), out_shape=...  57.1 us
    unnamed x68, local copies, waits for them, and re-layouts  28.2 us
  transfers between devices with their start and end apart: 3, of which 1 were waited for; matrix products, arithmetic and copies ran while one was open for 6% of the time, Pallas kernels for 16%

profile of v4, /device:TPU:0, one launch (start us, length us, event | category | flops | bytes accessed | tf_op | source)
XLA Modules:
  0.0 821.0 jit_solution(7780799376228833471)
XLA Ops:
  8.6 104.9 %shard_map.325 = (bf16[2048,2048]{1,0:T(8,128)(2,1)}, bf16[8,256,384]{2,1,0:T(8,128)(2,1)}, bf16[8,128,256]{2,1,0:T(8,128)(2,1)}, bf16[8,528,256]{2,1,0:T(8,128)(2,1)}, bf16[8,32,256]{2,1,0:T(8,128)(2,1)}) custom-call(bf16[512,2048]{1,0:T(8,128)(2,1)} %bitcast.126, bf16[4,256,384]{2,1,0:T(8,128)(2,1)} %pad_maximum_fusion.1.refs_1_, ...), custom_call_target="tpu_custom_call" | custom-call | tf_op jit(solution)/shard_map/pallas_call | solution.py:641
  119.4 5.3 fusion
  124.7 8.7 %fusion.2.refs_10_ = bf16[2048,2048]{1,0:T(8,128)(2,1)} fusion(bf16[2048,2048]{1,0:T(8,128)(2,1)} %get-tuple-element.65, f32[2048]{0:T(1024)S(1)} %bitcast.170, f32[2048]{0:T(1024)S(1)} %add_rsqrt_fusion), kind=kLoop, calls=%fused_computation.4 | loop fusion | flops 16777216 | bytes 16793600 | tf_op jit(solution)/shard_map/convert_element_type | solution.py:2103
  133.4 7.2 fusion.26
  143.6 8.6 %shard_map.326 = (bf16[2048,128]{1,0:T(8,128)(2,1)}, f32[2048,128]{1,0:T(8,128)}) custom-call(bf16[2048,128]{1,0:T(8,128)(2,1)} %get-tuple-element.177.q_ref.refs_3_, bf16[2048,128]{1,0:T(8,128)(2,1)} %get-tuple-element.178.k_ref.refs_4_, bf16[2048,128]{1,0:T(8,128)(2,1)} %slice.151.v_ref.refs_5_), custom_call_target="tpu_custom_call" | custom-call | tf_op jit(solution)/shard_map/pallas_call | solution.py:2012
  152.2 3.4 convolution_convert_fusion.in_ref
  155.6 57.1 %shard_map.327 = f32[128,2048]{1,0:T(8,128)S(1)} custom-call(bf16[2048,2048]{1,0:T(8,128)(2,1)S(1)} %convolution_convert_fusion.in_ref), custom_call_target="tpu_custom_call" | custom-call | tf_op jit(solution)/shard_map/pallas_call | solution.py:815
  214.9 2.6 copy.110
  217.5 65.9 %shard_map.328.refs_1_.refs_9_ = bf16[2048,2048]{1,0:T(8,128)(2,1)} custom-call(bf16[512,2048]{1,0:T(8,128)(2,1)} %bitcast.138), custom_call_target="tpu_custom_call" | custom-call | tf_op jit(solution)/shard_map/pallas_call | solution.py:641
  285.5 3.5 reshape.226
  295.2 4.5 collective-permute-done.2.refs_11_.refs_7_
  299.7 96.6 %shard_map.329 = (bf16[2048,2048]{1,0:T(8,128)(2,1)}, bf16[1024,2048]{1,0:T(8,128)(2,1)}, bf16[1024,2048]{1,0:T(8,128)(2,1)}, bf16[2,1024,704]{2,1,0:T(8,128)(2,...) custom-call(bf16[128,2048]{1,0:T(8,128)(2,1)} %copy-done.4, ...), custom_call_target="tpu_custom_call" | custom-call | tf_op jit(solution)/shard_map/pallas_call | solution.py:1026
  396.3 92.2 %shard_map.330 = (f32[128,2176]{1,0:T(8,128)}, bf16[352,2048]{1,0:T(8,128)(2,1)}, bf16[352,2048]{1,0:T(8,128)(2,1)}, bf16[352,2048]{1,0:T(8,128)(2,1)}, bf16[352...) custom-call(bf16[16,64,128]{2,1,0:T(8,128)(2,1)} %select_convert_fusion.refs_2_.refs_0_.refs_1_, ...), custom_call_target="tpu_custom_call" | custom-call | tf_op jit(solution)/shard_map/pallas_call | solution.py:1193
  495.5 91.4 %shard_map.331 = (bf16[2048,2048]{1,0:T(8,128)(2,1)}, bf16[2048,2048]{1,0:T(8,128)(2,1)}, bf16[768,2048]{1,0:T(8,128)(2,1)}, bf16[352,2048]{1,0:T(8,128)(2,1)}, bf16[352,2048]{1,0:T(8,128)(2,1)}) custom-call(bf16[128,2048]{1,0:T(8,128)(2,1)} %fusion.22.refs_0_, bf16[16,64,128]{2,1,0:T(8,128)(2,1)} %select_convert_fusion.refs_2_.refs_0_.refs_1_, ...), custom_call_target="tpu_custom_call" | custom-call | tf_op jit(solution)/shard_map/pallas_call | solution.py:1615
  586.9 69.4 %shard_map.332 = (f32[128,2048]{1,0:T(8,128)}, bf16[2048,2048]{1,0:T(8,128)(2,1)}, bf16[384,2048]{1,0:T(8,128)(2,1)}, bf16[128,2048]{1,0:T(8,128)(2,1)}, bf16[35...) custom-call(bf16[128,2048]{1,0:T(8,128)(2,1)} %bitcast.137, bf16[384,2048]{1,0:T(8,128)(2,1)} %bitcast.127, ...), custom_call_target="tpu_custom_call" | custom-call | tf_op jit(solution)/shard_map/pallas_call | solution.py:1389
  660.1 2.6 copy.100
  662.6 2.6 copy.102
  671.3 94.0 %shard_map.333 = (f32[128,2048]{1,0:T(8,128)}, bf16[352,2048]{1,0:T(8,128)(2,1)}, f32[704,2048]{1,0:T(8,128)}, f32[704,2048]{1,0:T(8,128)}, f32[704,2048]{1,0:T(...) custom-call(bf16[2048,2048]{1,0:T(8,128)(2,1)} %get-tuple-element.89.refs_0_, ...), custom_call_target="tpu_custom_call" | custom-call | tf_op jit(solution)/shard_map/pallas_call | solution.py:1850
  765.3 2.5 fusion.24
  775.3 21.1 %shard_map.334 = (bf16[512,2048]{1,0:T(8,128)(2,1)}, f32[8,256]{1,0:T(8,128)}, f32[32,256]{1,0:T(8,128)}) custom-call(bf16[128,2048]{1,0:T(8,128)(2,1)} %fusion.5.tokens_ref, f32[8,8,256]{2,1,0:T(8,128)} %pad.24.gain_ref, f32[32,256]{1,0:T(8,128)} %slice_reduce_fusion.small_ref), custom_call_target="tpu_custom_call" | custom-call | tf_op jit(solution)/shard_map/pallas_call | solution.py:1949
  804.6 3.2 copy.125
  809.1 6.6 copy.127
  815.7 2.5 copy.128
  818.2 2.5 copy.129
  (135 shorter events, 61.0 us)
Async XLA Ops:
  0.6 4.9 copy-start.21
  0.7 5.2 copy-start.22
  4.0 3.6 copy-start.18
  4.0 3.6 copy-start.19
  4.0 3.6 copy-start.20
  113.5 181.7 %collective-permute-start = (bf16[704,2048]{1,0:T(8,128)(2,1)}, bf16[704,2048]{1,0:T(8,128)(2,1)}, u32[]{:S(2)}, u32[]{:S(2)}) collective-permute-start(bf16[704,2048]{1,0:T(8,128)(2,1)} %bitcast.24.refs_6_.refs_9_), channel_id=1, source_target_pairs={{0,16},{16,0},{1,17},{17,1},{2,18},{18,2},{3,19},{19,3},{4,20},{20... | collective-permute-start | bytes 8650760 | tf_op jit(solution)/shard_map/ppermute | solution.py:1991
  114.6 180.6 %collective-permute-start.1 = (bf16[704,2048]{1,0:T(8,128)(2,1)}, bf16[704,2048]{1,0:T(8,128)(2,1)}, u32[]{:S(2)}, u32[]{:S(2)}) collective-permute-start(bf16[704,2048]{1,0:T(8,128)(2,1)} %bitcast.26.refs_7_.refs_10_), channel_id=1, source_target_pairs={{0,16},{16,0},{1,17},{17,1},{2,18},{18,2},{3,19},{19,3},{4,20},{20... | collective-permute-start | bytes 8650760 | tf_op jit(solution)/shard_map/ppermute | solution.py:1991
  115.6 184.0 %collective-permute-start.2 = (bf16[704,2048]{1,0:T(8,128)(2,1)}, bf16[704,2048]{1,0:T(8,128)(2,1)}, u32[]{:S(2)}, u32[]{:S(2)}) collective-permute-start(bf16[704,2048]{1,0:T(8,128)(2,1)} %bitcast.27.refs_8_.refs_6_), channel_id=1, source_target_pairs={{0,16},{16,0},{1,17},{17,1},{2,18},{18,2},{3,19},{19,3},{4,20},{20... | collective-permute-start | bytes 8650760 | tf_op jit(solution)/shard_map/ppermute | solution.py:1991
  119.4 32.8 %copy-start.8 = (bf16[8,16,8,256]{3,2,0,1:T(8,128)(2,1)}, bf16[8,16,8,256]{3,2,0,1:T(8,128)(2,1)S(1)}, u32[]{:S(2)}) copy-start(bf16[8,16,8,256]{3,2,0,1:T(8,128)(2,1)S(1)} %copy.113) | copy-start | bytes 1572868
  124.7 8.7 %copy-start.15 = (bf16[8,256,384]{2,1,0:T(8,128)(2,1)S(1)}, bf16[8,256,384]{2,1,0:T(8,128)(2,1)}, u32[]{:S(2)}) copy-start(bf16[8,256,384]{2,1,0:T(8,128)(2,1)} %get-tuple-element.63) | copy-start | bytes 4718596
  133.4 8.0 copy-start.16
  133.4 8.0 copy-start.17
  214.1 75.7 %copy-start = (f32[128,2048]{1,0:T(8,128)}, f32[128,2048]{1,0:T(8,128)S(1)}, u32[]{:S(2)}) copy-start(f32[128,2048]{1,0:T(8,128)S(1)} %get-tuple-element.159) | copy-start | bytes 3145732
  217.5 65.9 %copy-start.12 = (bf16[8,528,256]{2,1,0:T(8,128)(2,1)S(1)}, bf16[8,528,256]{2,1,0:T(8,128)(2,1)}, u32[]{:S(2)}) copy-start(bf16[8,528,256]{2,1,0:T(8,128)(2,1)} %get-tuple-element.69) | copy-start | bytes 6488068
  396.3 93.3 %copy-start.5 = (bf16[128,2048]{1,0:T(8,128)(2,1)S(1)}, bf16[128,2048]{1,0:T(8,128)(2,1)}, u32[]{:S(2)}) copy-start(bf16[128,2048]{1,0:T(8,128)(2,1)} %copy-done.4) | copy-start | bytes 1572868
  488.5 4.5 copy-start.1
  492.9 2.6 copy-start.9
  765.3 2.5 copy-start.3
  774.1 27.2 %copy-start.14 = (f32[4,128,256]{2,1,0:T(8,128)S(1)}, f32[4,128,256]{2,1,0:T(8,128)}, u32[]{:S(2)}) copy-start(f32[4,128,256]{2,1,0:T(8,128)} %get-tuple-element.169) | copy-start | bytes 1572868
  799.1 16.6 %slice-start.2 = ((s8[5767168]{0:T(1024)(128)(4,1)}), s8[1572864]{0:T(1024)(128)(4,1)S(1)}, s32[]{:S(2)}) async-start(s8[5767168]{0:T(1024)(128)(4,1)} %bitcast.132), calls=%async_computation.2 | async-start | bytes 3145728
  803.2 4.6 copy-start.13
  807.8 7.9 slice-start.3
  809.1 9.1 %slice-start = ((s8[5767168]{0:T(1024)(128)(4,1)}), s8[4194304]{0:T(1024)(128)(4,1)S(1)}, s32[]{:S(2)}) async-start(s8[5767168]{0:T(1024)(128)(4,1)} %bitcast.129), calls=%async_computation | async-start | bytes 8388608
  815.7 2.5 slice-start.1
  (6 other events, 9.2 us)

commit v5 on v4

--- a/solution.py
+++ b/solution.py
@@ -447,10 +447,21 @@
     )
 
 
-def cross(at, sent, got, send_sem, recv_sem):
+def half_of(array):
+    return jax.ShapeDtypeStruct((array.shape[0] // 2,) + array.shape[1:], array.dtype)
+
+
+def cross(at, sent, got, send_sem, recv_sem, starts=None):
+    starts = starts or (0,) * len(sent)
     return [
-        remote(a, b, send_sem.at[m], recv_sem.at[m], at.device(ox=at.dx))
-        for m, (a, b) in enumerate(zip(sent, got))
+        remote(
+            a.at[pl.ds(start, b.shape[0])],
+            b,
+            send_sem.at[m],
+            recv_sem.at[m],
+            at.device(ox=at.dx),
+        )
+        for m, (a, b, start) in enumerate(zip(sent, got, starts))
     ]
 
 
@@ -503,7 +514,8 @@
             copy.wait_send()
 
 
-def gather_kernel(block, rows, parts, extras, swaps, *refs):
+def gather_kernel(block, rows, parts, extras, starts, *refs):
+    swaps = len(starts)
     refs = list(refs)
 
     def take(count):
@@ -517,7 +529,7 @@
     extra_sems = take(3 if extras else 0)
     at = Place()
     greet(at, extras > 0, swaps > 0)
-    crossing = cross(at, given, taken, *refs) if swaps else []
+    crossing = cross(at, given, taken, *refs, starts) if swaps else []
     piece = rows // parts
     slot_z, slot_f, slot_s = 0, 3, 7
     started, inside = [], []
@@ -616,7 +628,7 @@
             gone(j)
 
 
-def all_rows(x, block, cid, sent=(), given=(), parts=2):
+def all_rows(x, block, cid, sent=(), given=(), starts=(), parts=2):
     rows, width = x.shape
     total = rows * (4 if block else 16)
     rows = rows // 4 if block else rows
@@ -624,7 +636,7 @@
     hbm = pl.BlockSpec(memory_space=pl.ANY)
     outs = [jax.ShapeDtypeStruct((total, width), x.dtype)]
     outs += [jax.ShapeDtypeStruct((8,) + a.shape[1:], a.dtype) for a in sent]
-    outs += [jax.ShapeDtypeStruct(a.shape, a.dtype) for a in given]
+    outs += [half_of(a) for a in given]
     scratch = [
         pltpu.SemaphoreType.DMA,
         pltpu.SemaphoreType.DMA((19 * parts,)),
@@ -639,7 +651,7 @@
     if swaps:
         scratch += [pltpu.SemaphoreType.DMA((swaps,)), pltpu.SemaphoreType.DMA((swaps,))]
     got = pl.pallas_call(
-        functools.partial(gather_kernel, block, rows, parts, extras, swaps),
+        functools.partial(gather_kernel, block, rows, parts, extras, starts),
         out_shape=outs,
         in_specs=[hbm] * len(outs),
         out_specs=[hbm] * len(outs),
@@ -650,7 +662,8 @@
 
 
 class Scatter:
-    def __init__(self, at, acc, got_s, got_f, got_z, send_sem, recv_sem, out_ref):
+    def __init__(self, at, acc, got_s, got_f, got_z, send_sem, recv_sem, out_ref, by_block=False):
+        self.by_block = by_block
         self.at, self.acc, self.got_s, self.got_f, self.got_z = at, acc, got_s, got_f, got_z
         self.send_sem, self.recv_sem, self.out_ref = send_sem, recv_sem, out_ref
         self.rows = acc.shape[1]
@@ -662,6 +675,10 @@
         self.twins = [[], [], [], []]
         self.started, self.in_middle, self.at_end = [], [], []
 
+    def held(self, f, zi, twin=0):
+        at = self.at
+        return zi * 4 + at.e + f * at.dy + twin * at.dc if self.by_block else f * 4 + zi
+
     def push(self, src, dst, slot, device, sends=None, record=None):
         j = slot if sends is None else sends
         remote(src, dst, self.send_sem.at[j], self.recv_sem.at[slot], device).start()
@@ -700,9 +717,9 @@
                 into[span, :] = total
 
     def first(self, zi):
-        k = 4 + zi
-        self.arrive(self.got_s.at[k], 9 + k)
-        self.add(k, (self.got_s, k))
+        k = self.held(1, zi)
+        self.arrive(self.got_s.at[4 + zi], 13 + zi)
+        self.add(k, (self.got_s, 4 + zi))
         self.push(self.acc.at[k], self.got_f.at[zi], 5 + zi, self.f_dev)
 
     def second(self, zi):
@@ -710,43 +727,44 @@
         self.arrive(self.got_s.at[zi], 9 + zi)
         self.arrive(self.got_f.at[zi], 5 + zi)
         others = [(self.got_s, zi), (self.got_f, zi)]
+        k = self.held(0, zi)
         if zi >= 2:
 
             @pl.when(at.middle)
             def _():
                 self.arrive(got_z.at[3 - zi], 3 - zi)
-                self.add(zi, *others, (got_z, 3 - zi))
+                self.add(k, *others, (got_z, 3 - zi))
                 there = 4 if zi == 2 else 3
-                self.push(acc.at[zi], got_z.at[there], there, at.inward(), zi, self.in_middle)
+                self.push(acc.at[k], got_z.at[there], there, at.inward(), zi, self.in_middle)
 
             @pl.when(jnp.logical_not(at.middle))
             def _():
-                self.add(zi, *others)
-                self.push(acc.at[zi], got_z.at[3 - zi], 3 - zi, self.z_dev, zi, self.at_end)
+                self.add(k, *others)
+                self.push(acc.at[k], got_z.at[3 - zi], 3 - zi, self.z_dev, zi, self.at_end)
         elif zi == 1:
 
             @pl.when(at.middle)
             def _():
                 self.arrive(got_z.at[3], 3)
-                self.add(zi, *others, (got_z, 3))
-                self.push(acc.at[zi], got_z.at[4], 4, self.z_dev, 1, self.in_middle)
+                self.add(k, *others, (got_z, 3))
+                self.push(acc.at[k], got_z.at[4], 4, self.z_dev, 1, self.in_middle)
 
             @pl.when(jnp.logical_not(at.middle))
             def _():
-                self.add(zi, *others)
-                self.push(acc.at[zi], got_z.at[2], 2, self.z_dev, 1, self.at_end)
+                self.add(k, *others)
+                self.push(acc.at[k], got_z.at[2], 2, self.z_dev, 1, self.at_end)
         else:
 
             @pl.when(at.middle)
             def _():
                 self.arrive(got_z.at[2], 2)
                 self.arrive(got_z.at[4], 4)
-                self.add(zi, *others, (got_z, 2), (got_z, 4), into=self.out_ref)
+                self.add(k, *others, (got_z, 2), (got_z, 4), into=self.out_ref)
 
             @pl.when(jnp.logical_not(at.middle))
             def _():
                 self.arrive(got_z.at[4], 4)
-                self.add(zi, *others, (got_z, 4), into=self.out_ref)
+                self.add(k, *others, (got_z, 4), into=self.out_ref)
 
     def finish(self):
         for zi in range(4):
@@ -765,9 +783,9 @@
                 self.gone(j)
 
 
-def scatter_buffers(rows, width):
+def scatter_buffers(rows, width, held=8):
     return [
-        pltpu.VMEM((8, rows, width), BF),
+        pltpu.VMEM((held, rows, width), BF),
         pltpu.VMEM((8, rows, width), BF),
         pltpu.VMEM((4, rows, width), BF),
         pltpu.VMEM((5, rows, width), BF),
@@ -776,13 +794,14 @@
     ]
 
 
-def scatter_kernel(rows, swaps, in_ref, *refs):
+def scatter_kernel(rows, starts, in_ref, *refs):
+    swaps = len(starts)
     given, out_ref, taken = refs[:swaps], refs[swaps], refs[swaps + 1 : 2 * swaps + 1]
     buffers, load_sem = refs[2 * swaps + 1 : 2 * swaps + 7], refs[2 * swaps + 7]
     acc = buffers[0]
     at = Place()
     greet(at, False, swaps > 0)
-    crossing = cross(at, given, taken, *refs[2 * swaps + 8 :]) if swaps else []
+    crossing = cross(at, given, taken, *refs[2 * swaps + 8 :], starts) if swaps else []
     total = Scatter(at, *buffers, out_ref)
 
     def rows_of(rank):
@@ -807,15 +826,15 @@
     total.finish()
 
 
-def own_rows(x, cid, given=()):
+def own_rows(x, cid, given=(), starts=()):
     rows, width = x.shape[0] // 16, x.shape[1]
     swaps = len(given)
     hbm = pl.BlockSpec(memory_space=pl.ANY)
     crossing = [pltpu.SemaphoreType.DMA((swaps,))] * 2 if swaps else []
     got = pl.pallas_call(
-        functools.partial(scatter_kernel, rows, swaps),
+        functools.partial(scatter_kernel, rows, starts),
         out_shape=[jax.ShapeDtypeStruct((rows, width), F32)]
-        + [jax.ShapeDtypeStruct(a.shape, a.dtype) for a in given],
+        + [half_of(a) for a in given],
         in_specs=[hbm] * (1 + swaps),
         out_specs=[pl.BlockSpec(memory_space=pltpu.VMEM)] + [hbm] * swaps,
         scratch_shapes=[
@@ -830,6 +849,103 @@
     return got if swaps else got[0]
 
 
+class Gather:
+    def __init__(self, at, x_ref, out_ref, own_sem, send_sem, recv_sem, block=False):
+        self.at, self.x_ref, self.out_ref, self.block = at, x_ref, out_ref, block
+        self.send_sem, self.recv_sem = send_sem, recv_sem
+        self.rows = x_ref.shape[0] // (4 if block else 1)
+        self.f_dev, self.s_dev, self.z_dev = (
+            at.device(oe=at.dy),
+            at.device(oe=at.dc),
+            at.device(zi=1),
+        )
+        self.started, self.inside = [], []
+        rows, self.source = self.rows, x_ref
+        spot = self.where(0, 0)
+        if block:
+            self.source = x_ref.at[pl.ds(pl.multiple_of(at.e * rows, rows), rows)]
+            spot = pl.ds(pl.multiple_of(at.z * 4 * rows, 4 * rows), 4 * rows)
+        self.own = pltpu.make_async_copy(x_ref, out_ref.at[spot], own_sem)
+
+    def where(self, f, zi):
+        rows = self.rows
+        return pl.ds(pl.multiple_of(self.at.shard(f * self.at.dy, zi) * rows, rows), rows)
+
+    def push(self, f, zi, slot, device, sends=None, record=None):
+        src = self.source if f == 0 and zi == 0 else self.out_ref.at[self.where(f, zi)]
+        dst = self.out_ref.at[self.where(f, zi)]
+        j = slot if sends is None else sends
+        remote(src, dst, self.send_sem.at[j], self.recv_sem.at[slot], device).start()
+        (self.started if record is None else record).append(j)
+
+    def spot(self):
+        return self.x_ref.at[pl.ds(0, self.rows)], self.out_ref.at[pl.ds(0, self.rows)]
+
+    def arrive(self, slot):
+        remote(*self.spot(), self.send_sem.at[slot], self.recv_sem.at[slot], self.s_dev).wait_recv()
+
+    def forward(self, f, zi):
+        if f == 0:
+            if zi == 0:
+                self.push(0, 0, 0, self.z_dev)
+            if zi < 2:
+                pl.when(self.at.middle)(
+                    lambda: self.push(0, zi, 1 + zi, self.at.inward(), 15 + zi, self.inside)
+                )
+            else:
+                pl.when(self.at.middle)(
+                    lambda: self.push(0, zi, zi - 1, self.z_dev, 15 + zi, self.inside)
+                )
+        if self.block and zi == 0:
+            return
+        if f == 0:
+            self.push(0, zi, 3 + zi, self.f_dev)
+        self.push(f, zi, 7 + f * 4 + zi, self.s_dev)
+
+    def begin(self):
+        self.forward(0, 0)
+        self.own.start()
+
+    def line(self, zi):
+        self.arrive(zi - 1)
+        self.forward(0, zi)
+
+    def other(self, zi):
+        self.arrive(3 + zi)
+        self.forward(1, zi)
+
+    def twin(self, zi):
+        self.arrive(7 + zi)
+        self.arrive(11 + zi)
+
+    def finish(self, arrived=False):
+        for zi in range(4):
+            if not arrived and not (self.block and zi == 0):
+                self.twin(zi)
+        if not arrived:
+            self.own.wait()
+        for j in self.started:
+            remote(*self.spot(), self.send_sem.at[j], self.recv_sem.at[0], self.s_dev).wait_send()
+
+        @pl.when(self.at.middle)
+        def _():
+            for j in self.inside:
+                remote(
+                    *self.spot(), self.send_sem.at[j], self.recv_sem.at[0], self.s_dev
+                ).wait_send()
+
+
+def columns_loop(width, parts):
+    size = width // parts
+
+    def over(run):
+        @pl.loop(0, parts)
+        def _(n):
+            run(pl.ds(pl.multiple_of(n * size, size), size))
+
+    return over
+
+
 def expert_gather_kernel(experts, *refs):
     refs = list(refs)
 
@@ -839,65 +955,26 @@
         return taken
 
     x_ref, dy_ref, disp, w_router, shared_in, shared_out = take(6)
-    weights = take(6)
+    weights, given = take(7), take(2)
     out_ref, picked, picked_dy, scaled_out, g_out, u_out, gb_out, sa_out, sg_out = take(9)
-    wg, wu, wd, xb, dyb, pk, pdy, sc, gg, uu, gb, sa, sg = take(13)
-    own_sem, send_sem, recv_sem, load_sem, block_sem, store_sem = take(6)
+    taken = take(2)
+    wg, wu, wd, xb, dyd, sb, pk, pdy, sc, gg, uu, hid, gb, sa, sg = take(15)
+    own_sem, send_sem, recv_sem, load_sem, block_sem, store_sem, cross_send, cross_recv = take(8)
     at = Place()
-    greet(at, False)
-    rows = x_ref.shape[0]
-    block = 4 * rows
-    slots = pk.shape[1]
-    groups = 4
-    slot_z, slot_f, slot_s = 0, 3, 7
-    started, inside = [], []
+    greet(at, False, True)
+    gather = Gather(at, x_ref, out_ref, own_sem, send_sem, recv_sem)
+    crossing = cross(at, given, taken, cross_send, cross_recv, (0, taken[0].shape[0]))
+    block = xb.shape[1]
+    slots = pk.shape[0] // 4
+    part = wd.shape[1] // 2
     mine = at.z * 4 + at.e
-
-    def where(f, zi):
-        return pl.ds(pl.multiple_of(at.shard(f * at.dy, zi) * rows, rows), rows)
-
-    def push(src, dst, slot, device, sends=None, record=None):
-        j = slot if sends is None else sends
-        remote(src, out_ref.at[dst], send_sem.at[j], recv_sem.at[slot], device).start()
-        (started if record is None else record).append(j)
-
-    f_dev, s_dev, z_dev = at.device(oe=at.dy), at.device(oe=at.dc), at.device(zi=1)
-
-    def gone(j):
-        remote(x_ref, out_ref.at[pl.ds(0, rows)], send_sem.at[j], recv_sem.at[0], s_dev).wait_send()
-
-    def arrive(slot):
-        remote(
-            x_ref, out_ref.at[pl.ds(0, rows)], send_sem.at[slot], recv_sem.at[slot], s_dev
-        ).wait_recv()
-
-    own = pltpu.make_async_copy(x_ref, out_ref.at[where(0, 0)], own_sem)
-
-    def source(f, zi):
-        return x_ref if f == 0 and zi == 0 else out_ref.at[where(f, zi)]
-
-    def along(zi):
-        src, dst = source(0, zi), where(0, zi)
-        if zi == 0:
-            push(src, dst, slot_z, z_dev)
-        if zi < 2:
-            pl.when(at.middle)(lambda: push(src, dst, slot_z + 1 + zi, at.inward(), 15 + zi, inside))
-        else:
-            pl.when(at.middle)(lambda: push(src, dst, slot_z + zi - 1, z_dev, 15 + zi, inside))
-
-    def forward(f, zi):
-        src, dst = source(f, zi), where(f, zi)
-        if f == 0:
-            along(zi)
-            push(src, dst, slot_f + zi, f_dev)
-        push(src, dst, slot_s + f * 4 + zi, s_dev)
 
     def span(zi, size):
         return pl.ds(pl.multiple_of(at.zs[zi] * size, size), size)
 
     def dy_load(zi):
         return pltpu.make_async_copy(
-            dy_ref.at[span(zi, block)], dyb.at[zi % 2], block_sem.at[2 + zi % 2]
+            dy_ref.at[span(zi, block)], xb.at[zi % 2], block_sem.at[2 + zi % 2]
         )
 
     def x_load(zi):
@@ -907,21 +984,10 @@
 
     def stores(zi):
         b = zi % 2
-        pairs = [
-            (pk.at[b], picked.at[span(zi, slots)]),
-            (pdy.at[b], picked_dy.at[span(zi, slots)]),
-            (gb.at[b], gb_out.at[span(zi, slots)]),
-            (sa.at[b], sa_out.at[span(zi, block)]),
-            (sg.at[b], sg_out.at[span(zi, block)]),
-        ]
-        for h in range(2):
-            pairs += [
-                (sc.at[b, h], scaled_out.at[h, span(zi, slots)]),
-                (gg.at[b, h], g_out.at[h, span(zi, slots)]),
-                (uu.at[b, h], u_out.at[h, span(zi, slots)]),
-            ]
+        pairs = [(sa.at[b], sa_out.at[span(zi, block)]), (sg.at[b], sg_out.at[span(zi, block)])]
         return [
-            pltpu.make_async_copy(src, dst, store_sem.at[b, j]) for j, (src, dst) in enumerate(pairs)
+            pltpu.make_async_copy(src, dst, store_sem.at[b * 2 + j])
+            for j, (src, dst) in enumerate(pairs)
         ]
 
     def parts_of(gate, up):
@@ -929,140 +995,183 @@
         act = gate * s
         return act * up, s * (1.0 + gate * (1.0 - s)) * up, act
 
+    def ahead(zi):
+        b = zi % 2
+        some = span(zi, slots)
+        dy_load(zi).wait()
+        pdy[some, :] = product(disp[at.zs[zi]], xb[b]).astype(BF)
+        sb[span(zi, block), :] = transposed_right(xb[b], shared_out[...])
+        if zi < 2:
+            dy_load(zi + 2).start()
+        dyd[some, :] = transposed_right(pdy[some, :], wd[0])
+
     def work(zi):
         b = zi % 2
-        dy_load(zi).wait()
+        some = span(zi, slots)
         x_load(zi).wait()
         if zi >= 2:
             for copy in stores(zi - 2):
                 copy.wait()
-
-        @pl.loop(0, groups)
-        def _(i):
-            hot = disp[at.zs[zi] * groups + i]
-            source_rows = pl.ds(pl.multiple_of(i * rows, rows), rows)
-            into = pl.ds(pl.multiple_of(i * (slots // groups), slots // groups), slots // groups)
-            pk[b, into, :] = product(hot, xb[b, source_rows, :]).astype(BF)
-            pdy[b, into, :] = product(hot, dyb[b, source_rows, :]).astype(BF)
-
-        logits = transposed_right(pk[b], w_router[...])
+        pk[some, :] = product(disp[at.zs[zi]], xb[b]).astype(BF)
+        logits = transposed_right(pk[some, :], w_router[...])
         lane = lax.broadcasted_iota(jnp.int32, logits.shape, 1)
         logits = jnp.where(lane < experts, logits, MASKED)
         powers = jnp.exp(logits - jnp.max(logits, axis=1, keepdims=True))
         own_power = jnp.sum(jnp.where(lane == mine, powers, 0.0), axis=1, keepdims=True)
         gate_of = own_power / jnp.sum(powers, axis=1, keepdims=True)
-        gb[b] = jnp.zeros(gb.shape[1:], F32)
-
-        @pl.loop(0, 2)
-        def _(h):
+        for h in range(2):
             hidden, by_gate, by_up = parts_of(
-                transposed_right(pk[b], wg[h]), transposed_right(pk[b], wu[h])
+                transposed_right(pk[some, :], wg[h]), transposed_right(pk[some, :], wu[h])
             )
-            dy_down = transposed_right(pdy[b], wd[h])
-            act_back = gate_of * dy_down
-            gg[b, h] = (act_back * by_gate).astype(BF)
-            uu[b, h] = (act_back * by_up).astype(BF)
-            sc[b, h] = (hidden * gate_of).astype(BF)
-            gb[b] += jnp.broadcast_to(
-                jnp.sum(hidden * dy_down, axis=1, keepdims=True), gb.shape[1:]
-            )
-
-        @pl.loop(0, groups)
-        def _(i):
-            token_rows = pl.ds(pl.multiple_of(i * rows, rows), rows)
-            both = transposed_right(xb[b, token_rows, :], shared_in[...])
-            wide = both.shape[1] // 2
-            hidden, by_gate, by_up = parts_of(both[:, :wide], both[:, wide:])
-            back = transposed_right(dyb[b, token_rows, :], shared_out[...])
-            sa[b, token_rows, :] = hidden.astype(BF)
-            sg[b, token_rows, :wide] = (back * by_gate).astype(BF)
-            sg[b, token_rows, wide:] = (back * by_up).astype(BF)
-
+            sc[h, some, :] = (hidden * gate_of).astype(BF)
+            if h == 0:
+                dy_down = dyd[some, :]
+                act_back = gate_of * dy_down
+                gg[0, some, :] = (act_back * by_gate).astype(BF)
+                uu[0, some, :] = (act_back * by_up).astype(BF)
+                gb[some, :] = jnp.broadcast_to(
+                    jnp.sum(hidden * dy_down, axis=1, keepdims=True), (slots, gb.shape[1])
+                )
+            else:
+                hid[some, :] = hidden.astype(BF)
+                gg[1, some, :] = (gate_of * by_gate).astype(BF)
+                uu[1, some, :] = (gate_of * by_up).astype(BF)
+        both = transposed_right(xb[b], shared_in[...])
+        wide = both.shape[1] // 2
+        hidden, by_gate, by_up = parts_of(both[:, :wide], both[:, wide:])
+        back = sb[span(zi, block), :]
+        sa[b] = hidden.astype(BF)
+        sg[b, :, :wide] = (back * by_gate).astype(BF)
+        sg[b, :, wide:] = (back * by_up).astype(BF)
         for copy in stores(zi):
             copy.start()
 
-    forward(0, 0)
-    own.start()
-    loads = []
-    for m, (ref, half) in enumerate([(wg, 0), (wu, 0), (wd, 0), (wg, 1), (wu, 1), (wd, 1)]):
-        loads.append(pltpu.make_async_copy(weights[m], ref.at[half], load_sem.at[m]))
-        loads[-1].start()
+    def other_half(zi):
+        some = span(zi, slots)
+        dy_down = transposed_right(pdy[some, :], wd[1])
+        gg[1, some, :] = (dy_down * gg[1, some, :].astype(F32)).astype(BF)
+        uu[1, some, :] = (dy_down * uu[1, some, :].astype(F32)).astype(BF)
+        gb[some, :] += jnp.broadcast_to(
+            jnp.sum(hid[some, :].astype(F32) * dy_down, axis=1, keepdims=True), (slots, gb.shape[1])
+        )
+
+    gather.begin()
+    places = [
+        wg.at[0],
+        wu.at[0],
+        wd.at[0],
+        wg.at[1, pl.ds(0, part)],
+        wg.at[1, pl.ds(part, part)],
+        wu.at[1, pl.ds(0, part)],
+        wu.at[1, pl.ds(part, part)],
+        wd.at[1, pl.ds(0, part)],
+        wd.at[1, pl.ds(part, part)],
+    ]
+    loads = [
+        pltpu.make_async_copy(a, b, load_sem.at[j]) for j, (a, b) in enumerate(zip(weights + taken, places))
+    ]
     dy_load(0).start()
+    dy_load(1).start()
+    for j in (2, 0, 1, 3, 4, 5, 6):
+        loads[j].start()
+    for copy in crossing:
+        copy.start()
+    loads[2].wait()
+    for zi in range(3):
+        ahead(zi)
     for zi in range(4):
-        arrive(slot_f + zi)
-        forward(1, zi)
+        gather.other(zi)
         if zi < 3:
-            arrive(slot_z + zi)
-            forward(0, zi + 1)
-            dy_load(zi + 1).start()
-        for f in range(2):
-            arrive(slot_s + f * 4 + zi)
+            gather.line(zi + 1)
         if zi == 0:
-            own.wait()
-            for copy in loads:
-                copy.wait()
+            ahead(3)
+        gather.twin(zi)
+        if zi == 0:
+            gather.own.wait()
         x_load(zi).start()
+        if zi == 0:
+            for j in (0, 1, 3, 4, 5, 6):
+                loads[j].wait()
         work(zi)
+    results = [(pk, picked), (pdy, picked_dy), (sc, scaled_out), (gg, g_out), (uu, u_out), (gb, gb_out)]
+    results = [
+        pltpu.make_async_copy(a, b, store_sem.at[4 + j]) for j, (a, b) in enumerate(results)
+    ]
+    for copy in results[:3]:
+        copy.start()
+    for m in range(2):
+        crossing[m].wait_recv()
+        loads[7 + m].start()
+    for m in range(2):
+        loads[7 + m].wait()
+    for zi in range(4):
+        other_half(zi)
+    for copy in results[3:]:
+        copy.start()
+    for copy in results:
+        copy.wait()
     for zi in (2, 3):
         for copy in stores(zi):
             copy.wait()
-    for j in started:
-        gone(j)
-
-    @pl.when(at.middle)
-    def _():
-        for j in inside:
-            gone(j)
-
-
-def expert_rows(x, dy_all, dispatch, w_router, experts, shared_in, shared_out, weights, cid):
+    for copy in crossing:
+        copy.wait_send()
+    gather.finish(True)
+
+
+def expert_rows(x, dy_all, dispatch, w_router, experts, shared_in, shared_out, weights, given, cid):
     rows, width = x.shape
     total, block = 16 * rows, 4 * rows
     slots = 4 * dispatch.shape[1]
     hidden = weights[0].shape[0]
     wide = shared_out.shape[0]
+    halves = [half_of(a) for a in given]
     hbm, vmem = pl.BlockSpec(memory_space=pl.ANY), pl.BlockSpec(memory_space=pltpu.VMEM)
-    shape = jax.ShapeDtypeStruct
+    shape, sems = jax.ShapeDtypeStruct, lambda n: pltpu.SemaphoreType.DMA((n,))
     return pl.pallas_call(
         functools.partial(expert_gather_kernel, experts),
         out_shape=[
             shape((total, width), BF),
-            shape((4 * slots, width), BF),
-            shape((4 * slots, width), BF),
-            shape((2, 4 * slots, hidden), BF),
-            shape((2, 4 * slots, hidden), BF),
-            shape((2, 4 * slots, hidden), BF),
-            shape((4 * slots, 128), F32),
+            shape((slots, width), BF),
+            shape((slots, width), BF),
+            shape((2, slots, hidden), BF),
+            shape((2, slots, hidden), BF),
+            shape((2, slots, hidden), BF),
+            shape((slots, 128), F32),
             shape((total, wide), BF),
             shape((total, 2 * wide), BF),
+            *halves,
         ],
-        in_specs=[hbm, hbm, vmem, vmem, vmem, vmem] + [hbm] * 6,
-        out_specs=[hbm] * 9,
+        in_specs=[hbm, hbm, vmem, vmem, vmem, vmem] + [hbm] * 9,
+        out_specs=[hbm] * 11,
         scratch_shapes=[
             pltpu.VMEM((2, hidden, width), BF),
             pltpu.VMEM((2, hidden, width), BF),
             pltpu.VMEM((2, hidden, width), BF),
             pltpu.VMEM((2, block, width), BF),
-            pltpu.VMEM((2, block, width), BF),
-            pltpu.VMEM((2, slots, width), BF),
-            pltpu.VMEM((2, slots, width), BF),
-            pltpu.VMEM((2, 2, slots, hidden), BF),
-            pltpu.VMEM((2, 2, slots, hidden), BF),
-            pltpu.VMEM((2, 2, slots, hidden), BF),
-            pltpu.VMEM((2, slots, 128), F32),
+            pltpu.VMEM((slots, hidden), F32),
+            pltpu.VMEM((total, wide), F32),
+            pltpu.VMEM((slots, width), BF),
+            pltpu.VMEM((slots, width), BF),
+            pltpu.VMEM((2, slots, hidden), BF),
+            pltpu.VMEM((2, slots, hidden), BF),
+            pltpu.VMEM((2, slots, hidden), BF),
+            pltpu.VMEM((slots, hidden), BF),
+            pltpu.VMEM((slots, 128), F32),
             pltpu.VMEM((2, block, wide), BF),
             pltpu.VMEM((2, block, 2 * wide), BF),
             pltpu.SemaphoreType.DMA,
-            pltpu.SemaphoreType.DMA((19,)),
-            pltpu.SemaphoreType.DMA((15,)),
-            pltpu.SemaphoreType.DMA((6,)),
-            pltpu.SemaphoreType.DMA((4,)),
-            pltpu.SemaphoreType.DMA((2, 11)),
+            sems(19),
+            sems(15),
+            sems(9),
+            sems(4),
+            sems(10),
+            sems(2),
+            sems(2),
         ],
         compiler_params=pltpu.CompilerParams(
-            collective_id=cid, has_side_effects=True, vmem_limit_bytes=60 * 1024 * 1024
+            collective_id=cid, has_side_effects=True, vmem_limit_bytes=62 * 1024 * 1024
         ),
-    )(x, dy_all, dispatch, w_router, shared_in, shared_out, *weights)
+    )(x, dy_all, dispatch, w_router, shared_in, shared_out, *weights, *given)
 
 
 def expert_scatter_kernel(*refs):
@@ -1074,25 +1183,29 @@
         return taken
 
     disp, gate_back, shared_in, g_ref, u_ref, sg_ref, picked_ref, dy_ref, scaled_ref = take(9)
-    weights = take(4)
+    weights = take(6)
     out_ref, taken, *grads = take(7)
     wg, wu, gs, us, sg, picked, picked_dy, scaled, ib, grad, turned = take(11)
     acc, got_s, got_f, got_z, send_sem, recv_sem = take(6)
-    out_s, load_sem, store_sem, cross_send, cross_recv = take(5)
+    load_sem, store_sem, cross_send, cross_recv = take(4)
     at = Place()
     greet(at, False, True)
     rows, full = acc.shape[1:]
     width = shared_in.shape[1]
     slots = ib.shape[0]
-    capacity = slots // 4
+    block = 4 * rows
+    over = columns_loop(width, 4)
     mine = at.z * 4 + at.e
-    total = Scatter(at, acc, got_s, got_f, got_z, send_sem, recv_sem, out_ref)
-
+    total = Scatter(at, acc, got_s, got_f, got_z, send_sem, recv_sem, out_ref, True)
+
+    part = wg.shape[1] // 2
     pairs = [
         (weights[0], wg.at[0]),
         (weights[1], wu.at[0]),
-        (weights[2], wg.at[1]),
-        (weights[3], wu.at[1]),
+        (weights[2], wg.at[1, pl.ds(0, part)]),
+        (weights[3], wg.at[1, pl.ds(part, part)]),
+        (weights[4], wu.at[1, pl.ds(0, part)]),
+        (weights[5], wu.at[1, pl.ds(part, part)]),
         (g_ref, gs),
         (u_ref, us),
         (sg_ref, sg),
@@ -1108,36 +1221,29 @@
         place = at.zs[zi]
         some = pl.ds(pl.multiple_of(place * slots, slots), slots)
 
-        @pl.loop(0, 4)
-        def _(n):
-            columns = pl.ds(pl.multiple_of(n * (width // 4), width // 4), width // 4)
+        hot = disp[place]
+        tokens = pl.ds(pl.multiple_of(place * block, block), block)
+
+        @over
+        def _(columns):
             terms = product(gs[0, some, :], wg[0, :, columns])
             terms += product(us[0, some, :], wu[0, :, columns])
             terms += product(gs[1, some, :], wg[1, :, columns])
             terms += product(us[1, some, :], wu[1, :, columns])
             ib[:, columns] = terms.astype(BF)
 
-        for twin in range(2):
-            for f in range(2):
-                e = at.e + f * at.dy + twin * at.dc
-                hot = disp[place * 4 + e]
-                mine_slots = pl.ds(pl.multiple_of(e * capacity, capacity), capacity)
-                tokens = pl.ds(pl.multiple_of((place * 4 + e) * rows, rows), rows)
-                into, k = (out_s, f * 2 + zi % 2) if twin else (acc, f * 4 + zi)
-
-                @pl.loop(0, 2)
-                def _(n):
-                    columns = pl.ds(pl.multiple_of(n * (width // 2), width // 2), width // 2)
-                    terms = transposed_left(hot, ib[mine_slots, columns])
-                    terms += product(sg[tokens, :], shared_in[:, columns])
-                    into[k, :, columns] = terms.astype(BF)
-
-                from_gates = gate_back[
-                    pl.ds(pl.multiple_of(place * slots + e * capacity, capacity), capacity), :
-                ]
-                lane = lax.broadcasted_iota(jnp.int32, from_gates.shape, 1)
-                from_gates = jnp.where(lane == mine, from_gates, 0.0).astype(BF)
-                into[k, :, width:] = transposed_left(hot, from_gates).astype(BF)
+        @over
+        def _(columns):
+            terms = transposed_left(hot, ib[:, columns])
+            terms += product(sg[tokens, :], shared_in[:, columns])
+            for e in range(4):
+                acc[zi * 4 + e, :, columns] = terms[e * rows : (e + 1) * rows].astype(BF)
+
+        from_gates = gate_back[some, :]
+        lane = lax.broadcasted_iota(jnp.int32, from_gates.shape, 1)
+        terms = transposed_left(hot, jnp.where(lane == mine, from_gates, 0.0).astype(BF))
+        for e in range(4):
+            acc[zi * 4 + e, :, width:] = terms[e * rows : (e + 1) * rows].astype(BF)
 
     def gradient(m):
         step = 256
@@ -1147,28 +1253,30 @@
         @pl.loop(0, width // step)
         def _(n):
             columns = pl.ds(pl.multiple_of(n * step, step), step)
-            grad[m, :, columns] = product(turned[...], right[:, columns]).astype(BF)
-
-    part = grad.shape[1] // 2
+            grad[min(m, 1), :, columns] = product(turned[...], right[:, columns]).astype(BF)
+
     crossing = cross(at, [grad.at[0, pl.ds(0, part)]], [taken], cross_send, cross_recv)[0]
     stores = [
-        pltpu.make_async_copy(grad.at[j // 2, pl.ds(j % 2 * part, part)], grads[j - 1], store_sem.at[j])
+        pltpu.make_async_copy(
+            grad.at[min(j // 2, 1), pl.ds(j % 2 * part, part)], grads[j - 1], store_sem.at[j]
+        )
         for j in range(1, 6)
     ]
-    for copy in loads[:7]:
+    for copy in loads[:9]:
         copy.wait()
     for zi in (3, 2, 1, 0):
-        if zi < 2:
-            total.twin_gone(zi + 2)
         work(zi)
         for f in range(2):
-            total.to_twin(out_s.at[f * 2 + zi % 2], f, zi)
+            total.to_twin(acc.at[total.held(f, zi, 1)], f, zi)
         total.first(zi)
         if zi == 1:
             total.second(3)
-    for copy in loads[7:]:
+    for copy in loads[9:]:
         copy.wait()
     for m, zi in ((0, 2), (1, 1), (2, 0)):
+        if m == 2:
+            stores[1].wait()
+            stores[2].wait()
         gradient(m)
         if m == 0:
             crossing.start()
@@ -1176,8 +1284,8 @@
             if j > 0:
                 stores[j - 1].start()
         total.second(zi)
-    for copy in stores:
-        copy.wait()
+    for j in (0, 3, 4):
+        stores[j].wait()
     crossing.wait()
     total.finish()
 
@@ -1196,7 +1304,7 @@
             shape((rows, full), F32),
             *[shape((hidden // 2, width), BF)] * 6,
         ],
-        in_specs=[vmem] * 3 + [hbm] * 10,
+        in_specs=[vmem] * 3 + [hbm] * 12,
         out_specs=[vmem] + [hbm] * 6,
         scratch_shapes=[
             pltpu.VMEM((2, hidden, width), BF),
@@ -1208,11 +1316,10 @@
             pltpu.VMEM((slots, width), BF),
             pltpu.VMEM((slots, hidden), BF),
             pltpu.VMEM((slots // 4, width), BF),
-            pltpu.VMEM((3, hidden, width), BF),
+            pltpu.VMEM((2, hidden, width), BF),
             pltpu.VMEM((hidden, slots), BF),
-            *scatter_buffers(rows, full),
-            pltpu.VMEM((4, rows, full), BF),
-            pltpu.SemaphoreType.DMA((10,)),
+            *scatter_buffers(rows, full, 16),
+            pltpu.SemaphoreType.DMA((12,)),
             pltpu.SemaphoreType.DMA((6,)),
             pltpu.SemaphoreType.DMA((1,)),
             pltpu.SemaphoreType.DMA((1,)),
@@ -1233,7 +1340,7 @@
 
     w_out, w_qkv, tables, q_ref, k_ref, v_ref, lse_ref, heads_out = take(8)
     in_ref, back_ref, normed_ref, *given = take(5)
-    out_ref, normed_back, qkv_grad, out_grad, *taken = take(6)
+    out_ref, normed_back, home_out, *taken = take(5)
     rows_in, do, dk, dv, qkv, out_sum, qkv_sum, staged = take(8)
     buffers = take(6)
     first_sem, in_sem, store_sem, cross_send, cross_recv = take(5)
@@ -1368,8 +1475,11 @@
         normed_rows(j)
     for j in range(4):
         qkv_rows(j)
-    qkv_grad[...] = qkv_sum[...].astype(BF)
-    out_grad[...] = out_sum[...].astype(BF)
+    size = home_out.shape[2]
+    for j in range(8):
+        columns = slice(j * size, (j + 1) * size)
+        home_out[j, : 3 * HDIM, :] = qkv_sum[:, columns].astype(BF)
+        home_out[j, 3 * HDIM :, :] = out_sum[:, columns].astype(BF)
     firsts[0].wait()
     total.second(0)
     for j in (6, 7):
@@ -1391,12 +1501,11 @@
         out_shape=[
             shape((rows, width), F32),
             shape((length, width), BF),
-            shape((3 * HDIM, width), BF),
-            shape((HDIM, width), BF),
+            shape((8, 4 * HDIM, width // 8), BF),
             *[shape(a.shape, BF) for a in given],
         ],
         in_specs=[vmem] * 8 + [hbm] * 5,
-        out_specs=[vmem, hbm, vmem, vmem, hbm, hbm],
+        out_specs=[vmem, hbm, vmem, hbm, hbm],
         scratch_shapes=[
             pltpu.VMEM((2, length // 4, width), BF),
             pltpu.VMEM((length, HDIM), BF),
@@ -1419,89 +1528,6 @@
     )(w_out, w_qkv, tables, q, k, v, lse, heads_out, mixed_part, attn_back, normed, *given)
 
 
-class Gather:
-    def __init__(self, at, x_ref, out_ref, own_sem, send_sem, recv_sem):
-        self.at, self.x_ref, self.out_ref = at, x_ref, out_ref
-        self.send_sem, self.recv_sem = send_sem, recv_sem
-        self.rows = x_ref.shape[0]
-        self.f_dev, self.s_dev, self.z_dev = (
-            at.device(oe=at.dy),
-            at.device(oe=at.dc),
-            at.device(zi=1),
-        )
-        self.started, self.inside = [], []
-        self.own = pltpu.make_async_copy(x_ref, out_ref.at[self.where(0, 0)], own_sem)
-
-    def where(self, f, zi):
-        rows = self.rows
-        return pl.ds(pl.multiple_of(self.at.shard(f * self.at.dy, zi) * rows, rows), rows)
-
-    def push(self, f, zi, slot, device, sends=None, record=None):
-        src = self.x_ref if f == 0 and zi == 0 else self.out_ref.at[self.where(f, zi)]
-        dst = self.out_ref.at[self.where(f, zi)]
-        j = slot if sends is None else sends
-        remote(src, dst, self.send_sem.at[j], self.recv_sem.at[slot], device).start()
-        (self.started if record is None else record).append(j)
-
-    def spot(self):
-        return self.x_ref, self.out_ref.at[pl.ds(0, self.rows)]
-
-    def arrive(self, slot):
-        remote(*self.spot(), self.send_sem.at[slot], self.recv_sem.at[slot], self.s_dev).wait_recv()
-
-    def forward(self, f, zi):
-        if f == 0:
-            if zi == 0:
-                self.push(0, 0, 0, self.z_dev)
-            if zi < 2:
-                pl.when(self.at.middle)(
-                    lambda: self.push(0, zi, 1 + zi, self.at.inward(), 15 + zi, self.inside)
-                )
-            else:
-                pl.when(self.at.middle)(
-                    lambda: self.push(0, zi, zi - 1, self.z_dev, 15 + zi, self.inside)
-                )
-            self.push(0, zi, 3 + zi, self.f_dev)
-        self.push(f, zi, 7 + f * 4 + zi, self.s_dev)
-
-    def begin(self):
-        self.forward(0, 0)
-        self.own.start()
-
-    def line(self, zi):
-        self.arrive(zi - 1)
-        self.forward(0, zi)
-
-    def other(self, zi):
-        self.arrive(3 + zi)
-        self.forward(1, zi)
-
-    def finish(self):
-        for k in range(8):
-            self.arrive(7 + k)
-        self.own.wait()
-        for j in self.started:
-            remote(*self.spot(), self.send_sem.at[j], self.recv_sem.at[0], self.s_dev).wait_send()
-
-        @pl.when(self.at.middle)
-        def _():
-            for j in self.inside:
-                remote(
-                    *self.spot(), self.send_sem.at[j], self.recv_sem.at[0], self.s_dev
-                ).wait_send()
-
-
-def columns_loop(width, parts):
-    size = width // parts
-
-    def over(run):
-        @pl.loop(0, parts)
-        def _(n):
-            run(pl.ds(pl.multiple_of(n * size, size), size))
-
-    return over
-
-
 def gather_back_kernel(*refs):
     refs = list(refs)
 
@@ -1511,19 +1537,19 @@
         return taken
 
     x_ref, disp, shared_out = take(3)
-    scaled_ref, act_ref, sg_ref, wd_a, wd_b, mix_ref, dy_ref, *given = take(9)
+    scaled_ref, act_ref, sg_ref, wd_a, wd_0, wd_1, mix_ref, dy_ref, *given = take(10)
     out_ref, mixed_part, units_grad, *taken = take(5)
-    scaled, acts, sg, wd, eb, rows_in, staged, unit_sum = take(8)
-    own_sem, send_sem, recv_sem, cross_send, cross_recv, load_sem, in_sem, store_sem = take(8)
+    scaled, acts, sg, wd, eb, mixes, dys, staged, turned, turned_acts = take(10)
+    own_sem, send_sem, recv_sem, cross_send, cross_recv, load_sem, store_sem = take(7)
     at = Place()
     greet(at, False, True)
     gather = Gather(at, x_ref, out_ref, own_sem, send_sem, recv_sem)
     crossing = cross(at, given, taken, cross_send, cross_recv)
     rows, width = x_ref.shape
     slots = eb.shape[0]
-    capacity = slots // 4
     block = 4 * rows
     units = acts.shape[1]
+    cut = units_grad.shape[1] // 3
     over = columns_loop(width, 4)
 
     gather.begin()
@@ -1533,18 +1559,15 @@
         (scaled_ref, scaled),
         (act_ref, acts),
         (wd_a, wd.at[0]),
-        (wd_b, wd.at[1]),
+        (wd_0, wd.at[1, pl.ds(0, wd_0.shape[0])]),
+        (wd_1, wd.at[1, pl.ds(wd_0.shape[0], wd_0.shape[0])]),
         (sg_ref, sg),
+        (mix_ref, mixes),
+        (dy_ref, dys),
     ]
     loads = [pltpu.make_async_copy(a, b, load_sem.at[j]) for j, (a, b) in enumerate(pairs)]
     for copy in loads:
         copy.start()
-
-    def rows_load(j):
-        ref = mix_ref if j < 4 else dy_ref
-        return pltpu.make_async_copy(
-            ref.at[pl.ds(j % 4 * block, block)], rows_in.at[j % 2], in_sem.at[j % 2]
-        )
 
     def mixed_store(j):
         return pltpu.make_async_copy(
@@ -1562,43 +1585,41 @@
 
         if j >= 2:
             mixed_store(j - 2).wait()
-        for i in range(4):
-            hot = disp[j * 4 + i]
-
-            @over
-            def _(columns):
-                terms = transposed_left(hot, eb[pl.ds(i * capacity, capacity), columns])
-                terms += product(acts[pl.ds((j * 4 + i) * rows, rows), :], shared_out[:, columns])
-                staged[j % 2, pl.ds(i * rows, rows), columns] = terms.astype(BF)
-
-        mixed_store(j).start()
-
-    def units_of(j):
-        rows_load(j).wait()
-        here = pl.ds(j % 4 * block, block)
-        turned = (sg[here, :] if j < 4 else acts[here, :]).T
-        into = pl.ds(0, 2 * units) if j < 4 else pl.ds(2 * units, units)
+        tokens = pl.ds(j * block, block)
 
         @over
         def _(columns):
-            terms = product(turned, rows_in[j % 2, :, columns])
-            unit_sum[into, columns] = terms if j % 4 == 0 else unit_sum[into, columns] + terms
-
-        if j < 6:
-            rows_load(j + 2).start()
-
-    rows_load(0).start()
-    rows_load(1).start()
-    for copy in loads:
+            terms = transposed_left(disp[j], eb[:, columns])
+            terms += product(acts[tokens, :], shared_out[:, columns])
+            staged[j % 2, :, columns] = terms.astype(BF)
+
+        mixed_store(j).start()
+
+    def units_of(first, count):
+        size = units_grad.shape[2]
+
+        @pl.loop(first, first + count)
+        def _(n):
+            columns = pl.ds(pl.multiple_of(n * size, size), size)
+            terms = product(turned[...], mixes[:, columns]).astype(BF)
+            units_grad[n, 0:cut, :] = terms[:cut]
+            units_grad[n, cut : 2 * cut, :] = terms[units : units + cut]
+            terms = product(turned_acts[...], dys[:, columns]).astype(BF)
+            units_grad[n, 2 * cut :, :] = terms[:cut]
+
+    for copy in loads[:5]:
         copy.wait()
     for zi in range(4):
         if zi > 0:
             gather.line(zi)
         mixed_rows_of(zi)
+        if zi == 0:
+            for copy in loads[5:]:
+                copy.wait()
+            turned[...] = sg[...].T
+            turned_acts[...] = acts[...].T
         gather.other(zi)
-        units_of(2 * zi)
-        units_of(2 * zi + 1)
-    units_grad[...] = unit_sum[...].astype(BF)
+        units_of(2 * zi, 2)
     for j in (2, 3):
         mixed_store(j).wait()
     for copy in crossing:
@@ -1606,7 +1627,7 @@
     gather.finish()
 
 
-def gather_back(x, given, dispatch, shared_out, scaled, acts, sg, wd_a, wd_b, mix_all, dy_all, cid):
+def gather_back(x, given, dispatch, shared_out, scaled, acts, sg, wd, mix_all, dy_all, cut, cid):
     rows, width = x.shape
     length, units = acts.shape
     slots, hidden = scaled.shape[1:]
@@ -1617,10 +1638,10 @@
         out_shape=[
             shape((length, width), BF),
             shape((length, width), BF),
-            shape((3 * units, width), BF),
+            shape((8, 3 * cut, width // 8), BF),
             *[shape(a.shape, BF) for a in given],
         ],
-        in_specs=[hbm, vmem, vmem] + [hbm] * 9,
+        in_specs=[hbm, vmem, vmem] + [hbm] * 10,
         out_specs=[hbm, hbm, vmem, hbm, hbm],
         scratch_shapes=[
             pltpu.VMEM((2, slots, hidden), BF),
@@ -1628,88 +1649,94 @@
             pltpu.VMEM(sg.shape, BF),
             pltpu.VMEM((2, hidden, width), BF),
             pltpu.VMEM((slots // 4, width), BF),
+            pltpu.VMEM((length, width), BF),
+            pltpu.VMEM((length, width), BF),
             pltpu.VMEM((2, 4 * rows, width), BF),
-            pltpu.VMEM((2, 4 * rows, width), BF),
-            pltpu.VMEM((3 * units, width), F32),
+            pltpu.VMEM((2 * units, length), BF),
+            pltpu.VMEM((units, length), BF),
             pltpu.SemaphoreType.DMA,
             pltpu.SemaphoreType.DMA((19,)),
             pltpu.SemaphoreType.DMA((15,)),
             pltpu.SemaphoreType.DMA((2,)),
             pltpu.SemaphoreType.DMA((2,)),
-            pltpu.SemaphoreType.DMA((5,)),
-            pltpu.SemaphoreType.DMA((2,)),
+            pltpu.SemaphoreType.DMA((8,)),
             pltpu.SemaphoreType.DMA((2,)),
         ],
         compiler_params=pltpu.CompilerParams(
             collective_id=cid, has_side_effects=True, vmem_limit_bytes=60 * 1024 * 1024
         ),
-    )(x, dispatch, shared_out, scaled, acts, sg, wd_a, wd_b, mix_all, dy_all, *given)
+    )(x, dispatch, shared_out, scaled, acts, sg, *wd, mix_all, dy_all, *given)
 
 
 class Home:
-    def __init__(self, at, home, home_out, mine, got, load_sem, x_send, x_recv, z_send, z_recv):
-        self.at, self.home, self.home_out, self.mine, self.got = at, home, home_out, mine, got
+    def __init__(self, at, arrays, outs, mine, got, load_sem, x_send, x_recv, z_send, z_recv):
+        self.at, self.outs, self.mine, self.got = at, outs, mine, got
         self.z_send, self.z_recv = z_send, z_recv
         there = (1 - at.x) * 4
-        self.loads, self.crossing = [], []
-        for k in range(4):
-            spot = at.zs[k]
-            self.loads.append(
-                pltpu.make_async_copy(home.at[at.x * 4 + spot], mine.at[spot], load_sem.at[k])
+        self.loads, self.crossing, self.keep = {}, {}, []
+        self.count = len(arrays)
+        for m, array in enumerate(arrays):
+            for k in range(4):
+                spot, j = at.zs[k], m * 4 + k
+                self.loads[m, k] = pltpu.make_async_copy(
+                    array.at[at.x * 4 + spot], mine[m].at[spot], load_sem.at[m * 5 + k]
+                )
+                self.crossing[m, k] = remote(
+                    array.at[there + spot],
+                    got[m].at[spot],
+                    x_send.at[j],
+                    x_recv.at[j],
+                    at.device(ox=at.dx),
+                )
+            self.keep.append(
+                pltpu.make_async_copy(mine[m].at[at.z], outs[m].at[at.z], load_sem.at[m * 5 + 4])
             )
-            self.crossing.append(
-                remote(
-                    home.at[there + spot], got.at[spot], x_send.at[k], x_recv.at[k], at.device(ox=at.dx)
-                )
-            )
-        self.keep = pltpu.make_async_copy(mine.at[at.z], home_out.at[at.z], load_sem.at[4])
 
     def start(self):
         for k in (3, 2, 1, 0):
-            self.loads[k].start()
-            self.crossing[k].start()
+            for m in range(self.count):
+                self.loads[m, k].start()
+                self.crossing[m, k].start()
 
     def line(self, k):
-        at = self.at
-        spot = at.zs[k]
-        self.loads[k].wait()
-        self.crossing[k].wait_recv()
-        mine, got = self.mine, self.got
-
-        @pl.loop(0, mine.shape[1] // 16)
-        def _(i):
-            span = pl.ds(pl.multiple_of(i * 16, 16), 16)
-            both = mine[spot, span, :].astype(F32) + got[spot, span, :].astype(F32)
-            mine[spot, span, :] = both.astype(BF)
-
-        if k == 0:
-            self.keep.start()
-        else:
-            self.copy(k).start()
-
-    def copy(self, k):
+        spot = self.at.zs[k]
+        for m in range(self.count):
+            mine, got = self.mine[m], self.got[m]
+            self.loads[m, k].wait()
+            self.crossing[m, k].wait_recv()
+
+            @pl.loop(0, mine.shape[1] // 16)
+            def _(i):
+                span = pl.ds(pl.multiple_of(i * 16, 16), 16)
+                both = mine[spot, span, :].astype(F32) + got[spot, span, :].astype(F32)
+                mine[spot, span, :] = both.astype(BF)
+
+            (self.copy(m, k) if k else self.keep[m]).start()
+
+    def copy(self, m, k):
         at = self.at
         return remote(
-            self.mine.at[at.zs[k]],
-            self.home_out.at[at.z],
-            self.z_send.at[k - 1],
-            self.z_recv.at[at.z],
+            self.mine[m].at[at.zs[k]],
+            self.outs[m].at[at.z],
+            self.z_send.at[m * 3 + k - 1],
+            self.z_recv.at[m * 4 + at.z],
             at.device(zi=k),
         )
 
     def finish(self):
         at = self.at
-        for k in (1, 2, 3):
-            remote(
-                self.mine.at[at.z],
-                self.home_out.at[at.zs[k]],
-                self.z_send.at[k - 1],
-                self.z_recv.at[at.zs[k]],
-                at.device(zi=k),
-            ).wait_recv()
-            self.copy(k).wait_send()
-        self.keep.wait()
-        for copy in self.crossing:
+        for m in range(self.count):
+            for k in (1, 2, 3):
+                remote(
+                    self.mine[m].at[at.z],
+                    self.outs[m].at[at.zs[k]],
+                    self.z_send.at[m * 3 + k - 1],
+                    self.z_recv.at[m * 4 + at.zs[k]],
+                    at.device(zi=k),
+                ).wait_recv()
+                self.copy(m, k).wait_send()
+            self.keep[m].wait()
+        for copy in self.crossing.values():
             copy.wait_send()
 
 
@@ -1746,10 +1773,12 @@
         del refs[:count]
         return taken
 
-    in_ref, g_ref, u_ref, scaled_ref, picked_ref, dy_ref, home_ref, mixed_ref, given = take(9)
-    halves = take(5)
-    out_ref, taken, grad_gate, grad_up, grad_down, home_out, mixed_out = take(7)
-    right, left, other, grad, turned, mine, got = take(7)
+    in_ref, g_ref, u_ref, scaled_ref, picked_ref, dy_ref, mixed_ref, given = take(8)
+    halves, home_refs = take(5), take(3)
+    out_ref, taken, grad_gate, grad_up, grad_down, mixed_out = take(6)
+    home_outs = take(3)
+    right, left, other, grad, turned = take(5)
+    mine, got = take(3), take(3)
     buffers = take(6)
     first_sem, cross_send, cross_recv, load_sem, store_sem = take(5)
     home_sems, share_sems = take(5), take(3)
@@ -1760,7 +1789,7 @@
     rows, width = acc.shape[1:]
     part = given.shape[0]
     crossing = cross(at, [given], [taken], cross_send, cross_recv)[0]
-    home = Home(at, home_ref, home_out, mine, got, *home_sems)
+    home = Home(at, home_refs, home_outs, mine, got, *home_sems)
     sharing = Share(at, mixed_ref, mixed_out, *share_sems)
 
     def rows_of(rank):
@@ -1853,30 +1882,29 @@
             shape((rows, width), F32),
             shape(given.shape, BF),
             *[shape((hidden, width), F32)] * 3,
-            shape((4,) + home.shape[1:], BF),
             shape((4 * rows, width), BF),
+            *[shape((4,) + a.shape[1:], BF) for a in home],
         ],
-        in_specs=[hbm] * 14,
-        out_specs=[vmem] + [hbm] * 6,
+        in_specs=[hbm] * 16,
+        out_specs=[vmem] + [hbm] * 8,
         scratch_shapes=[
             pltpu.VMEM((2, slots, width), BF),
             pltpu.VMEM((3, slots, hidden), BF),
             pltpu.VMEM((2, hidden, width), BF),
             pltpu.VMEM((2, hidden, width), F32),
             pltpu.VMEM((hidden, slots), BF),
-            pltpu.VMEM((4,) + home.shape[1:], BF),
-            pltpu.VMEM((4,) + home.shape[1:], BF),
+            *[pltpu.VMEM((4,) + a.shape[1:], BF) for a in home] * 2,
             *scatter_buffers(rows, width),
             sems(8),
             sems(1),
             sems(1),
             sems(11),
             sems(3),
-            sems(5),
-            sems(4),
-            sems(4),
-            sems(3),
-            sems(4),
+            sems(15),
+            sems(12),
+            sems(12),
+            sems(9),
+            sems(12),
             pltpu.SemaphoreType.DMA,
             sems(3),
             sems(3),
@@ -1884,7 +1912,7 @@
         compiler_params=pltpu.CompilerParams(
             collective_id=cid, has_side_effects=True, vmem_limit_bytes=62 * 1024 * 1024
         ),
-    )(x, g, u, scaled, picked, picked_dy, home, mixed_own, given, *halves)
+    )(x, g, u, scaled, picked, picked_dy, mixed_own, given, *halves, *home)
 
 
 def end_kernel(tokens_ref, gain_ref, small_ref, out_ref, gain_out, small_out, *scratch):
@@ -1974,62 +2002,174 @@
     )(tokens_own, gain_part, small)
 
 
-ALL = ("dp", "ctx", "exp")
-DENSE = ("dp", "ctx")
-
-
-def swap(blocks):
-    return lax.all_to_all(blocks, DENSE, split_axis=0, concat_axis=0, tiled=True)
+def front_kernel(scale, *refs):
+    refs = list(refs)
+
+    def take(count):
+        taken = refs[:count]
+        del refs[:count]
+        return taken
+
+    dy_ref, tokens_ref, units, given, gain, w_qkv, w_out, tables = take(8)
+    dy_out, units_out, taken, normed_out, part_out, q_out, k_out, v_out, heads_out, lse_out = take(10)
+    rows_in, normed, staged = take(3)
+    own_sem, send_sem, recv_sem, local_sem, swap_send, swap_recv = take(6)
+    cross_send, cross_recv, in_sem, normed_sem, part_sem = take(5)
+    at = Place()
+    greet(at, True)
+    gather = Gather(at, dy_ref, dy_out, own_sem, send_sem, recv_sem, True)
+    swap_in = Exchange(at, [units], [units_out], local_sem, swap_send, swap_recv)
+    crossing = cross(at, [given], [taken], cross_send, cross_recv, (taken.shape[0],))[0]
+    length, width = tokens_ref.shape
+    block = length // 4
+    step = 256
+    over = columns_loop(width, 4)
+
+    def rows_load(j):
+        return pltpu.make_async_copy(
+            tokens_ref.at[pl.ds(j * block, block)], rows_in.at[j % 2], in_sem.at[j % 2]
+        )
+
+    def normed_store(j):
+        return pltpu.make_async_copy(
+            normed.at[j % 2], normed_out.at[pl.ds(j * block, block)], normed_sem.at[j % 2]
+        )
+
+    def part_store(i):
+        return pltpu.make_async_copy(
+            staged.at[i % 2], part_out.at[pl.ds(i * step, step)], part_sem.at[i % 2]
+        )
+
+    def turn_rows(values, here):
+        other = pltpu.roll(values, HDIM // 2, 1)
+        return (values * tables[0, here, :] - other * tables[1, here, :]).astype(BF)
+
+    def project(j):
+        rows_load(j).wait()
+        if j >= 2:
+            normed_store(j - 2).wait()
+
+        @pl.loop(0, block // 64)
+        def _(n):
+            span = pl.ds(pl.multiple_of(n * 64, 64), 64)
+            values = rows_in[j % 2, span, :].astype(F32)
+            size = jnp.mean(values * values, axis=-1, keepdims=True)
+            normed[j % 2, span, :] = (values * lax.rsqrt(size + EPSILON) * gain[0:1, :]).astype(BF)
+
+        normed_store(j).start()
+        if j < 2:
+            rows_load(j + 2).start()
+        here = pl.ds(j * block, block)
+        qkv = product(normed[j % 2], w_qkv[...])
+        q_out[here, :] = turn_rows(qkv[:, :HDIM], here)
+        k_out[here, :] = turn_rows(qkv[:, HDIM : 2 * HDIM], here)
+        v_out[here, :] = qkv[:, 2 * HDIM :].astype(BF)
+
+    def attend_rows(i):
+        seen = (i + 1) * step
+        here = pl.ds(i * step, step)
+        scores = transposed_right(q_out[here, :], k_out[0:seen, :]) * scale
+        row_at = lax.broadcasted_iota(jnp.int32, scores.shape, 0) + i * step
+        col_at = lax.broadcasted_iota(jnp.int32, scores.shape, 1)
+        scores = jnp.where(row_at >= col_at, scores, MASKED)
+        top = jnp.max(scores, axis=-1, keepdims=True)
+        powers = jnp.exp(scores - top)
+        lse = top + jnp.log(jnp.sum(powers, axis=-1, keepdims=True))
+        probs = jnp.exp(scores - lse).astype(BF)
+        heads_out[here, :] = product(probs, v_out[0:seen, :]).astype(BF)
+        lse_out[here, :] = jnp.broadcast_to(lse, (step, HDIM))
+        if i >= 2:
+            part_store(i - 2).wait()
+
+        @over
+        def _(columns):
+            staged[i % 2, :, columns] = product(heads_out[here, :], w_out[:, columns]).astype(BF)
+
+        part_store(i).start()
+
+    gather.begin()
+    swap_in.start()
+    crossing.start()
+    rows_load(0).start()
+    rows_load(1).start()
+    project(0)
+    project(1)
+    attend_rows(0)
+    gather.line(1)
+    swap_in.forward(1)
+    project(2)
+    attend_rows(1)
+    attend_rows(2)
+    gather.other(1)
+    gather.line(2)
+    swap_in.forward(2)
+    project(3)
+    attend_rows(3)
+    attend_rows(4)
+    gather.other(2)
+    gather.line(3)
+    swap_in.forward(3)
+    attend_rows(5)
+    attend_rows(6)
+    attend_rows(7)
+    gather.other(3)
+    for j in (2, 3):
+        normed_store(j).wait()
+    for i in (6, 7):
+        part_store(i).wait()
+    swap_in.finish()
+    crossing.wait()
+    gather.finish()
+
+
+def front(dy, tokens_all, units, given, gain, w_qkv, w_out, tables, cid):
+    length, width = tokens_all.shape
+    hbm, vmem = pl.BlockSpec(memory_space=pl.ANY), pl.BlockSpec(memory_space=pltpu.VMEM)
+    shape, sems = jax.ShapeDtypeStruct, lambda n: pltpu.SemaphoreType.DMA((n,))
+    return pl.pallas_call(
+        functools.partial(front_kernel, HDIM ** (-0.5)),
+        out_shape=[
+            shape((length, width), BF),
+            shape((8,) + units.shape[1:], BF),
+            half_of(given),
+            shape((length, width), BF),
+            shape((length, width), BF),
+            *[shape((length, HDIM), BF)] * 4,
+            shape((length, HDIM), F32),
+        ],
+        in_specs=[hbm] * 4 + [vmem] * 4,
+        out_specs=[hbm] * 5 + [vmem] * 5,
+        scratch_shapes=[
+            pltpu.VMEM((2, length // 4, width), BF),
+            pltpu.VMEM((2, length // 4, width), BF),
+            pltpu.VMEM((2, 256, width), BF),
+            pltpu.SemaphoreType.DMA,
+            sems(19),
+            sems(15),
+            sems(1),
+            sems(7),
+            sems(8),
+            sems(1),
+            sems(1),
+            sems(2),
+            sems(2),
+            sems(2),
+        ],
+        compiler_params=pltpu.CompilerParams(
+            collective_id=cid, has_side_effects=True, vmem_limit_bytes=60 * 1024 * 1024
+        ),
+    )(dy, tokens_all, units, given, gain, w_qkv, w_out, tables)
 
 
 def by_four(matrix):
     rows, columns = matrix.shape
     return matrix.reshape(rows, 4, columns // 4).transpose(1, 0, 2)
-
-
-def across(values):
-    return lax.ppermute(values, "dp", [(0, 1), (1, 0)])
-
-
-def attend_kernel(scale, block, q_ref, k_ref, v_ref, out_ref, lse_ref):
-    length = q_ref.shape[0]
-    for i in range(length // block):
-        seen = (i + 1) * block
-        rows = pl.ds(i * block, block)
-        scores = transposed_right(q_ref[rows, :], k_ref[0:seen, :]) * scale
-        row_at = lax.broadcasted_iota(jnp.int32, scores.shape, 0) + i * block
-        col_at = lax.broadcasted_iota(jnp.int32, scores.shape, 1)
-        scores = jnp.where(row_at >= col_at, scores, MASKED)
-        top = jnp.max(scores, axis=-1, keepdims=True)
-        lse = top + jnp.log(jnp.sum(jnp.exp(scores - top), axis=-1, keepdims=True))
-        probs = jnp.exp(scores - lse).astype(BF)
-        out_ref[rows, :] = product(probs, v_ref[0:seen, :]).astype(BF)
-        lse_ref[rows, :] = jnp.broadcast_to(lse, (block, HDIM))
-
-
-def attend(q, k, v):
-    length = q.shape[0]
-    return pl.pallas_call(
-        functools.partial(attend_kernel, HDIM ** (-0.5), 256),
-        out_shape=(
-            jax.ShapeDtypeStruct((length, HDIM), BF),
-            jax.ShapeDtypeStruct((length, HDIM), F32),
-        ),
-        in_specs=[pl.BlockSpec(memory_space=pltpu.VMEM)] * 3,
-        out_specs=(pl.BlockSpec(memory_space=pltpu.VMEM),) * 2,
-        compiler_params=pltpu.CompilerParams(vmem_limit_bytes=56 * 1024 * 1024),
-    )(q, k, v)
 
 
 def turn_tables(length):
     inverse = 10000.0 ** (-np.arange(HDIM // 2).astype(np.float64) * 2.0 / HDIM)
     angles = np.arange(length).astype(np.float64)[:, None] * inverse[None, :]
     return np.cos(angles).astype(np.float32), np.sin(angles).astype(np.float32)
-
-
-def turn(rows, cosine, sine):
-    a, b = rows[:, : HDIM // 2], rows[:, HDIM // 2 :]
-    return jnp.concatenate([a * cosine - b * sine, b * cosine + a * sine], axis=1)
 
 
 def fast_body(
@@ -2075,15 +2215,11 @@
     sent_out = w_out.reshape(4, HDIM, dense)
     sent_units = jnp.stack([shared_gate.T, shared_up.T, shared_down], axis=0)
     sent_units = sent_units.reshape(3, 4, cut, dense).transpose(1, 0, 2, 3).reshape(4, 3 * cut, dense)
-    tokens_all, early, early_out, late, early_little = all_rows(
-        tokens[0], True, 1, (sent_head, sent_out, sent_units, little)
-    )
-
     own_gate, own_up, own_down = expert_gate[0].T, expert_up[0].T, expert_down[0]
-    tokens_all, sent_gate, sent_up, sent_down = lax.optimization_barrier(
-        (tokens_all, own_gate, own_up, own_down)
-    )
-    other_gate, other_up, other_down = across(sent_gate), across(sent_up), across(sent_down)
+    part = own_gate.shape[0] // 2
+    tokens_all, early, early_out, early_little, gate_0 = all_rows(
+        tokens[0], True, 1, (sent_head, sent_out, little), (own_gate,), (0,)
+    )
     w_qkv = early.reshape(width, 3 * HDIM)
     early_little = early_little.transpose(1, 0, 2)
     router_rows = early_little[:experts].reshape(experts, width)
@@ -2093,48 +2229,64 @@
     hits = lax.dynamic_index_in_dim(hits, dp, 0, False).astype(F32).reshape(groups, quarter)
     w_out_head = early_out.transpose(1, 0, 2).reshape(HDIM, width)
 
-    dy_all = all_rows(out_grad[0], True, 2)
+    cosine, sine = turn_tables(length)
+    tables = np.stack(
+        [np.concatenate([cosine, cosine], axis=1), np.concatenate([sine, -sine], axis=1)]
+    )
+    dy_all, late, gate_1, normed, attn_part, query, key, value, heads_out, lse = front(
+        out_grad[0],
+        tokens_all,
+        sent_units,
+        own_gate,
+        jnp.broadcast_to(attention_gain[None], (8, width)),
+        w_qkv,
+        w_out_head,
+        tables,
+        2,
+    )
     late = late.transpose(1, 0, 2).reshape(3, cut, width)
     late = jnp.pad(late, ((0, 0), (0, wide - cut), (0, 0)))
     shared_in = late[:2].reshape(2 * wide, width)
     shared_out = late[2]
-
-    cosine, sine = turn_tables(length)
-    normed = rms_scale(tokens_all.astype(F32), attention_gain).astype(BF)
-    qkv = product(normed, w_qkv)
-    query = turn(qkv[:, :HDIM], cosine, sine).astype(BF)
-    key = turn(qkv[:, HDIM : 2 * HDIM], cosine, sine).astype(BF)
-    value = qkv[:, 2 * HDIM :].astype(BF)
-    heads_out, lse = attend(query, key, value)
-    attn = own_rows(product(heads_out, w_out_head).astype(BF), 3)
+    attn, up_0, up_1 = own_rows(attn_part, 3, (own_up, own_up), (0, part))
     middle = tokens_own.astype(F32) + attn
     normed_own = rms_scale(middle, mixer_gain).astype(BF)
 
     mine = ctx * 4 + exp
     place = jnp.cumsum(hits, axis=1) - 1.0
-    dispatch = jnp.where(
-        (jnp.arange(capacity).astype(F32)[None, :, None] == place[:, None, :])
-        & (hits[:, None, :] > 0.5),
-        1.0,
-        0.0,
-    ).astype(BF)
+    first = (jnp.arange(groups) % 4 * capacity).astype(F32)[:, None]
+    place = jnp.where(hits > 0.5, place + first, -1.0).reshape(4, 1, 4 * quarter)
+    blocks = place == jnp.arange(4 * capacity).astype(F32)[None, :, None]
+    blocks = blocks.astype(BF)
     router_wide = jnp.pad(router_rows, ((0, HDIM - experts), (0, 0)))
-    mix_all, picked, picked_dy, scaled, g_back, u_back, gate_back, shared_act, shared_gu_back = (
-        expert_rows(
-            normed_own,
-            dy_all,
-            dispatch,
-            router_wide,
-            experts,
-            shared_in,
-            shared_out,
-            (own_gate, own_up, own_down, other_gate, other_up, other_down),
-            4,
-        )
-    )
+    (
+        mix_all,
+        picked,
+        picked_dy,
+        scaled,
+        g_back,
+        u_back,
+        gate_back,
+        shared_act,
+        shared_gu_back,
+        down_0,
+        down_1,
+    ) = expert_rows(
+        normed_own,
+        dy_all,
+        blocks,
+        router_wide,
+        experts,
+        shared_in,
+        shared_out,
+        (own_gate, own_up, own_down, gate_0, gate_1, up_0, up_1),
+        (own_down, own_down),
+        4,
+    )
+    other_down = (down_0, down_1)
 
     mix_back, gate_0, gate_1, up_0, up_1, down_0, down_1 = expert_back(
-        dispatch,
+        blocks,
         gate_back,
         shared_in,
         g_back,
@@ -2143,7 +2295,7 @@
         picked,
         picked_dy,
         scaled,
-        (own_gate, own_up, other_gate, other_up),
+        (own_gate, own_up, gate_0, gate_1, up_0, up_1),
         5,
     )
     gate_back_own = mix_back[:, width : width + experts]
@@ -2163,21 +2315,18 @@
     attn_back_all, mixed_part, units_part, gate_1, up_0 = gather_back(
         attn_back,
         (gate_1, up_0),
-        dispatch,
+        blocks,
         shared_out,
         scaled,
         shared_act,
         shared_gu_back,
-        own_down,
-        other_down,
+        (own_down, *other_down),
         mix_all,
         dy_all,
+        cut,
         7,
     )
-    tables = jnp.stack(
-        [jnp.concatenate([cosine, cosine], axis=1), jnp.concatenate([sine, -sine], axis=1)]
-    )
-    mixed_sum, normed_part, qkv_part, out_part, up_1, down_0 = mixed_rows(
+    mixed_sum, normed_part, head_part, up_1, down_0 = mixed_rows(
         w_out_head,
         w_qkv.T,
         tables,
@@ -2193,27 +2342,25 @@
         9,
     )
     mixed_own = (middle + mixed_sum).astype(BF)
-    units_part = units_part.reshape(3, wide, width)[:, :cut].reshape(3 * cut, width)
     small_part = jnp.concatenate([gain_mix_part[None], router_part], axis=0).astype(BF)
     small_rows = -(-(experts + 1) // 16) * 16
     small_part = jnp.pad(small_part, ((0, small_rows - experts - 1), (0, 0)))
-    home = jnp.concatenate([qkv_part, out_part, units_part, small_part], axis=0)
-    home = home.reshape(-1, 8, dense).transpose(1, 0, 2)
-    normed_back, _, gate_grad, up_grad, down_grad, home, mixed = last_rows(
+    small_part = small_part.reshape(small_rows, 8, dense).transpose(1, 0, 2)
+    normed_back, _, gate_grad, up_grad, down_grad, mixed, head_grad, units_grad, small = last_rows(
         normed_part,
         g_back,
         u_back,
         scaled,
         picked,
         picked_dy,
-        home,
+        (head_part, units_part, small_part),
         mixed_own,
         down_1,
         (gate_0, gate_1, up_0, up_1, down_0),
         8,
     )
-    home = home.astype(F32)
-    small_part = jnp.sum(home[:, -small_rows:], axis=0)
+    head_grad, units_grad = head_grad.astype(F32), units_grad.astype(F32)
+    small_part = jnp.sum(small.astype(F32), axis=0)
     _, norm_attn_back = jax.vjp(rms_scale, tokens_own.astype(F32), attention_gain)
     input_norm_back, gain_attn_part = norm_attn_back(normed_back)
     tokens_back_own = (middle_back + input_norm_back).astype(BF)
@@ -2227,20 +2374,19 @@
     def rows_of(parts):
         return parts.reshape(-1, dense)
 
-    units = 4 * HDIM
     return (
         mixed[None],
         tokens_back[None],
         gain_attn[0],
-        columns_of(home[:, :HDIM]),
-        columns_of(home[:, HDIM : 2 * HDIM]),
-        columns_of(home[:, 2 * HDIM : 3 * HDIM]),
-        rows_of(home[:, 3 * HDIM : units]),
+        columns_of(head_grad[:, :HDIM]),
+        columns_of(head_grad[:, HDIM : 2 * HDIM]),
+        columns_of(head_grad[:, 2 * HDIM : 3 * HDIM]),
+        rows_of(head_grad[:, 3 * HDIM :]),
         small[0],
         small[1 : experts + 1].T,
-        rows_of(home[:, units : units + cut]).T,
-        rows_of(home[:, units + cut : units + 2 * cut]).T,
-        rows_of(home[:, units + 2 * cut : units + 3 * cut]),
+        rows_of(units_grad[:, :cut]).T,
+        rows_of(units_grad[:, cut : 2 * cut]).T,
+        rows_of(units_grad[:, 2 * cut :]),
         gate_grad.T[None],
         up_grad.T[None],
         down_grad[None],

time: 827 us -> 749 us (0.906)
  Pallas kernels: 701 us -> 670 us
  other arithmetic: 34.7 us -> 19.5 us
  local copies, waits for them, and re-layouts: 62.1 us -> 50.7 us
  matrix products: 14.1 us -> 3.53 us
    pallas_call x2 -> x1, Pallas kernels: 171 us -> 79.2 us  [all_rows(): pl.pallas_call(functools.partial(gather_kernel, block, rows, parts, extra...]
    pallas_call x2, Pallas kernels: 65.7 us -> 144 us  [the longest x1 79.5 us: front(): pl.pallas_call(functools.partial(front_kernel, HDIM ** (-0.5)), out_shape...]
    pallas_call x1, Pallas kernels: 96.6 us -> 83.3 us  [expert_rows(): pl.pallas_call(functools.partial(expert_gather_kernel, experts), out_shap...]
    dot_general x3 -> x1, matrix products: 12.7 us -> 2.12 us  [product(): return jnp.dot(left_side, right_side, preferred_element_type=jnp.float32)]
    convert_element_type x5 -> x3, other arithmetic: 9.95 us -> 1.33 us  [the longest x1 1.32 us: fast_body(): blocks = blocks.astype(BF)]
    unnamed x68 -> x64, local copies, waits for them, and re-layouts: 28.2 us -> 24.6 us
  transfers between devices with their start and end apart: 3 -> 0, of which waited for: 1 -> 0; matrix products, arithmetic and copies ran while one was open for 6% -> 0% of each run, Pallas kernels for 16% -> 0%
where the time goes in v5:
time: 749 us; the launch traced here: 745 us
  Pallas kernels  670 us (89%)
  local copies, waits for them, and re-layouts  50.7 us (7%)
  other arithmetic  19.5 us (3%)
    pallas_call x1, Pallas kernels, last_rows(): pl.pallas_call(last_scatter_kernel, out_shape=[shape((rows, width), F32),...  95.9 us
    pallas_call x1, Pallas kernels, expert_back(): pl.pallas_call(expert_scatter_kernel, out_shape=[shape((rows, full), F32)...  89.5 us
    pallas_call x1, Pallas kernels, gather_back(): pl.pallas_call(gather_back_kernel, out_shape=[shape((length, width), BF),...  85.9 us
    pallas_call x1, Pallas kernels, expert_rows(): pl.pallas_call(functools.partial(expert_gather_kernel, experts), out_shap...  83.3 us
    pallas_call x1, Pallas kernels, front(): pl.pallas_call(functools.partial(front_kernel, HDIM ** (-0.5)), out_shape...  79.5 us
    pallas_call x1, Pallas kernels, all_rows(): pl.pallas_call(functools.partial(gather_kernel, block, rows, parts, extra...  79.2 us
    pallas_call x1, Pallas kernels, mixed_rows(): pl.pallas_call(mixed_kernel, out_shape=[shape((rows, width), F32), shape(...  71.5 us
    pallas_call x1, Pallas kernels, own_rows(): pl.pallas_call(functools.partial(scatter_kernel, rows, starts), out_shape...  64.6 us

profile of v5, /device:TPU:0, one launch (start us, length us, event | category | flops | bytes accessed | tf_op | source)
XLA Modules:
  0.0 744.7 jit_solution(2115655000120468225)
XLA Ops:
  9.4 79.2 %shard_map.280 = (bf16[2048,2048]{1,0:T(8,128)(2,1)}, bf16[8,256,384]{2,1,0:T(8,128)(2,1)}, bf16[8,128,256]{2,1,0:T(8,128)(2,1)}, bf16[8,32,256]{2,1,0:T(8,128)(2,1)}, bf16[352,2048]{1,0:T(8,128)(2,1)}) custom-call(bf16[512,2048]{1,0:T(8,128)(2,1)} %bitcast.133, bf16[4,256,384]{2,1,0:T(8,128)(2,1)} %pad_maximum_fusion.1.refs_1_, ...), custom_call_target="tpu_custom_call" | custom-call | tf_op jit(solution)/shard_map/pallas_call | solution.py:653
  88.7 2.0 copy.85
  96.3 2.1 copy.82
  98.5 79.5 %shard_map.281 = (bf16[2048,2048]{1,0:T(8,128)(2,1)}, bf16[8,528,256]{2,1,0:T(8,128)(2,1)}, bf16[352,2048]{1,0:T(8,128)(2,1)}, bf16[2048,2048]{1,0:T(8,128)(2,1)...) custom-call(bf16[512,2048]{1,0:T(8,128)(2,1)} %bitcast.148, ...), custom_call_target="tpu_custom_call" | custom-call | tf_op jit(solution)/shard_map/pallas_call | solution.py:2129
  178.0 3.7 copy.76
  181.7 3.5 reshape.230
  188.9 64.6 %shard_map.282 = (f32[128,2048]{1,0:T(8,128)S(1)}, bf16[352,2048]{1,0:T(8,128)(2,1)S(1)}, bf16[352,2048]{1,0:T(8,128)(2,1)S(1)}) custom-call(bf16[2048,2048]{1,0:T(8,128)(2,1)} %get-tuple-element.81.in_ref, bf16[704,2048]{1,0:T(8,128)(2,1)S(1)} %bitcast.121, bf16[704,2048]{1,0:T(8,128)(2,1)S(1)} %bitcast.122), custom_call_target="tpu_custom_call" | custom-call | tf_op jit(solution)/shard_map/pallas_call | solution.py:834
  253.5 1.7 multiply_reduce_fusion.2
  256.5 83.3 %shard_map.283 = (bf16[2048,2048]{1,0:T(8,128)(2,1)}, bf16[1024,2048]{1,0:T(8,128)(2,1)}, bf16[1024,2048]{1,0:T(8,128)(2,1)}, bf16[2,1024,704]{2,1,0:T(8,128)(2,...) custom-call(bf16[128,2048]{1,0:T(8,128)(2,1)} %copy-done.6, ...), custom_call_target="tpu_custom_call" | custom-call | tf_op jit(solution)/shard_map/pallas_call | solution.py:1130
  339.8 89.5 %shard_map.284 = (f32[128,2176]{1,0:T(8,128)}, bf16[352,2048]{1,0:T(8,128)(2,1)}, bf16[352,2048]{1,0:T(8,128)(2,1)}, bf16[352,2048]{1,0:T(8,128)(2,1)}, bf16[352...) custom-call(bf16[4,256,512]{2,1,0:T(8,128)(2,1)} %compare_convert_fusion.refs_2_.refs_0_.refs_1_, ...), custom_call_target="tpu_custom_call" | custom-call | tf_op jit(solution)/shard_map/pallas_call | solution.py:1301
  431.6 2.1 multiply_reduce_fusion
  434.7 2.2 fusion.24.refs_0_
  437.0 85.9 %shard_map.285 = (bf16[2048,2048]{1,0:T(8,128)(2,1)}, bf16[2048,2048]{1,0:T(8,128)(2,1)}, bf16[8,528,256]{2,1,0:T(8,128)(2,1)}, bf16[352,2048]{1,0:T(8,128)(2,1)}, bf16[352,2048]{1,0:T(8,128)(2,1)}) custom-call(bf16[128,2048]{1,0:T(8,128)(2,1)} %fusion.24.refs_0_, bf16[4,256,512]{2,1,0:T(8,128)(2,1)} %compare_convert_fusion.refs_2_.refs_0_.refs_1_, ...), custom_call_target="tpu_custom_call" | custom-call | tf_op jit(solution)/shard_map/pallas_call | solution.py:1636
  522.9 71.5 %shard_map.286 = (f32[128,2048]{1,0:T(8,128)}, bf16[2048,2048]{1,0:T(8,128)(2,1)}, bf16[8,512,256]{2,1,0:T(8,128)(2,1)}, bf16[352,2048]{1,0:T(8,128)(2,1)}, bf16[352,2048]{1,0:T(8,128)(2,1)}) custom-call(bf16[128,2048]{1,0:T(8,128)(2,1)} %bitcast.147, bf16[384,2048]{1,0:T(8,128)(2,1)} %bitcast.134, f32[2,2048,128]{2,1,0:T(8,128)} %constant.73.clone.refs_7_.refs_2_, ...), custom_call_target="tpu_custom_call" | custom-call | tf_op jit(solution)/shard_map/pallas_call | solution.py:1499
  594.3 2.5 add_convert_fusion.refs_6_
  596.8 95.9 %shard_map.287 = (f32[128,2048]{1,0:T(8,128)}, bf16[352,2048]{1,0:T(8,128)(2,1)}, f32[704,2048]{1,0:T(8,128)}, f32[704,2048]{1,0:T(8,128)}, f32[704,2048]{1,0:T(...) custom-call(bf16[2048,2048]{1,0:T(8,128)(2,1)} %get-tuple-element.10, ...), custom_call_target="tpu_custom_call" | custom-call | tf_op jit(solution)/shard_map/pallas_call | solution.py:1879
  692.7 1.9 fusion.6
  694.6 3.0 fusion.2.tokens_ref
  698.9 20.2 %shard_map.288 = (bf16[512,2048]{1,0:T(8,128)(2,1)}, f32[8,256]{1,0:T(8,128)}, f32[32,256]{1,0:T(8,128)}) custom-call(bf16[128,2048]{1,0:T(8,128)(2,1)} %fusion.2.tokens_ref, f32[8,8,256]{2,1,0:T(8,128)} %pad.24.gain_ref, f32[32,256]{1,0:T(8,128)} %convert_reduce_fusion.small_ref), custom_call_target="tpu_custom_call" | custom-call | tf_op jit(solution)/shard_map/pallas_call | solution.py:1977
  725.2 2.2 copy.80
  729.7 3.9 copy.98
  735.0 2.9 copy.100
  738.0 2.9 copy.101
  741.9 2.5 copy.102
  (112 shorter events, 34.5 us)
Async XLA Ops:
  0.6 6.3 copy-start.17
  5.4 2.9 copy-start.14
  5.4 2.9 copy-start.15
  5.4 2.9 copy-start.16
  88.7 7.7 %copy-start.8 = (bf16[8,256,384]{2,1,0:T(8,128)(2,1)S(1)}, bf16[8,256,384]{2,1,0:T(8,128)(2,1)}, u32[]{:S(2)}) copy-start(bf16[8,256,384]{2,1,0:T(8,128)(2,1)} %get-tuple-element.73) | copy-start | bytes 4718596
  186.3 2.6 copy-start
  253.5 1.9 copy-start.1
  253.5 1.9 copy-start.2
  255.4 1.1 copy-start.6
  339.8 90.7 %copy-start.7 = (bf16[128,2048]{1,0:T(8,128)(2,1)S(1)}, bf16[128,2048]{1,0:T(8,128)(2,1)}, u32[]{:S(2)}) copy-start(bf16[128,2048]{1,0:T(8,128)(2,1)} %copy-done.6) | copy-start | bytes 1572868
  429.3 5.4 copy-start.4
  433.7 1.0 copy-start.11
  596.8 97.8 %copy-start.12 = (f32[128,2048]{1,0:T(8,128)S(1)}, f32[128,2048]{1,0:T(8,128)}, u32[]{:S(2)}) copy-start(f32[128,2048]{1,0:T(8,128)} %copy-done.11) | copy-start | bytes 3145732
  692.7 1.9 copy-start.5
  694.6 3.1 copy-start.18
  694.6 28.4 %copy-start.10 = (bf16[4,512,256]{2,1,0:T(8,128)(2,1)S(1)}, bf16[4,512,256]{2,1,0:T(8,128)(2,1)}, u32[]{:S(2)}) copy-start(bf16[4,512,256]{2,1,0:T(8,128)(2,1)} %get-tuple-element.123) | copy-start | bytes 3145732
  724.2 4.2 copy-start.9
  725.2 9.8 %slice-start.4 = ((s8[5767168]{0:T(1024)(128)(4,1)}), s8[1572864]{0:T(1024)(128)(4,1)S(1)}, s32[]{:S(2)}) async-start(s8[5767168]{0:T(1024)(128)(4,1)} %bitcast.143), calls=%async_computation.4 | async-start | bytes 3145728
  728.3 5.3 copy-start.13
  728.3 9.6 %slice-start.2 = ((s8[5767168]{0:T(1024)(128)(4,1)}), s8[4194304]{0:T(1024)(128)(4,1)S(1)}, s32[]{:S(2)}) async-start(s8[5767168]{0:T(1024)(128)(4,1)} %bitcast.140), calls=%async_computation.2 | async-start | bytes 8388608
  729.7 5.3 slice-start.5
  733.7 4.3 slice-start.3
  735.0 5.8 slice-start
  738.0 4.0 slice-start.1
  (1 other events, 1.0 us)

commit v6 on v5

--- a/solution.py
+++ b/solution.py
@@ -447,6 +447,16 @@
     )
 
 
+def keep(src, dst):
+    def run(held, sems):
+        for j, (a, b) in enumerate(((src, held), (held, dst))):
+            copy = pltpu.make_async_copy(a, b, sems.at[j])
+            copy.start()
+            copy.wait()
+
+    pl.run_scoped(run, pltpu.VMEM(src.shape, src.dtype), pltpu.SemaphoreType.DMA((2,)))
+
+
 def half_of(array):
     return jax.ShapeDtypeStruct((array.shape[0] // 2,) + array.shape[1:], array.dtype)
 
@@ -466,9 +476,9 @@
 
 
 class Exchange:
-    def __init__(self, at, sent, got, local_sem, send_sem, recv_sem):
+    def __init__(self, at, sent, got, send_sem, recv_sem):
         self.at, self.sent, self.got = at, sent, got
-        self.local_sem, self.send_sem, self.recv_sem = local_sem, send_sem, recv_sem
+        self.send_sem, self.recv_sem = send_sem, recv_sem
         self.waits = []
 
     def push(self, src, m, z_from, slot, device):
@@ -483,12 +493,14 @@
     def start(self):
         at = self.at
         for m, sent in enumerate(self.sent):
-            for zi in (1, 2, 3):
-                self.push(sent.at[at.zs[zi]], m, at.z, zi - 1, at.device(zi=zi))
             self.push(sent.at[at.z], m, at.z, 3, at.device(ox=at.dx))
-            pltpu.make_async_copy(
-                sent.at[at.z], self.got[m].at[at.x * 4 + at.z], self.local_sem.at[m]
-            ).start()
+        for m, sent in enumerate(self.sent):
+            keep(sent.at[at.z], self.got[m].at[at.x * 4 + at.z])
+
+    def along(self, zi):
+        at = self.at
+        for m, sent in enumerate(self.sent):
+            self.push(sent.at[at.zs[zi]], m, at.z, zi - 1, at.device(zi=zi))
 
     def arrive(self, m, slot):
         src = self.sent[m].at[0]
@@ -507,9 +519,6 @@
         for m, sent in enumerate(self.sent):
             for z in range(4):
                 self.arrive(m, m * 8 + 4 + z)
-            pltpu.make_async_copy(
-                sent.at[at.z], self.got[m].at[at.x * 4 + at.z], self.local_sem.at[m]
-            ).wait()
         for copy in self.waits:
             copy.wait_send()
 
@@ -525,8 +534,8 @@
 
     (x_ref,), sent, given = take(1), take(extras), take(swaps)
     (out_ref,), got, taken = take(1), take(extras), take(swaps)
-    own_sem, send_sem, recv_sem = take(3)
-    extra_sems = take(3 if extras else 0)
+    send_sem, recv_sem = take(2)
+    extra_sems = take(2 if extras else 0)
     at = Place()
     greet(at, extras > 0, swaps > 0)
     crossing = cross(at, given, taken, *refs, starts) if swaps else []
@@ -564,7 +573,6 @@
         spot = pl.ds(pl.multiple_of(at.z * 4 * rows, 4 * rows), 4 * rows)
     else:
         spot = pl.ds(pl.multiple_of(at.shard(0, 0) * rows, rows), rows)
-    own = pltpu.make_async_copy(x_ref, out_ref.at[spot], own_sem)
 
     def source(f, zi, p):
         if f == 0 and zi == 0:
@@ -593,28 +601,28 @@
 
     for p in range(parts):
         forward(0, 0, p)
-    own.start()
+    if extras:
+        swap_in = Exchange(at, sent, got, *extra_sems)
+        for zi in (1, 2, 3):
+            swap_in.along(zi)
+        swap_in.start()
     for copy in crossing:
         copy.start()
-    if extras:
-        swap_in = Exchange(at, sent, got, *extra_sems)
-        swap_in.start()
-    for zi in range(4):
-        if zi > 0:
-            for p in range(parts):
+    keep(x_ref, out_ref.at[spot])
+    for zi in range(1, 5):
+        for p in range(parts):
+            if zi < 4:
                 arrive(slot_z + zi - 1, p)
                 forward(0, zi, p)
-        if zi >= firsts:
-            for p in range(parts):
-                arrive(slot_f + zi, p)
-                forward(1, zi, p)
-        if extras and zi > 0:
-            swap_in.forward(zi)
+            if zi - 1 >= firsts:
+                arrive(slot_f + zi - 1, p)
+                forward(1, zi - 1, p)
+        if extras and zi > 1:
+            swap_in.forward(zi - 1)
     for f in range(2):
         for zi in range(firsts, 4):
             for p in range(parts):
                 arrive(slot_s + f * 4 + zi, p)
-    own.wait()
     if extras:
         swap_in.finish()
     for copy in crossing:
@@ -638,13 +646,11 @@
     outs += [jax.ShapeDtypeStruct((8,) + a.shape[1:], a.dtype) for a in sent]
     outs += [half_of(a) for a in given]
     scratch = [
-        pltpu.SemaphoreType.DMA,
         pltpu.SemaphoreType.DMA((19 * parts,)),
         pltpu.SemaphoreType.DMA((15 * parts,)),
     ]
     if extras:
         scratch += [
-            pltpu.SemaphoreType.DMA((extras,)),
             pltpu.SemaphoreType.DMA((7 * extras,)),
             pltpu.SemaphoreType.DMA((8 * extras,)),
         ]
@@ -722,49 +728,41 @@
         self.add(k, (self.got_s, 4 + zi))
         self.push(self.acc.at[k], self.got_f.at[zi], 5 + zi, self.f_dev)
 
-    def second(self, zi):
-        at, acc, got_z = self.at, self.acc, self.got_z
+    def second(self, zi, who="all"):
+        if who != "middle":
+            pl.when(jnp.logical_not(self.at.middle))(lambda: self.from_end(zi))
+        if who != "end":
+            pl.when(self.at.middle)(lambda: self.from_middle(zi))
+
+    def terms(self, zi):
         self.arrive(self.got_s.at[zi], 9 + zi)
         self.arrive(self.got_f.at[zi], 5 + zi)
-        others = [(self.got_s, zi), (self.got_f, zi)]
-        k = self.held(0, zi)
-        if zi >= 2:
-
-            @pl.when(at.middle)
-            def _():
-                self.arrive(got_z.at[3 - zi], 3 - zi)
-                self.add(k, *others, (got_z, 3 - zi))
-                there = 4 if zi == 2 else 3
-                self.push(acc.at[k], got_z.at[there], there, at.inward(), zi, self.in_middle)
-
-            @pl.when(jnp.logical_not(at.middle))
-            def _():
-                self.add(k, *others)
-                self.push(acc.at[k], got_z.at[3 - zi], 3 - zi, self.z_dev, zi, self.at_end)
-        elif zi == 1:
-
-            @pl.when(at.middle)
-            def _():
-                self.arrive(got_z.at[3], 3)
-                self.add(k, *others, (got_z, 3))
-                self.push(acc.at[k], got_z.at[4], 4, self.z_dev, 1, self.in_middle)
-
-            @pl.when(jnp.logical_not(at.middle))
-            def _():
-                self.add(k, *others)
-                self.push(acc.at[k], got_z.at[2], 2, self.z_dev, 1, self.at_end)
-        else:
-
-            @pl.when(at.middle)
-            def _():
-                self.arrive(got_z.at[2], 2)
-                self.arrive(got_z.at[4], 4)
-                self.add(k, *others, (got_z, 2), (got_z, 4), into=self.out_ref)
-
-            @pl.when(jnp.logical_not(at.middle))
-            def _():
-                self.arrive(got_z.at[4], 4)
-                self.add(k, *others, (got_z, 4), into=self.out_ref)
+        return self.held(0, zi), [(self.got_s, zi), (self.got_f, zi)]
+
+    def from_end(self, zi):
+        k, others = self.terms(zi)
+        acc, got_z = self.acc, self.got_z
+        if zi == 0:
+            self.arrive(got_z.at[4], 4)
+            self.add(k, *others, (got_z, 4), into=self.out_ref)
+            return
+        self.add(k, *others)
+        self.push(acc.at[k], got_z.at[3 - zi], 3 - zi, self.z_dev, zi, self.at_end)
+
+    def from_middle(self, zi):
+        k, others = self.terms(zi)
+        acc, got_z = self.acc, self.got_z
+        if zi == 0:
+            self.arrive(got_z.at[2], 2)
+            self.arrive(got_z.at[4], 4)
+            self.add(k, *others, (got_z, 2), (got_z, 4), into=self.out_ref)
+            return
+        came = 3 if zi == 1 else 3 - zi
+        self.arrive(got_z.at[came], came)
+        self.add(k, *others, (got_z, came))
+        there = 3 if zi == 3 else 4
+        device = self.z_dev if zi == 1 else self.at.inward()
+        self.push(acc.at[k], got_z.at[there], there, device, zi, self.in_middle)
 
     def finish(self):
         for zi in range(4):
@@ -850,89 +848,98 @@
 
 
 class Gather:
-    def __init__(self, at, x_ref, out_ref, own_sem, send_sem, recv_sem, block=False):
+    parts = 2
+
+    def __init__(self, at, x_ref, out_ref, send_sem, recv_sem, block=False):
         self.at, self.x_ref, self.out_ref, self.block = at, x_ref, out_ref, block
         self.send_sem, self.recv_sem = send_sem, recv_sem
-        self.rows = x_ref.shape[0] // (4 if block else 1)
+        rows = x_ref.shape[0] // (4 if block else 1)
+        self.rows, self.piece = rows, rows // self.parts
         self.f_dev, self.s_dev, self.z_dev = (
             at.device(oe=at.dy),
             at.device(oe=at.dc),
             at.device(zi=1),
         )
         self.started, self.inside = [], []
-        rows, self.source = self.rows, x_ref
-        spot = self.where(0, 0)
         if block:
-            self.source = x_ref.at[pl.ds(pl.multiple_of(at.e * rows, rows), rows)]
             spot = pl.ds(pl.multiple_of(at.z * 4 * rows, 4 * rows), 4 * rows)
-        self.own = pltpu.make_async_copy(x_ref, out_ref.at[spot], own_sem)
-
-    def where(self, f, zi):
-        rows = self.rows
-        return pl.ds(pl.multiple_of(self.at.shard(f * self.at.dy, zi) * rows, rows), rows)
-
-    def push(self, f, zi, slot, device, sends=None, record=None):
-        src = self.source if f == 0 and zi == 0 else self.out_ref.at[self.where(f, zi)]
-        dst = self.out_ref.at[self.where(f, zi)]
-        j = slot if sends is None else sends
-        remote(src, dst, self.send_sem.at[j], self.recv_sem.at[slot], device).start()
+        else:
+            spot = pl.ds(pl.multiple_of(at.shard(0, 0) * rows, rows), rows)
+        self.place = spot
+
+    def push(self, f, zi, p, slot, device, sends=None, record=None):
+        at, piece = self.at, self.piece
+        spot = at.shard(f * at.dy, zi) * self.rows + p * piece
+        dst = self.out_ref.at[pl.ds(pl.multiple_of(spot, piece), piece)]
+        src = dst
+        if f == 0 and zi == 0:
+            spot = (at.e * self.rows if self.block else 0) + p * piece
+            src = self.x_ref.at[pl.ds(pl.multiple_of(spot, piece), piece)]
+        j = (slot if sends is None else sends) * self.parts + p
+        k = slot * self.parts + p
+        remote(src, dst, self.send_sem.at[j], self.recv_sem.at[k], device).start()
         (self.started if record is None else record).append(j)
 
     def spot(self):
-        return self.x_ref.at[pl.ds(0, self.rows)], self.out_ref.at[pl.ds(0, self.rows)]
-
-    def arrive(self, slot):
-        remote(*self.spot(), self.send_sem.at[slot], self.recv_sem.at[slot], self.s_dev).wait_recv()
-
-    def forward(self, f, zi):
+        span = pl.ds(0, self.piece)
+        return self.x_ref.at[span], self.out_ref.at[span]
+
+    def arrive(self, slot, p):
+        k = slot * self.parts + p
+        remote(*self.spot(), self.send_sem.at[k], self.recv_sem.at[k], self.s_dev).wait_recv()
+
+    def forward(self, f, zi, p):
         if f == 0:
             if zi == 0:
-                self.push(0, 0, 0, self.z_dev)
+                self.push(0, 0, p, 0, self.z_dev)
             if zi < 2:
                 pl.when(self.at.middle)(
-                    lambda: self.push(0, zi, 1 + zi, self.at.inward(), 15 + zi, self.inside)
+                    lambda: self.push(0, zi, p, 1 + zi, self.at.inward(), 15 + zi, self.inside)
                 )
             else:
                 pl.when(self.at.middle)(
-                    lambda: self.push(0, zi, zi - 1, self.z_dev, 15 + zi, self.inside)
+                    lambda: self.push(0, zi, p, zi - 1, self.z_dev, 15 + zi, self.inside)
                 )
         if self.block and zi == 0:
             return
         if f == 0:
-            self.push(0, zi, 3 + zi, self.f_dev)
-        self.push(f, zi, 7 + f * 4 + zi, self.s_dev)
+            self.push(0, zi, p, 3 + zi, self.f_dev)
+        self.push(f, zi, p, 7 + f * 4 + zi, self.s_dev)
 
     def begin(self):
-        self.forward(0, 0)
-        self.own.start()
-
-    def line(self, zi):
-        self.arrive(zi - 1)
-        self.forward(0, zi)
-
-    def other(self, zi):
-        self.arrive(3 + zi)
-        self.forward(1, zi)
+        for p in range(self.parts):
+            self.forward(0, 0, p)
+        keep(self.x_ref, self.out_ref.at[self.place])
+
+    def step(self, zi):
+        for p in range(self.parts):
+            if zi < 4:
+                self.arrive(zi - 1, p)
+                self.forward(0, zi, p)
+            if zi > 1 or not self.block:
+                self.arrive(2 + zi, p)
+                self.forward(1, zi - 1, p)
 
     def twin(self, zi):
-        self.arrive(7 + zi)
-        self.arrive(11 + zi)
+        for p in range(self.parts):
+            self.arrive(7 + zi, p)
+            self.arrive(11 + zi, p)
 
     def finish(self, arrived=False):
         for zi in range(4):
             if not arrived and not (self.block and zi == 0):
                 self.twin(zi)
-        if not arrived:
-            self.own.wait()
+
+        def gone(j):
+            remote(*self.spot(), self.send_sem.at[j], self.recv_sem.at[0], self.s_dev).wait_send()
+
         for j in self.started:
-            remote(*self.spot(), self.send_sem.at[j], self.recv_sem.at[0], self.s_dev).wait_send()
+            gone(j)
 
         @pl.when(self.at.middle)
         def _():
             for j in self.inside:
-                remote(
-                    *self.spot(), self.send_sem.at[j], self.recv_sem.at[0], self.s_dev
-                ).wait_send()
+                gone(j)
 
 
 def columns_loop(width, parts):
@@ -954,15 +961,16 @@
         del refs[:count]
         return taken
 
-    x_ref, dy_ref, disp, w_router, shared_in, shared_out = take(6)
+    x_ref, dy_ref, disp, w_router, units = take(5)
     weights, given = take(7), take(2)
     out_ref, picked, picked_dy, scaled_out, g_out, u_out, gb_out, sa_out, sg_out = take(9)
-    taken = take(2)
+    taken, units_out = take(2), take(2)
+    shared_in, shared_out = take(2)
     wg, wu, wd, xb, dyd, sb, pk, pdy, sc, gg, uu, hid, gb, sa, sg = take(15)
-    own_sem, send_sem, recv_sem, load_sem, block_sem, store_sem, cross_send, cross_recv = take(8)
+    send_sem, recv_sem, load_sem, block_sem, store_sem, cross_send, cross_recv, unit_sem = take(8)
     at = Place()
     greet(at, False, True)
-    gather = Gather(at, x_ref, out_ref, own_sem, send_sem, recv_sem)
+    gather = Gather(at, x_ref, out_ref, send_sem, recv_sem)
     crossing = cross(at, given, taken, cross_send, cross_recv, (0, taken[0].shape[0]))
     block = xb.shape[1]
     slots = pk.shape[0] // 4
@@ -994,6 +1002,20 @@
         s = 1.0 / (1.0 + jnp.exp(-gate))
         act = gate * s
         return act * up, s * (1.0 + gate * (1.0 - s)) * up, act
+
+    cut, size = units.shape[1] // 3, units.shape[2]
+    wide = shared_out.shape[0]
+    unit_loads = []
+    for d in range(8):
+        for m in range(3):
+            ref, first = (shared_out, 0) if m == 2 else (shared_in, m * wide)
+            unit_loads.append(
+                pltpu.make_async_copy(
+                    units.at[d, pl.ds(m * cut, cut)],
+                    ref.at[pl.ds(first, cut), pl.ds(d * size, size)],
+                    unit_sem.at[d * 3 + m],
+                )
+            )
 
     def ahead(zi):
         b = zi % 2
@@ -1076,28 +1098,32 @@
         loads[j].start()
     for copy in crossing:
         copy.start()
+    shared_in[...] = jnp.zeros_like(shared_in)
+    shared_out[...] = jnp.zeros_like(shared_out)
+    for copy in unit_loads:
+        copy.start()
+    for copy in unit_loads:
+        copy.wait()
     loads[2].wait()
     for zi in range(3):
         ahead(zi)
     for zi in range(4):
-        gather.other(zi)
-        if zi < 3:
-            gather.line(zi + 1)
+        gather.step(zi + 1)
         if zi == 0:
             ahead(3)
         gather.twin(zi)
-        if zi == 0:
-            gather.own.wait()
         x_load(zi).start()
         if zi == 0:
             for j in (0, 1, 3, 4, 5, 6):
                 loads[j].wait()
         work(zi)
-    results = [(pk, picked), (pdy, picked_dy), (sc, scaled_out), (gg, g_out), (uu, u_out), (gb, gb_out)]
+    results = [(pk, picked), (pdy, picked_dy), (sc, scaled_out)]
+    results += [(shared_in, units_out[0]), (shared_out, units_out[1])]
+    results += [(gg, g_out), (uu, u_out), (gb, gb_out)]
     results = [
         pltpu.make_async_copy(a, b, store_sem.at[4 + j]) for j, (a, b) in enumerate(results)
     ]
-    for copy in results[:3]:
+    for copy in results[:5]:
         copy.start()
     for m in range(2):
         crossing[m].wait_recv()
@@ -1106,7 +1132,7 @@
         loads[7 + m].wait()
     for zi in range(4):
         other_half(zi)
-    for copy in results[3:]:
+    for copy in results[5:]:
         copy.start()
     for copy in results:
         copy.wait()
@@ -1118,12 +1144,11 @@
     gather.finish(True)
 
 
-def expert_rows(x, dy_all, dispatch, w_router, experts, shared_in, shared_out, weights, given, cid):
+def expert_rows(x, dy_all, dispatch, w_router, experts, units, wide, weights, given, cid):
     rows, width = x.shape
     total, block = 16 * rows, 4 * rows
     slots = 4 * dispatch.shape[1]
     hidden = weights[0].shape[0]
-    wide = shared_out.shape[0]
     halves = [half_of(a) for a in given]
     hbm, vmem = pl.BlockSpec(memory_space=pl.ANY), pl.BlockSpec(memory_space=pltpu.VMEM)
     shape, sems = jax.ShapeDtypeStruct, lambda n: pltpu.SemaphoreType.DMA((n,))
@@ -1140,10 +1165,14 @@
             shape((total, wide), BF),
             shape((total, 2 * wide), BF),
             *halves,
+            shape((2 * wide, width), BF),
+            shape((wide, width), BF),
         ],
-        in_specs=[hbm, hbm, vmem, vmem, vmem, vmem] + [hbm] * 9,
-        out_specs=[hbm] * 11,
+        in_specs=[hbm, hbm, vmem, vmem] + [hbm] * 10,
+        out_specs=[hbm] * 13,
         scratch_shapes=[
+            pltpu.VMEM((2 * wide, width), BF),
+            pltpu.VMEM((wide, width), BF),
             pltpu.VMEM((2, hidden, width), BF),
             pltpu.VMEM((2, hidden, width), BF),
             pltpu.VMEM((2, hidden, width), BF),
@@ -1159,19 +1188,19 @@
             pltpu.VMEM((slots, 128), F32),
             pltpu.VMEM((2, block, wide), BF),
             pltpu.VMEM((2, block, 2 * wide), BF),
-            pltpu.SemaphoreType.DMA,
-            sems(19),
-            sems(15),
+            sems(38),
+            sems(30),
             sems(9),
             sems(4),
-            sems(10),
+            sems(12),
             sems(2),
             sems(2),
+            sems(24),
         ],
         compiler_params=pltpu.CompilerParams(
             collective_id=cid, has_side_effects=True, vmem_limit_bytes=62 * 1024 * 1024
         ),
-    )(x, dy_all, dispatch, w_router, shared_in, shared_out, *weights, *given)
+    )(x, dy_all, dispatch, w_router, units, *weights, *given)
 
 
 def expert_scatter_kernel(*refs):
@@ -1270,7 +1299,7 @@
             total.to_twin(acc.at[total.held(f, zi, 1)], f, zi)
         total.first(zi)
         if zi == 1:
-            total.second(3)
+            total.second(3, "end")
     for copy in loads[9:]:
         copy.wait()
     for m, zi in ((0, 2), (1, 1), (2, 0)):
@@ -1278,6 +1307,8 @@
             stores[1].wait()
             stores[2].wait()
         gradient(m)
+        if m == 0:
+            total.second(3, "middle")
         if m == 0:
             crossing.start()
         for j in (2 * m, 2 * m + 1):
@@ -1456,23 +1487,25 @@
         total.first(zi)
     for j in range(4):
         heads_back(j)
-    firsts[3].wait()
-    total.second(3)
+    for m in (3, 2, 1, 0):
+        firsts[m].wait()
+    total.second(3, "end")
     dk[...] = jnp.zeros_like(dk)
     dv[...] = jnp.zeros_like(dv)
-    for i in range(3):
+    for i in range(5):
         attend_rows(i)
-    firsts[2].wait()
-    total.second(2)
-    for i in range(3, 6):
-        attend_rows(i)
-    firsts[1].wait()
-    total.second(1)
-    for i in range(6, 8):
+    total.second(3, "middle")
+    total.second(2, "end")
+    for i in range(5, 8):
         attend_rows(i)
     finish_heads()
-    for j in range(8):
+    for j in range(3):
         normed_rows(j)
+    total.second(2, "middle")
+    total.second(1, "end")
+    for j in range(3, 8):
+        normed_rows(j)
+    total.second(1, "middle")
     for j in range(4):
         qkv_rows(j)
     size = home_out.shape[2]
@@ -1480,7 +1513,6 @@
         columns = slice(j * size, (j + 1) * size)
         home_out[j, : 3 * HDIM, :] = qkv_sum[:, columns].astype(BF)
         home_out[j, 3 * HDIM :, :] = out_sum[:, columns].astype(BF)
-    firsts[0].wait()
     total.second(0)
     for j in (6, 7):
         normed_store(j).wait()
@@ -1540,10 +1572,10 @@
     scaled_ref, act_ref, sg_ref, wd_a, wd_0, wd_1, mix_ref, dy_ref, *given = take(10)
     out_ref, mixed_part, units_grad, *taken = take(5)
     scaled, acts, sg, wd, eb, mixes, dys, staged, turned, turned_acts = take(10)
-    own_sem, send_sem, recv_sem, cross_send, cross_recv, load_sem, store_sem = take(7)
+    send_sem, recv_sem, cross_send, cross_recv, load_sem, store_sem = take(6)
     at = Place()
     greet(at, False, True)
-    gather = Gather(at, x_ref, out_ref, own_sem, send_sem, recv_sem)
+    gather = Gather(at, x_ref, out_ref, send_sem, recv_sem)
     crossing = cross(at, given, taken, cross_send, cross_recv)
     rows, width = x_ref.shape
     slots = eb.shape[0]
@@ -1610,16 +1642,14 @@
     for copy in loads[:5]:
         copy.wait()
     for zi in range(4):
-        if zi > 0:
-            gather.line(zi)
         mixed_rows_of(zi)
         if zi == 0:
             for copy in loads[5:]:
                 copy.wait()
             turned[...] = sg[...].T
             turned_acts[...] = acts[...].T
-        gather.other(zi)
         units_of(2 * zi, 2)
+        gather.step(zi + 1)
     for j in (2, 3):
         mixed_store(j).wait()
     for copy in crossing:
@@ -1654,9 +1684,8 @@
             pltpu.VMEM((2, 4 * rows, width), BF),
             pltpu.VMEM((2 * units, length), BF),
             pltpu.VMEM((units, length), BF),
-            pltpu.SemaphoreType.DMA,
-            pltpu.SemaphoreType.DMA((19,)),
-            pltpu.SemaphoreType.DMA((15,)),
+            pltpu.SemaphoreType.DMA((38,)),
+            pltpu.SemaphoreType.DMA((30,)),
             pltpu.SemaphoreType.DMA((2,)),
             pltpu.SemaphoreType.DMA((2,)),
             pltpu.SemaphoreType.DMA((8,)),
@@ -1741,18 +1770,19 @@
 
 
 class Share:
-    def __init__(self, at, ref, out, own_sem, send_sem, recv_sem):
+    def __init__(self, at, ref, out, send_sem, recv_sem):
         self.at, rows = at, ref.shape[0]
         spot = lambda oe: out.at[pl.ds(pl.multiple_of((at.e + oe) * rows, rows), rows)]
         f_dev, s_dev = at.device(oe=at.dy), at.device(oe=at.dc)
-        self.local = pltpu.make_async_copy(ref, spot(0), own_sem)
+        self.ref, self.place = ref, spot(0)
         self.far = remote(ref, spot(0), send_sem.at[0], recv_sem.at[0], f_dev)
         self.near = remote(ref, spot(0), send_sem.at[1], recv_sem.at[1], s_dev)
         self.over = remote(spot(at.dy), spot(at.dy), send_sem.at[2], recv_sem.at[2], s_dev)
 
     def start(self):
-        for copy in (self.far, self.near, self.local):
+        for copy in (self.far, self.near):
             copy.start()
+        keep(self.ref, self.place)
 
     def forward(self):
         self.far.wait_recv()
@@ -1762,7 +1792,6 @@
         self.far.wait_send()
         self.near.wait()
         self.over.wait()
-        self.local.wait()
 
 
 def last_scatter_kernel(*refs):
@@ -1781,7 +1810,7 @@
     mine, got = take(3), take(3)
     buffers = take(6)
     first_sem, cross_send, cross_recv, load_sem, store_sem = take(5)
-    home_sems, share_sems = take(5), take(3)
+    home_sems, share_sems = take(5), take(2)
     at = Place()
     greet(at, True)
     total = Scatter(at, *buffers, out_ref)
@@ -1825,15 +1854,17 @@
         ref = (grad_gate, grad_up, grad_down)[m]
         return pltpu.make_async_copy(grad.at[m % 2], ref, store_sem.at[m])
 
-    def gradient(m):
+    def gradient(m, half=None):
         turned[...] = left[m].T
+        span = slice(None) if half is None else pl.ds(half * part, part)
 
         @columns_loop(width, 8)
         def _(columns):
-            terms = product(turned[...], right[m // 2, :, columns])
-            grad[m % 2, :, columns] = terms + other[m % 2, :, columns].astype(F32)
-
-        store(m).start()
+            terms = product(turned[span, :], right[m // 2, :, columns])
+            grad[m % 2, span, columns] = terms + other[m % 2, span, columns].astype(F32)
+
+        if half != 0:
+            store(m).start()
 
     for zi in (3, 2, 1, 0):
         firsts[4 + zi].wait()
@@ -1841,28 +1872,30 @@
     sharing.start()
     for copy in loads[:9]:
         copy.wait()
+    for m in (3, 2, 1, 0):
+        firsts[m].wait()
     gradient(0)
     loads[9].start()
+    total.second(3, "end")
     home.line(3)
-    firsts[3].wait()
-    total.second(3)
+    total.second(3, "middle")
+    total.second(2, "end")
+    home.line(2)
     gradient(1)
-    home.line(2)
-    firsts[2].wait()
-    total.second(2)
+    total.second(2, "middle")
+    total.second(1, "end")
     home.line(1)
-    firsts[1].wait()
-    total.second(1)
+    total.second(1, "middle")
     home.line(0)
     sharing.forward()
+    loads[9].wait()
+    store(0).wait()
+    gradient(2, 0)
+    total.second(0)
     crossing.wait_recv()
     loads[10].start()
-    loads[9].wait()
     loads[10].wait()
-    store(0).wait()
-    gradient(2)
-    firsts[0].wait()
-    total.second(0)
+    gradient(2, 1)
     home.finish()
     sharing.finish()
     store(1).wait()
@@ -1905,7 +1938,6 @@
             sems(12),
             sems(9),
             sems(12),
-            pltpu.SemaphoreType.DMA,
             sems(3),
             sems(3),
         ],
@@ -1917,8 +1949,8 @@
 
 def end_kernel(tokens_ref, gain_ref, small_ref, out_ref, gain_out, small_out, *scratch):
     gain_got, gain_sum, gain_all, small_all = scratch[:4]
-    share_sems = scratch[4:7]
-    gain_send, gain_recv, sum_send, sum_recv, small_send, small_recv = scratch[7:]
+    share_sems = scratch[4:6]
+    gain_send, gain_recv, sum_send, sum_recv, small_send, small_recv = scratch[6:]
     at = Place()
     barrier = pltpu.get_barrier_semaphore()
     blocks = [(at.device(ox=ox, zi=k), m * 4 + k) for m, ox in enumerate((0, at.dx)) for k in range(4)]
@@ -1988,7 +2020,6 @@
             pltpu.VMEM(gain_part.shape[1:], F32),
             pltpu.VMEM((3,) + gain_part.shape[1:], F32),
             pltpu.VMEM((3,) + small.shape, F32),
-            pltpu.SemaphoreType.DMA,
             sems(3),
             sems(3),
             sems(8),
@@ -2010,15 +2041,16 @@
         del refs[:count]
         return taken
 
-    dy_ref, tokens_ref, units, given, gain, w_qkv, w_out, tables = take(8)
+    dy_ref, tokens_ref, units, given, gain, w_qkv, w_out_blocks, tables = take(8)
     dy_out, units_out, taken, normed_out, part_out, q_out, k_out, v_out, heads_out, lse_out = take(10)
+    w_out, w_qkv_turned = take(2)
     rows_in, normed, staged = take(3)
-    own_sem, send_sem, recv_sem, local_sem, swap_send, swap_recv = take(6)
+    send_sem, recv_sem, swap_send, swap_recv = take(4)
     cross_send, cross_recv, in_sem, normed_sem, part_sem = take(5)
     at = Place()
     greet(at, True)
-    gather = Gather(at, dy_ref, dy_out, own_sem, send_sem, recv_sem, True)
-    swap_in = Exchange(at, [units], [units_out], local_sem, swap_send, swap_recv)
+    gather = Gather(at, dy_ref, dy_out, send_sem, recv_sem, True)
+    swap_in = Exchange(at, [units], [units_out], swap_send, swap_recv)
     crossing = cross(at, [given], [taken], cross_send, cross_recv, (taken.shape[0],))[0]
     length, width = tokens_ref.shape
     block = length // 4
@@ -2088,31 +2120,35 @@
         part_store(i).start()
 
     gather.begin()
+    for zi in (1, 2, 3):
+        swap_in.along(zi)
     swap_in.start()
     crossing.start()
     rows_load(0).start()
     rows_load(1).start()
+    size = w_out_blocks.shape[2]
+    for d in range(8):
+        w_out[:, d * size : (d + 1) * size] = w_out_blocks[d]
+    w_qkv_turned[...] = w_qkv[...].T
     project(0)
     project(1)
     attend_rows(0)
-    gather.line(1)
-    swap_in.forward(1)
+    gather.step(1)
     project(2)
     attend_rows(1)
     attend_rows(2)
-    gather.other(1)
-    gather.line(2)
-    swap_in.forward(2)
+    gather.step(2)
+    swap_in.forward(1)
     project(3)
     attend_rows(3)
     attend_rows(4)
-    gather.other(2)
-    gather.line(3)
-    swap_in.forward(3)
+    gather.step(3)
+    swap_in.forward(2)
     attend_rows(5)
     attend_rows(6)
     attend_rows(7)
-    gather.other(3)
+    gather.step(4)
+    swap_in.forward(3)
     for j in (2, 3):
         normed_store(j).wait()
     for i in (6, 7):
@@ -2136,17 +2172,17 @@
             shape((length, width), BF),
             *[shape((length, HDIM), BF)] * 4,
             shape((length, HDIM), F32),
+            shape((HDIM, width), BF),
+            shape((3 * HDIM, width), BF),
         ],
         in_specs=[hbm] * 4 + [vmem] * 4,
-        out_specs=[hbm] * 5 + [vmem] * 5,
+        out_specs=[hbm] * 5 + [vmem] * 7,
         scratch_shapes=[
             pltpu.VMEM((2, length // 4, width), BF),
             pltpu.VMEM((2, length // 4, width), BF),
             pltpu.VMEM((2, 256, width), BF),
-            pltpu.SemaphoreType.DMA,
-            sems(19),
-            sems(15),
-            sems(1),
+            sems(38),
+            sems(30),
             sems(7),
             sems(8),
             sems(1),
@@ -2227,27 +2263,22 @@
     mixer_gain = early_little[experts + 1].reshape(width).astype(F32)
     hits = early_little[experts + 2 : experts + 4].transpose(1, 0, 2).reshape(2, length)
     hits = lax.dynamic_index_in_dim(hits, dp, 0, False).astype(F32).reshape(groups, quarter)
-    w_out_head = early_out.transpose(1, 0, 2).reshape(HDIM, width)
 
     cosine, sine = turn_tables(length)
     tables = np.stack(
         [np.concatenate([cosine, cosine], axis=1), np.concatenate([sine, -sine], axis=1)]
     )
-    dy_all, late, gate_1, normed, attn_part, query, key, value, heads_out, lse = front(
+    dy_all, late, gate_1, normed, attn_part, query, key, value, heads_out, lse, w_out_head, w_qkv_turned = front(
         out_grad[0],
         tokens_all,
         sent_units,
         own_gate,
         jnp.broadcast_to(attention_gain[None], (8, width)),
         w_qkv,
-        w_out_head,
+        early_out,
         tables,
         2,
     )
-    late = late.transpose(1, 0, 2).reshape(3, cut, width)
-    late = jnp.pad(late, ((0, 0), (0, wide - cut), (0, 0)))
-    shared_in = late[:2].reshape(2 * wide, width)
-    shared_out = late[2]
     attn, up_0, up_1 = own_rows(attn_part, 3, (own_up, own_up), (0, part))
     middle = tokens_own.astype(F32) + attn
     normed_own = rms_scale(middle, mixer_gain).astype(BF)
@@ -2271,14 +2302,16 @@
         shared_gu_back,
         down_0,
         down_1,
+        shared_in,
+        shared_out,
     ) = expert_rows(
         normed_own,
         dy_all,
         blocks,
         router_wide,
         experts,
-        shared_in,
-        shared_out,
+        late,
+        wide,
         (own_gate, own_up, own_down, gate_0, gate_1, up_0, up_1),
         (own_down, own_down),
         4,
@@ -2328,7 +2361,7 @@
     )
     mixed_sum, normed_part, head_part, up_1, down_0 = mixed_rows(
         w_out_head,
-        w_qkv.T,
+        w_qkv_turned,
         tables,
         query,
         key,

time: 749 us -> 709 us (0.947)
  Pallas kernels: 670 us -> 644 us
  local copies, waits for them, and re-layouts: 50.7 us -> 35.7 us
    pallas_call x1, Pallas kernels: 85.9 us -> 70.2 us  [gather_back(): pl.pallas_call(gather_back_kernel, out_shape=[shape((length, width), BF),...]
    pallas_call x1, Pallas kernels: 20.2 us -> 28.6 us  [end(): pl.pallas_call(end_kernel, out_shape=[shape((4 * rows, width), tokens_own...]
    reshape x3 -> x0, local copies, waits for them, and re-layouts: 7.62 us -> none  [the longest x1 3.49 us: fast_body(): late = late.transpose(1, 0, 2).reshape(3, cut, width)]
    unnamed x64 -> x62, local copies, waits for them, and re-layouts: 24.6 us -> 23.6 us
where the time goes in v6:
time: 709 us; the launch traced here: 704 us
  Pallas kernels  644 us (91%)
  local copies, waits for them, and re-layouts  35.7 us (5%)
  other arithmetic  19.4 us (3%)
    pallas_call x1, Pallas kernels, last_rows(): pl.pallas_call(last_scatter_kernel, out_shape=[shape((rows, width), F32),...  90.7 us
    pallas_call x1, Pallas kernels, expert_back(): pl.pallas_call(expert_scatter_kernel, out_shape=[shape((rows, full), F32)...  89.4 us
    pallas_call x1, Pallas kernels, expert_rows(): pl.pallas_call(functools.partial(expert_gather_kernel, experts), out_shap...  83.4 us
    pallas_call x1, Pallas kernels, front(): pl.pallas_call(functools.partial(front_kernel, HDIM ** (-0.5)), out_shape...  73.5 us
    pallas_call x1, Pallas kernels, all_rows(): pl.pallas_call(functools.partial(gather_kernel, block, rows, parts, extra...  73.3 us
    pallas_call x1, Pallas kernels, gather_back(): pl.pallas_call(gather_back_kernel, out_shape=[shape((length, width), BF),...  70.2 us
    pallas_call x1, Pallas kernels, mixed_rows(): pl.pallas_call(mixed_kernel, out_shape=[shape((rows, width), F32), shape(...  69.7 us
    pallas_call x1, Pallas kernels, own_rows(): pl.pallas_call(functools.partial(scatter_kernel, rows, starts), out_shape...  65.1 us

profile of v6, /device:TPU:0, one launch (start us, length us, event | category | flops | bytes accessed | tf_op | source)
XLA Modules:
  0.0 704.1 jit_solution(9759628252611163620)
XLA Ops:
  9.4 73.3 %shard_map.280 = (bf16[2048,2048]{1,0:T(8,128)(2,1)}, bf16[8,256,384]{2,1,0:T(8,128)(2,1)}, bf16[8,128,256]{2,1,0:T(8,128)(2,1)}, bf16[8,32,256]{2,1,0:T(8,128)(2,1)}, bf16[352,2048]{1,0:T(8,128)(2,1)}) custom-call(bf16[512,2048]{1,0:T(8,128)(2,1)} %bitcast.123, bf16[4,256,384]{2,1,0:T(8,128)(2,1)} %pad_maximum_fusion.1.refs_1_, ...), custom_call_target="tpu_custom_call" | custom-call | tf_op jit(solution)/shard_map/pallas_call | solution.py:659
  88.3 73.5 %shard_map.281 = (bf16[2048,2048]{1,0:T(8,128)(2,1)}, bf16[8,528,256]{2,1,0:T(8,128)(2,1)}, bf16[352,2048]{1,0:T(8,128)(2,1)}, bf16[2048,2048]{1,0:T(8,128)(2,1)...) custom-call(bf16[512,2048]{1,0:T(8,128)(2,1)} %bitcast.133, ...), custom_call_target="tpu_custom_call" | custom-call | tf_op jit(solution)/shard_map/pallas_call | solution.py:2165
  161.7 65.1 %shard_map.282 = (f32[128,2048]{1,0:T(8,128)S(1)}, bf16[352,2048]{1,0:T(8,128)(2,1)S(1)}, bf16[352,2048]{1,0:T(8,128)(2,1)S(1)}) custom-call(bf16[2048,2048]{1,0:T(8,128)(2,1)} %get-tuple-element.87.in_ref, bf16[704,2048]{1,0:T(8,128)(2,1)S(1)} %bitcast.113, bf16[704,2048]{1,0:T(8,128)(2,1)S(1)} %bitcast.114), custom_call_target="tpu_custom_call" | custom-call | tf_op jit(solution)/shard_map/pallas_call | solution.py:832
  226.9 1.7 multiply_reduce_fusion.2
  229.9 83.4 %shard_map.283 = (bf16[2048,2048]{1,0:T(8,128)(2,1)}, bf16[1024,2048]{1,0:T(8,128)(2,1)}, bf16[1024,2048]{1,0:T(8,128)(2,1)}, bf16[2,1024,704]{2,1,0:T(8,128)(2,...) custom-call(bf16[128,2048]{1,0:T(8,128)(2,1)} %copy-done.6, ...), custom_call_target="tpu_custom_call" | custom-call | tf_op jit(solution)/shard_map/pallas_call | solution.py:1155
  313.4 89.4 %shard_map.284 = (f32[128,2176]{1,0:T(8,128)}, bf16[352,2048]{1,0:T(8,128)(2,1)}, bf16[352,2048]{1,0:T(8,128)(2,1)}, bf16[352,2048]{1,0:T(8,128)(2,1)}, bf16[352...) custom-call(bf16[4,256,512]{2,1,0:T(8,128)(2,1)} %compare_convert_fusion.refs_2_.refs_0_.refs_1_, ...), custom_call_target="tpu_custom_call" | custom-call | tf_op jit(solution)/shard_map/pallas_call | solution.py:1332
  405.0 2.1 multiply_reduce_fusion
  408.2 2.2 fusion.23.refs_0_
  410.4 70.2 %shard_map.285 = (bf16[2048,2048]{1,0:T(8,128)(2,1)}, bf16[2048,2048]{1,0:T(8,128)(2,1)}, bf16[8,528,256]{2,1,0:T(8,128)(2,1)}, bf16[352,2048]{1,0:T(8,128)(2,1)}, bf16[352,2048]{1,0:T(8,128)(2,1)}) custom-call(bf16[128,2048]{1,0:T(8,128)(2,1)} %fusion.23.refs_0_, bf16[4,256,512]{2,1,0:T(8,128)(2,1)} %compare_convert_fusion.refs_2_.refs_0_.refs_1_, ...), custom_call_target="tpu_custom_call" | custom-call | tf_op jit(solution)/shard_map/pallas_call | solution.py:1666
  480.6 69.7 %shard_map.286 = (f32[128,2048]{1,0:T(8,128)}, bf16[2048,2048]{1,0:T(8,128)(2,1)}, bf16[8,512,256]{2,1,0:T(8,128)(2,1)}, bf16[352,2048]{1,0:T(8,128)(2,1)}, bf16[352,2048]{1,0:T(8,128)(2,1)}) custom-call(bf16[128,2048]{1,0:T(8,128)(2,1)} %get-tuple-element.80.refs_0_, bf16[384,2048]{1,0:T(8,128)(2,1)} %get-tuple-element.81.refs_1_, ...), custom_call_target="tpu_custom_call" | custom-call | tf_op jit(solution)/shard_map/pallas_call | solution.py:1531
  550.3 2.5 add_convert_fusion.refs_6_
  552.8 90.7 %shard_map.287 = (f32[128,2048]{1,0:T(8,128)}, bf16[352,2048]{1,0:T(8,128)(2,1)}, f32[704,2048]{1,0:T(8,128)}, f32[704,2048]{1,0:T(8,128)}, f32[704,2048]{1,0:T(...) custom-call(bf16[2048,2048]{1,0:T(8,128)(2,1)} %get-tuple-element.11, ...), custom_call_target="tpu_custom_call" | custom-call | tf_op jit(solution)/shard_map/pallas_call | solution.py:1912
  643.5 1.9 fusion.6
  645.5 3.0 fusion.2.tokens_ref
  649.8 28.6 %shard_map.288 = (bf16[512,2048]{1,0:T(8,128)(2,1)}, f32[8,256]{1,0:T(8,128)}, f32[32,256]{1,0:T(8,128)}) custom-call(bf16[128,2048]{1,0:T(8,128)(2,1)} %fusion.2.tokens_ref, f32[8,8,256]{2,1,0:T(8,128)} %pad.19.gain_ref, f32[32,256]{1,0:T(8,128)} %convert_reduce_fusion.small_ref), custom_call_target="tpu_custom_call" | custom-call | tf_op jit(solution)/shard_map/pallas_call | solution.py:2009
  678.3 1.3 slice.54
  680.9 1.3 slice_bitcast_fusion.1
  684.4 2.2 copy.68
  687.5 1.4 fusion.24
  688.9 3.9 copy.84
  692.9 1.3 copy.85
  694.2 2.9 copy.86
  697.2 2.9 copy.87
  701.1 2.5 copy.88
  (104 shorter events, 25.5 us)
Async XLA Ops:
  0.6 6.3 copy-start.16
  5.4 2.9 copy-start.13
  5.4 2.9 copy-start.14
  5.4 2.9 copy-start.15
  88.3 73.5 %copy-start = (bf16[1,2048,704]{1,2,0:T(8,128)(2,1)S(1)}, bf16[1,2048,704]{1,2,0:T(8,128)(2,1)}, u32[]{:S(2)}) copy-start(bf16[1,2048,704]{1,2,0:T(8,128)(2,1)} %param.30) | copy-start | bytes 8650756
  226.9 1.9 copy-start.1
  226.9 1.9 copy-start.2
  228.6 1.0 copy-start.3
  228.8 1.1 copy-start.6
  313.3 90.5 %copy-start.7 = (bf16[128,2048]{1,0:T(8,128)(2,1)S(1)}, bf16[128,2048]{1,0:T(8,128)(2,1)}, u32[]{:S(2)}) copy-start(bf16[128,2048]{1,0:T(8,128)(2,1)} %copy-done.6) | copy-start | bytes 1572868
  402.8 5.4 copy-start.4
  407.2 1.0 copy-start.10
  552.8 92.6 %copy-start.11 = (f32[128,2048]{1,0:T(8,128)S(1)}, f32[128,2048]{1,0:T(8,128)}, u32[]{:S(2)}) copy-start(f32[128,2048]{1,0:T(8,128)} %copy-done.10) | copy-start | bytes 3145732
  643.5 1.9 copy-start.5
  645.4 3.1 copy-start.17
  645.4 36.8 %copy-start.9 = (bf16[4,512,256]{2,1,0:T(8,128)(2,1)S(1)}, bf16[4,512,256]{2,1,0:T(8,128)(2,1)}, u32[]{:S(2)}) copy-start(bf16[4,512,256]{2,1,0:T(8,128)(2,1)} %get-tuple-element.131) | copy-start | bytes 3145732
  683.4 4.2 copy-start.8
  684.4 9.8 %slice-start.4 = ((s8[5767168]{0:T(1024)(128)(4,1)}), s8[1572864]{0:T(1024)(128)(4,1)S(1)}, s32[]{:S(2)}) async-start(s8[5767168]{0:T(1024)(128)(4,1)} %bitcast.130), calls=%async_computation.4 | async-start | bytes 3145728
  687.5 5.3 copy-start.12
  687.5 9.6 %slice-start.2 = ((s8[5767168]{0:T(1024)(128)(4,1)}), s8[4194304]{0:T(1024)(128)(4,1)S(1)}, s32[]{:S(2)}) async-start(s8[5767168]{0:T(1024)(128)(4,1)} %bitcast.127), calls=%async_computation.2 | async-start | bytes 8388608
  688.9 5.3 slice-start.5
  692.9 4.3 slice-start.3
  694.2 5.8 slice-start
  697.2 4.0 slice-start.1

commit v7 on v6

--- a/solution.py
+++ b/solution.py
@@ -678,42 +678,43 @@
             at.device(oe=at.dc),
             at.device(zi=1),
         )
-        self.twins = [[], [], [], []]
         self.started, self.in_middle, self.at_end = [], [], []
 
     def held(self, f, zi, twin=0):
         at = self.at
         return zi * 4 + at.e + f * at.dy + twin * at.dc if self.by_block else f * 4 + zi
 
-    def push(self, src, dst, slot, device, sends=None, record=None):
-        j = slot if sends is None else sends
-        remote(src, dst, self.send_sem.at[j], self.recv_sem.at[slot], device).start()
+    def span(self, p):
+        size = self.rows // 2
+        return pl.ds(p * size, size)
+
+    def push(self, src, dst, slot, p, device, sends=None, record=None):
+        j = (slot if sends is None else sends) * 2 + p
+        src, dst = src.at[self.span(p)], dst.at[self.span(p)]
+        remote(src, dst, self.send_sem.at[j], self.recv_sem.at[slot * 2 + p], device).start()
         (self.started if record is None else record).append(j)
 
     def gone(self, j):
-        spot = self.acc.at[0]
+        spot = self.acc.at[0, self.span(0)]
         remote(spot, spot, self.send_sem.at[j], self.recv_sem.at[0], self.s_dev).wait_send()
 
-    def arrive(self, dst, slot):
-        remote(
-            self.acc.at[0], dst, self.send_sem.at[slot], self.recv_sem.at[slot], self.s_dev
-        ).wait_recv()
+    def arrive(self, dst, slot, p):
+        j, dst = slot * 2 + p, dst.at[self.span(p)]
+        src = self.acc.at[0, self.span(p)]
+        remote(src, dst, self.send_sem.at[j], self.recv_sem.at[j], self.s_dev).wait_recv()
 
     def to_twin(self, src, f, zi):
         k = f * 4 + zi
-        self.push(src, self.got_s.at[k], 9 + k, self.s_dev, None, self.twins[zi])
-
-    def twin_gone(self, zi):
-        for j in self.twins[zi]:
-            self.gone(j)
-        self.twins[zi] = []
-
-    def add(self, k, *others, into=None):
+        for p in range(2):
+            self.push(src, self.got_s.at[k], 9 + k, p, self.s_dev)
+
+    def add(self, k, p, *others, into=None):
         acc = self.acc
-
-        @pl.loop(0, self.rows // 16)
+        size = self.rows // 2
+
+        @pl.loop(0, size // 16)
         def _(i):
-            span = pl.ds(pl.multiple_of(i * 16, 16), 16)
+            span = pl.ds(pl.multiple_of(p * size + i * 16, 16), 16)
             total = acc[k, span, :].astype(F32)
             for ref, j in others:
                 total = total + ref[j, span, :].astype(F32)
@@ -724,9 +725,10 @@
 
     def first(self, zi):
         k = self.held(1, zi)
-        self.arrive(self.got_s.at[4 + zi], 13 + zi)
-        self.add(k, (self.got_s, 4 + zi))
-        self.push(self.acc.at[k], self.got_f.at[zi], 5 + zi, self.f_dev)
+        for p in range(2):
+            self.arrive(self.got_s.at[4 + zi], 13 + zi, p)
+            self.add(k, p, (self.got_s, 4 + zi))
+            self.push(self.acc.at[k], self.got_f.at[zi], 5 + zi, p, self.f_dev)
 
     def second(self, zi, who="all"):
         if who != "middle":
@@ -734,39 +736,39 @@
         if who != "end":
             pl.when(self.at.middle)(lambda: self.from_middle(zi))
 
-    def terms(self, zi):
-        self.arrive(self.got_s.at[zi], 9 + zi)
-        self.arrive(self.got_f.at[zi], 5 + zi)
+    def terms(self, zi, p):
+        self.arrive(self.got_s.at[zi], 9 + zi, p)
+        self.arrive(self.got_f.at[zi], 5 + zi, p)
         return self.held(0, zi), [(self.got_s, zi), (self.got_f, zi)]
 
     def from_end(self, zi):
-        k, others = self.terms(zi)
         acc, got_z = self.acc, self.got_z
-        if zi == 0:
-            self.arrive(got_z.at[4], 4)
-            self.add(k, *others, (got_z, 4), into=self.out_ref)
-            return
-        self.add(k, *others)
-        self.push(acc.at[k], got_z.at[3 - zi], 3 - zi, self.z_dev, zi, self.at_end)
+        for p in range(2):
+            k, others = self.terms(zi, p)
+            if zi == 0:
+                self.arrive(got_z.at[4], 4, p)
+                self.add(k, p, *others, (got_z, 4), into=self.out_ref)
+                continue
+            self.add(k, p, *others)
+            self.push(acc.at[k], got_z.at[3 - zi], 3 - zi, p, self.z_dev, zi, self.at_end)
 
     def from_middle(self, zi):
-        k, others = self.terms(zi)
         acc, got_z = self.acc, self.got_z
-        if zi == 0:
-            self.arrive(got_z.at[2], 2)
-            self.arrive(got_z.at[4], 4)
-            self.add(k, *others, (got_z, 2), (got_z, 4), into=self.out_ref)
-            return
-        came = 3 if zi == 1 else 3 - zi
-        self.arrive(got_z.at[came], came)
-        self.add(k, *others, (got_z, came))
-        there = 3 if zi == 3 else 4
-        device = self.z_dev if zi == 1 else self.at.inward()
-        self.push(acc.at[k], got_z.at[there], there, device, zi, self.in_middle)
+        for p in range(2):
+            k, others = self.terms(zi, p)
+            if zi == 0:
+                self.arrive(got_z.at[2], 2, p)
+                self.arrive(got_z.at[4], 4, p)
+                self.add(k, p, *others, (got_z, 2), (got_z, 4), into=self.out_ref)
+                continue
+            came = 3 if zi == 1 else 3 - zi
+            self.arrive(got_z.at[came], came, p)
+            self.add(k, p, *others, (got_z, came))
+            there = 3 if zi == 3 else 4
+            device = self.z_dev if zi == 1 else self.at.inward()
+            self.push(acc.at[k], got_z.at[there], there, p, device, zi, self.in_middle)
 
     def finish(self):
-        for zi in range(4):
-            self.twin_gone(zi)
         for j in self.started:
             self.gone(j)
 
@@ -787,8 +789,8 @@
         pltpu.VMEM((8, rows, width), BF),
         pltpu.VMEM((4, rows, width), BF),
         pltpu.VMEM((5, rows, width), BF),
-        pltpu.SemaphoreType.DMA((17,)),
-        pltpu.SemaphoreType.DMA((17,)),
+        pltpu.SemaphoreType.DMA((34,)),
+        pltpu.SemaphoreType.DMA((34,)),
     ]
 
 
@@ -805,6 +807,8 @@
     def rows_of(rank):
         return in_ref.at[pl.ds(pl.multiple_of(rank * rows, rows), rows)]
 
+    for copy in crossing:
+        copy.start()
     order = [(f, zi) for f in (1, 0) for zi in (3, 2, 1, 0)]
     loads = {}
     for f, zi in order:
@@ -814,8 +818,6 @@
             rows_of(at.shard(f * at.dy, zi)), acc.at[k], load_sem.at[k]
         )
         loads[k].start()
-    for copy in crossing:
-        copy.start()
     for f, zi in order:
         loads[f * 4 + zi].wait()
         (total.first if f else total.second)(zi)
@@ -969,7 +971,6 @@
     wg, wu, wd, xb, dyd, sb, pk, pdy, sc, gg, uu, hid, gb, sa, sg = take(15)
     send_sem, recv_sem, load_sem, block_sem, store_sem, cross_send, cross_recv, unit_sem = take(8)
     at = Place()
-    greet(at, False, True)
     gather = Gather(at, x_ref, out_ref, send_sem, recv_sem)
     crossing = cross(at, given, taken, cross_send, cross_recv, (0, taken[0].shape[0]))
     block = xb.shape[1]
@@ -1077,7 +1078,6 @@
             jnp.sum(hid[some, :].astype(F32) * dy_down, axis=1, keepdims=True), (slots, gb.shape[1])
         )
 
-    gather.begin()
     places = [
         wg.at[0],
         wu.at[0],
@@ -1096,12 +1096,14 @@
     dy_load(1).start()
     for j in (2, 0, 1, 3, 4, 5, 6):
         loads[j].start()
-    for copy in crossing:
-        copy.start()
     shared_in[...] = jnp.zeros_like(shared_in)
     shared_out[...] = jnp.zeros_like(shared_out)
     for copy in unit_loads:
         copy.start()
+    greet(at, False, True)
+    for copy in crossing:
+        copy.start()
+    gather.begin()
     for copy in unit_loads:
         copy.wait()
     loads[2].wait()
@@ -1218,7 +1220,6 @@
     acc, got_s, got_f, got_z, send_sem, recv_sem = take(6)
     load_sem, store_sem, cross_send, cross_recv = take(4)
     at = Place()
-    greet(at, False, True)
     rows, full = acc.shape[1:]
     width = shared_in.shape[1]
     slots = ib.shape[0]
@@ -1245,6 +1246,7 @@
     loads = [pltpu.make_async_copy(a, b, load_sem.at[j]) for j, (a, b) in enumerate(pairs)]
     for copy in loads:
         copy.start()
+    greet(at, False, True)
 
     def work(zi):
         place = at.zs[zi]
@@ -1376,7 +1378,6 @@
     buffers = take(6)
     first_sem, in_sem, store_sem, cross_send, cross_recv = take(5)
     at = Place()
-    greet(at, False, True)
     total = Scatter(at, *buffers, out_ref)
     acc = buffers[0]
     rows, width = acc.shape[1:]
@@ -1387,6 +1388,17 @@
     def rows_of(rank):
         return in_ref.at[pl.ds(pl.multiple_of(rank * rows, rows), rows)]
 
+    def rows_load(j):
+        ref = back_ref if j < 4 else normed_ref
+        return pltpu.make_async_copy(
+            ref.at[pl.ds(j % 4 * block, block)], rows_in.at[j % 2], in_sem.at[j % 2]
+        )
+
+    rows_load(0).start()
+    rows_load(1).start()
+    greet(at, False, True)
+    for copy in crossing:
+        copy.start()
     order = [(f, zi) for f in (1, 0) for zi in (3, 2, 1, 0)]
     firsts = {}
     for f, zi in order:
@@ -1396,17 +1408,6 @@
             rows_of(at.shard(f * at.dy, zi)), acc.at[m], first_sem.at[m]
         )
         firsts[m].start()
-    for copy in crossing:
-        copy.start()
-
-    def rows_load(j):
-        ref = back_ref if j < 4 else normed_ref
-        return pltpu.make_async_copy(
-            ref.at[pl.ds(j % 4 * block, block)], rows_in.at[j % 2], in_sem.at[j % 2]
-        )
-
-    rows_load(0).start()
-    rows_load(1).start()
 
     def heads_back(j):
         rows_load(j).wait()
@@ -1574,7 +1575,6 @@
     scaled, acts, sg, wd, eb, mixes, dys, staged, turned, turned_acts = take(10)
     send_sem, recv_sem, cross_send, cross_recv, load_sem, store_sem = take(6)
     at = Place()
-    greet(at, False, True)
     gather = Gather(at, x_ref, out_ref, send_sem, recv_sem)
     crossing = cross(at, given, taken, cross_send, cross_recv)
     rows, width = x_ref.shape
@@ -1584,9 +1584,6 @@
     cut = units_grad.shape[1] // 3
     over = columns_loop(width, 4)
 
-    gather.begin()
-    for copy in crossing:
-        copy.start()
     pairs = [
         (scaled_ref, scaled),
         (act_ref, acts),
@@ -1600,6 +1597,10 @@
     loads = [pltpu.make_async_copy(a, b, load_sem.at[j]) for j, (a, b) in enumerate(pairs)]
     for copy in loads:
         copy.start()
+    greet(at, False, True)
+    for copy in crossing:
+        copy.start()
+    gather.begin()
 
     def mixed_store(j):
         return pltpu.make_async_copy(

time: 709 us -> 699 us (0.986)
  Pallas kernels: 644 us -> 635 us
where the time goes in v7:
time: 699 us; the launch traced here: 695 us
  Pallas kernels  635 us (91%)
  local copies, waits for them, and re-layouts  35.7 us (5%)
  other arithmetic  19.4 us (3%)
    pallas_call x1, Pallas kernels, last_rows(): pl.pallas_call(last_scatter_kernel, out_shape=[shape((rows, width), F32),...  91.7 us
    pallas_call x1, Pallas kernels, expert_back(): pl.pallas_call(expert_scatter_kernel, out_shape=[shape((rows, full), F32)...  84.6 us
    pallas_call x1, Pallas kernels, expert_rows(): pl.pallas_call(functools.partial(expert_gather_kernel, experts), out_shap...  82.8 us
    pallas_call x1, Pallas kernels, front(): pl.pallas_call(functools.partial(front_kernel, HDIM ** (-0.5)), out_shape...  73.5 us
    pallas_call x1, Pallas kernels, all_rows(): pl.pallas_call(functools.partial(gather_kernel, block, rows, parts, extra...  73.3 us
    pallas_call x1, Pallas kernels, mixed_rows(): pl.pallas_call(mixed_kernel, out_shape=[shape((rows, width), F32), shape(...  69.6 us
    pallas_call x1, Pallas kernels, gather_back(): pl.pallas_call(gather_back_kernel, out_shape=[shape((length, width), BF),...  69 us
    pallas_call x1, Pallas kernels, own_rows(): pl.pallas_call(functools.partial(scatter_kernel, rows, starts), out_shape...  65.5 us

profile of v7, /device:TPU:0, one launch (start us, length us, event | category | flops | bytes accessed | tf_op | source)
XLA Modules:
  0.0 694.8 jit_solution(8514820534660534837)
XLA Ops:
  9.4 73.3 %shard_map.280 = (bf16[2048,2048]{1,0:T(8,128)(2,1)}, bf16[8,256,384]{2,1,0:T(8,128)(2,1)}, bf16[8,128,256]{2,1,0:T(8,128)(2,1)}, bf16[8,32,256]{2,1,0:T(8,128)(2,1)}, bf16[352,2048]{1,0:T(8,128)(2,1)}) custom-call(bf16[512,2048]{1,0:T(8,128)(2,1)} %bitcast.123, bf16[4,256,384]{2,1,0:T(8,128)(2,1)} %pad_maximum_fusion.1.refs_1_, ...), custom_call_target="tpu_custom_call" | custom-call | tf_op jit(solution)/shard_map/pallas_call | solution.py:659
  88.3 73.5 %shard_map.281 = (bf16[2048,2048]{1,0:T(8,128)(2,1)}, bf16[8,528,256]{2,1,0:T(8,128)(2,1)}, bf16[352,2048]{1,0:T(8,128)(2,1)}, bf16[2048,2048]{1,0:T(8,128)(2,1)...) custom-call(bf16[512,2048]{1,0:T(8,128)(2,1)} %bitcast.133, ...), custom_call_target="tpu_custom_call" | custom-call | tf_op jit(solution)/shard_map/pallas_call | solution.py:2166
  161.7 65.5 %shard_map.282 = (f32[128,2048]{1,0:T(8,128)S(1)}, bf16[352,2048]{1,0:T(8,128)(2,1)S(1)}, bf16[352,2048]{1,0:T(8,128)(2,1)S(1)}) custom-call(bf16[2048,2048]{1,0:T(8,128)(2,1)} %get-tuple-element.87.in_ref, bf16[704,2048]{1,0:T(8,128)(2,1)S(1)} %bitcast.113, bf16[704,2048]{1,0:T(8,128)(2,1)S(1)} %bitcast.114), custom_call_target="tpu_custom_call" | custom-call | tf_op jit(solution)/shard_map/pallas_call | solution.py:834
  227.2 1.7 multiply_reduce_fusion.2
  230.2 82.8 %shard_map.283 = (bf16[2048,2048]{1,0:T(8,128)(2,1)}, bf16[1024,2048]{1,0:T(8,128)(2,1)}, bf16[1024,2048]{1,0:T(8,128)(2,1)}, bf16[2,1024,704]{2,1,0:T(8,128)(2,...) custom-call(bf16[128,2048]{1,0:T(8,128)(2,1)} %copy-done.6, ...), custom_call_target="tpu_custom_call" | custom-call | tf_op jit(solution)/shard_map/pallas_call | solution.py:1157
  313.0 84.6 %shard_map.284 = (f32[128,2176]{1,0:T(8,128)}, bf16[352,2048]{1,0:T(8,128)(2,1)}, bf16[352,2048]{1,0:T(8,128)(2,1)}, bf16[352,2048]{1,0:T(8,128)(2,1)}, bf16[352...) custom-call(bf16[4,256,512]{2,1,0:T(8,128)(2,1)} %compare_convert_fusion.refs_2_.refs_0_.refs_1_, ...), custom_call_target="tpu_custom_call" | custom-call | tf_op jit(solution)/shard_map/pallas_call | solution.py:1334
  399.9 2.1 multiply_reduce_fusion
  403.1 2.2 fusion.23.refs_0_
  405.3 69.0 %shard_map.285 = (bf16[2048,2048]{1,0:T(8,128)(2,1)}, bf16[2048,2048]{1,0:T(8,128)(2,1)}, bf16[8,528,256]{2,1,0:T(8,128)(2,1)}, bf16[352,2048]{1,0:T(8,128)(2,1)}, bf16[352,2048]{1,0:T(8,128)(2,1)}) custom-call(bf16[128,2048]{1,0:T(8,128)(2,1)} %fusion.23.refs_0_, bf16[4,256,512]{2,1,0:T(8,128)(2,1)} %compare_convert_fusion.refs_2_.refs_0_.refs_1_, ...), custom_call_target="tpu_custom_call" | custom-call | tf_op jit(solution)/shard_map/pallas_call | solution.py:1667
  474.3 69.6 %shard_map.286 = (f32[128,2048]{1,0:T(8,128)}, bf16[2048,2048]{1,0:T(8,128)(2,1)}, bf16[8,512,256]{2,1,0:T(8,128)(2,1)}, bf16[352,2048]{1,0:T(8,128)(2,1)}, bf16[352,2048]{1,0:T(8,128)(2,1)}) custom-call(bf16[128,2048]{1,0:T(8,128)(2,1)} %get-tuple-element.80.refs_0_, bf16[384,2048]{1,0:T(8,128)(2,1)} %get-tuple-element.81.refs_1_, ...), custom_call_target="tpu_custom_call" | custom-call | tf_op jit(solution)/shard_map/pallas_call | solution.py:1532
  544.0 2.5 add_convert_fusion.refs_6_
  546.4 91.7 %shard_map.287 = (f32[128,2048]{1,0:T(8,128)}, bf16[352,2048]{1,0:T(8,128)(2,1)}, f32[704,2048]{1,0:T(8,128)}, f32[704,2048]{1,0:T(8,128)}, f32[704,2048]{1,0:T(...) custom-call(bf16[2048,2048]{1,0:T(8,128)(2,1)} %get-tuple-element.11, ...), custom_call_target="tpu_custom_call" | custom-call | tf_op jit(solution)/shard_map/pallas_call | solution.py:1913
  638.1 1.9 fusion.6
  640.1 3.0 fusion.2.tokens_ref
  644.4 24.7 %shard_map.288 = (bf16[512,2048]{1,0:T(8,128)(2,1)}, f32[8,256]{1,0:T(8,128)}, f32[32,256]{1,0:T(8,128)}) custom-call(bf16[128,2048]{1,0:T(8,128)(2,1)} %fusion.2.tokens_ref, f32[8,8,256]{2,1,0:T(8,128)} %pad.19.gain_ref, f32[32,256]{1,0:T(8,128)} %convert_reduce_fusion.small_ref), custom_call_target="tpu_custom_call" | custom-call | tf_op jit(solution)/shard_map/pallas_call | solution.py:2010
  669.1 1.3 slice.54
  671.6 1.3 slice_bitcast_fusion.1
  675.1 2.2 copy.68
  678.3 1.4 fusion.24
  679.7 3.9 copy.84
  683.6 1.3 copy.85
  684.9 2.9 copy.86
  687.9 2.9 copy.87
  691.8 2.5 copy.88
  (104 shorter events, 25.5 us)
Async XLA Ops:
  0.6 6.3 copy-start.16
  5.4 2.9 copy-start.13
  5.4 2.9 copy-start.14
  5.4 2.9 copy-start.15
  88.3 73.5 %copy-start = (bf16[1,2048,704]{1,2,0:T(8,128)(2,1)S(1)}, bf16[1,2048,704]{1,2,0:T(8,128)(2,1)}, u32[]{:S(2)}) copy-start(bf16[1,2048,704]{1,2,0:T(8,128)(2,1)} %param.30) | copy-start | bytes 8650756
  227.2 1.9 copy-start.1
  227.2 1.9 copy-start.2
  229.0 1.0 copy-start.3
  229.2 1.1 copy-start.6
  313.0 85.7 %copy-start.7 = (bf16[128,2048]{1,0:T(8,128)(2,1)S(1)}, bf16[128,2048]{1,0:T(8,128)(2,1)}, u32[]{:S(2)}) copy-start(bf16[128,2048]{1,0:T(8,128)(2,1)} %copy-done.6) | copy-start | bytes 1572868
  397.6 5.4 copy-start.4
  402.1 1.0 copy-start.10
  546.4 93.6 %copy-start.11 = (f32[128,2048]{1,0:T(8,128)S(1)}, f32[128,2048]{1,0:T(8,128)}, u32[]{:S(2)}) copy-start(f32[128,2048]{1,0:T(8,128)} %copy-done.10) | copy-start | bytes 3145732
  638.1 1.9 copy-start.5
  640.0 3.1 copy-start.17
  640.0 32.9 %copy-start.9 = (bf16[4,512,256]{2,1,0:T(8,128)(2,1)S(1)}, bf16[4,512,256]{2,1,0:T(8,128)(2,1)}, u32[]{:S(2)}) copy-start(bf16[4,512,256]{2,1,0:T(8,128)(2,1)} %get-tuple-element.131) | copy-start | bytes 3145732
  674.1 4.2 copy-start.8
  675.1 9.8 %slice-start.4 = ((s8[5767168]{0:T(1024)(128)(4,1)}), s8[1572864]{0:T(1024)(128)(4,1)S(1)}, s32[]{:S(2)}) async-start(s8[5767168]{0:T(1024)(128)(4,1)} %bitcast.130), calls=%async_computation.4 | async-start | bytes 3145728
  678.3 5.3 copy-start.12
  678.3 9.6 %slice-start.2 = ((s8[5767168]{0:T(1024)(128)(4,1)}), s8[4194304]{0:T(1024)(128)(4,1)S(1)}, s32[]{:S(2)}) async-start(s8[5767168]{0:T(1024)(128)(4,1)} %bitcast.127), calls=%async_computation.2 | async-start | bytes 8388608
  679.7 5.3 slice-start.5
  683.6 4.3 slice-start.3
  684.9 5.8 slice-start
  687.9 4.0 slice-start.1

commit v8 on v7

--- a/solution.py
+++ b/solution.py
@@ -1881,12 +1881,11 @@
     home.line(3)
     total.second(3, "middle")
     total.second(2, "end")
-    home.line(2)
     gradient(1)
     total.second(2, "middle")
-    total.second(1, "end")
+    home.line(2)
+    total.second(1)
     home.line(1)
-    total.second(1, "middle")
     home.line(0)
     sharing.forward()
     loads[9].wait()

time: 699 us -> 694 us (level)
  no operation moved by 1% of the time
where the time goes in v8:
time: 694 us; the launch traced here: 690 us
  Pallas kernels  630 us (91%)
  local copies, waits for them, and re-layouts  35.7 us (5%)
  other arithmetic  19.4 us (3%)
    pallas_call x1, Pallas kernels, last_rows(): pl.pallas_call(last_scatter_kernel, out_shape=[shape((rows, width), F32),...  91.7 us
    pallas_call x1, Pallas kernels, expert_back(): pl.pallas_call(expert_scatter_kernel, out_shape=[shape((rows, full), F32)...  84.6 us
    pallas_call x1, Pallas kernels, expert_rows(): pl.pallas_call(functools.partial(expert_gather_kernel, experts), out_shap...  82.8 us
    pallas_call x1, Pallas kernels, front(): pl.pallas_call(functools.partial(front_kernel, HDIM ** (-0.5)), out_shape...  73.5 us
    pallas_call x1, Pallas kernels, all_rows(): pl.pallas_call(functools.partial(gather_kernel, block, rows, parts, extra...  73.3 us
    pallas_call x1, Pallas kernels, mixed_rows(): pl.pallas_call(mixed_kernel, out_shape=[shape((rows, width), F32), shape(...  69.6 us
    pallas_call x1, Pallas kernels, gather_back(): pl.pallas_call(gather_back_kernel, out_shape=[shape((length, width), BF),...  69 us
    pallas_call x1, Pallas kernels, own_rows(): pl.pallas_call(functools.partial(scatter_kernel, rows, starts), out_shape...  65.5 us

profile of v8, /device:TPU:0, one launch (start us, length us, event | category | flops | bytes accessed | tf_op | source)
XLA Modules:
  0.0 689.7 jit_solution(15248173889396376743)
XLA Ops:
  9.4 73.3 %shard_map.280 = (bf16[2048,2048]{1,0:T(8,128)(2,1)}, bf16[8,256,384]{2,1,0:T(8,128)(2,1)}, bf16[8,128,256]{2,1,0:T(8,128)(2,1)}, bf16[8,32,256]{2,1,0:T(8,128)(2,1)}, bf16[352,2048]{1,0:T(8,128)(2,1)}) custom-call(bf16[512,2048]{1,0:T(8,128)(2,1)} %bitcast.123, bf16[4,256,384]{2,1,0:T(8,128)(2,1)} %pad_maximum_fusion.1.refs_1_, ...), custom_call_target="tpu_custom_call" | custom-call | tf_op jit(solution)/shard_map/pallas_call | solution.py:659
  88.3 73.5 %shard_map.281 = (bf16[2048,2048]{1,0:T(8,128)(2,1)}, bf16[8,528,256]{2,1,0:T(8,128)(2,1)}, bf16[352,2048]{1,0:T(8,128)(2,1)}, bf16[2048,2048]{1,0:T(8,128)(2,1)...) custom-call(bf16[512,2048]{1,0:T(8,128)(2,1)} %bitcast.133, ...), custom_call_target="tpu_custom_call" | custom-call | tf_op jit(solution)/shard_map/pallas_call | solution.py:2165
  161.7 65.5 %shard_map.282 = (f32[128,2048]{1,0:T(8,128)S(1)}, bf16[352,2048]{1,0:T(8,128)(2,1)S(1)}, bf16[352,2048]{1,0:T(8,128)(2,1)S(1)}) custom-call(bf16[2048,2048]{1,0:T(8,128)(2,1)} %get-tuple-element.87.in_ref, bf16[704,2048]{1,0:T(8,128)(2,1)S(1)} %bitcast.113, bf16[704,2048]{1,0:T(8,128)(2,1)S(1)} %bitcast.114), custom_call_target="tpu_custom_call" | custom-call | tf_op jit(solution)/shard_map/pallas_call | solution.py:834
  227.2 1.7 multiply_reduce_fusion.2
  230.2 82.8 %shard_map.283 = (bf16[2048,2048]{1,0:T(8,128)(2,1)}, bf16[1024,2048]{1,0:T(8,128)(2,1)}, bf16[1024,2048]{1,0:T(8,128)(2,1)}, bf16[2,1024,704]{2,1,0:T(8,128)(2,...) custom-call(bf16[128,2048]{1,0:T(8,128)(2,1)} %copy-done.6, ...), custom_call_target="tpu_custom_call" | custom-call | tf_op jit(solution)/shard_map/pallas_call | solution.py:1157
  313.0 84.6 %shard_map.284 = (f32[128,2176]{1,0:T(8,128)}, bf16[352,2048]{1,0:T(8,128)(2,1)}, bf16[352,2048]{1,0:T(8,128)(2,1)}, bf16[352,2048]{1,0:T(8,128)(2,1)}, bf16[352...) custom-call(bf16[4,256,512]{2,1,0:T(8,128)(2,1)} %compare_convert_fusion.refs_2_.refs_0_.refs_1_, ...), custom_call_target="tpu_custom_call" | custom-call | tf_op jit(solution)/shard_map/pallas_call | solution.py:1334
  399.9 2.1 multiply_reduce_fusion
  403.1 2.2 fusion.23.refs_0_
  405.3 69.0 %shard_map.285 = (bf16[2048,2048]{1,0:T(8,128)(2,1)}, bf16[2048,2048]{1,0:T(8,128)(2,1)}, bf16[8,528,256]{2,1,0:T(8,128)(2,1)}, bf16[352,2048]{1,0:T(8,128)(2,1)}, bf16[352,2048]{1,0:T(8,128)(2,1)}) custom-call(bf16[128,2048]{1,0:T(8,128)(2,1)} %fusion.23.refs_0_, bf16[4,256,512]{2,1,0:T(8,128)(2,1)} %compare_convert_fusion.refs_2_.refs_0_.refs_1_, ...), custom_call_target="tpu_custom_call" | custom-call | tf_op jit(solution)/shard_map/pallas_call | solution.py:1667
  474.3 69.6 %shard_map.286 = (f32[128,2048]{1,0:T(8,128)}, bf16[2048,2048]{1,0:T(8,128)(2,1)}, bf16[8,512,256]{2,1,0:T(8,128)(2,1)}, bf16[352,2048]{1,0:T(8,128)(2,1)}, bf16[352,2048]{1,0:T(8,128)(2,1)}) custom-call(bf16[128,2048]{1,0:T(8,128)(2,1)} %get-tuple-element.80.refs_0_, bf16[384,2048]{1,0:T(8,128)(2,1)} %get-tuple-element.81.refs_1_, ...), custom_call_target="tpu_custom_call" | custom-call | tf_op jit(solution)/shard_map/pallas_call | solution.py:1532
  544.0 2.5 add_convert_fusion.refs_6_
  546.4 91.7 %shard_map.287 = (f32[128,2048]{1,0:T(8,128)}, bf16[352,2048]{1,0:T(8,128)(2,1)}, f32[704,2048]{1,0:T(8,128)}, f32[704,2048]{1,0:T(8,128)}, f32[704,2048]{1,0:T(...) custom-call(bf16[2048,2048]{1,0:T(8,128)(2,1)} %get-tuple-element.11, ...), custom_call_target="tpu_custom_call" | custom-call | tf_op jit(solution)/shard_map/pallas_call | solution.py:1912
  638.1 1.9 fusion.6
  640.1 3.0 fusion.2.tokens_ref
  644.4 19.6 %shard_map.288 = (bf16[512,2048]{1,0:T(8,128)(2,1)}, f32[8,256]{1,0:T(8,128)}, f32[32,256]{1,0:T(8,128)}) custom-call(bf16[128,2048]{1,0:T(8,128)(2,1)} %fusion.2.tokens_ref, f32[8,8,256]{2,1,0:T(8,128)} %pad.19.gain_ref, f32[32,256]{1,0:T(8,128)} %convert_reduce_fusion.small_ref), custom_call_target="tpu_custom_call" | custom-call | tf_op jit(solution)/shard_map/pallas_call | solution.py:2009
  664.0 1.3 slice.54
  666.5 1.3 slice_bitcast_fusion.1
  670.0 2.2 copy.68
  673.2 1.4 fusion.24
  674.6 3.9 copy.84
  678.5 1.3 copy.85
  679.9 2.9 copy.86
  682.8 2.9 copy.87
  686.8 2.5 copy.88
  (104 shorter events, 25.5 us)
Async XLA Ops:
  0.6 6.3 copy-start.16
  5.4 2.9 copy-start.13
  5.4 2.9 copy-start.14
  5.4 2.9 copy-start.15
  88.3 73.5 %copy-start = (bf16[1,2048,704]{1,2,0:T(8,128)(2,1)S(1)}, bf16[1,2048,704]{1,2,0:T(8,128)(2,1)}, u32[]{:S(2)}) copy-start(bf16[1,2048,704]{1,2,0:T(8,128)(2,1)} %param.30) | copy-start | bytes 8650756
  227.2 1.9 copy-start.1
  227.2 1.9 copy-start.2
  229.0 1.0 copy-start.3
  229.2 1.1 copy-start.6
  313.0 85.7 %copy-start.7 = (bf16[128,2048]{1,0:T(8,128)(2,1)S(1)}, bf16[128,2048]{1,0:T(8,128)(2,1)}, u32[]{:S(2)}) copy-start(bf16[128,2048]{1,0:T(8,128)(2,1)} %copy-done.6) | copy-start | bytes 1572868
  397.6 5.4 copy-start.4
  402.1 1.0 copy-start.10
  546.4 93.6 %copy-start.11 = (f32[128,2048]{1,0:T(8,128)S(1)}, f32[128,2048]{1,0:T(8,128)}, u32[]{:S(2)}) copy-start(f32[128,2048]{1,0:T(8,128)} %copy-done.10) | copy-start | bytes 3145732
  638.1 1.9 copy-start.5
  640.0 3.1 copy-start.17
  640.0 27.8 %copy-start.9 = (bf16[4,512,256]{2,1,0:T(8,128)(2,1)S(1)}, bf16[4,512,256]{2,1,0:T(8,128)(2,1)}, u32[]{:S(2)}) copy-start(bf16[4,512,256]{2,1,0:T(8,128)(2,1)} %get-tuple-element.131) | copy-start | bytes 3145732
  669.0 4.2 copy-start.8
  670.0 9.8 %slice-start.4 = ((s8[5767168]{0:T(1024)(128)(4,1)}), s8[1572864]{0:T(1024)(128)(4,1)S(1)}, s32[]{:S(2)}) async-start(s8[5767168]{0:T(1024)(128)(4,1)} %bitcast.130), calls=%async_computation.4 | async-start | bytes 3145728
  673.2 5.3 copy-start.12
  673.2 9.6 %slice-start.2 = ((s8[5767168]{0:T(1024)(128)(4,1)}), s8[4194304]{0:T(1024)(128)(4,1)S(1)}, s32[]{:S(2)}) async-start(s8[5767168]{0:T(1024)(128)(4,1)} %bitcast.127), calls=%async_computation.2 | async-start | bytes 8388608
  674.6 5.3 slice-start.5
  678.5 4.3 slice-start.3
  679.9 5.8 slice-start
  682.8 4.0 slice-start.1
